TPU v7x, 32 devices: a whole 2x2x4 slice. The times are simulated.
32 devices in a mesh: groups: 2 (over y), row: 4 (over z), col: 4 (over x, core).
Axes of the slice: x: 2, y: 2, z: 4, core: 2. Of those that a mesh axis runs over, the one named last changes fastest.
Arguments:
- a_tiles: bfloat16 [16, 16, 128, 128], P(('groups', 'row'), 'col'), parts along dimension 0, may hold values from -0.1875 to 0.1875
- a_cols: int32 [16, 16], P(('groups', 'row'), 'col'), parts along dimension 0, may hold values from -1 to 7, as said below
- b_tiles: bfloat16 [16, 32, 128, 128], P(('groups', 'row'), 'col'), parts along dimension 0, may hold values from -6 to 6
- b_cols: int32 [16, 32], P(('groups', 'row'), 'col'), parts along dimension 0, may hold values from 0 to 63, as said below
- c_cols: int32 [16, 24], P(('groups', 'row'), 'col'), parts along dimension 0, may hold values from 0 to 63, as said below
Outputs:
- c_tiles: bfloat16 [16, 24, 128, 128], P(('groups', 'row'), 'col'), parts along dimension 0
There are 2 independent parts, one for each index of `groups`. A program takes and returns all parts, laid end to end along the dimension named above; each array names one. Nothing has to cross between parts.
Inputs may be any that keep to these rules, and one draw needn't show every extreme that they name: `a_cols`: within a row the indices that are not -1 are distinct; -1 marks an empty slot and row 0 has no empty slot among its first min(16, 8) slots. `b_cols`: slots q * 8 to (q + 1) * 8 - 1 of a row hold distinct columns of q * 16 to (q + 1) * 16 - 1. `c_cols`: slots q * 6 to (q + 1) * 6 - 1 of a row hold distinct columns of q * 16 to (q + 1) * 16 - 1.
All inputs are finite; a program needn't handle non-finite values.
Results may differ from a plain program's by a relative error of at most 0.001.
Values may be sent and summed in bfloat16 or wider, within the bound.
No kernel may reach another device: no remote copies, remote signals or barrier semaphores. Data moves between devices by JAX's collectives and lax.ppermute only.
A program may use at most 192 MiB of HBM per device.

v0:
```python
import jax
import jax.numpy as jnp
from jax import lax
from jax.sharding import PartitionSpec as P

COLS_DEV = 16


def body(a_tiles, a_cols, b_tiles, b_cols, c_cols):
    left_all, left_index = (
        lax.all_gather(a_tiles, "col", axis=1, tiled=True),
        lax.all_gather(a_cols, "col", axis=1, tiled=True),
    )
    rows = left_all.shape[0]
    block = left_all.shape[-1]
    width = COLS_DEV
    first = lax.axis_index("col") * width
    span = jnp.arange(width, dtype=jnp.int32)
    pick = ((b_cols - first)[:, :, None] == span[None, None, :]).astype(jnp.bfloat16)
    slab = jnp.einsum("mlc,mlyz->mycz", pick, b_tiles, preferred_element_type=jnp.float32)
    prepared = slab.astype(jnp.bfloat16)
    slab = lax.all_gather(prepared, "row", axis=0, tiled=True)
    count = slab.shape[0]
    inner = jnp.arange(count, dtype=jnp.int32)
    pick = ((left_index - jnp.int32(0))[:, :, None] == inner[None, None, :]).astype(jnp.bfloat16)
    chosen = jnp.einsum("ikm,ikxy->ixmy", pick, left_all, preferred_element_type=jnp.float32)
    chosen = chosen.astype(jnp.bfloat16).reshape(rows * block, count * block)
    right = slab.reshape(count * block, width * block)
    total = jnp.dot(chosen, right, preferred_element_type=jnp.float32)
    grid = total.reshape(rows, block, width, block)
    local = c_cols - first
    picked = jnp.take_along_axis(grid, local[:, None, :, None], axis=2)
    return picked.transpose(0, 2, 1, 3).astype(jnp.bfloat16)


def solution(mesh):
    return jax.shard_map(
        body,
        mesh=mesh,
        in_specs=(
            P(("groups", "row"), "col", None, None),
            P(("groups", "row"), "col"),
            P(("groups", "row"), "col", None, None),
            P(("groups", "row"), "col"),
            P(("groups", "row"), "col"),
        ),
        out_specs=P(("groups", "row"), "col", None, None),
        check_vma=False,
    )
```

profile of v0, /device:TPU:0, one launch (start us, length us, event | category | flops | bytes accessed | tf_op | source)
XLA Modules:
  0.0 135.3 jit_solution(17135707577522388599)
XLA Ops:
  6.5 0.0 copy-start
  6.5 0.0 all-gather.4.cloned.1.call-start
  6.5 1.7 %copy.11 = bf16[2,4,128,128]{3,2,0,1:T(8,128)(2,1)} copy(bf16[2,4,128,128]{3,2,1,0:T(8,128)(2,1)} %param.5) | data formatting | bytes 524288 | tf_op args[0]
  8.3 0.0 all-gather.4.cloned.1.call-update
  8.3 0.0 all-gather.6.cloned.1.call-start
  8.3 0.7 broadcast_subtract_fusion
  9.0 0.0 copy-done
  9.0 1.6 %fusion = bf16[2,128,16,128]{3,2,1,0:T(8,128)(2,1)} fusion(bf16[2,8,128,128]{3,2,1,0:T(8,128)(2,1)S(1)} %copy-done, s32[2,8]{1,0:T(2,128)S(1)} %broadcast_subtract_fusion), kind=kOutput, calls=%fused_computation.3 | convolution fusion | flops 8913152 | bytes 1572928 | tf_op jit(solution)/shard_map/mlc,mlyz->mycz/dot_general | solution.py:20
  10.6 0.0 all-gather.6.cloned.1.call-update
  10.7 6.3 %all-gather = s32[4,4,2]{1,2,0:T(2,128)S(1)} all-gather(s32[1,4,2]{1,2,0:T(2,128)} %bitcast.46), channel_id=1, replica_groups=mesh['groups'=2,'row'=4,'col'=4] {'col'}, dimensions={0}, use_global_device_ids=true | all-gather | bytes 160 | tf_op jit(solution)/shard_map/all_gather | solution.py:12
  16.9 0.1 reshape.44
  17.0 0.7 bitcast_or_fusion
  17.7 0.1 reshape.32
  17.8 0.7 compare_and_fusion
  18.5 9.9 %all-gather.4.cloned.1.call-done = bf16[2,16,128,128]{3,2,0,1:T(8,128)(2,1)} async-done(((bf16[2,4,128,128]{3,2,0,1:T(8,128)(2,1)}), bf16[2,16,128,128]{3,2,0,1:T(8,128)(2,1)}) %all-gather.4.cloned.1.call-update) | async-done | bytes 1048592 | tf_op jit(solution)/shard_map/all_gather | solution.py:11
  28.4 1.9 %fusion.1 = bf16[2,128,8,128]{3,2,1,0:T(8,128)(2,1)S(1)} fusion(bf16[2,16,128,128]{3,2,0,1:T(8,128)(2,1)} %all-gather.4.cloned.1.call-done, s32[2,16]{1,0:T(2,128)S(1)} %bitcast.45), kind=kOutput, calls=%fused_computation.5 | convolution fusion | flops 8651008 | bytes 1572992 | tf_op jit(solution)/shard_map/ikm,ikxy->ixmy/dot_general | solution.py:26
  30.3 0.2 reshape.47
  30.5 80.2 %all-gather.6.cloned.1.call-done = bf16[8,128,16,128]{3,2,1,0:T(8,128)(2,1)} async-done(((bf16[2,128,16,128]{3,2,1,0:T(8,128)(2,1)}), bf16[8,128,16,128]{3,2,1,0:T(8,128)(2,1)}) %all-gather.6.cloned.1.call-update) | async-done | bytes 4194320 | tf_op jit(solution)/shard_map/all_gather | solution.py:22
  110.7 6.3 %copy.24 = bf16[128,8,16,128]{3,1,2,0:T(8,128)(2,1)} copy(bf16[128,8,16,128]{3,2,1,0:T(8,128)(2,1)} %bitcast.42) | data formatting | bytes 8388608
  117.0 6.4 %copy.14 = bf16[1024,2048]{0,1:T(8,128)(2,1)} copy(bf16[1024,2048]{1,0:T(8,128)(2,1)} %bitcast.41) | data formatting | bytes 8388608 | tf_op jit(solution)/shard_map/reshape | solution.py:28
  123.4 3.5 %fusion.3 = bf16[2,128,16,128]{3,1,2,0:T(8,128)(2,1)S(1)} fusion(bf16[16,128,1024,1]{2,1,0,3:T(8,128)(2,1)} %bitcast.43, bf16[2,128,1024,1]{2,1,0,3:T(8,128)(2,1)S(1)} %reshape.47), kind=kOutput, calls=%fused_computation.8 | convolution fusion | flops 1073741824 | bytes 5767168 | tf_op jit(solution)/shard_map/dot_general | solution.py:29
  126.9 0.7 gather_fusion
  127.6 0.9 select_convert_fusion
  (1 shorter events, 0.0 us)
Async XLA Ops:
  6.5 2.5 %copy-start = (bf16[2,8,128,128]{3,2,1,0:T(8,128)(2,1)S(1)}, bf16[2,8,128,128]{3,2,1,0:T(8,128)(2,1)}, u32[]{:S(2)}) copy-start(bf16[2,8,128,128]{3,2,1,0:T(8,128)(2,1)} %param.7) | copy-start | bytes 1572868
  6.5 21.8 %all-gather.4.cloned.1.call-start = ((), (), s32[]{:S(2)}) async-start(), calls=%async_computation | async-start | bytes 1310720 | tf_op jit(solution)/shard_map/all_gather | solution.py:11
  8.3 102.4 %all-gather.6.cloned.1.call-start = ((), (), s32[]{:S(2)}) async-start(), calls=%async_computation.1 | async-start | bytes 5242880 | tf_op jit(solution)/shard_map/all_gather | solution.py:22
Sparse Core Ops, SparseCore 0:
  8.9 19.4 all-gather.3
  29.9 80.7 all-gather.5
where the time goes:
time: 136 us; the launch traced here: 135 us
  waiting for transfers between devices  90.2 us (66%)
  local copies, waits for them, and re-layouts  15.5 us (11%)
  between operations  13.4 us (10%)
  matrix products  6.96 us (5%)
  blocking collectives  6.25 us (5%)
  other arithmetic  2.96 us (2%)
    all_gather x1, waiting for transfers between devices, body(): slab = lax.all_gather(prepared, 'row', axis=0, tiled=True)  80.2 us
    all_gather x1, waiting for transfers between devices, body(): lax.all_gather(a_tiles, 'col', axis=1, tiled=True)  9.9 us
    unnamed x5, local copies, waits for them, and re-layouts  8.1 us
    reshape x1, local copies, waits for them, and re-layouts, body(): right = slab.reshape(count * block, width * block)  6.39 us
    all_gather x1, blocking collectives, body(): lax.all_gather(a_cols, 'col', axis=1, tiled=True)  6.25 us
    dot_general x1, matrix products, body(): total = jnp.dot(chosen, right, preferred_element_type=jnp.float32)  3.47 us
  transfers between devices with their start and end apart: 2, of which 2 were waited for; matrix products, arithmetic and copies ran while one was open for 4% of the time, Pallas kernels for 0%

commit v1 on v0

v1 whole, which is shorter than its diff:
```python
import functools

import jax
import jax.numpy as jnp
from jax import lax
from jax.experimental import pallas as pl
from jax.experimental.pallas import tpu as pltpu
from jax.sharding import PartitionSpec as P

COLS_DEV = 16

SMEM = pl.BlockSpec(memory_space=pltpu.SMEM)
VMEM = pl.BlockSpec(memory_space=pltpu.VMEM)


def left_kernel(parts, *refs):
    cols, tiles, dense = refs[:parts], refs[parts : 2 * parts], refs[2 * parts]
    dense[...] = jnp.zeros_like(dense)
    for index, source in zip(cols, tiles):
        for i in range(index.shape[0]):
            for s in range(index.shape[1]):
                inner = index[i, s]

                @pl.when(inner >= 0)
                def _():
                    dense[i, inner] = source[i, s]


def step_kernel(parts, last, place, wanted, *refs):
    cols, refs = refs[:parts], refs[parts:]
    tiles, refs = refs[:parts], refs[parts:]
    dense, before, out, total, right, slot = refs
    first = place[0]
    rows, slots = wanted.shape
    inner_rows, inner_slots, block, _ = tiles[0].shape
    total[...] = before[...]

    for p in range(parts):
        source = place[1 + p]

        @pl.when(source >= 0)
        def _():
            for m in range(inner_rows):
                for c in range(COLS_DEV):
                    slot[m, c] = -1
                for l in range(inner_slots):
                    slot[m, cols[p][m, l] - first] = l
            for i in range(rows):
                for m in range(inner_rows):
                    for j in range(slots):
                        l = slot[m, wanted[i, j] - first]
                        tile = tiles[p][m, jnp.maximum(l, 0)]
                        right[m * block : (m + 1) * block, j * block : (j + 1) * block] = jnp.where(
                            l >= 0, tile, jnp.zeros_like(tile)
                        )
                left = jnp.concatenate(
                    [dense[i, source * inner_rows + m] for m in range(inner_rows)], axis=1
                )
                total[i] += jnp.dot(left, right[...], preferred_element_type=jnp.float32)

    if last:
        for i in range(rows):
            for j in range(slots):
                out[i, j] = total[i, :, j * block : (j + 1) * block].astype(out.dtype)
    else:
        out[...] = total[...]


def body(row_count, col_count, a_tiles, a_cols, b_tiles, b_cols, c_cols):
    rows, slots = c_cols.shape
    inner_rows = b_tiles.shape[0]
    block = a_tiles.shape[-1]
    r = lax.axis_index("row")
    first = lax.axis_index("col") * COLS_DEV

    def ring(x, axis, n, shift):
        return lax.ppermute(x, axis, [(k, (k + shift) % n) for k in range(n)])

    def up(x, s):
        return lax.ppermute(x, "row", [(k, k + 1) for k in range(s, row_count - 1)])

    def down(x, s):
        return lax.ppermute(x, "row", [(k, k - 1) for k in range(1, row_count - s)])

    ups, downs = [b_tiles], [b_tiles]
    for s in range(row_count - 1):
        ups.append(up(ups[-1], s))
        downs.append(down(downs[-1], s))
    b_index = [b_cols] + [ring(b_cols, "row", row_count, s) for s in range(1, row_count)]
    a_index = [a_cols] + [ring(a_cols, "col", col_count, s) for s in range(1, col_count)]
    a_parts = [a_tiles] + [ring(a_tiles, "col", col_count, s) for s in range(1, col_count)]

    dense = pl.pallas_call(
        functools.partial(left_kernel, col_count),
        out_shape=jax.ShapeDtypeStruct((rows, inner_rows * row_count, block, block), a_tiles.dtype),
        in_specs=[SMEM] * col_count + [VMEM] * col_count,
        out_specs=VMEM,
        compiler_params=pltpu.CompilerParams(vmem_limit_bytes=32 * 2**20),
    )(*a_index, *a_parts)

    def step(sources, cols, tiles, before, last):
        parts = len(tiles)
        place = jnp.stack([first] + sources).astype(jnp.int32)
        if last:
            out = jax.ShapeDtypeStruct((rows, slots, block, block), a_tiles.dtype)
        else:
            out = jax.ShapeDtypeStruct((rows, block, slots * block), jnp.float32)
        flops = 2 * rows * parts * inner_rows * slots * block**3
        return pl.pallas_call(
            functools.partial(step_kernel, parts, last),
            out_shape=out,
            in_specs=[SMEM] * (2 + parts) + [VMEM] * (parts + 2),
            out_specs=VMEM,
            scratch_shapes=[
                pltpu.VMEM((rows, block, slots * block), jnp.float32),
                pltpu.VMEM((inner_rows * block, slots * block), b_tiles.dtype),
                pltpu.SMEM((inner_rows, COLS_DEV), jnp.int32),
            ],
            compiler_params=pltpu.CompilerParams(vmem_limit_bytes=32 * 2**20),
            cost_estimate=pl.CostEstimate(flops=flops, bytes_accessed=2**21, transcendentals=0),
        )(place, c_cols, *cols, *tiles, dense, before)

    total = jnp.zeros((rows, block, slots * block), jnp.float32)
    for s in range(1, row_count):
        below = r - s
        above = jnp.where(r + s < row_count, r + s, -1)
        sources, cols, tiles = [below, above], [b_index[s], b_index[row_count - s]], [ups[s], downs[s]]
        if s == 1:
            sources, cols, tiles = [r] + sources, [b_cols] + cols, [b_tiles] + tiles
        total = step(sources, cols, tiles, total, s == row_count - 1)
    return total


def solution(mesh):
    return jax.shard_map(
        functools.partial(body, mesh.shape["row"], mesh.shape["col"]),
        mesh=mesh,
        in_specs=(
            P(("groups", "row"), "col", None, None),
            P(("groups", "row"), "col"),
            P(("groups", "row"), "col", None, None),
            P(("groups", "row"), "col"),
            P(("groups", "row"), "col"),
        ),
        out_specs=P(("groups", "row"), "col", None, None),
        check_vma=False,
    )
```

time: 136 us -> 68.1 us (0.50)
  waiting for transfers between devices: 90.2 us -> 37.8 us
  starting transfers between devices: 0.04 us -> 20.3 us
  between operations: 13.4 us -> 0.17 us
  local copies, waits for them, and re-layouts: 15.5 us -> 2.55 us
  matrix products: 6.96 us -> 0 us
  Pallas kernels: 0 us -> 6.31 us
  blocking collectives: 6.25 us -> 0 us
  other arithmetic: 2.96 us -> 0.15 us
    all_gather x2 -> x0, waiting for transfers between devices: 90.1 us -> none  [the longest x1 80.2 us: body(): slab = lax.all_gather(prepared, 'row', axis=0, tiled=True)]
    ppermute x0 -> x15, waiting for transfers between devices: none -> 37.8 us  [the longest x3 15.9 us: down(): return lax.ppermute(x, 'row', [(k, k - 1) for k in range(1, row_count - s)])]
    ppermute x0 -> x15, starting transfers between devices: none -> 20.3 us  [the longest x9 10.1 us: ring(): return lax.ppermute(x, axis, [(k, (k + shift) % n) for k in range(n)])]
    dot_general x3 -> x0, matrix products: 6.96 us -> none  [the longest x1 3.47 us: body(): total = jnp.dot(chosen, right, preferred_element_type=jnp.float32)]
    reshape x1 -> x0, local copies, waits for them, and re-layouts: 6.39 us -> none  [body(): right = slab.reshape(count * block, width * block)]
    pallas_call x0 -> x4, Pallas kernels: none -> 6.31 us  [the longest x3 4.95 us: step(): pl.pallas_call(functools.partial(step_kernel, parts, last), out_shape=out...]
    all_gather x1 -> x0, blocking collectives: 6.25 us -> none  [body(): lax.all_gather(a_cols, 'col', axis=1, tiled=True)]
    unnamed x5 -> x10, local copies, waits for them, and re-layouts: 8.1 us -> 2.5 us
  transfers between devices with their start and end apart: 2 -> 15, of which waited for: 2 -> 7; matrix products, arithmetic and copies ran while one was open for 4% -> 0% of each run, Pallas kernels for 0% -> 6%
where the time goes in v1:
time: 68.1 us; the launch traced here: 67.3 us
  waiting for transfers between devices  37.8 us (56%)
  starting transfers between devices  20.3 us (30%)
  Pallas kernels  6.31 us (9%)
  local copies, waits for them, and re-layouts  2.55 us (4%)
    ppermute x3, waiting for transfers between devices, down(): return lax.ppermute(x, 'row', [(k, k - 1) for k in range(1, row_count - s)])  15.9 us
    ppermute x9, waiting for transfers between devices, ring(): return lax.ppermute(x, axis, [(k, (k + shift) % n) for k in range(n)])  11.8 us
    ppermute x3, waiting for transfers between devices, up(): return lax.ppermute(x, 'row', [(k, k + 1) for k in range(s, row_count - 1)])  10.2 us
    ppermute x9, starting transfers between devices, ring(): return lax.ppermute(x, axis, [(k, (k + shift) % n) for k in range(n)])  10.1 us
    ppermute x3, starting transfers between devices, up(): return lax.ppermute(x, 'row', [(k, k + 1) for k in range(s, row_count - 1)])  6.33 us
    pallas_call x3, Pallas kernels, step(): pl.pallas_call(functools.partial(step_kernel, parts, last), out_shape=out...  4.95 us
    ppermute x3, starting transfers between devices, down(): return lax.ppermute(x, 'row', [(k, k - 1) for k in range(1, row_count - s)])  3.85 us
    unnamed x10, local copies, waits for them, and re-layouts  2.5 us
  transfers between devices with their start and end apart: 15, of which 7 were waited for; matrix products, arithmetic and copies ran while one was open for 0% of the time, Pallas kernels for 6%

profile of v1, /device:TPU:0, one launch (start us, length us, event | category | flops | bytes accessed | tf_op | source)
XLA Modules:
  0.0 67.3 jit_solution(3589939271927719928)
XLA Ops:
  0.0 5.0 %collective-permute-start.2 = (bf16[2,8,128,128]{3,2,1,0:T(8,128)(2,1)}, bf16[2,8,128,128]{3,2,1,0:T(8,128)(2,1)S(1)}, u32[]{:S(2)}, u32[]{:S(2)}) collective-permute-start(bf16[2,8,128,128]{3,2,1,0:T(8,128)(2,1)} %refs_3_.1), channel_id=1, source_target_pairs={{0,4},{4,8},{8,12},{1,5},{5,9},{9,13},{2,6},{6,10},{10,14},{3,7},{... | collective-permute-start | bytes 1572872 | tf_op jit(solution)/shard_map/ppermute | solution.py:80
  5.0 1.3 %collective-permute-start.5 = (bf16[2,8,128,128]{3,2,1,0:T(8,128)(2,1)}, bf16[2,8,128,128]{3,2,1,0:T(8,128)(2,1)S(1)}, u32[]{:S(2)}, u32[]{:S(2)}) collective-permute-start(bf16[2,8,128,128]{3,2,1,0:T(8,128)(2,1)} %refs_3_.1), channel_id=1, source_target_pairs={{4,0},{8,4},{12,8},{5,1},{9,5},{13,9},{6,2},{10,6},{14,10},{7,3},{... | collective-permute-start | bytes 1572872 | tf_op jit(solution)/shard_map/ppermute | solution.py:83
  6.3 10.1 %collective-permute-done.2.refs_4_ = bf16[2,8,128,128]{3,2,1,0:T(8,128)(2,1)S(1)} collective-permute-done((bf16[2,8,128,128]{3,2,1,0:T(8,128)(2,1)}, bf16[2,8,128,128]{3,2,1,0:T(8,128)(2,1)S(1)}, u32[]{:S(2)}, u32[]{:S(2)}) %collective-permute-start.2) | collective-permute-done | bytes 524320 | tf_op jit(solution)/shard_map/ppermute | solution.py:80
  16.4 0.7 %collective-permute-start.3 = (bf16[2,8,128,128]{3,2,1,0:T(8,128)(2,1)S(1)}, bf16[2,8,128,128]{3,2,1,0:T(8,128)(2,1)S(1)}, u32[]{:S(2)}, u32[]{:S(2)}) collective-permute-start(bf16[2,8,128,128]{3,2,1,0:T(8,128)(2,1)S(1)} %collective-permute-done.2.refs_4_), channel_id=1, source_target_pairs={{4,8},{8,12},{5,9},{9,13},{6,10},{10,14},{7,11},{11,15},{20,24},{2... | collective-permute-start | bytes 1572872 | tf_op jit(solution)/shard_map/ppermute | solution.py:80
  17.1 3.4 %collective-permute-done.5.refs_5_ = bf16[2,8,128,128]{3,2,1,0:T(8,128)(2,1)S(1)} collective-permute-done((bf16[2,8,128,128]{3,2,1,0:T(8,128)(2,1)}, bf16[2,8,128,128]{3,2,1,0:T(8,128)(2,1)S(1)}, u32[]{:S(2)}, u32[]{:S(2)}) %collective-permute-start.5) | collective-permute-done | bytes 524320 | tf_op jit(solution)/shard_map/ppermute | solution.py:83
  20.4 1.3 %collective-permute-start.6 = (bf16[2,8,128,128]{3,2,1,0:T(8,128)(2,1)S(1)}, bf16[2,8,128,128]{3,2,1,0:T(8,128)(2,1)S(1)}, u32[]{:S(2)}, u32[]{:S(2)}) collective-permute-start(bf16[2,8,128,128]{3,2,1,0:T(8,128)(2,1)S(1)} %collective-permute-done.5.refs_5_), channel_id=1, source_target_pairs={{4,0},{8,4},{5,1},{9,5},{6,2},{10,6},{7,3},{11,7},{20,16},{24,20},... | collective-permute-start | bytes 1572872 | tf_op jit(solution)/shard_map/ppermute | solution.py:83
  21.7 0.7 %collective-permute-start.4 = (bf16[2,8,128,128]{3,2,1,0:T(8,128)(2,1)S(1)}, bf16[2,8,128,128]{3,2,1,0:T(8,128)(2,1)S(1)}, u32[]{:S(2)}, u32[]{:S(2)}) collective-permute-start(bf16[2,8,128,128]{3,2,1,0:T(8,128)(2,1)S(1)} %collective-permute-done.3.refs_2_), channel_id=1, source_target_pairs={{8,12},{9,13},{10,14},{11,15},{24,28},{25,29},{26,30},{27,31}} | collective-permute-start | bytes 1572872 | tf_op jit(solution)/shard_map/ppermute | solution.py:80
  22.5 12.5 %collective-permute-done.6.refs_3_ = bf16[2,8,128,128]{3,2,1,0:T(8,128)(2,1)S(1)} collective-permute-done((bf16[2,8,128,128]{3,2,1,0:T(8,128)(2,1)S(1)}, bf16[2,8,128,128]{3,2,1,0:T(8,128)(2,1)S(1)}, u32[]{:S(2)}, u32[]{:S(2)}) %collective-permute-start.6) | collective-permute-done | bytes 524320 | tf_op jit(solution)/shard_map/ppermute | solution.py:83
  35.0 1.3 %collective-permute-start.7 = (bf16[2,8,128,128]{3,2,1,0:T(8,128)(2,1)S(1)}, bf16[2,8,128,128]{3,2,1,0:T(8,128)(2,1)S(1)}, u32[]{:S(2)}, u32[]{:S(2)}) collective-permute-start(bf16[2,8,128,128]{3,2,1,0:T(8,128)(2,1)S(1)} %collective-permute-done.6.refs_3_), channel_id=1, source_target_pairs={{4,0},{5,1},{6,2},{7,3},{20,16},{21,17},{22,18},{23,19}} | collective-permute-start | bytes 1572872 | tf_op jit(solution)/shard_map/ppermute | solution.py:83
  36.3 0.1 collective-permute-start.11
  36.3 1.6 %collective-permute-start.12 = (bf16[2,4,128,128]{3,2,1,0:T(8,128)(2,1)}, bf16[2,4,128,128]{3,2,1,0:T(8,128)(2,1)}, u32[]{:S(2)}, u32[]{:S(2)}) collective-permute-start(bf16[2,4,128,128]{3,2,1,0:T(8,128)(2,1)} %refs_4_.1), channel_id=1, source_target_pairs={{0,2},{1,3},{2,0},{3,1},{4,6},{5,7},{6,4},{7,5},{8,10},{9,11},{10,... | collective-permute-start | bytes 786440 | tf_op jit(solution)/shard_map/ppermute | solution.py:77
  37.9 1.4 %collective-permute-start.10 = (s32[2,4]{1,0:T(2,128)}, s32[2,4]{1,0:T(2,128)S(1)}, u32[]{:S(2)}, u32[]{:S(2)}) collective-permute-start(s32[2,4]{1,0:T(2,128)} %refs_0_.2), channel_id=1, source_target_pairs={{0,3},{1,0},{2,1},{3,2},{4,7},{5,4},{6,5},{7,6},{8,11},{9,8},{10,9... | collective-permute-start | bytes 104 | tf_op jit(solution)/shard_map/ppermute | solution.py:77
  39.3 5.6 %collective-permute-done.10.refs_3_ = s32[2,4]{1,0:T(2,128)S(1)} collective-permute-done((s32[2,4]{1,0:T(2,128)}, s32[2,4]{1,0:T(2,128)S(1)}, u32[]{:S(2)}, u32[]{:S(2)}) %collective-permute-start.10) | collective-permute-done | bytes 64 | tf_op jit(solution)/shard_map/ppermute | solution.py:77
  44.9 1.1 %collective-permute-start.8 = (s32[2,4]{1,0:T(2,128)}, s32[2,4]{1,0:T(2,128)S(1)}, u32[]{:S(2)}, u32[]{:S(2)}) collective-permute-start(s32[2,4]{1,0:T(2,128)} %refs_0_.2), channel_id=1, source_target_pairs={{0,1},{1,2},{2,3},{3,0},{4,5},{5,6},{6,7},{7,4},{8,9},{9,10},{10,1... | collective-permute-start | bytes 104 | tf_op jit(solution)/shard_map/ppermute | solution.py:77
  46.0 2.6 %collective-permute-done.8.refs_1_ = s32[2,4]{1,0:T(2,128)S(1)} collective-permute-done((s32[2,4]{1,0:T(2,128)}, s32[2,4]{1,0:T(2,128)S(1)}, u32[]{:S(2)}, u32[]{:S(2)}) %collective-permute-start.8) | collective-permute-done | bytes 64 | tf_op jit(solution)/shard_map/ppermute | solution.py:77
  48.5 0.9 %collective-permute-start.9 = (s32[2,4]{1,0:T(2,128)}, s32[2,4]{1,0:T(2,128)S(1)}, u32[]{:S(2)}, u32[]{:S(2)}) collective-permute-start(s32[2,4]{1,0:T(2,128)} %refs_0_.2), channel_id=1, source_target_pairs={{0,2},{1,3},{2,0},{3,1},{4,6},{5,7},{6,4},{7,5},{8,10},{9,11},{10,... | collective-permute-start | bytes 104 | tf_op jit(solution)/shard_map/ppermute | solution.py:77
  49.4 2.8 %collective-permute-done.9.refs_2_ = s32[2,4]{1,0:T(2,128)S(1)} collective-permute-done((s32[2,4]{1,0:T(2,128)}, s32[2,4]{1,0:T(2,128)S(1)}, u32[]{:S(2)}, u32[]{:S(2)}) %collective-permute-start.9) | collective-permute-done | bytes 64 | tf_op jit(solution)/shard_map/ppermute | solution.py:77
  52.3 0.1 pad_add_fusion.2.place
  52.4 0.1 pad_add_fusion
  52.5 0.6 copy-done.4
  53.1 1.2 %collective-permute-start = (s32[2,8]{1,0:T(2,128)S(1)}, s32[2,8]{1,0:T(2,128)S(1)}, u32[]{:S(2)}, u32[]{:S(2)}) collective-permute-start(s32[2,8]{1,0:T(2,128)S(1)} %copy-done.4), channel_id=1, source_target_pairs={{0,12},{4,0},{8,4},{12,8},{1,13},{5,1},{9,5},{13,9},{2,14},{6,2},{... | collective-permute-start | bytes 200 | tf_op jit(solution)/shard_map/ppermute | solution.py:77
  54.3 1.5 %collective-permute-start.1 = (s32[2,8]{1,0:T(2,128)S(1)}, s32[2,8]{1,0:T(2,128)S(1)}, u32[]{:S(2)}, u32[]{:S(2)}) collective-permute-start(s32[2,8]{1,0:T(2,128)S(1)} %copy-done.4), channel_id=1, source_target_pairs={{0,4},{4,8},{8,12},{12,0},{1,5},{5,9},{9,13},{13,1},{2,6},{6,10},{... | collective-permute-start | bytes 200 | tf_op jit(solution)/shard_map/ppermute | solution.py:77
  55.7 0.8 %collective-permute-done.13.refs_7_ = bf16[2,4,128,128]{3,2,1,0:T(8,128)(2,1)} collective-permute-done((bf16[2,4,128,128]{3,2,1,0:T(8,128)(2,1)}, bf16[2,4,128,128]{3,2,1,0:T(8,128)(2,1)}, u32[]{:S(2)}, u32[]{:S(2)}) %collective-permute-start.13) | collective-permute-done | bytes 262176 | tf_op jit(solution)/shard_map/ppermute | solution.py:77
  56.5 2.4 %collective-permute-start.14 = (s32[2,8]{1,0:T(2,128)S(1)}, s32[2,8]{1,0:T(2,128)S(1)}, u32[]{:S(2)}, u32[]{:S(2)}) collective-permute-start(s32[2,8]{1,0:T(2,128)S(1)} %copy-done.4), channel_id=1, source_target_pairs={{0,8},{4,12},{8,0},{12,4},{1,9},{5,13},{9,1},{13,5},{2,10},{6,14},... | collective-permute-start | bytes 200 | tf_op jit(solution)/shard_map/ppermute | solution.py:77
  58.9 0.9 %copy-done.1 = bf16[2,4,128,128]{3,2,1,0:T(8,128)(2,1)S(1)} copy-done((bf16[2,4,128,128]{3,2,1,0:T(8,128)(2,1)S(1)}, bf16[2,4,128,128]{3,2,1,0:T(8,128)(2,1)}, u32[]{:S(2)}) %copy-start.1) | copy-done | bytes 262168
  59.9 1.4 %shard_map.55.refs_6_.refs_4_ = bf16[2,8,128,128]{3,2,1,0:T(8,128)(2,1)S(1)} custom-call(s32[2,4]{1,0:T(2,128)S(1)} %copy-done.3, s32[2,4]{1,0:T(2,128)S(1)} %collective-permute-done.8.refs_1_, s32[2,4]{1,0:T(2,128)S(1)} %collective-permute-done.9.refs_2_, s32[2,4]{1,0:T(2,128)S(1)} %collective-permute-done.10.refs_3_, ...), custom_call_target="tpu_custom_call" | custom-call | tf_op jit(solution)/shard_map/pallas_call | solution.py:93
  61.3 0.0 copy-start
  61.3 0.1 broadcast_in_dim.3.refs_7_
  61.4 0.9 %copy-done = bf16[2,8,128,128]{3,2,1,0:T(8,128)(2,1)S(1)} copy-done((bf16[2,8,128,128]{3,2,1,0:T(8,128)(2,1)S(1)}, bf16[2,8,128,128]{3,2,1,0:T(8,128)(2,1)}, u32[]{:S(2)}) %copy-start) | copy-done | bytes 524312
  62.3 1.8 %shard_map.56.refs_5_ = f32[2,128,768]{2,1,0:T(8,128)S(1)} custom-call(s32[4]{0:T(128)S(1)} %pad_add_fusion.2.place, s32[2,6]{1,0:T(2,128)S(1)} %copy-done.2, s32[2,8]{1,0:T(2,128)S(1)} %copy-done.4, s32[2,8]{1,0:T(2,128)S(1)} %collective-permute-done.1.refs_1_, s32[2,8]{1,0:T(2,128)S(1)} %collective-permute-done.refs_2_.refs_0_, ...), custom_call_target="tpu_custom_call" | custom-call | flops 301989888 | bytes 2097152 | tf_op jit(solution)/shard_map/pallas_call | solution.py:109
  64.1 1.2 %shard_map.57.refs_5_ = f32[2,128,768]{2,1,0:T(8,128)S(1)} custom-call(s32[3]{0:T(128)S(1)} %get-tuple-element.6.place, s32[2,6]{1,0:T(2,128)S(1)} %copy-done.2, s32[2,8]{1,0:T(2,128)S(1)} %collective-permute-done.14.refs_0_.refs_1_, s32[2,8]{1,0:T(2,128)S(1)} %collective-permute-done.14.refs_0_.refs_1_, ...), custom_call_target="tpu_custom_call" | custom-call | flops 201326592 | bytes 2097152 | tf_op jit(solution)/shard_map/pallas_call | solution.py:109
  65.3 2.0 %shard_map.58 = bf16[2,6,128,128]{3,2,1,0:T(8,128)(2,1)} custom-call(s32[3]{0:T(128)S(1)} %get-tuple-element.5.place, s32[2,6]{1,0:T(2,128)S(1)} %copy-done.2, s32[2,8]{1,0:T(2,128)S(1)} %collective-permute-done.refs_2_.refs_0_, s32[2,8]{1,0:T(2,128)S(1)} %collective-permute-done.1.refs_1_, bf16[2,8,128,128]{3,2,1,0:T(8,128)(2,1)S(1)} %collective-permute-done.4.refs_2_, ...), custom_call_target="tpu_custom_call" | custom-call | flops 201326592 | bytes 2097152 | tf_op jit(solution)/shard_map/pallas_call | solution.py:109
  (15 shorter events, 0.0 us)
Async XLA Ops:
  0.0 16.4 %collective-permute-start.2 = (bf16[2,8,128,128]{3,2,1,0:T(8,128)(2,1)}, bf16[2,8,128,128]{3,2,1,0:T(8,128)(2,1)S(1)}, u32[]{:S(2)}, u32[]{:S(2)}) collective-permute-start(bf16[2,8,128,128]{3,2,1,0:T(8,128)(2,1)} %refs_3_.1), channel_id=1, source_target_pairs={{0,4},{4,8},{8,12},{1,5},{5,9},{9,13},{2,6},{6,10},{10,14},{3,7},{... | collective-permute-start | bytes 1572872 | tf_op jit(solution)/shard_map/ppermute | solution.py:80
  5.0 15.5 %collective-permute-start.5 = (bf16[2,8,128,128]{3,2,1,0:T(8,128)(2,1)}, bf16[2,8,128,128]{3,2,1,0:T(8,128)(2,1)S(1)}, u32[]{:S(2)}, u32[]{:S(2)}) collective-permute-start(bf16[2,8,128,128]{3,2,1,0:T(8,128)(2,1)} %refs_3_.1), channel_id=1, source_target_pairs={{4,0},{8,4},{12,8},{5,1},{9,5},{13,9},{6,2},{10,6},{14,10},{7,3},{... | collective-permute-start | bytes 1572872 | tf_op jit(solution)/shard_map/ppermute | solution.py:83
  16.4 5.3 %collective-permute-start.3 = (bf16[2,8,128,128]{3,2,1,0:T(8,128)(2,1)S(1)}, bf16[2,8,128,128]{3,2,1,0:T(8,128)(2,1)S(1)}, u32[]{:S(2)}, u32[]{:S(2)}) collective-permute-start(bf16[2,8,128,128]{3,2,1,0:T(8,128)(2,1)S(1)} %collective-permute-done.2.refs_4_), channel_id=1, source_target_pairs={{4,8},{8,12},{5,9},{9,13},{6,10},{10,14},{7,11},{11,15},{20,24},{2... | collective-permute-start | bytes 1572872 | tf_op jit(solution)/shard_map/ppermute | solution.py:80
  20.4 14.5 %collective-permute-start.6 = (bf16[2,8,128,128]{3,2,1,0:T(8,128)(2,1)S(1)}, bf16[2,8,128,128]{3,2,1,0:T(8,128)(2,1)S(1)}, u32[]{:S(2)}, u32[]{:S(2)}) collective-permute-start(bf16[2,8,128,128]{3,2,1,0:T(8,128)(2,1)S(1)} %collective-permute-done.5.refs_5_), channel_id=1, source_target_pairs={{4,0},{8,4},{5,1},{9,5},{6,2},{10,6},{7,3},{11,7},{20,16},{24,20},... | collective-permute-start | bytes 1572872 | tf_op jit(solution)/shard_map/ppermute | solution.py:83
  21.7 43.6 %collective-permute-start.4 = (bf16[2,8,128,128]{3,2,1,0:T(8,128)(2,1)S(1)}, bf16[2,8,128,128]{3,2,1,0:T(8,128)(2,1)S(1)}, u32[]{:S(2)}, u32[]{:S(2)}) collective-permute-start(bf16[2,8,128,128]{3,2,1,0:T(8,128)(2,1)S(1)} %collective-permute-done.3.refs_2_), channel_id=1, source_target_pairs={{8,12},{9,13},{10,14},{11,15},{24,28},{25,29},{26,30},{27,31}} | collective-permute-start | bytes 1572872 | tf_op jit(solution)/shard_map/ppermute | solution.py:80
  35.0 30.4 %collective-permute-start.7 = (bf16[2,8,128,128]{3,2,1,0:T(8,128)(2,1)S(1)}, bf16[2,8,128,128]{3,2,1,0:T(8,128)(2,1)S(1)}, u32[]{:S(2)}, u32[]{:S(2)}) collective-permute-start(bf16[2,8,128,128]{3,2,1,0:T(8,128)(2,1)S(1)} %collective-permute-done.6.refs_3_), channel_id=1, source_target_pairs={{4,0},{5,1},{6,2},{7,3},{20,16},{21,17},{22,18},{23,19}} | collective-permute-start | bytes 1572872 | tf_op jit(solution)/shard_map/ppermute | solution.py:83
  36.3 16.2 %collective-permute-start.11 = (bf16[2,4,128,128]{3,2,1,0:T(8,128)(2,1)}, bf16[2,4,128,128]{3,2,1,0:T(8,128)(2,1)S(1)}, u32[]{:S(2)}, u32[]{:S(2)}) collective-permute-start(bf16[2,4,128,128]{3,2,1,0:T(8,128)(2,1)} %refs_4_.1), channel_id=1, source_target_pairs={{0,1},{1,2},{2,3},{3,0},{4,5},{5,6},{6,7},{7,4},{8,9},{9,10},{10,1... | collective-permute-start | bytes 786440 | tf_op jit(solution)/shard_map/ppermute | solution.py:77
  36.3 18.0 %collective-permute-start.12 = (bf16[2,4,128,128]{3,2,1,0:T(8,128)(2,1)}, bf16[2,4,128,128]{3,2,1,0:T(8,128)(2,1)}, u32[]{:S(2)}, u32[]{:S(2)}) collective-permute-start(bf16[2,4,128,128]{3,2,1,0:T(8,128)(2,1)} %refs_4_.1), channel_id=1, source_target_pairs={{0,2},{1,3},{2,0},{3,1},{4,6},{5,7},{6,4},{7,5},{8,10},{9,11},{10,... | collective-permute-start | bytes 786440 | tf_op jit(solution)/shard_map/ppermute | solution.py:77
  37.9 7.0 %collective-permute-start.10 = (s32[2,4]{1,0:T(2,128)}, s32[2,4]{1,0:T(2,128)S(1)}, u32[]{:S(2)}, u32[]{:S(2)}) collective-permute-start(s32[2,4]{1,0:T(2,128)} %refs_0_.2), channel_id=1, source_target_pairs={{0,3},{1,0},{2,1},{3,2},{4,7},{5,4},{6,5},{7,6},{8,11},{9,8},{10,9... | collective-permute-start | bytes 104 | tf_op jit(solution)/shard_map/ppermute | solution.py:77
  44.9 3.7 %collective-permute-start.8 = (s32[2,4]{1,0:T(2,128)}, s32[2,4]{1,0:T(2,128)S(1)}, u32[]{:S(2)}, u32[]{:S(2)}) collective-permute-start(s32[2,4]{1,0:T(2,128)} %refs_0_.2), channel_id=1, source_target_pairs={{0,1},{1,2},{2,3},{3,0},{4,5},{5,6},{6,7},{7,4},{8,9},{9,10},{10,1... | collective-permute-start | bytes 104 | tf_op jit(solution)/shard_map/ppermute | solution.py:77
  48.5 3.8 %collective-permute-start.9 = (s32[2,4]{1,0:T(2,128)}, s32[2,4]{1,0:T(2,128)S(1)}, u32[]{:S(2)}, u32[]{:S(2)}) collective-permute-start(s32[2,4]{1,0:T(2,128)} %refs_0_.2), channel_id=1, source_target_pairs={{0,2},{1,3},{2,0},{3,1},{4,6},{5,7},{6,4},{7,5},{8,10},{9,11},{10,... | collective-permute-start | bytes 104 | tf_op jit(solution)/shard_map/ppermute | solution.py:77
  52.3 4.2 %collective-permute-start.13 = (bf16[2,4,128,128]{3,2,1,0:T(8,128)(2,1)}, bf16[2,4,128,128]{3,2,1,0:T(8,128)(2,1)}, u32[]{:S(2)}, u32[]{:S(2)}) collective-permute-start(bf16[2,4,128,128]{3,2,1,0:T(8,128)(2,1)} %refs_4_.1), channel_id=1, source_target_pairs={{0,3},{1,0},{2,1},{3,2},{4,7},{5,4},{6,5},{7,6},{8,11},{9,8},{10,9... | collective-permute-start | bytes 786440 | tf_op jit(solution)/shard_map/ppermute | solution.py:77
  52.4 0.7 %copy-start.4 = (s32[2,8]{1,0:T(2,128)S(1)}, s32[2,8]{1,0:T(2,128)}, u32[]{:S(2)}) copy-start(s32[2,8]{1,0:T(2,128)} %refs_0_.3) | copy-start | bytes 196
  52.4 6.6 %copy-start.3 = (s32[2,4]{1,0:T(2,128)S(1)}, s32[2,4]{1,0:T(2,128)}, u32[]{:S(2)}) copy-start(s32[2,4]{1,0:T(2,128)} %refs_0_.2) | copy-start | bytes 100
  53.1 8.2 %collective-permute-start = (s32[2,8]{1,0:T(2,128)S(1)}, s32[2,8]{1,0:T(2,128)S(1)}, u32[]{:S(2)}, u32[]{:S(2)}) collective-permute-start(s32[2,8]{1,0:T(2,128)S(1)} %copy-done.4), channel_id=1, source_target_pairs={{0,12},{4,0},{8,4},{12,8},{1,13},{5,1},{9,5},{13,9},{2,14},{6,2},{... | collective-permute-start | bytes 200 | tf_op jit(solution)/shard_map/ppermute | solution.py:77
  54.3 7.0 %collective-permute-start.1 = (s32[2,8]{1,0:T(2,128)S(1)}, s32[2,8]{1,0:T(2,128)S(1)}, u32[]{:S(2)}, u32[]{:S(2)}) collective-permute-start(s32[2,8]{1,0:T(2,128)S(1)} %copy-done.4), channel_id=1, source_target_pairs={{0,4},{4,8},{8,12},{12,0},{1,5},{5,9},{9,13},{13,1},{2,6},{6,10},{... | collective-permute-start | bytes 200 | tf_op jit(solution)/shard_map/ppermute | solution.py:77
  56.5 7.6 %collective-permute-start.14 = (s32[2,8]{1,0:T(2,128)S(1)}, s32[2,8]{1,0:T(2,128)S(1)}, u32[]{:S(2)}, u32[]{:S(2)}) collective-permute-start(s32[2,8]{1,0:T(2,128)S(1)} %copy-done.4), channel_id=1, source_target_pairs={{0,8},{4,12},{8,0},{12,4},{1,9},{5,13},{9,1},{13,5},{2,10},{6,14},... | collective-permute-start | bytes 200 | tf_op jit(solution)/shard_map/ppermute | solution.py:77
  58.9 1.0 %copy-start.1 = (bf16[2,4,128,128]{3,2,1,0:T(8,128)(2,1)S(1)}, bf16[2,4,128,128]{3,2,1,0:T(8,128)(2,1)}, u32[]{:S(2)}) copy-start(bf16[2,4,128,128]{3,2,1,0:T(8,128)(2,1)} %refs_4_.1) | copy-start | bytes 786436
  61.3 1.0 %copy-start = (bf16[2,8,128,128]{3,2,1,0:T(8,128)(2,1)S(1)}, bf16[2,8,128,128]{3,2,1,0:T(8,128)(2,1)}, u32[]{:S(2)}) copy-start(bf16[2,8,128,128]{3,2,1,0:T(8,128)(2,1)} %refs_3_.1) | copy-start | bytes 1572868
  61.3 1.0 %copy-start.2 = (s32[2,6]{1,0:T(2,128)S(1)}, s32[2,6]{1,0:T(2,128)}, u32[]{:S(2)}) copy-start(s32[2,6]{1,0:T(2,128)} %wanted.5) | copy-start | bytes 148

commit v2 on v1

v2 whole, which is shorter than its diff:
```python
import functools

import jax
import jax.numpy as jnp
from jax import lax
from jax.experimental import pallas as pl
from jax.experimental.pallas import tpu as pltpu
from jax.sharding import PartitionSpec as P

COLS_DEV = 16

SMEM = pl.BlockSpec(memory_space=pltpu.SMEM)
VMEM = pl.BlockSpec(memory_space=pltpu.VMEM)
PARAMS = pltpu.CompilerParams(vmem_limit_bytes=32 * 2**20)


def left_kernel(index, *refs):
    tiles, dense = refs[:-1], refs[-1]
    dense[...] = jnp.zeros_like(dense)
    rows, slots = tiles[0].shape[:2]
    for p, source in enumerate(tiles):
        for i in range(rows):
            for s in range(slots):
                inner = index[i, p * slots + s]

                @pl.when(inner >= 0)
                def _():
                    dense[i, inner] = source[i, s]


def step_kernel(parts, last, place, wanted, index, *refs):
    tiles, refs = refs[:parts], refs[parts:]
    if last:
        dense, before, out, total, right, slot = refs
        total[...] = before[...]
    elif len(refs) == 5:
        dense, before, total, right, slot = refs
        total[...] = before[...]
    else:
        dense, total, right, slot = refs
        total[...] = jnp.zeros_like(total)
    first, me = place[0], place[1]
    rows, slots = wanted.shape
    inner_slots, block, _ = tiles[0].shape[-3:]

    for p in range(parts):
        source = place[2 + 2 * p]

        @pl.when(source >= 0)
        def _():
            chunk = tiles[p].shape[0]
            held = source ^ me
            per = index.shape[1]
            start = place[3 + 2 * p]
            for m in range(chunk):
                for c in range(COLS_DEV):
                    slot[m, c] = -1
                for l in range(inner_slots):
                    slot[m, index[held, (start + m) * inner_slots + l] - first] = l
            for i in range(rows):
                for m in range(chunk):
                    for j in range(slots):
                        l = slot[m, wanted[i, j] - first]
                        tile = tiles[p][m, jnp.maximum(l, 0)]
                        right[m * block : (m + 1) * block, j * block : (j + 1) * block] = jnp.where(
                            l >= 0, tile, jnp.zeros_like(tile)
                        )
                inner = source * (per // inner_slots) + start
                left = jnp.concatenate([dense[i, inner + m] for m in range(chunk)], axis=1)
                total[i] += jnp.dot(
                    left, right[: chunk * block, :], preferred_element_type=jnp.float32
                )

    if last:
        for i in range(rows):
            for j in range(slots):
                out[i, j] = total[i, :, j * block : (j + 1) * block].astype(out.dtype)


def butterfly(x, axis, n):
    d = 1
    while d < n:
        other = lax.ppermute(x, axis, [(k, k ^ d) for k in range(n)])
        x = jnp.concatenate([x, other], axis=0)
        d *= 2
    return x


def body(row_count, col_count, a_tiles, a_cols, b_tiles, b_cols, c_cols):
    rows, slots = c_cols.shape
    inner_rows, inner_slots = b_cols.shape
    block = a_tiles.shape[-1]
    r = lax.axis_index("row")
    first = lax.axis_index("col") * COLS_DEV
    odd = r % 2

    def pairs(kind, t):
        found = []
        for k in range(row_count):
            side = 1 if k % 2 == kind else -1
            if 0 <= k + side < row_count and 0 <= k + side * t < row_count:
                found.append((k + side, k))
        return found

    def origin(kind, t):
        side = jnp.where(odd == kind, 1, -1)
        row = r + side * t
        return jnp.where((row >= 0) & (row < row_count), row, -1)

    def send(x, kind, t):
        return lax.ppermute(x, "row", pairs(kind, t))

    chunks = [b_tiles[m : m + 1] for m in range(inner_rows)]
    rounds = {1: {}}
    whole = send(b_tiles, 0, 1)
    rounds[1][1] = [send(c, 1, 1) for c in chunks]
    rounds[1][0] = [whole[m : m + 1] for m in range(inner_rows)]
    b_index = butterfly(b_cols.reshape(1, -1), "row", row_count)
    a_index = butterfly(a_cols[None], "col", col_count)
    a_index = a_index.transpose(1, 0, 2).reshape(rows, -1)
    a_parts = [a_tiles] + [
        lax.ppermute(a_tiles, "col", [(k, k ^ d) for k in range(col_count)]) for d in range(1, col_count)
    ]
    dense = pl.pallas_call(
        left_kernel,
        out_shape=jax.ShapeDtypeStruct((rows, inner_rows * row_count, block, block), a_tiles.dtype),
        in_specs=[SMEM] + [VMEM] * col_count,
        out_specs=VMEM,
        compiler_params=PARAMS,
    )(a_index, *a_parts)

    def step(pieces, before, last):
        parts = len(pieces)
        place = [first, r]
        for source, start, _ in pieces:
            place += [source, jnp.int32(start)]
        place = jnp.stack(place).astype(jnp.int32)
        if last:
            out = jax.ShapeDtypeStruct((rows, slots, block, block), a_tiles.dtype)
        else:
            out = jax.ShapeDtypeStruct((rows, block, slots * block), jnp.float32)
        scratch = [
            pltpu.VMEM((inner_rows * block, slots * block), b_tiles.dtype),
            pltpu.SMEM((inner_rows, COLS_DEV), jnp.int32),
        ]
        if last:
            scratch = [pltpu.VMEM((rows, block, slots * block), jnp.float32)] + scratch
        flops = 2 * rows * parts * inner_rows * slots * block**3
        held = [dense] if before is None else [dense, before]
        return pl.pallas_call(
            functools.partial(step_kernel, parts, last),
            out_shape=out,
            in_specs=[SMEM] * 3 + [VMEM] * (parts + len(held)),
            out_specs=VMEM,
            scratch_shapes=scratch,
            compiler_params=PARAMS,
            cost_estimate=pl.CostEstimate(flops=flops, bytes_accessed=2**21, transcendentals=0),
        )(place, c_cols, b_index, *[tiles for _, _, tiles in pieces], *held)

    total = None
    for t in range(1, row_count):
        pieces = [(r, 0, b_tiles), (origin(0, 1), 0, whole)] if t == 1 else []
        for kind in (0, 1):
            if not pairs(kind, t) or (kind, t) == (0, 1):
                continue
            pieces += [(origin(kind, t), m, c) for m, c in enumerate(rounds[t][kind])]
        if t + 1 < row_count:
            rounds[t + 1] = {
                kind: [send(c, kind, t + 1) for c in rounds[t][1 - kind]]
                for kind in (0, 1)
                if pairs(kind, t + 1)
            }
        total = step(pieces, total, t + 1 == row_count)
    return total


def solution(mesh):
    return jax.shard_map(
        functools.partial(body, mesh.shape["row"], mesh.shape["col"]),
        mesh=mesh,
        in_specs=(
            P(("groups", "row"), "col", None, None),
            P(("groups", "row"), "col"),
            P(("groups", "row"), "col", None, None),
            P(("groups", "row"), "col"),
            P(("groups", "row"), "col"),
        ),
        out_specs=P(("groups", "row"), "col", None, None),
        check_vma=False,
    )
```

time: 68.1 us -> 58.3 us (0.86)
  waiting for transfers between devices: 37.8 us -> 30.6 us
  starting transfers between devices: 20.3 us -> 17.5 us
    ppermute x15 -> x16, waiting for transfers between devices: 37.8 us -> 30.6 us  [the longest x9 22.8 us: send(): return lax.ppermute(x, 'row', pairs(kind, t))]
    ppermute x15 -> x16, starting transfers between devices: 20.3 us -> 17.5 us  [the longest x9 10.9 us: send(): return lax.ppermute(x, 'row', pairs(kind, t))]
    unnamed x10 -> x8, local copies, waits for them, and re-layouts: 2.5 us -> 0.14 us
    slice x0 -> x2, local copies, waits for them, and re-layouts: none -> 1.88 us  [the longest x1 1.06 us: body(): chunks = [b_tiles[m:m + 1] for m in range(inner_rows)]]
    reshape x0 -> x2, local copies, waits for them, and re-layouts: none -> 0.84 us  [the longest x1 0.76 us: body(): b_index = butterfly(b_cols.reshape(1, -1), 'row', row_count)]
  transfers between devices with their start and end apart: 15 -> 16, of which waited for: 7 -> 6; matrix products, arithmetic and copies ran while one was open for 0% -> 5% of each run, Pallas kernels for 6% -> 7%
where the time goes in v2:
time: 58.3 us; the launch traced here: 58 us
  waiting for transfers between devices  30.6 us (52%)
  starting transfers between devices  17.5 us (30%)
  Pallas kernels  6.49 us (11%)
  local copies, waits for them, and re-layouts  3.12 us (5%)
    ppermute x9, waiting for transfers between devices, send(): return lax.ppermute(x, 'row', pairs(kind, t))  22.8 us
    ppermute x9, starting transfers between devices, send(): return lax.ppermute(x, 'row', pairs(kind, t))  10.9 us
    ppermute x4, waiting for transfers between devices, butterfly(): other = lax.ppermute(x, axis, [(k, k ^ d) for k in range(n)])  7.84 us
    pallas_call x3, Pallas kernels, step(): pl.pallas_call(functools.partial(step_kernel, parts, last), out_shape=out...  5.61 us
    ppermute x4, starting transfers between devices, butterfly(): other = lax.ppermute(x, axis, [(k, k ^ d) for k in range(n)])  5.02 us
    ppermute x3, starting transfers between devices, body(): lax.ppermute(a_tiles, 'col', [(k, k ^ d) for k in range(col_count)])  1.56 us
  transfers between devices with their start and end apart: 16, of which 6 were waited for; matrix products, arithmetic and copies ran while one was open for 5% of the time, Pallas kernels for 7%

profile of v2, /device:TPU:0, one launch (start us, length us, event | category | flops | bytes accessed | tf_op | source)
XLA Modules:
  0.0 58.0 jit_solution(14975961334562921524)
XLA Ops:
  0.0 3.0 %collective-permute-start.2 = (bf16[2,8,128,128]{3,2,1,0:T(8,128)(2,1)}, bf16[2,8,128,128]{3,2,1,0:T(8,128)(2,1)S(1)}, u32[]{:S(2)}, u32[]{:S(2)}) collective-permute-start(bf16[2,8,128,128]{3,2,1,0:T(8,128)(2,1)} %refs_0_.3), channel_id=1, source_target_pairs={{4,0},{0,4},{12,8},{8,12},{5,1},{1,5},{13,9},{9,13},{6,2},{2,6},{1... | collective-permute-start | bytes 1572872 | tf_op jit(solution)/shard_map/ppermute | solution.py:111
  3.0 1.5 %collective-permute-start.10 = (bf16[2,4,128,128]{3,2,1,0:T(8,128)(2,1)}, bf16[2,4,128,128]{3,2,1,0:T(8,128)(2,1)S(1)}, u32[]{:S(2)}, u32[]{:S(2)}) collective-permute-start(bf16[2,4,128,128]{3,2,1,0:T(8,128)(2,1)} %refs_0_.2), channel_id=1, source_target_pairs={{0,2},{1,3},{2,0},{3,1},{4,6},{5,7},{6,4},{7,5},{8,10},{9,11},{10,... | collective-permute-start | bytes 786440 | tf_op jit(solution)/shard_map/ppermute | solution.py:122
  4.5 0.6 %collective-permute-start.7 = (s32[1,2,4]{2,1,0:T(2,128)S(1)}, s32[1,2,4]{2,1,0:T(2,128)S(1)}, u32[]{:S(2)}, u32[]{:S(2)}) collective-permute-start(s32[1,2,4]{2,1,0:T(2,128)S(1)} %bitcast.10), channel_id=1, source_target_pairs={{0,1},{1,0},{2,3},{3,2},{4,5},{5,4},{6,7},{7,6},{8,9},{9,8},{10,11... | collective-permute-start | bytes 104 | tf_op jit(solution)/shard_map/ppermute | solution.py:83
  5.2 0.8 %reshape.6 = s32[1,16]{1,0:T(1,128)S(1)} reshape(s32[2,8]{1,0:T(2,128)} %param.8) | data formatting | bytes 128 | tf_op jit(solution)/shard_map/reshape | solution.py:118
  6.0 1.1 %fusion = (bf16[1,8,128,128]{3,2,1,0:T(8,128)(2,1)S(1)}, bf16[1,8,128,128]{3,2,1,0:T(8,128)(2,1)S(1)}) fusion(bf16[2,8,128,128]{3,2,1,0:T(8,128)(2,1)} %refs_0_.3), kind=kLoop, calls=%fused_computation.4 | loop fusion | bytes 1048576 | tf_op jit(solution)/shard_map/slice | solution.py:113
  7.1 0.7 %collective-permute-start.12 = (bf16[1,8,128,128]{3,2,1,0:T(8,128)(2,1)S(1)}, bf16[1,8,128,128]{3,2,1,0:T(8,128)(2,1)S(1)}, u32[]{:S(2)}, u32[]{:S(2)}) collective-permute-start(bf16[1,8,128,128]{3,2,1,0:T(8,128)(2,1)S(1)} %get-tuple-element.6), channel_id=1, source_target_pairs={{8,4},{4,8},{9,5},{5,9},{10,6},{6,10},{11,7},{7,11},{24,20},{20,24... | collective-permute-start | bytes 786440 | tf_op jit(solution)/shard_map/ppermute | solution.py:111
  7.8 7.5 %collective-permute-done = s32[1,16]{1,0:T(1,128)S(1)} collective-permute-done((s32[1,16]{1,0:T(1,128)S(1)}, s32[1,16]{1,0:T(1,128)S(1)}, u32[]{:S(2)}, u32[]{:S(2)}) %collective-permute-start) | collective-permute-done | bytes 96 | tf_op jit(solution)/shard_map/ppermute | solution.py:83
  15.2 1.7 %collective-permute-start.8 = (s32[2,2,4]{2,1,0:T(2,128)S(1)}, s32[2,2,4]{2,1,0:T(2,128)S(1)}, u32[]{:S(2)}, u32[]{:S(2)}) collective-permute-start(s32[2,2,4]{2,1,0:T(2,128)S(1)} %pad_add_fusion.1), channel_id=1, source_target_pairs={{0,2},{1,3},{2,0},{3,1},{4,6},{5,7},{6,4},{7,5},{8,10},{9,11},{10,... | collective-permute-start | bytes 200 | tf_op jit(solution)/shard_map/ppermute | solution.py:83
  16.9 2.7 %collective-permute-start.1 = (s32[2,16]{1,0:T(2,128)S(1)}, s32[2,16]{1,0:T(2,128)S(1)}, u32[]{:S(2)}, u32[]{:S(2)}) collective-permute-start(s32[2,16]{1,0:T(2,128)S(1)} %pad_add_fusion.2), channel_id=1, source_target_pairs={{0,8},{4,12},{8,0},{12,4},{1,9},{5,13},{9,1},{13,5},{2,10},{6,14},... | collective-permute-start | bytes 392 | tf_op jit(solution)/shard_map/ppermute | solution.py:83
  19.6 0.8 %fusion.1 = (bf16[1,8,128,128]{3,2,1,0:T(8,128)(2,1)}, bf16[1,8,128,128]{3,2,1,0:T(8,128)(2,1)}) fusion(bf16[2,8,128,128]{3,2,1,0:T(8,128)(2,1)S(1)} %collective-permute-done.2.refs_1_), kind=kLoop, calls=%fused_computation.5 | loop fusion | bytes 1048576 | tf_op jit(solution)/shard_map/slice | solution.py:117
  20.4 0.7 %collective-permute-start.14 = (bf16[1,8,128,128]{3,2,1,0:T(8,128)(2,1)S(1)}, bf16[1,8,128,128]{3,2,1,0:T(8,128)(2,1)S(1)}, u32[]{:S(2)}, u32[]{:S(2)}) collective-permute-start(bf16[1,8,128,128]{3,2,1,0:T(8,128)(2,1)S(1)} %get-tuple-element.5), channel_id=1, source_target_pairs={{8,4},{4,8},{9,5},{5,9},{10,6},{6,10},{11,7},{7,11},{24,20},{20,24... | collective-permute-start | bytes 786440 | tf_op jit(solution)/shard_map/ppermute | solution.py:111
  21.1 0.4 collective-permute-done.1
  21.4 0.7 %collective-permute-start.3 = (bf16[1,8,128,128]{3,2,1,0:T(8,128)(2,1)}, bf16[1,8,128,128]{3,2,1,0:T(8,128)(2,1)S(1)}, u32[]{:S(2)}, u32[]{:S(2)}) collective-permute-start(bf16[1,8,128,128]{3,2,1,0:T(8,128)(2,1)} %get-tuple-element.8), channel_id=1, source_target_pairs={{8,4},{4,8},{9,5},{5,9},{10,6},{6,10},{11,7},{7,11},{24,20},{20,24... | collective-permute-start | bytes 786440 | tf_op jit(solution)/shard_map/ppermute | solution.py:111
  22.1 0.7 %collective-permute-start.5 = (bf16[1,8,128,128]{3,2,1,0:T(8,128)(2,1)}, bf16[1,8,128,128]{3,2,1,0:T(8,128)(2,1)S(1)}, u32[]{:S(2)}, u32[]{:S(2)}) collective-permute-start(bf16[1,8,128,128]{3,2,1,0:T(8,128)(2,1)} %get-tuple-element.7), channel_id=1, source_target_pairs={{8,4},{4,8},{9,5},{5,9},{10,6},{6,10},{11,7},{7,11},{24,20},{20,24... | collective-permute-start | bytes 786440 | tf_op jit(solution)/shard_map/ppermute | solution.py:111
  22.8 0.1 collective-permute-start.9
  23.0 0.1 stack.42.place
  23.1 0.1 stack.48.place
  23.1 0.1 stack.45.place
  23.2 1.3 %collective-permute-start.13 = (bf16[1,8,128,128]{3,2,1,0:T(8,128)(2,1)S(1)}, bf16[1,8,128,128]{3,2,1,0:T(8,128)(2,1)S(1)}, u32[]{:S(2)}, u32[]{:S(2)}) collective-permute-start(bf16[1,8,128,128]{3,2,1,0:T(8,128)(2,1)S(1)} %collective-permute-done.12.refs_2_), channel_id=1, source_target_pairs={{4,0},{8,12},{5,1},{9,13},{6,2},{10,14},{7,3},{11,15},{20,16},{24,... | collective-permute-start | bytes 786440 | tf_op jit(solution)/shard_map/ppermute | solution.py:111
  24.6 1.3 %collective-permute-start.15 = (bf16[1,8,128,128]{3,2,1,0:T(8,128)(2,1)S(1)}, bf16[1,8,128,128]{3,2,1,0:T(8,128)(2,1)S(1)}, u32[]{:S(2)}, u32[]{:S(2)}) collective-permute-start(bf16[1,8,128,128]{3,2,1,0:T(8,128)(2,1)S(1)} %collective-permute-done.14.refs_3_), channel_id=1, source_target_pairs={{4,0},{8,12},{5,1},{9,13},{6,2},{10,14},{7,3},{11,15},{20,16},{24,... | collective-permute-start | bytes 786440 | tf_op jit(solution)/shard_map/ppermute | solution.py:111
  25.9 1.3 %collective-permute-start.4 = (bf16[1,8,128,128]{3,2,1,0:T(8,128)(2,1)S(1)}, bf16[1,8,128,128]{3,2,1,0:T(8,128)(2,1)S(1)}, u32[]{:S(2)}, u32[]{:S(2)}) collective-permute-start(bf16[1,8,128,128]{3,2,1,0:T(8,128)(2,1)S(1)} %collective-permute-done.3.refs_2_), channel_id=1, source_target_pairs={{4,0},{8,12},{5,1},{9,13},{6,2},{10,14},{7,3},{11,15},{20,16},{24,... | collective-permute-start | bytes 786440 | tf_op jit(solution)/shard_map/ppermute | solution.py:111
  27.2 1.3 %collective-permute-start.6 = (bf16[1,8,128,128]{3,2,1,0:T(8,128)(2,1)S(1)}, bf16[1,8,128,128]{3,2,1,0:T(8,128)(2,1)}, u32[]{:S(2)}, u32[]{:S(2)}) collective-permute-start(bf16[1,8,128,128]{3,2,1,0:T(8,128)(2,1)S(1)} %collective-permute-done.5.refs_3_), channel_id=1, source_target_pairs={{4,0},{8,12},{5,1},{9,13},{6,2},{10,14},{7,3},{11,15},{20,16},{24,... | collective-permute-start | bytes 786440 | tf_op jit(solution)/shard_map/ppermute | solution.py:111
  28.5 0.1 reshape.7.index
  28.6 0.9 %shard_map.55.refs_4_.refs_2_ = bf16[2,8,128,128]{3,2,1,0:T(8,128)(2,1)S(1)} custom-call(s32[2,16]{1,0:T(2,128)S(1)} %reshape.7.index, bf16[2,4,128,128]{3,2,1,0:T(8,128)(2,1)S(1)} %copy-done.1, bf16[2,4,128,128]{3,2,1,0:T(8,128)(2,1)S(1)} %collective-permute-done.9.refs_1_, bf16[2,4,128,128]{3,2,1,0:T(8,128)(2,1)S(1)} %collective-permute-done.10.refs_2_, ...), custom_call_target="tpu_custom_call" | custom-call | tf_op jit(solution)/shard_map/pallas_call | solution.py:124
  29.5 0.1 copy-done
  29.6 1.7 %shard_map.56.refs_5_ = f32[2,128,768]{2,1,0:T(8,128)S(1)} custom-call(s32[10]{0:T(128)S(1)} %stack.48.place, s32[2,6]{1,0:T(2,128)S(1)} %copy-done.2, s32[4,16]{1,0:T(4,128)S(1)} %pad_add_fusion.index, bf16[2,8,128,128]{3,2,1,0:T(8,128)(2,1)S(1)} %copy-done, bf16[2,8,128,128]{3,2,1,0:T(8,128)(2,1)S(1)} %collective-permute-done.2.refs_1_, ...), custom_call_target="tpu_custom_call" | custom-call | flops 402653184 | bytes 2097152 | tf_op jit(solution)/shard_map/pallas_call | solution.py:150
  31.4 7.4 %collective-permute-done.13.refs_0_ = bf16[1,8,128,128]{3,2,1,0:T(8,128)(2,1)S(1)} collective-permute-done((bf16[1,8,128,128]{3,2,1,0:T(8,128)(2,1)S(1)}, bf16[1,8,128,128]{3,2,1,0:T(8,128)(2,1)S(1)}, u32[]{:S(2)}, u32[]{:S(2)}) %collective-permute-start.13) | collective-permute-done | bytes 262176 | tf_op jit(solution)/shard_map/ppermute | solution.py:111
  38.8 5.6 %collective-permute-done.15.refs_1_ = bf16[1,8,128,128]{3,2,1,0:T(8,128)(2,1)S(1)} collective-permute-done((bf16[1,8,128,128]{3,2,1,0:T(8,128)(2,1)S(1)}, bf16[1,8,128,128]{3,2,1,0:T(8,128)(2,1)S(1)}, u32[]{:S(2)}, u32[]{:S(2)}) %collective-permute-start.15) | collective-permute-done | bytes 262176 | tf_op jit(solution)/shard_map/ppermute | solution.py:111
  44.4 1.4 %shard_map.57.refs_3_ = f32[2,128,768]{2,1,0:T(8,128)S(1)} custom-call(s32[10]{0:T(128)S(1)} %stack.45.place, s32[2,6]{1,0:T(2,128)S(1)} %copy-done.2, s32[4,16]{1,0:T(4,128)S(1)} %pad_add_fusion.index, bf16[1,8,128,128]{3,2,1,0:T(8,128)(2,1)S(1)} %collective-permute-done.13.refs_0_, bf16[1,8,128,128]{3,2,1,0:T(8,128)(2,1)S(1)} %collective-permute-done.15.refs_1_, ...), custom_call_target="tpu_custom_call" | custom-call | flops 402653184 | bytes 2097152 | tf_op jit(solution)/shard_map/pallas_call | solution.py:150
  45.8 4.2 %collective-permute-done.4.refs_0_ = bf16[1,8,128,128]{3,2,1,0:T(8,128)(2,1)S(1)} collective-permute-done((bf16[1,8,128,128]{3,2,1,0:T(8,128)(2,1)S(1)}, bf16[1,8,128,128]{3,2,1,0:T(8,128)(2,1)S(1)}, u32[]{:S(2)}, u32[]{:S(2)}) %collective-permute-start.4) | collective-permute-done | bytes 262176 | tf_op jit(solution)/shard_map/ppermute | solution.py:111
  50.0 5.5 %collective-permute-done.6.refs_1_ = bf16[1,8,128,128]{3,2,1,0:T(8,128)(2,1)} collective-permute-done((bf16[1,8,128,128]{3,2,1,0:T(8,128)(2,1)S(1)}, bf16[1,8,128,128]{3,2,1,0:T(8,128)(2,1)}, u32[]{:S(2)}, u32[]{:S(2)}) %collective-permute-start.6) | collective-permute-done | bytes 262176 | tf_op jit(solution)/shard_map/ppermute | solution.py:111
  55.5 2.5 %shard_map.58 = bf16[2,6,128,128]{3,2,1,0:T(8,128)(2,1)} custom-call(s32[6]{0:T(128)S(1)} %stack.42.place, s32[2,6]{1,0:T(2,128)S(1)} %copy-done.2, s32[4,16]{1,0:T(4,128)S(1)} %pad_add_fusion.index, bf16[1,8,128,128]{3,2,1,0:T(8,128)(2,1)S(1)} %collective-permute-done.4.refs_0_, bf16[1,8,128,128]{3,2,1,0:T(8,128)(2,1)} %collective-permute-done.6.refs_1_, ...), custom_call_target="tpu_custom_call" | custom-call | flops 201326592 | bytes 2097152 | tf_op jit(solution)/shard_map/pallas_call | solution.py:150
  (24 shorter events, 0.1 us)
Async XLA Ops:
  0.0 4.5 %copy-start.3 = (s32[2,4]{1,0:T(2,128)S(1)}, s32[2,4]{1,0:T(2,128)}, u32[]{:S(2)}) copy-start(s32[2,4]{1,0:T(2,128)} %param.6) | copy-start | bytes 100
  0.0 16.9 %collective-permute-start.2 = (bf16[2,8,128,128]{3,2,1,0:T(8,128)(2,1)}, bf16[2,8,128,128]{3,2,1,0:T(8,128)(2,1)S(1)}, u32[]{:S(2)}, u32[]{:S(2)}) collective-permute-start(bf16[2,8,128,128]{3,2,1,0:T(8,128)(2,1)} %refs_0_.3), channel_id=1, source_target_pairs={{4,0},{0,4},{12,8},{8,12},{5,1},{1,5},{13,9},{9,13},{6,2},{2,6},{1... | collective-permute-start | bytes 1572872 | tf_op jit(solution)/shard_map/ppermute | solution.py:111
  3.0 19.1 %collective-permute-start.10 = (bf16[2,4,128,128]{3,2,1,0:T(8,128)(2,1)}, bf16[2,4,128,128]{3,2,1,0:T(8,128)(2,1)S(1)}, u32[]{:S(2)}, u32[]{:S(2)}) collective-permute-start(bf16[2,4,128,128]{3,2,1,0:T(8,128)(2,1)} %refs_0_.2), channel_id=1, source_target_pairs={{0,2},{1,3},{2,0},{3,1},{4,6},{5,7},{6,4},{7,5},{8,10},{9,11},{10,... | collective-permute-start | bytes 786440 | tf_op jit(solution)/shard_map/ppermute | solution.py:122
  4.5 18.3 %collective-permute-start.11 = (bf16[2,4,128,128]{3,2,1,0:T(8,128)(2,1)}, bf16[2,4,128,128]{3,2,1,0:T(8,128)(2,1)S(1)}, u32[]{:S(2)}, u32[]{:S(2)}) collective-permute-start(bf16[2,4,128,128]{3,2,1,0:T(8,128)(2,1)} %refs_0_.2), channel_id=1, source_target_pairs={{0,3},{1,2},{2,1},{3,0},{4,7},{5,6},{6,5},{7,4},{8,11},{9,10},{10,... | collective-permute-start | bytes 786440 | tf_op jit(solution)/shard_map/ppermute | solution.py:122
  4.5 2.5 %collective-permute-start.7 = (s32[1,2,4]{2,1,0:T(2,128)S(1)}, s32[1,2,4]{2,1,0:T(2,128)S(1)}, u32[]{:S(2)}, u32[]{:S(2)}) collective-permute-start(s32[1,2,4]{2,1,0:T(2,128)S(1)} %bitcast.10), channel_id=1, source_target_pairs={{0,1},{1,0},{2,3},{3,2},{4,5},{5,4},{6,7},{7,6},{8,9},{9,8},{10,11... | collective-permute-start | bytes 104 | tf_op jit(solution)/shard_map/ppermute | solution.py:83
  5.9 9.3 %collective-permute-start = (s32[1,16]{1,0:T(1,128)S(1)}, s32[1,16]{1,0:T(1,128)S(1)}, u32[]{:S(2)}, u32[]{:S(2)}) collective-permute-start(s32[1,16]{1,0:T(1,128)S(1)} %reshape.6), channel_id=1, source_target_pairs={{0,4},{4,0},{8,12},{12,8},{1,5},{5,1},{9,13},{13,9},{2,6},{6,2},{1... | collective-permute-start | bytes 200 | tf_op jit(solution)/shard_map/ppermute | solution.py:83
  7.1 16.2 %collective-permute-start.12 = (bf16[1,8,128,128]{3,2,1,0:T(8,128)(2,1)S(1)}, bf16[1,8,128,128]{3,2,1,0:T(8,128)(2,1)S(1)}, u32[]{:S(2)}, u32[]{:S(2)}) collective-permute-start(bf16[1,8,128,128]{3,2,1,0:T(8,128)(2,1)S(1)} %get-tuple-element.6), channel_id=1, source_target_pairs={{8,4},{4,8},{9,5},{5,9},{10,6},{6,10},{11,7},{7,11},{24,20},{20,24... | collective-permute-start | bytes 786440 | tf_op jit(solution)/shard_map/ppermute | solution.py:111
  15.2 5.2 %collective-permute-start.8 = (s32[2,2,4]{2,1,0:T(2,128)S(1)}, s32[2,2,4]{2,1,0:T(2,128)S(1)}, u32[]{:S(2)}, u32[]{:S(2)}) collective-permute-start(s32[2,2,4]{2,1,0:T(2,128)S(1)} %pad_add_fusion.1), channel_id=1, source_target_pairs={{0,2},{1,3},{2,0},{3,1},{4,6},{5,7},{6,4},{7,5},{8,10},{9,11},{10,... | collective-permute-start | bytes 200 | tf_op jit(solution)/shard_map/ppermute | solution.py:83
  16.9 5.9 %copy-start.1 = (bf16[2,4,128,128]{3,2,1,0:T(8,128)(2,1)S(1)}, bf16[2,4,128,128]{3,2,1,0:T(8,128)(2,1)}, u32[]{:S(2)}) copy-start(bf16[2,4,128,128]{3,2,1,0:T(8,128)(2,1)} %refs_0_.2) | copy-start | bytes 786436
  16.9 4.5 %collective-permute-start.1 = (s32[2,16]{1,0:T(2,128)S(1)}, s32[2,16]{1,0:T(2,128)S(1)}, u32[]{:S(2)}, u32[]{:S(2)}) collective-permute-start(s32[2,16]{1,0:T(2,128)S(1)} %pad_add_fusion.2), channel_id=1, source_target_pairs={{0,8},{4,12},{8,0},{12,4},{1,9},{5,13},{9,1},{13,5},{2,10},{6,14},... | collective-permute-start | bytes 392 | tf_op jit(solution)/shard_map/ppermute | solution.py:83
  20.4 4.2 %collective-permute-start.14 = (bf16[1,8,128,128]{3,2,1,0:T(8,128)(2,1)S(1)}, bf16[1,8,128,128]{3,2,1,0:T(8,128)(2,1)S(1)}, u32[]{:S(2)}, u32[]{:S(2)}) collective-permute-start(bf16[1,8,128,128]{3,2,1,0:T(8,128)(2,1)S(1)} %get-tuple-element.5), channel_id=1, source_target_pairs={{8,4},{4,8},{9,5},{5,9},{10,6},{6,10},{11,7},{7,11},{24,20},{20,24... | collective-permute-start | bytes 786440 | tf_op jit(solution)/shard_map/ppermute | solution.py:111
  21.4 4.4 %collective-permute-start.3 = (bf16[1,8,128,128]{3,2,1,0:T(8,128)(2,1)}, bf16[1,8,128,128]{3,2,1,0:T(8,128)(2,1)S(1)}, u32[]{:S(2)}, u32[]{:S(2)}) collective-permute-start(bf16[1,8,128,128]{3,2,1,0:T(8,128)(2,1)} %get-tuple-element.8), channel_id=1, source_target_pairs={{8,4},{4,8},{9,5},{5,9},{10,6},{6,10},{11,7},{7,11},{24,20},{20,24... | collective-permute-start | bytes 786440 | tf_op jit(solution)/shard_map/ppermute | solution.py:111
  22.1 5.0 %collective-permute-start.5 = (bf16[1,8,128,128]{3,2,1,0:T(8,128)(2,1)}, bf16[1,8,128,128]{3,2,1,0:T(8,128)(2,1)S(1)}, u32[]{:S(2)}, u32[]{:S(2)}) collective-permute-start(bf16[1,8,128,128]{3,2,1,0:T(8,128)(2,1)} %get-tuple-element.7), channel_id=1, source_target_pairs={{8,4},{4,8},{9,5},{5,9},{10,6},{6,10},{11,7},{7,11},{24,20},{20,24... | collective-permute-start | bytes 786440 | tf_op jit(solution)/shard_map/ppermute | solution.py:111
  22.8 5.8 %collective-permute-start.9 = (bf16[2,4,128,128]{3,2,1,0:T(8,128)(2,1)S(1)}, bf16[2,4,128,128]{3,2,1,0:T(8,128)(2,1)S(1)}, u32[]{:S(2)}, u32[]{:S(2)}) collective-permute-start(bf16[2,4,128,128]{3,2,1,0:T(8,128)(2,1)S(1)} %copy-done.1), channel_id=1, source_target_pairs={{0,1},{1,0},{2,3},{3,2},{4,5},{5,4},{6,7},{7,6},{8,9},{9,8},{10,11... | collective-permute-start | bytes 786440 | tf_op jit(solution)/shard_map/ppermute | solution.py:122
  23.2 15.5 %collective-permute-start.13 = (bf16[1,8,128,128]{3,2,1,0:T(8,128)(2,1)S(1)}, bf16[1,8,128,128]{3,2,1,0:T(8,128)(2,1)S(1)}, u32[]{:S(2)}, u32[]{:S(2)}) collective-permute-start(bf16[1,8,128,128]{3,2,1,0:T(8,128)(2,1)S(1)} %collective-permute-done.12.refs_2_), channel_id=1, source_target_pairs={{4,0},{8,12},{5,1},{9,13},{6,2},{10,14},{7,3},{11,15},{20,16},{24,... | collective-permute-start | bytes 786440 | tf_op jit(solution)/shard_map/ppermute | solution.py:111
  24.6 19.8 %collective-permute-start.15 = (bf16[1,8,128,128]{3,2,1,0:T(8,128)(2,1)S(1)}, bf16[1,8,128,128]{3,2,1,0:T(8,128)(2,1)S(1)}, u32[]{:S(2)}, u32[]{:S(2)}) collective-permute-start(bf16[1,8,128,128]{3,2,1,0:T(8,128)(2,1)S(1)} %collective-permute-done.14.refs_3_), channel_id=1, source_target_pairs={{4,0},{8,12},{5,1},{9,13},{6,2},{10,14},{7,3},{11,15},{20,16},{24,... | collective-permute-start | bytes 786440 | tf_op jit(solution)/shard_map/ppermute | solution.py:111
  25.9 24.1 %collective-permute-start.4 = (bf16[1,8,128,128]{3,2,1,0:T(8,128)(2,1)S(1)}, bf16[1,8,128,128]{3,2,1,0:T(8,128)(2,1)S(1)}, u32[]{:S(2)}, u32[]{:S(2)}) collective-permute-start(bf16[1,8,128,128]{3,2,1,0:T(8,128)(2,1)S(1)} %collective-permute-done.3.refs_2_), channel_id=1, source_target_pairs={{4,0},{8,12},{5,1},{9,13},{6,2},{10,14},{7,3},{11,15},{20,16},{24,... | collective-permute-start | bytes 786440 | tf_op jit(solution)/shard_map/ppermute | solution.py:111
  27.2 28.3 %collective-permute-start.6 = (bf16[1,8,128,128]{3,2,1,0:T(8,128)(2,1)S(1)}, bf16[1,8,128,128]{3,2,1,0:T(8,128)(2,1)}, u32[]{:S(2)}, u32[]{:S(2)}) collective-permute-start(bf16[1,8,128,128]{3,2,1,0:T(8,128)(2,1)S(1)} %collective-permute-done.5.refs_3_), channel_id=1, source_target_pairs={{4,0},{8,12},{5,1},{9,13},{6,2},{10,14},{7,3},{11,15},{20,16},{24,... | collective-permute-start | bytes 786440 | tf_op jit(solution)/shard_map/ppermute | solution.py:111
  28.6 1.0 %copy-start = (bf16[2,8,128,128]{3,2,1,0:T(8,128)(2,1)S(1)}, bf16[2,8,128,128]{3,2,1,0:T(8,128)(2,1)}, u32[]{:S(2)}) copy-start(bf16[2,8,128,128]{3,2,1,0:T(8,128)(2,1)} %refs_0_.3) | copy-start | bytes 1572868
  28.6 1.0 %copy-start.2 = (s32[2,6]{1,0:T(2,128)S(1)}, s32[2,6]{1,0:T(2,128)}, u32[]{:S(2)}) copy-start(s32[2,6]{1,0:T(2,128)} %wanted.5) | copy-start | bytes 148

commit v3 on v2

v3 whole, which is shorter than its diff:
```python
import functools

import jax
import jax.numpy as jnp
from jax import lax
from jax.experimental import pallas as pl
from jax.experimental.pallas import tpu as pltpu
from jax.sharding import PartitionSpec as P

COLS_DEV = 16

SMEM = pl.BlockSpec(memory_space=pltpu.SMEM)
VMEM = pl.BlockSpec(memory_space=pltpu.VMEM)
PARAMS = pltpu.CompilerParams(vmem_limit_bytes=32 * 2**20)


def prepare_kernel(row_count, col_count, place, wanted, a_index, b_index, *refs):
    tiles, refs = refs[:col_count], refs[col_count:]
    dense, table, slot = refs
    first, r = place[0], place[1]
    rows, slots = wanted.shape
    inner_rows, inner_slots = b_index.shape[0] // row_count, b_index.shape[1]
    for s in range(row_count):
        source = r ^ s
        for m in range(inner_rows):
            for c in range(COLS_DEV):
                slot[c] = -1
            for l in range(inner_slots):
                slot[b_index[s * inner_rows + m, l] - first] = l
            for i in range(rows):
                for j in range(slots):
                    table[i, (source * inner_rows + m) * slots + j] = slot[wanted[i, j] - first]
    dense[...] = jnp.zeros_like(dense)
    for p, source in enumerate(tiles):
        for i in range(rows):
            for s in range(a_index.shape[1]):
                inner = a_index[p * rows + i, s]

                @pl.when(inner >= 0)
                def _():
                    dense[i, inner] = source[i, s]


def step_kernel(parts, last, place, table, *refs):
    tiles, refs = refs[:parts], refs[parts:]
    if last:
        dense, before, out, total, right = refs
        total[...] = before[...]
    elif len(refs) == 4:
        dense, before, total, right = refs
        total[...] = before[...]
    else:
        dense, total, right = refs
        total[...] = jnp.zeros_like(total)
    rows, _, block, _ = dense.shape
    inner_rows = tiles[0].shape[0]
    slots = right.shape[1] // block

    for p in range(parts):
        source = place[2 + p]

        @pl.when(source >= 0)
        def _():
            for i in range(rows):
                for m in range(inner_rows):
                    for j in range(slots):
                        l = table[i, (source * inner_rows + m) * slots + j]
                        tile = tiles[p][m, jnp.maximum(l, 0)]
                        right[m * block : (m + 1) * block, j * block : (j + 1) * block] = jnp.where(
                            l >= 0, tile, jnp.zeros_like(tile)
                        )
                left = jnp.concatenate(
                    [dense[i, source * inner_rows + m] for m in range(inner_rows)], axis=1
                )
                total[i] += jnp.dot(left, right[...], preferred_element_type=jnp.float32)

    if last:
        for i in range(rows):
            for j in range(slots):
                out[i, j] = total[i, :, j * block : (j + 1) * block].astype(out.dtype)


def body(row_count, col_count, a_tiles, a_cols, b_tiles, b_cols, c_cols):
    rows, slots = c_cols.shape
    inner_rows = b_tiles.shape[0]
    block = a_tiles.shape[-1]
    inner_count = inner_rows * row_count
    r = lax.axis_index("row")
    first = lax.axis_index("col") * COLS_DEV
    sides = [jnp.where(r % 2 == kind, 1, -1) for kind in (0, 1)]

    def pairs(kind, t):
        found = []
        for k in range(row_count):
            side = 1 if k % 2 == kind else -1
            if 0 <= k + side < row_count and 0 <= k + side * t < row_count:
                found.append((k + side, k))
        return found

    def origin(kind, t):
        row = r + sides[kind] * t
        return jnp.where((row >= 0) & (row < row_count), row, -1)

    def swap(x, axis, n, d):
        return lax.ppermute(x, axis, [(k, k ^ d) for k in range(n)])

    def halves(n):
        d = n // 2
        while d:
            yield d
            d //= 2

    def gather(x, axis, n, stages):
        for d in stages:
            x = jnp.concatenate([x, swap(x, axis, n, d)], axis=0)
            yield x

    rounds = [[lax.ppermute(b_tiles, "row", pairs(kind, 1)) for kind in (0, 1)]]
    a_parts = [a_tiles]
    for d in halves(col_count):
        a_parts = a_parts + [swap(x, "col", col_count, d) for x in a_parts]
    a_index = list(gather(a_cols, "col", col_count, halves(col_count)))
    b_index = list(gather(b_cols, "row", row_count, reversed(list(halves(row_count)))))
    for t in range(2, row_count):
        even, odd = rounds[-1]
        if t == 2:
            early = (even, odd, a_index[0], b_index[0], a_parts[1])
            even, odd, a_index[0], b_index[0], a_parts[1] = lax.optimization_barrier(early)
        if t == 3:
            odd, a_index, b_index, a_parts = lax.optimization_barrier((odd, a_index, b_index, a_parts))
        rounds[-1] = [even, odd]
        rounds.append(
            [
                lax.ppermute(x, "row", pairs(kind, t)) if pairs(kind, t) else None
                for kind, x in ((0, odd), (1, even))
            ]
        )

    here = jnp.stack([first, r]).astype(jnp.int32)
    dense, table = pl.pallas_call(
        functools.partial(prepare_kernel, row_count, col_count),
        out_shape=(
            jax.ShapeDtypeStruct((rows, inner_count, block, block), a_tiles.dtype),
            jax.ShapeDtypeStruct((rows, inner_count * slots), jnp.int32),
        ),
        in_specs=[SMEM] * 4 + [VMEM] * col_count,
        out_specs=(VMEM, SMEM),
        scratch_shapes=[pltpu.SMEM((COLS_DEV,), jnp.int32)],
        compiler_params=PARAMS,
    )(here, c_cols, a_index[-1], b_index[-1], *a_parts)

    def step(pieces, before, last):
        parts = len(pieces)
        place = jnp.stack([first, r] + [source for source, _ in pieces]).astype(jnp.int32)
        if last:
            out = jax.ShapeDtypeStruct((rows, slots, block, block), a_tiles.dtype)
        else:
            out = jax.ShapeDtypeStruct((rows, block, slots * block), jnp.float32)
        scratch = [pltpu.VMEM((inner_rows * block, slots * block), b_tiles.dtype)]
        if last:
            scratch = [pltpu.VMEM((rows, block, slots * block), jnp.float32)] + scratch
        flops = 2 * rows * parts * inner_rows * slots * block**3
        held = [dense] if before is None else [dense, before]
        return pl.pallas_call(
            functools.partial(step_kernel, parts, last),
            out_shape=out,
            in_specs=[SMEM] * 2 + [VMEM] * (parts + len(held)),
            out_specs=VMEM,
            scratch_shapes=scratch,
            compiler_params=PARAMS,
            cost_estimate=pl.CostEstimate(flops=flops, bytes_accessed=2**21, transcendentals=0),
        )(place, table, *[tiles for _, tiles in pieces], *held)

    total = None
    for t in range(1, row_count):
        pieces = [(r, b_tiles)] if t == 1 else []
        for kind in (0, 1):
            if rounds[t - 1][kind] is not None:
                pieces.append((origin(kind, t), rounds[t - 1][kind]))
        total = step(pieces, total, t + 1 == row_count)
    return total


def solution(mesh):
    return jax.shard_map(
        functools.partial(body, mesh.shape["row"], mesh.shape["col"]),
        mesh=mesh,
        in_specs=(
            P(("groups", "row"), "col", None, None),
            P(("groups", "row"), "col"),
            P(("groups", "row"), "col", None, None),
            P(("groups", "row"), "col"),
            P(("groups", "row"), "col"),
        ),
        out_specs=P(("groups", "row"), "col", None, None),
        check_vma=False,
    )
```

time: 58.3 us -> 53.2 us (0.913)
  waiting for transfers between devices: 30.6 us -> 22.3 us
  starting transfers between devices: 17.5 us -> 21.4 us
  local copies, waits for them, and re-layouts: 3.12 us -> 1.65 us
  other arithmetic: 0.03 us -> 0.94 us
    ppermute x16 -> x12, waiting for transfers between devices: 30.6 us -> 22.3 us  [the longest x7 13.3 us: swap(): return lax.ppermute(x, axis, [(k, k ^ d) for k in range(n)])]
    ppermute x16 -> x12, starting transfers between devices: 17.5 us -> 21.4 us  [the longest x7 14.4 us: swap(): return lax.ppermute(x, axis, [(k, k ^ d) for k in range(n)])]
    slice x2 -> x0, local copies, waits for them, and re-layouts: 1.88 us -> none  [the longest x1 1.06 us: body(): chunks = [b_tiles[m:m + 1] for m in range(inner_rows)]]
    unnamed x8 -> x10, local copies, waits for them, and re-layouts: 0.14 us -> 1.56 us
    pallas_call x3, Pallas kernels: 5.61 us -> 4.52 us  [step(): pl.pallas_call(functools.partial(step_kernel, parts, last), out_shape=out...]
    pallas_call x1, Pallas kernels: 0.88 us -> 1.95 us  [body(): pl.pallas_call(functools.partial(prepare_kernel, row_count, col_count), o...]
    reshape x2 -> x0, local copies, waits for them, and re-layouts: 0.84 us -> none  [the longest x1 0.76 us: body(): b_index = butterfly(b_cols.reshape(1, -1), 'row', row_count)]
    concatenate x3 -> x4, other arithmetic: 0.02 us -> 0.71 us  [gather(): x = jnp.concatenate([x, swap(x, axis, n, d)], axis=0)]
  transfers between devices with their start and end apart: 16 -> 12, of which waited for: 6 -> 4; matrix products, arithmetic and copies ran while one was open for 5% -> 2% of each run, Pallas kernels for 7% -> 9%
where the time goes in v3:
time: 53.2 us; the launch traced here: 53 us
  waiting for transfers between devices  22.3 us (42%)
  starting transfers between devices  21.4 us (40%)
  Pallas kernels  6.47 us (12%)
  local copies, waits for them, and re-layouts  1.65 us (3%)
  other arithmetic  0.94 us (2%)
    ppermute x7, starting transfers between devices, swap(): return lax.ppermute(x, axis, [(k, k ^ d) for k in range(n)])  14.4 us
    ppermute x7, waiting for transfers between devices, swap(): return lax.ppermute(x, axis, [(k, k ^ d) for k in range(n)])  13.3 us
    ppermute x3, waiting for transfers between devices, body(): lax.ppermute(x, 'row', pairs(kind, t))  8.98 us
    pallas_call x3, Pallas kernels, step(): pl.pallas_call(functools.partial(step_kernel, parts, last), out_shape=out...  4.52 us
    ppermute x2, starting transfers between devices, body(): rounds = [[lax.ppermute(b_tiles, 'row', pairs(kind, 1)) for kind in (0, 1)]]  3.71 us
    ppermute x3, starting transfers between devices, body(): lax.ppermute(x, 'row', pairs(kind, t))  3.28 us
    pallas_call x1, Pallas kernels, body(): pl.pallas_call(functools.partial(prepare_kernel, row_count, col_count), o...  1.95 us
    unnamed x10, local copies, waits for them, and re-layouts  1.56 us
  transfers between devices with their start and end apart: 12, of which 4 were waited for; matrix products, arithmetic and copies ran while one was open for 2% of the time, Pallas kernels for 9%

profile of v3, /device:TPU:0, one launch (start us, length us, event | category | flops | bytes accessed | tf_op | source)
XLA Modules:
  0.0 53.0 jit_solution(13094755196265284060)
XLA Ops:
  0.0 3.0 %collective-permute-start = (bf16[2,8,128,128]{3,2,1,0:T(8,128)(2,1)}, bf16[2,8,128,128]{3,2,1,0:T(8,128)(2,1)S(1)}, u32[]{:S(2)}, u32[]{:S(2)}) collective-permute-start(bf16[2,8,128,128]{3,2,1,0:T(8,128)(2,1)} %refs_0_.2), channel_id=1, source_target_pairs={{4,0},{0,4},{12,8},{8,12},{5,1},{1,5},{13,9},{9,13},{6,2},{2,6},{1... | collective-permute-start | bytes 1572872 | tf_op jit(solution)/shard_map/ppermute | solution.py:118
  3.0 0.7 %collective-permute-start.1 = (bf16[2,8,128,128]{3,2,1,0:T(8,128)(2,1)}, bf16[2,8,128,128]{3,2,1,0:T(8,128)(2,1)S(1)}, u32[]{:S(2)}, u32[]{:S(2)}) collective-permute-start(bf16[2,8,128,128]{3,2,1,0:T(8,128)(2,1)} %refs_0_.2), channel_id=1, source_target_pairs={{8,4},{4,8},{9,5},{5,9},{10,6},{6,10},{11,7},{7,11},{24,20},{20,24... | collective-permute-start | bytes 1572872 | tf_op jit(solution)/shard_map/ppermute | solution.py:118
  3.7 1.6 %collective-permute-start.4 = (bf16[2,4,128,128]{3,2,1,0:T(8,128)(2,1)}, bf16[2,4,128,128]{3,2,1,0:T(8,128)(2,1)S(1)}, u32[]{:S(2)}, u32[]{:S(2)}) collective-permute-start(bf16[2,4,128,128]{3,2,1,0:T(8,128)(2,1)} %refs_0_.1), channel_id=1, source_target_pairs={{0,2},{1,3},{2,0},{3,1},{4,6},{5,7},{6,4},{7,5},{8,10},{9,11},{10,... | collective-permute-start | bytes 786440 | tf_op jit(solution)/shard_map/ppermute | solution.py:105
  5.3 0.5 %collective-permute-start.2 = (s32[2,4]{1,0:T(2,128)}, s32[2,4]{1,0:T(2,128)S(1)}, u32[]{:S(2)}, u32[]{:S(2)}) collective-permute-start(s32[2,4]{1,0:T(2,128)} %param.6), channel_id=1, source_target_pairs={{0,2},{1,3},{2,0},{3,1},{4,6},{5,7},{6,4},{7,5},{8,10},{9,11},{10,... | collective-permute-start | bytes 104 | tf_op jit(solution)/shard_map/ppermute | solution.py:105
  5.8 4.4 %collective-permute-start.3 = (s32[2,8]{1,0:T(2,128)}, s32[2,8]{1,0:T(2,128)S(1)}, u32[]{:S(2)}, u32[]{:S(2)}) collective-permute-start(s32[2,8]{1,0:T(2,128)} %param.8), channel_id=1, source_target_pairs={{0,4},{4,0},{8,12},{12,8},{1,5},{5,1},{9,13},{13,9},{2,6},{6,2},{1... | collective-permute-start | bytes 200 | tf_op jit(solution)/shard_map/ppermute | solution.py:105
  10.2 1.6 %collective-permute-done.2 = s32[2,4]{1,0:T(2,128)S(1)} collective-permute-done((s32[2,4]{1,0:T(2,128)}, s32[2,4]{1,0:T(2,128)S(1)}, u32[]{:S(2)}, u32[]{:S(2)}) %collective-permute-start.2) | collective-permute-done | bytes 64 | tf_op jit(solution)/shard_map/ppermute | solution.py:105
  11.8 0.7 %pad_add_fusion.2 = s32[4,4]{1,0:T(4,128)S(1)} fusion(s32[2,4]{1,0:T(2,128)S(1)} %collective-permute-done.2, s32[2,4]{1,0:T(2,128)} %param.6), kind=kLoop, calls=%fused_computation.2 | loop fusion | flops 16 | bytes 128 | tf_op jit(solution)/shard_map/concatenate | solution.py:115
  12.5 2.7 %collective-permute-done.3 = s32[2,8]{1,0:T(2,128)S(1)} collective-permute-done((s32[2,8]{1,0:T(2,128)}, s32[2,8]{1,0:T(2,128)S(1)}, u32[]{:S(2)}, u32[]{:S(2)}) %collective-permute-start.3) | collective-permute-done | bytes 96 | tf_op jit(solution)/shard_map/ppermute | solution.py:105
  15.2 0.0 collective-permute-done.refs_1_
  15.3 0.0 collective-permute-done.1.refs_2_
  15.3 0.7 %collective-permute-start.5 = (bf16[2,8,128,128]{3,2,1,0:T(8,128)(2,1)S(1)}, bf16[2,8,128,128]{3,2,1,0:T(8,128)(2,1)S(1)}, u32[]{:S(2)}, u32[]{:S(2)}) collective-permute-start(bf16[2,8,128,128]{3,2,1,0:T(8,128)(2,1)S(1)} %collective-permute-done.refs_1_), channel_id=1, source_target_pairs={{8,4},{4,8},{9,5},{5,9},{10,6},{6,10},{11,7},{7,11},{24,20},{20,24... | collective-permute-start | bytes 1572872 | tf_op jit(solution)/shard_map/ppermute | solution.py:134
  16.0 0.1 collective-permute-start.8
  16.0 0.5 collective-permute-start.9
  16.5 0.1 collective-permute-start.6
  16.6 7.3 %collective-permute-start.7 = (s32[4,8]{1,0:T(4,128)S(1)}, s32[4,8]{1,0:T(4,128)S(1)}, u32[]{:S(2)}, u32[]{:S(2)}) collective-permute-start(s32[4,8]{1,0:T(4,128)S(1)} %pad_add_fusion.3), channel_id=1, source_target_pairs={{0,8},{4,12},{8,0},{12,4},{1,9},{5,13},{9,1},{13,5},{2,10},{6,14},... | collective-permute-start | bytes 392 | tf_op jit(solution)/shard_map/ppermute | solution.py:105
  23.9 0.0 collective-permute-done.6
  24.0 1.3 %collective-permute-start.11 = (bf16[2,8,128,128]{3,2,1,0:T(8,128)(2,1)S(1)}, bf16[2,8,128,128]{3,2,1,0:T(8,128)(2,1)S(1)}, u32[]{:S(2)}, u32[]{:S(2)}) collective-permute-start(bf16[2,8,128,128]{3,2,1,0:T(8,128)(2,1)S(1)} %collective-permute-done.1.refs_2_), channel_id=1, source_target_pairs={{4,0},{8,12},{5,1},{9,13},{6,2},{10,14},{7,3},{11,15},{20,16},{24,... | collective-permute-start | bytes 1572872 | tf_op jit(solution)/shard_map/ppermute | solution.py:134
  25.3 9.0 %collective-permute-done.7 = s32[4,8]{1,0:T(4,128)S(1)} collective-permute-done((s32[4,8]{1,0:T(4,128)S(1)}, s32[4,8]{1,0:T(4,128)S(1)}, u32[]{:S(2)}, u32[]{:S(2)}) %collective-permute-start.7) | collective-permute-done | bytes 160 | tf_op jit(solution)/shard_map/ppermute | solution.py:105
  34.2 0.0 collective-permute-done.9.refs_3_
  34.3 0.0 collective-permute-done.5.refs_1_
  34.3 1.3 %collective-permute-start.10 = (bf16[2,8,128,128]{3,2,1,0:T(8,128)(2,1)S(1)}, bf16[2,8,128,128]{3,2,1,0:T(8,128)(2,1)S(1)}, u32[]{:S(2)}, u32[]{:S(2)}) collective-permute-start(bf16[2,8,128,128]{3,2,1,0:T(8,128)(2,1)S(1)} %collective-permute-done.5.refs_1_), channel_id=1, source_target_pairs={{4,0},{8,12},{5,1},{9,13},{6,2},{10,14},{7,3},{11,15},{20,16},{24,... | collective-permute-start | bytes 1572872 | tf_op jit(solution)/shard_map/ppermute | solution.py:134
  35.6 0.1 stack.50.place
  35.7 0.1 pad_add_fusion.5.place
  35.8 0.1 pad_add_fusion.4.place
  35.9 0.1 pad_add_fusion.6.place
  35.9 0.6 %copy-done.2 = s32[2,6]{1,0:T(2,128)S(1)} copy-done((s32[2,6]{1,0:T(2,128)S(1)}, s32[2,6]{1,0:T(2,128)}, u32[]{:S(2)}) %copy-start.2) | copy-done | bytes 72
  36.6 0.9 %copy-done.1 = bf16[2,4,128,128]{3,2,1,0:T(8,128)(2,1)S(1)} copy-done((bf16[2,4,128,128]{3,2,1,0:T(8,128)(2,1)S(1)}, bf16[2,4,128,128]{3,2,1,0:T(8,128)(2,1)}, u32[]{:S(2)}) %copy-start.1) | copy-done | bytes 262168
  37.5 1.9 %shard_map.55 = (bf16[2,8,128,128]{3,2,1,0:T(8,128)(2,1)S(1)}, s32[2,48]{1,0:T(2,128)S(1)}) custom-call(s32[2]{0:T(128)S(1)} %pad_add_fusion.5.place, s32[2,6]{1,0:T(2,128)S(1)} %copy-done.2, s32[8,4]{1,0:T(8,128)S(1)} %pad_add_fusion.a_index, s32[8,8]{1,0:T(8,128)S(1)} %pad_add_fusion.1.b_index, bf16[2,4,128,128]{3,2,1,0:T(8,128)(2,1)S(1)} %copy-done.1, ...), custom_call_target="tpu_custom_call" | custom-call | tf_op jit(solution)/shard_map/pallas_call | solution.py:140
  39.5 1.6 %shard_map.56.refs_3_ = f32[2,128,768]{2,1,0:T(8,128)S(1)} custom-call(s32[5]{0:T(128)S(1)} %stack.50.place, s32[2,48]{1,0:T(2,128)S(1)} %get-tuple-element.25.table, bf16[2,8,128,128]{3,2,1,0:T(8,128)(2,1)S(1)} %copy-done, bf16[2,8,128,128]{3,2,1,0:T(8,128)(2,1)S(1)} %collective-permute-done.refs_1_, ...), custom_call_target="tpu_custom_call" | custom-call | flops 301989888 | bytes 2097152 | tf_op jit(solution)/shard_map/pallas_call | solution.py:164
  41.1 1.1 %shard_map.57.refs_2_ = f32[2,128,768]{2,1,0:T(8,128)S(1)} custom-call(s32[4]{0:T(128)S(1)} %pad_add_fusion.6.place, s32[2,48]{1,0:T(2,128)S(1)} %get-tuple-element.25.table, bf16[2,8,128,128]{3,2,1,0:T(8,128)(2,1)S(1)} %collective-permute-done.11.refs_0_, bf16[2,8,128,128]{3,2,1,0:T(8,128)(2,1)S(1)} %collective-permute-done.5.refs_1_, ...), custom_call_target="tpu_custom_call" | custom-call | flops 201326592 | bytes 2097152 | tf_op jit(solution)/shard_map/pallas_call | solution.py:164
  42.2 9.0 %collective-permute-done.10.refs_0_ = bf16[2,8,128,128]{3,2,1,0:T(8,128)(2,1)S(1)} collective-permute-done((bf16[2,8,128,128]{3,2,1,0:T(8,128)(2,1)S(1)}, bf16[2,8,128,128]{3,2,1,0:T(8,128)(2,1)S(1)}, u32[]{:S(2)}, u32[]{:S(2)}) %collective-permute-start.10) | collective-permute-done | bytes 524320 | tf_op jit(solution)/shard_map/ppermute | solution.py:134
  51.1 1.9 %shard_map.58 = bf16[2,6,128,128]{3,2,1,0:T(8,128)(2,1)} custom-call(s32[3]{0:T(128)S(1)} %pad_add_fusion.4.place, s32[2,48]{1,0:T(2,128)S(1)} %get-tuple-element.25.table, bf16[2,8,128,128]{3,2,1,0:T(8,128)(2,1)S(1)} %collective-permute-done.10.refs_0_, bf16[2,8,128,128]{3,2,1,0:T(8,128)(2,1)S(1)} %get-tuple-element.27.refs_3_.refs_2_.refs_1_, ...), custom_call_target="tpu_custom_call" | custom-call | flops 100663296 | bytes 2097152 | tf_op jit(solution)/shard_map/pallas_call | solution.py:164
  (14 shorter events, 0.0 us)
Async XLA Ops:
  0.0 15.2 %copy-start.4 = (s32[2,8]{1,0:T(2,128)S(1)}, s32[2,8]{1,0:T(2,128)}, u32[]{:S(2)}) copy-start(s32[2,8]{1,0:T(2,128)} %param.8) | copy-start | bytes 196
  0.0 15.2 %collective-permute-start = (bf16[2,8,128,128]{3,2,1,0:T(8,128)(2,1)}, bf16[2,8,128,128]{3,2,1,0:T(8,128)(2,1)S(1)}, u32[]{:S(2)}, u32[]{:S(2)}) collective-permute-start(bf16[2,8,128,128]{3,2,1,0:T(8,128)(2,1)} %refs_0_.2), channel_id=1, source_target_pairs={{4,0},{0,4},{12,8},{8,12},{5,1},{1,5},{13,9},{9,13},{6,2},{2,6},{1... | collective-permute-start | bytes 1572872 | tf_op jit(solution)/shard_map/ppermute | solution.py:118
  3.0 12.2 %collective-permute-start.1 = (bf16[2,8,128,128]{3,2,1,0:T(8,128)(2,1)}, bf16[2,8,128,128]{3,2,1,0:T(8,128)(2,1)S(1)}, u32[]{:S(2)}, u32[]{:S(2)}) collective-permute-start(bf16[2,8,128,128]{3,2,1,0:T(8,128)(2,1)} %refs_0_.2), channel_id=1, source_target_pairs={{8,4},{4,8},{9,5},{5,9},{10,6},{6,10},{11,7},{7,11},{24,20},{20,24... | collective-permute-start | bytes 1572872 | tf_op jit(solution)/shard_map/ppermute | solution.py:118
  3.7 11.5 %collective-permute-start.4 = (bf16[2,4,128,128]{3,2,1,0:T(8,128)(2,1)}, bf16[2,4,128,128]{3,2,1,0:T(8,128)(2,1)S(1)}, u32[]{:S(2)}, u32[]{:S(2)}) collective-permute-start(bf16[2,4,128,128]{3,2,1,0:T(8,128)(2,1)} %refs_0_.1), channel_id=1, source_target_pairs={{0,2},{1,3},{2,0},{3,1},{4,6},{5,7},{6,4},{7,5},{8,10},{9,11},{10,... | collective-permute-start | bytes 786440 | tf_op jit(solution)/shard_map/ppermute | solution.py:105
  5.3 6.5 %collective-permute-start.2 = (s32[2,4]{1,0:T(2,128)}, s32[2,4]{1,0:T(2,128)S(1)}, u32[]{:S(2)}, u32[]{:S(2)}) collective-permute-start(s32[2,4]{1,0:T(2,128)} %param.6), channel_id=1, source_target_pairs={{0,2},{1,3},{2,0},{3,1},{4,6},{5,7},{6,4},{7,5},{8,10},{9,11},{10,... | collective-permute-start | bytes 104 | tf_op jit(solution)/shard_map/ppermute | solution.py:105
  5.8 9.4 %collective-permute-start.3 = (s32[2,8]{1,0:T(2,128)}, s32[2,8]{1,0:T(2,128)S(1)}, u32[]{:S(2)}, u32[]{:S(2)}) collective-permute-start(s32[2,8]{1,0:T(2,128)} %param.8), channel_id=1, source_target_pairs={{0,4},{4,0},{8,12},{12,8},{1,5},{5,1},{9,13},{13,9},{2,6},{6,2},{1... | collective-permute-start | bytes 200 | tf_op jit(solution)/shard_map/ppermute | solution.py:105
  12.5 11.4 %copy-start.3 = (s32[2,4]{1,0:T(2,128)S(1)}, s32[2,4]{1,0:T(2,128)}, u32[]{:S(2)}) copy-start(s32[2,4]{1,0:T(2,128)} %param.6) | copy-start | bytes 100
  15.3 19.0 %collective-permute-start.5 = (bf16[2,8,128,128]{3,2,1,0:T(8,128)(2,1)S(1)}, bf16[2,8,128,128]{3,2,1,0:T(8,128)(2,1)S(1)}, u32[]{:S(2)}, u32[]{:S(2)}) collective-permute-start(bf16[2,8,128,128]{3,2,1,0:T(8,128)(2,1)S(1)} %collective-permute-done.refs_1_), channel_id=1, source_target_pairs={{8,4},{4,8},{9,5},{5,9},{10,6},{6,10},{11,7},{7,11},{24,20},{20,24... | collective-permute-start | bytes 1572872 | tf_op jit(solution)/shard_map/ppermute | solution.py:134
  16.0 18.3 %collective-permute-start.8 = (bf16[2,4,128,128]{3,2,1,0:T(8,128)(2,1)}, bf16[2,4,128,128]{3,2,1,0:T(8,128)(2,1)S(1)}, u32[]{:S(2)}, u32[]{:S(2)}) collective-permute-start(bf16[2,4,128,128]{3,2,1,0:T(8,128)(2,1)} %refs_0_.1), channel_id=1, source_target_pairs={{0,1},{1,0},{2,3},{3,2},{4,5},{5,4},{6,7},{7,6},{8,9},{9,8},{10,11... | collective-permute-start | bytes 786440 | tf_op jit(solution)/shard_map/ppermute | solution.py:105
  16.0 18.2 %collective-permute-start.9 = (bf16[2,4,128,128]{3,2,1,0:T(8,128)(2,1)S(1)}, bf16[2,4,128,128]{3,2,1,0:T(8,128)(2,1)S(1)}, u32[]{:S(2)}, u32[]{:S(2)}) collective-permute-start(bf16[2,4,128,128]{3,2,1,0:T(8,128)(2,1)S(1)} %collective-permute-done.4.refs_1_), channel_id=1, source_target_pairs={{0,1},{1,0},{2,3},{3,2},{4,5},{5,4},{6,7},{7,6},{8,9},{9,8},{10,11... | collective-permute-start | bytes 786440 | tf_op jit(solution)/shard_map/ppermute | solution.py:105
  16.5 7.4 %collective-permute-start.6 = (s32[4,4]{1,0:T(4,128)S(1)}, s32[4,4]{1,0:T(4,128)S(1)}, u32[]{:S(2)}, u32[]{:S(2)}) collective-permute-start(s32[4,4]{1,0:T(4,128)S(1)} %pad_add_fusion.2), channel_id=1, source_target_pairs={{0,1},{1,0},{2,3},{3,2},{4,5},{5,4},{6,7},{7,6},{8,9},{9,8},{10,11... | collective-permute-start | bytes 200 | tf_op jit(solution)/shard_map/ppermute | solution.py:105
  16.6 17.6 %collective-permute-start.7 = (s32[4,8]{1,0:T(4,128)S(1)}, s32[4,8]{1,0:T(4,128)S(1)}, u32[]{:S(2)}, u32[]{:S(2)}) collective-permute-start(s32[4,8]{1,0:T(4,128)S(1)} %pad_add_fusion.3), channel_id=1, source_target_pairs={{0,8},{4,12},{8,0},{12,4},{1,9},{5,13},{9,1},{13,5},{2,10},{6,14},... | collective-permute-start | bytes 392 | tf_op jit(solution)/shard_map/ppermute | solution.py:105
  24.0 17.1 %collective-permute-start.11 = (bf16[2,8,128,128]{3,2,1,0:T(8,128)(2,1)S(1)}, bf16[2,8,128,128]{3,2,1,0:T(8,128)(2,1)S(1)}, u32[]{:S(2)}, u32[]{:S(2)}) collective-permute-start(bf16[2,8,128,128]{3,2,1,0:T(8,128)(2,1)S(1)} %collective-permute-done.1.refs_2_), channel_id=1, source_target_pairs={{4,0},{8,12},{5,1},{9,13},{6,2},{10,14},{7,3},{11,15},{20,16},{24,... | collective-permute-start | bytes 1572872 | tf_op jit(solution)/shard_map/ppermute | solution.py:134
  34.3 16.9 %collective-permute-start.10 = (bf16[2,8,128,128]{3,2,1,0:T(8,128)(2,1)S(1)}, bf16[2,8,128,128]{3,2,1,0:T(8,128)(2,1)S(1)}, u32[]{:S(2)}, u32[]{:S(2)}) collective-permute-start(bf16[2,8,128,128]{3,2,1,0:T(8,128)(2,1)S(1)} %collective-permute-done.5.refs_1_), channel_id=1, source_target_pairs={{4,0},{8,12},{5,1},{9,13},{6,2},{10,14},{7,3},{11,15},{20,16},{24,... | collective-permute-start | bytes 1572872 | tf_op jit(solution)/shard_map/ppermute | solution.py:134
  35.9 0.7 %copy-start.2 = (s32[2,6]{1,0:T(2,128)S(1)}, s32[2,6]{1,0:T(2,128)}, u32[]{:S(2)}) copy-start(s32[2,6]{1,0:T(2,128)} %wanted.1) | copy-start | bytes 148
  36.5 0.9 %copy-start.1 = (bf16[2,4,128,128]{3,2,1,0:T(8,128)(2,1)S(1)}, bf16[2,4,128,128]{3,2,1,0:T(8,128)(2,1)}, u32[]{:S(2)}) copy-start(bf16[2,4,128,128]{3,2,1,0:T(8,128)(2,1)} %refs_0_.1) | copy-start | bytes 786436
  37.5 2.0 %copy-start = (bf16[2,8,128,128]{3,2,1,0:T(8,128)(2,1)S(1)}, bf16[2,8,128,128]{3,2,1,0:T(8,128)(2,1)}, u32[]{:S(2)}) copy-start(bf16[2,8,128,128]{3,2,1,0:T(8,128)(2,1)} %refs_0_.2) | copy-start | bytes 1572868

commit v4 on v0

v4 whole, which is shorter than its diff:
```python
import functools

import jax
import jax.numpy as jnp
from jax import lax
from jax.experimental import pallas as pl
from jax.experimental.pallas import tpu as pltpu
from jax.sharding import PartitionSpec as P

COLS_DEV = 16

HBM = pl.BlockSpec(memory_space=pltpu.HBM)
SMEM = pl.BlockSpec(memory_space=pltpu.SMEM)
VMEM = pl.BlockSpec(memory_space=pltpu.VMEM)
PARAMS = pltpu.CompilerParams(vmem_limit_bytes=32 * 2**20)


def tail(count):
    return -(-count // 16) * 16


def pack_kernel(a_index, b_index, a_tiles, b_tiles, a_out, *refs):
    b_outs, sems = refs[:-1], refs[-1]
    size = a_tiles.shape[0]
    copies = [pltpu.make_async_copy(a_tiles, a_out.at[:size], sems.at[0])]
    size = b_tiles.shape[1]
    for m, out in enumerate(b_outs):
        copies.append(pltpu.make_async_copy(b_tiles.at[m], out.at[:size], sems.at[1 + m]))
    for copy in copies:
        copy.start()
    for index, out in ((a_index, a_out), (b_index, b_outs[0])):
        count = index.shape[0] * index.shape[1]
        rows = tail(count)
        row = lax.broadcasted_iota(jnp.int32, (rows, out.shape[1]), 0)
        found = jnp.zeros(row.shape, jnp.float32)
        for k in range(count):
            value = index[k // index.shape[1], k % index.shape[1]].astype(jnp.float32)
            found = jnp.where(row == k, value, found)
        out[out.shape[0] - rows :, :] = found.astype(out.dtype)
    for copy in copies:
        copy.wait()


def left_kernel(index, own, *refs):
    parts, dense = (own,) + refs[:-1], refs[-1]
    dense[...] = jnp.zeros_like(dense)
    rows, _, block, _ = dense.shape
    slots = index.shape[1] // rows
    for p, part in enumerate(parts):
        for i in range(rows):
            for s in range(slots):
                inner = index[p, i * slots + s]
                start = (i * slots + s) * block

                @pl.when(inner >= 0)
                def _():
                    dense[i, inner] = part[start : start + block, :]


def step_kernel(which, last, first_step, place, wanted, index, *refs):
    parts = len(which)
    tiles, refs = refs[:parts], refs[parts:]
    dense, refs = refs[0], refs[1:]
    before, refs = (None, refs) if first_step else (refs[0], refs[1:])
    if last:
        out, total, right, slot = refs
    else:
        total, right, slot = refs
    total[...] = jnp.zeros_like(total) if first_step else before[...]
    first = place[0]
    rows, slots = wanted.shape
    block = dense.shape[2]
    inner_slots = tiles[0].shape[0] // block

    for p, (at, m) in enumerate(which):
        inner = place[1 + p]

        @pl.when(inner >= 0)
        def _():
            for c in range(COLS_DEV):
                slot[c] = -1
            for l in range(inner_slots):
                slot[index[at, m * inner_slots + l] - first] = l
            for i in range(rows):
                for j in range(slots):
                    l = slot[wanted[i, j] - first]
                    start = pl.multiple_of(jnp.maximum(l, 0) * block, block)
                    tile = tiles[p][pl.ds(start, block), :]
                    right[i, :, j * block : (j + 1) * block] = jnp.where(l >= 0, tile, jnp.zeros_like(tile))
            for i in range(rows):
                total[i] += jnp.dot(dense[i, inner], right[i], preferred_element_type=jnp.float32)

    if last:
        for i in range(rows):
            for j in range(slots):
                out[i, j] = total[i, :, j * block : (j + 1) * block].astype(out.dtype)


def body(row_count, col_count, a_tiles, a_cols, b_tiles, b_cols, c_cols):
    rows, slots = c_cols.shape
    inner_rows, inner_slots = b_cols.shape
    block = a_tiles.shape[-1]
    dtype = b_tiles.dtype
    a_count, b_count = a_cols.size, b_cols.size
    r = lax.axis_index("row")
    first = lax.axis_index("col") * COLS_DEV
    sides = [jnp.where(r % 2 == kind, 1, -1) for kind in (0, 1)]

    sizes = [inner_slots * block] * inner_rows
    sizes[0] += tail(b_count)
    packed = pl.pallas_call(
        pack_kernel,
        out_shape=[
            jax.ShapeDtypeStruct((size, block), dtype) for size in [a_count * block + tail(a_count)] + sizes
        ],
        in_specs=[SMEM, SMEM, HBM, HBM],
        out_specs=[VMEM] * (1 + inner_rows),
        scratch_shapes=[pltpu.SemaphoreType.DMA((1 + inner_rows,))],
        compiler_params=PARAMS,
    )(a_cols, b_cols, a_tiles.reshape(-1, block), b_tiles.reshape(inner_rows, -1, block))
    a_own, b_own = packed[0], packed[1:]

    def exchange(x, kind):
        pairs = []
        for k in range(row_count):
            other = k + (1 if k % 2 == kind else -1)
            pairs.append((k, other if 0 <= other < row_count else k))
        return lax.ppermute(x, "row", pairs)

    def useful(kind, t):
        return any(0 <= k + (t if k % 2 == kind else -t) < row_count for k in range(row_count))

    def origin(kind, t):
        row = r + sides[kind] * t
        return jnp.where((row >= 0) & (row < row_count), row, -1)

    def in_order(chunks):
        chunks = list(chunks)
        for m in range(1, len(chunks)):
            chunks[m] = lax.optimization_barrier((chunks[m - 1], chunks[m]))[1]
        return chunks

    rounds = [[[None] * inner_rows, [None] * inner_rows]]
    for m in range(inner_rows):
        for kind in (0, 1):
            rounds[0][kind][m] = exchange(b_own[m], kind)
    a_parts = [a_own]
    d = col_count // 2
    while d:
        sent = a_parts
        if d < col_count // 2:
            sent = lax.optimization_barrier((a_parts, rounds[0][0][-1]))[0]
        a_parts = a_parts + [lax.ppermute(x, "col", [(k, k ^ d) for k in range(col_count)]) for x in sent]
        d //= 2
    for t in range(2, row_count):
        before = [None if chunks is None else in_order(chunks) for chunks in rounds[-1]]
        if t == 3:
            before[1][-1] = lax.optimization_barrier((before[1][-1], a_parts))[0]
        rounds[-1] = before
        rounds.append(
            [[exchange(x, kind) for x in before[1 - kind]] if useful(kind, t) else None for kind in (0, 1)]
        )

    def index_of(parts, count):
        rows_of = [x[x.shape[0] - tail(count) :, 0][:count] for x in parts]
        return jnp.stack(rows_of).astype(jnp.int32)

    dense = pl.pallas_call(
        left_kernel,
        out_shape=jax.ShapeDtypeStruct((rows, inner_rows * row_count, block, block), dtype),
        in_specs=[SMEM] + [VMEM] * col_count,
        out_specs=VMEM,
        compiler_params=PARAMS,
    )(index_of(a_parts, a_count), *a_parts)

    def step(groups, picks, before, last):
        place = jnp.stack([first] + [groups[g][0] * inner_rows + m for g, m, _ in picks]).astype(jnp.int32)
        valid = [jnp.int32(0)] + [groups[g][0] for g, _, _ in picks]
        place = jnp.where(jnp.stack(valid) >= 0, place, -1)
        if last:
            out = jax.ShapeDtypeStruct((rows, slots, block, block), dtype)
        else:
            out = jax.ShapeDtypeStruct((rows, block, slots * block), jnp.float32)
        scratch = [pltpu.VMEM((rows, block, slots * block), dtype), pltpu.SMEM((COLS_DEV,), jnp.int32)]
        if last:
            scratch = [pltpu.VMEM((rows, block, slots * block), jnp.float32)] + scratch
        flops = 2 * rows * len(picks) * slots * block**3
        held = [dense] if before is None else [dense, before]
        return pl.pallas_call(
            functools.partial(step_kernel, [(g, m) for g, m, _ in picks], last, before is None),
            out_shape=out,
            in_specs=[SMEM] * 3 + [VMEM] * (len(picks) + len(held)),
            out_specs=VMEM,
            scratch_shapes=scratch,
            compiler_params=PARAMS,
            cost_estimate=pl.CostEstimate(flops=flops, bytes_accessed=2**21, transcendentals=0),
        )(place, c_cols, index_of([x for _, x in groups], b_count), *[x for _, _, x in picks], *held)

    def of_round(t):
        return [(origin(kind, t), chunks) for kind, chunks in enumerate(rounds[t - 1]) if chunks is not None]

    total = None
    for t in range(1, row_count):
        pieces = ([(r, b_own)] if t == 1 else []) + of_round(t)
        groups = [(source, chunks[0]) for source, chunks in pieces]
        picks = [(g, m, x) for g, (_, chunks) in enumerate(pieces) for m, x in enumerate(chunks)]
        if t + 1 < row_count:
            total = step(groups, picks, total, False)
        else:
            if len(picks) > 1:
                total = step(groups, picks[:-1], total, False)
            total = step(groups, picks[-1:], total, True)
    return total


def solution(mesh):
    return jax.shard_map(
        functools.partial(body, mesh.shape["row"], mesh.shape["col"]),
        mesh=mesh,
        in_specs=(
            P(("groups", "row"), "col", None, None),
            P(("groups", "row"), "col"),
            P(("groups", "row"), "col", None, None),
            P(("groups", "row"), "col"),
            P(("groups", "row"), "col"),
        ),
        out_specs=P(("groups", "row"), "col", None, None),
        check_vma=False,
    )
```

time: 136 us -> 53.1 us (0.39)
  waiting for transfers between devices: 90.2 us -> 12.4 us
  starting transfers between devices: 0.04 us -> 28.5 us
  between operations: 13.4 us -> 0.18 us
  local copies, waits for them, and re-layouts: 15.5 us -> 4.06 us
  Pallas kernels: 0 us -> 7.48 us
  matrix products: 6.96 us -> 0 us
  blocking collectives: 6.25 us -> 0 us
  other arithmetic: 2.96 us -> 0.24 us
    all_gather x2 -> x0, waiting for transfers between devices: 90.1 us -> none  [the longest x1 80.2 us: body(): slab = lax.all_gather(prepared, 'row', axis=0, tiled=True)]
    ppermute x0 -> x13, starting transfers between devices: none -> 28.5 us  [the longest x10 26.4 us: exchange(): return lax.ppermute(x, 'row', pairs)]
    ppermute x0 -> x13, waiting for transfers between devices: none -> 12.4 us  [the longest x10 11.3 us: exchange(): return lax.ppermute(x, 'row', pairs)]
    pallas_call x0 -> x6, Pallas kernels: none -> 7.48 us  [the longest x4 5.92 us: step(): pl.pallas_call(functools.partial(step_kernel, [(g, m) for g, m, _ in pick...]
    dot_general x3 -> x0, matrix products: 6.96 us -> none  [the longest x1 3.47 us: body(): total = jnp.dot(chosen, right, preferred_element_type=jnp.float32)]
    reshape x1 -> x0, local copies, waits for them, and re-layouts: 6.39 us -> none  [body(): right = slab.reshape(count * block, width * block)]
    all_gather x1 -> x0, blocking collectives: 6.25 us -> none  [body(): lax.all_gather(a_cols, 'col', axis=1, tiled=True)]
    unnamed x5 -> x10, local copies, waits for them, and re-layouts: 8.1 us -> 2.69 us
  transfers between devices with their start and end apart: 2 -> 13, of which waited for: 2 -> 4; matrix products, arithmetic and copies ran while one was open for 4% -> 3% of each run, Pallas kernels for 0% -> 10%
where the time goes in v4:
time: 53.1 us; the launch traced here: 52.9 us
  starting transfers between devices  28.5 us (54%)
  waiting for transfers between devices  12.4 us (23%)
  Pallas kernels  7.48 us (14%)
  local copies, waits for them, and re-layouts  4.06 us (8%)
    ppermute x10, starting transfers between devices, exchange(): return lax.ppermute(x, 'row', pairs)  26.4 us
    ppermute x10, waiting for transfers between devices, exchange(): return lax.ppermute(x, 'row', pairs)  11.3 us
    pallas_call x4, Pallas kernels, step(): pl.pallas_call(functools.partial(step_kernel, [(g, m) for g, m, _ in pick...  5.92 us
    unnamed x10, local copies, waits for them, and re-layouts  2.69 us
    ppermute x3, starting transfers between devices, body(): lax.ppermute(x, 'col', [(k, k ^ d) for k in range(col_count)])  2.07 us
    ppermute x3, waiting for transfers between devices, body(): lax.ppermute(x, 'col', [(k, k ^ d) for k in range(col_count)])  1.15 us
  transfers between devices with their start and end apart: 13, of which 4 were waited for; matrix products, arithmetic and copies ran while one was open for 3% of the time, Pallas kernels for 10%

profile of v4, /device:TPU:0, one launch (start us, length us, event | category | flops | bytes accessed | tf_op | source)
XLA Modules:
  0.0 52.9 jit_solution(6798262401838587135)
XLA Ops:
  0.0 0.7 %copy-done.4 = s32[2,8]{1,0:T(2,128)S(1)} copy-done((s32[2,8]{1,0:T(2,128)S(1)}, s32[2,8]{1,0:T(2,128)}, u32[]{:S(2)}) %copy-start.4) | copy-done | bytes 88
  0.7 1.0 %copy-done = bf16[2,8,128,128]{3,2,1,0:T(8,128)(2,1)S(1)} copy-done((bf16[2,8,128,128]{3,2,1,0:T(8,128)(2,1)S(1)}, bf16[2,8,128,128]{3,2,1,0:T(8,128)(2,1)}, u32[]{:S(2)}) %copy-start) | copy-done | bytes 524312
  1.7 0.9 %copy-done.1 = bf16[2,4,128,128]{3,2,1,0:T(8,128)(2,1)S(1)} copy-done((bf16[2,4,128,128]{3,2,1,0:T(8,128)(2,1)S(1)}, bf16[2,4,128,128]{3,2,1,0:T(8,128)(2,1)}, u32[]{:S(2)}) %copy-start.1) | copy-done | bytes 262168
  2.7 0.7 %shard_map.55 = (bf16[1040,128]{1,0:T(8,128)(2,1)S(1)}, bf16[1040,128]{1,0:T(8,128)(2,1)S(1)}, bf16[1024,128]{1,0:T(8,128)(2,1)S(1)}) custom-call(s32[2,4]{1,0:T(2,128)S(1)} %copy-done.3, s32[2,8]{1,0:T(2,128)S(1)} %copy-done.4, bf16[1024,128]{1,0:T(8,128)(2,1)S(1)} %bitcast.32, bf16[2,1024,128]{2,1,0:T(8,128)(2,1)S(1)} %bitcast.31), custom_call_target="tpu_custom_call" | custom-call | tf_op jit(solution)/shard_map/pallas_call | solution.py:111
  3.4 3.1 %collective-permute-start = (bf16[1040,128]{1,0:T(8,128)(2,1)S(1)}, bf16[1040,128]{1,0:T(8,128)(2,1)S(1)}, u32[]{:S(2)}, u32[]{:S(2)}) collective-permute-start(bf16[1040,128]{1,0:T(8,128)(2,1)S(1)} %get-tuple-element.15.refs_0_), channel_id=1, source_target_pairs={{0,4},{4,0},{8,12},{12,8},{1,5},{5,1},{9,13},{13,9},{2,6},{6,2},{1... | collective-permute-start | bytes 798728 | tf_op jit(solution)/shard_map/ppermute | solution.py:128
  6.5 0.7 %collective-permute-start.9 = (bf16[1040,128]{1,0:T(8,128)(2,1)S(1)}, bf16[1040,128]{1,0:T(8,128)(2,1)S(1)}, u32[]{:S(2)}, u32[]{:S(2)}) collective-permute-start(bf16[1040,128]{1,0:T(8,128)(2,1)S(1)} %get-tuple-element.15.refs_0_), channel_id=1, source_target_pairs={{0,0},{4,8},{8,4},{12,12},{1,1},{5,9},{9,5},{13,13},{2,2},{6,10},{... | collective-permute-start | bytes 798728 | tf_op jit(solution)/shard_map/ppermute | solution.py:128
  7.1 4.4 %collective-permute-start.3 = (bf16[1024,128]{1,0:T(8,128)(2,1)S(1)}, bf16[1024,128]{1,0:T(8,128)(2,1)S(1)}, u32[]{:S(2)}, u32[]{:S(2)}) collective-permute-start(bf16[1024,128]{1,0:T(8,128)(2,1)S(1)} %get-tuple-element.16.refs_1_), channel_id=1, source_target_pairs={{0,4},{4,0},{8,12},{12,8},{1,5},{5,1},{9,13},{13,9},{2,6},{6,2},{1... | collective-permute-start | bytes 786440 | tf_op jit(solution)/shard_map/ppermute | solution.py:128
  11.6 0.7 %collective-permute-start.11 = (bf16[1024,128]{1,0:T(8,128)(2,1)S(1)}, bf16[1024,128]{1,0:T(8,128)(2,1)S(1)}, u32[]{:S(2)}, u32[]{:S(2)}) collective-permute-start(bf16[1024,128]{1,0:T(8,128)(2,1)S(1)} %get-tuple-element.16.refs_1_), channel_id=1, source_target_pairs={{0,0},{4,8},{8,4},{12,12},{1,1},{5,9},{9,5},{13,13},{2,2},{6,10},{... | collective-permute-start | bytes 786440 | tf_op jit(solution)/shard_map/ppermute | solution.py:128
  12.2 1.6 %collective-permute-start.5 = (bf16[1040,128]{1,0:T(8,128)(2,1)S(1)}, bf16[1040,128]{1,0:T(8,128)(2,1)S(1)}, u32[]{:S(2)}, u32[]{:S(2)}) collective-permute-start(bf16[1040,128]{1,0:T(8,128)(2,1)S(1)} %get-tuple-element.20.own), channel_id=1, source_target_pairs={{0,2},{1,3},{2,0},{3,1},{4,6},{5,7},{6,4},{7,5},{8,10},{9,11},{10,... | collective-permute-start | bytes 798728 | tf_op jit(solution)/shard_map/ppermute | solution.py:153
  13.8 0.1 slice_reduce_fusion.8
  14.5 4.0 %collective-permute-done.3.refs_3_ = bf16[1024,128]{1,0:T(8,128)(2,1)S(1)} collective-permute-done((bf16[1024,128]{1,0:T(8,128)(2,1)S(1)}, bf16[1024,128]{1,0:T(8,128)(2,1)S(1)}, u32[]{:S(2)}, u32[]{:S(2)}) %collective-permute-start.3) | collective-permute-done | bytes 262176 | tf_op jit(solution)/shard_map/ppermute | solution.py:128
  18.5 1.1 %collective-permute-done.5.refs_0_ = bf16[1040,128]{1,0:T(8,128)(2,1)S(1)} collective-permute-done((bf16[1040,128]{1,0:T(8,128)(2,1)S(1)}, bf16[1040,128]{1,0:T(8,128)(2,1)S(1)}, u32[]{:S(2)}, u32[]{:S(2)}) %collective-permute-start.5) | collective-permute-done | bytes 266272 | tf_op jit(solution)/shard_map/ppermute | solution.py:153
  19.6 0.5 collective-permute-start.7
  20.1 0.7 %collective-permute-start.4 = (bf16[1024,128]{1,0:T(8,128)(2,1)S(1)}, bf16[1024,128]{1,0:T(8,128)(2,1)S(1)}, u32[]{:S(2)}, u32[]{:S(2)}) collective-permute-start(bf16[1024,128]{1,0:T(8,128)(2,1)S(1)} %collective-permute-done.3.refs_3_), channel_id=1, source_target_pairs={{0,0},{4,8},{8,4},{12,12},{1,1},{5,9},{9,5},{13,13},{2,2},{6,10},{... | collective-permute-start | bytes 786440 | tf_op jit(solution)/shard_map/ppermute | solution.py:128
  20.8 6.1 %collective-permute-start.12 = (bf16[1024,128]{1,0:T(8,128)(2,1)S(1)}, bf16[1024,128]{1,0:T(8,128)(2,1)S(1)}, u32[]{:S(2)}, u32[]{:S(2)}) collective-permute-start(bf16[1024,128]{1,0:T(8,128)(2,1)S(1)} %collective-permute-done.11.refs_5_), channel_id=1, source_target_pairs={{0,4},{4,0},{8,12},{12,8},{1,5},{5,1},{9,13},{13,9},{2,6},{6,2},{1... | collective-permute-start | bytes 786440 | tf_op jit(solution)/shard_map/ppermute | solution.py:128
  27.0 0.7 %collective-permute-start.1 = (bf16[1040,128]{1,0:T(8,128)(2,1)S(1)}, bf16[1040,128]{1,0:T(8,128)(2,1)S(1)}, u32[]{:S(2)}, u32[]{:S(2)}) collective-permute-start(bf16[1040,128]{1,0:T(8,128)(2,1)S(1)} %collective-permute-done.refs_2_), channel_id=1, source_target_pairs={{0,0},{4,8},{8,4},{12,12},{1,1},{5,9},{9,5},{13,13},{2,2},{6,10},{... | collective-permute-start | bytes 798728 | tf_op jit(solution)/shard_map/ppermute | solution.py:128
  27.7 0.1 slice_reduce_fusion
  27.9 0.1 slice_reduce_fusion.7
  28.0 6.4 %collective-permute-start.10 = (bf16[1040,128]{1,0:T(8,128)(2,1)S(1)}, bf16[1040,128]{1,0:T(8,128)(2,1)S(1)}, u32[]{:S(2)}, u32[]{:S(2)}) collective-permute-start(bf16[1040,128]{1,0:T(8,128)(2,1)S(1)} %collective-permute-done.9.refs_4_), channel_id=1, source_target_pairs={{0,4},{4,0},{8,12},{12,8},{1,5},{5,1},{9,13},{13,9},{2,6},{6,2},{1... | collective-permute-start | bytes 798728 | tf_op jit(solution)/shard_map/ppermute | solution.py:128
  34.4 3.6 %collective-permute-start.8 = (bf16[1024,128]{1,0:T(8,128)(2,1)S(1)}, bf16[1024,128]{1,0:T(8,128)(2,1)S(1)}, u32[]{:S(2)}, u32[]{:S(2)}) collective-permute-start(bf16[1024,128]{1,0:T(8,128)(2,1)S(1)} %collective-permute-done.4.refs_3_), channel_id=1, source_target_pairs={{0,4},{4,0},{8,12},{12,8},{1,5},{5,1},{9,13},{13,9},{2,6},{6,2},{1... | collective-permute-start | bytes 786440 | tf_op jit(solution)/shard_map/ppermute | solution.py:128
  38.0 0.1 slice_reduce_fusion.6
  38.1 0.1 slice_reduce_fusion.5
  38.3 0.9 %shard_map.56.refs_6_.refs_4_.refs_1_ = bf16[2,8,128,128]{3,2,1,0:T(8,128)(2,1)S(1)} custom-call(s32[4,8]{1,0:T(4,128)S(1)} %maximum_convert_fusion.index, bf16[1040,128]{1,0:T(8,128)(2,1)S(1)} %get-tuple-element.20.own, bf16[1040,128]{1,0:T(8,128)(2,1)S(1)} %collective-permute-done.5.refs_0_, bf16[1040,128]{1,0:T(8,128)(2,1)S(1)} %collective-permute-done.6.refs_1_, ...), custom_call_target="tpu_custom_call" | custom-call | tf_op jit(solution)/shard_map/pallas_call | solution.py:168
  39.2 0.1 slice_reduce_fusion.2
  39.3 1.3 %collective-permute-done.10.refs_0_ = bf16[1040,128]{1,0:T(8,128)(2,1)S(1)} collective-permute-done((bf16[1040,128]{1,0:T(8,128)(2,1)S(1)}, bf16[1040,128]{1,0:T(8,128)(2,1)S(1)}, u32[]{:S(2)}, u32[]{:S(2)}) %collective-permute-start.10) | collective-permute-done | bytes 266272 | tf_op jit(solution)/shard_map/ppermute | solution.py:128
  40.6 0.1 slice_reduce_fusion.3
  40.7 2.0 %shard_map.57.refs_5_ = f32[2,128,768]{2,1,0:T(8,128)S(1)} custom-call(s32[7]{0:T(128)S(1)} %compare_select_fusion.place, s32[2,6]{1,0:T(2,128)S(1)} %copy-done.2, s32[3,16]{1,0:T(4,128)S(1)} %maximum_convert_fusion.1.index, bf16[1040,128]{1,0:T(8,128)(2,1)S(1)} %get-tuple-element.15.refs_0_, bf16[1024,128]{1,0:T(8,128)(2,1)S(1)} %get-tuple-element.16.refs_1_, ...), custom_call_target="tpu_custom_call" | custom-call | flops 301989888 | bytes 2097152 | tf_op jit(solution)/shard_map/pallas_call | solution.py:189
  42.7 1.3 %shard_map.58.refs_2_ = f32[2,128,768]{2,1,0:T(8,128)S(1)} custom-call(s32[5]{0:T(128)S(1)} %compare_select_fusion.1.place, s32[2,6]{1,0:T(2,128)S(1)} %copy-done.2, s32[2,16]{1,0:T(2,128)S(1)} %maximum_convert_fusion.2.index, bf16[1040,128]{1,0:T(8,128)(2,1)S(1)} %collective-permute-done.10.refs_0_, bf16[1024,128]{1,0:T(8,128)(2,1)S(1)} %collective-permute-done.12.refs_1_, ...), custom_call_target="tpu_custom_call" | custom-call | flops 201326592 | bytes 2097152 | tf_op jit(solution)/shard_map/pallas_call | solution.py:189
  44.0 6.0 %collective-permute-done.2.refs_0_ = bf16[1040,128]{1,0:T(8,128)(2,1)S(1)} collective-permute-done((bf16[1040,128]{1,0:T(8,128)(2,1)S(1)}, bf16[1040,128]{1,0:T(8,128)(2,1)S(1)}, u32[]{:S(2)}, u32[]{:S(2)}) %collective-permute-start.2) | collective-permute-done | bytes 266272 | tf_op jit(solution)/shard_map/ppermute | solution.py:128
  50.1 0.1 convert_reduce_fusion
  50.2 0.9 %shard_map.59.refs_2_ = f32[2,128,768]{2,1,0:T(8,128)S(1)} custom-call(s32[2]{0:T(128)S(1)} %get-tuple-element.25.place, s32[2,6]{1,0:T(2,128)S(1)} %copy-done.2, s32[1,16]{1,0:T(1,128)S(1)} %bitcast.33, bf16[1040,128]{1,0:T(8,128)(2,1)S(1)} %collective-permute-done.2.refs_0_, bf16[2,8,128,128]{3,2,1,0:T(8,128)(2,1)S(1)} %shard_map.56.refs_6_.refs_4_.refs_1_, ...), custom_call_target="tpu_custom_call" | custom-call | flops 50331648 | bytes 2097152 | tf_op jit(solution)/shard_map/pallas_call | solution.py:189
  51.1 1.7 %shard_map.60 = bf16[2,6,128,128]{3,2,1,0:T(8,128)(2,1)} custom-call(s32[2]{0:T(128)S(1)} %get-tuple-element.26.place, s32[2,6]{1,0:T(2,128)S(1)} %copy-done.2, s32[1,16]{1,0:T(1,128)S(1)} %bitcast.34, bf16[1024,128]{1,0:T(8,128)(2,1)S(1)} %collective-permute-done.8.refs_0_, bf16[2,8,128,128]{3,2,1,0:T(8,128)(2,1)S(1)} %shard_map.56.refs_6_.refs_4_.refs_1_, ...), custom_call_target="tpu_custom_call" | custom-call | flops 50331648 | bytes 2097152 | tf_op jit(solution)/shard_map/pallas_call | solution.py:189
  (30 shorter events, 0.8 us)
Async XLA Ops:
  0.0 0.7 %copy-start.4 = (s32[2,8]{1,0:T(2,128)S(1)}, s32[2,8]{1,0:T(2,128)}, u32[]{:S(2)}) copy-start(s32[2,8]{1,0:T(2,128)} %b_index.1) | copy-start | bytes 196
  0.0 0.7 %copy-start.3 = (s32[2,4]{1,0:T(2,128)S(1)}, s32[2,4]{1,0:T(2,128)}, u32[]{:S(2)}) copy-start(s32[2,4]{1,0:T(2,128)} %a_index.1) | copy-start | bytes 100
  0.7 1.0 %copy-start = (bf16[2,8,128,128]{3,2,1,0:T(8,128)(2,1)S(1)}, bf16[2,8,128,128]{3,2,1,0:T(8,128)(2,1)}, u32[]{:S(2)}) copy-start(bf16[2,8,128,128]{3,2,1,0:T(8,128)(2,1)} %param.7) | copy-start | bytes 1572868
  1.7 0.9 %copy-start.1 = (bf16[2,4,128,128]{3,2,1,0:T(8,128)(2,1)S(1)}, bf16[2,4,128,128]{3,2,1,0:T(8,128)(2,1)}, u32[]{:S(2)}) copy-start(bf16[2,4,128,128]{3,2,1,0:T(8,128)(2,1)} %param.5) | copy-start | bytes 786436
  3.4 16.8 %collective-permute-start = (bf16[1040,128]{1,0:T(8,128)(2,1)S(1)}, bf16[1040,128]{1,0:T(8,128)(2,1)S(1)}, u32[]{:S(2)}, u32[]{:S(2)}) collective-permute-start(bf16[1040,128]{1,0:T(8,128)(2,1)S(1)} %get-tuple-element.15.refs_0_), channel_id=1, source_target_pairs={{0,4},{4,0},{8,12},{12,8},{1,5},{5,1},{9,13},{13,9},{2,6},{6,2},{1... | collective-permute-start | bytes 798728 | tf_op jit(solution)/shard_map/ppermute | solution.py:128
  6.5 13.7 %collective-permute-start.9 = (bf16[1040,128]{1,0:T(8,128)(2,1)S(1)}, bf16[1040,128]{1,0:T(8,128)(2,1)S(1)}, u32[]{:S(2)}, u32[]{:S(2)}) collective-permute-start(bf16[1040,128]{1,0:T(8,128)(2,1)S(1)} %get-tuple-element.15.refs_0_), channel_id=1, source_target_pairs={{0,0},{4,8},{8,4},{12,12},{1,1},{5,9},{9,5},{13,13},{2,2},{6,10},{... | collective-permute-start | bytes 798728 | tf_op jit(solution)/shard_map/ppermute | solution.py:128
  7.1 11.3 %collective-permute-start.3 = (bf16[1024,128]{1,0:T(8,128)(2,1)S(1)}, bf16[1024,128]{1,0:T(8,128)(2,1)S(1)}, u32[]{:S(2)}, u32[]{:S(2)}) collective-permute-start(bf16[1024,128]{1,0:T(8,128)(2,1)S(1)} %get-tuple-element.16.refs_1_), channel_id=1, source_target_pairs={{0,4},{4,0},{8,12},{12,8},{1,5},{5,1},{9,13},{13,9},{2,6},{6,2},{1... | collective-permute-start | bytes 786440 | tf_op jit(solution)/shard_map/ppermute | solution.py:128
  11.6 8.5 %collective-permute-start.11 = (bf16[1024,128]{1,0:T(8,128)(2,1)S(1)}, bf16[1024,128]{1,0:T(8,128)(2,1)S(1)}, u32[]{:S(2)}, u32[]{:S(2)}) collective-permute-start(bf16[1024,128]{1,0:T(8,128)(2,1)S(1)} %get-tuple-element.16.refs_1_), channel_id=1, source_target_pairs={{0,0},{4,8},{8,4},{12,12},{1,1},{5,9},{9,5},{13,13},{2,2},{6,10},{... | collective-permute-start | bytes 786440 | tf_op jit(solution)/shard_map/ppermute | solution.py:128
  12.2 7.4 %collective-permute-start.5 = (bf16[1040,128]{1,0:T(8,128)(2,1)S(1)}, bf16[1040,128]{1,0:T(8,128)(2,1)S(1)}, u32[]{:S(2)}, u32[]{:S(2)}) collective-permute-start(bf16[1040,128]{1,0:T(8,128)(2,1)S(1)} %get-tuple-element.20.own), channel_id=1, source_target_pairs={{0,2},{1,3},{2,0},{3,1},{4,6},{5,7},{6,4},{7,5},{8,10},{9,11},{10,... | collective-permute-start | bytes 798728 | tf_op jit(solution)/shard_map/ppermute | solution.py:153
  19.6 14.8 %collective-permute-start.6 = (bf16[1040,128]{1,0:T(8,128)(2,1)S(1)}, bf16[1040,128]{1,0:T(8,128)(2,1)S(1)}, u32[]{:S(2)}, u32[]{:S(2)}) collective-permute-start(bf16[1040,128]{1,0:T(8,128)(2,1)S(1)} %get-tuple-element.20.own), channel_id=1, source_target_pairs={{0,1},{1,0},{2,3},{3,2},{4,5},{5,4},{6,7},{7,6},{8,9},{9,8},{10,11... | collective-permute-start | bytes 798728 | tf_op jit(solution)/shard_map/ppermute | solution.py:153
  19.6 14.8 %collective-permute-start.7 = (bf16[1040,128]{1,0:T(8,128)(2,1)S(1)}, bf16[1040,128]{1,0:T(8,128)(2,1)S(1)}, u32[]{:S(2)}, u32[]{:S(2)}) collective-permute-start(bf16[1040,128]{1,0:T(8,128)(2,1)S(1)} %collective-permute-done.5.refs_0_), channel_id=1, source_target_pairs={{0,1},{1,0},{2,3},{3,2},{4,5},{5,4},{6,7},{7,6},{8,9},{9,8},{10,11... | collective-permute-start | bytes 798728 | tf_op jit(solution)/shard_map/ppermute | solution.py:153
  20.1 7.8 %collective-permute-start.4 = (bf16[1024,128]{1,0:T(8,128)(2,1)S(1)}, bf16[1024,128]{1,0:T(8,128)(2,1)S(1)}, u32[]{:S(2)}, u32[]{:S(2)}) collective-permute-start(bf16[1024,128]{1,0:T(8,128)(2,1)S(1)} %collective-permute-done.3.refs_3_), channel_id=1, source_target_pairs={{0,0},{4,8},{8,4},{12,12},{1,1},{5,9},{9,5},{13,13},{2,2},{6,10},{... | collective-permute-start | bytes 786440 | tf_op jit(solution)/shard_map/ppermute | solution.py:128
  20.8 21.9 %collective-permute-start.12 = (bf16[1024,128]{1,0:T(8,128)(2,1)S(1)}, bf16[1024,128]{1,0:T(8,128)(2,1)S(1)}, u32[]{:S(2)}, u32[]{:S(2)}) collective-permute-start(bf16[1024,128]{1,0:T(8,128)(2,1)S(1)} %collective-permute-done.11.refs_5_), channel_id=1, source_target_pairs={{0,4},{4,0},{8,12},{12,8},{1,5},{5,1},{9,13},{13,9},{2,6},{6,2},{1... | collective-permute-start | bytes 786440 | tf_op jit(solution)/shard_map/ppermute | solution.py:128
  27.0 7.3 %collective-permute-start.1 = (bf16[1040,128]{1,0:T(8,128)(2,1)S(1)}, bf16[1040,128]{1,0:T(8,128)(2,1)S(1)}, u32[]{:S(2)}, u32[]{:S(2)}) collective-permute-start(bf16[1040,128]{1,0:T(8,128)(2,1)S(1)} %collective-permute-done.refs_2_), channel_id=1, source_target_pairs={{0,0},{4,8},{8,4},{12,12},{1,1},{5,9},{9,5},{13,13},{2,2},{6,10},{... | collective-permute-start | bytes 798728 | tf_op jit(solution)/shard_map/ppermute | solution.py:128
  28.0 12.6 %collective-permute-start.10 = (bf16[1040,128]{1,0:T(8,128)(2,1)S(1)}, bf16[1040,128]{1,0:T(8,128)(2,1)S(1)}, u32[]{:S(2)}, u32[]{:S(2)}) collective-permute-start(bf16[1040,128]{1,0:T(8,128)(2,1)S(1)} %collective-permute-done.9.refs_4_), channel_id=1, source_target_pairs={{0,4},{4,0},{8,12},{12,8},{1,5},{5,1},{9,13},{13,9},{2,6},{6,2},{1... | collective-permute-start | bytes 798728 | tf_op jit(solution)/shard_map/ppermute | solution.py:128
  34.4 16.8 %collective-permute-start.8 = (bf16[1024,128]{1,0:T(8,128)(2,1)S(1)}, bf16[1024,128]{1,0:T(8,128)(2,1)S(1)}, u32[]{:S(2)}, u32[]{:S(2)}) collective-permute-start(bf16[1024,128]{1,0:T(8,128)(2,1)S(1)} %collective-permute-done.4.refs_3_), channel_id=1, source_target_pairs={{0,4},{4,0},{8,12},{12,8},{1,5},{5,1},{9,13},{13,9},{2,6},{6,2},{1... | collective-permute-start | bytes 786440 | tf_op jit(solution)/shard_map/ppermute | solution.py:128
  38.2 11.8 %collective-permute-start.2 = (bf16[1040,128]{1,0:T(8,128)(2,1)S(1)}, bf16[1040,128]{1,0:T(8,128)(2,1)S(1)}, u32[]{:S(2)}, u32[]{:S(2)}) collective-permute-start(bf16[1040,128]{1,0:T(8,128)(2,1)S(1)} %collective-permute-done.1.refs_2_), channel_id=1, source_target_pairs={{0,4},{4,0},{8,12},{12,8},{1,5},{5,1},{9,13},{13,9},{2,6},{6,2},{1... | collective-permute-start | bytes 798728 | tf_op jit(solution)/shard_map/ppermute | solution.py:128
  39.3 1.4 %copy-start.2 = (s32[2,6]{1,0:T(2,128)S(1)}, s32[2,6]{1,0:T(2,128)}, u32[]{:S(2)}) copy-start(s32[2,6]{1,0:T(2,128)} %wanted.7) | copy-start | bytes 148

commit v5 on v3

--- a/solution.py
+++ b/solution.py
@@ -87,18 +87,24 @@
     inner_count = inner_rows * row_count
     r = lax.axis_index("row")
     first = lax.axis_index("col") * COLS_DEV
-    sides = [jnp.where(r % 2 == kind, 1, -1) for kind in (0, 1)]
-
-    def pairs(kind, t):
-        found = []
+    q = lax.axis_index("col")
+
+    def side_of(kind, row, col):
+        return 1 - 2 * ((row + col + kind) % 2)
+
+    def exchange(x, kind, t):
+        pairs = []
         for k in range(row_count):
-            side = 1 if k % 2 == kind else -1
-            if 0 <= k + side < row_count and 0 <= k + side * t < row_count:
-                found.append((k + side, k))
-        return found
+            for c in range(col_count):
+                side = side_of(kind, k, c)
+                other = k + side
+                inside = 0 <= other < row_count
+                wanted = inside and (0 <= k + side * t < row_count or 0 <= other - side * t < row_count)
+                pairs.append(((other if wanted else k) * col_count + c, k * col_count + c))
+        return lax.ppermute(x, ("row", "col"), pairs)
 
     def origin(kind, t):
-        row = r + sides[kind] * t
+        row = r + side_of(kind, r, q) * t
         return jnp.where((row >= 0) & (row < row_count), row, -1)
 
     def swap(x, axis, n, d):
@@ -115,26 +121,22 @@
             x = jnp.concatenate([x, swap(x, axis, n, d)], axis=0)
             yield x
 
-    rounds = [[lax.ppermute(b_tiles, "row", pairs(kind, 1)) for kind in (0, 1)]]
+    def kinds(t):
+        return (0, 1) if t % 2 else (1, 0)
+
+    rounds = [[exchange(b_tiles, kind, 1) for kind in kinds(1)]]
     a_parts = [a_tiles]
     for d in halves(col_count):
         a_parts = a_parts + [swap(x, "col", col_count, d) for x in a_parts]
     a_index = list(gather(a_cols, "col", col_count, halves(col_count)))
     b_index = list(gather(b_cols, "row", row_count, reversed(list(halves(row_count)))))
     for t in range(2, row_count):
-        even, odd = rounds[-1]
+        one, two = rounds[-1]
         if t == 2:
-            early = (even, odd, a_index[0], b_index[0], a_parts[1])
-            even, odd, a_index[0], b_index[0], a_parts[1] = lax.optimization_barrier(early)
+            two = lax.optimization_barrier((two, a_index[0], b_index[0], a_parts[1]))[0]
         if t == 3:
-            odd, a_index, b_index, a_parts = lax.optimization_barrier((odd, a_index, b_index, a_parts))
-        rounds[-1] = [even, odd]
-        rounds.append(
-            [
-                lax.ppermute(x, "row", pairs(kind, t)) if pairs(kind, t) else None
-                for kind, x in ((0, odd), (1, even))
-            ]
-        )
+            two = lax.optimization_barrier((two, a_index, b_index, a_parts))[0]
+        rounds.append([exchange(x, kind, t) for kind, x in zip(kinds(t), (one, two))])
 
     here = jnp.stack([first, r]).astype(jnp.int32)
     dense, table = pl.pallas_call(
@@ -173,11 +175,14 @@
 
     total = None
     for t in range(1, row_count):
-        pieces = [(r, b_tiles)] if t == 1 else []
-        for kind in (0, 1):
-            if rounds[t - 1][kind] is not None:
-                pieces.append((origin(kind, t), rounds[t - 1][kind]))
-        total = step(pieces, total, t + 1 == row_count)
+        pieces = [(origin(kind, t), x) for kind, x in zip(kinds(t), rounds[t - 1])]
+        if t == 1:
+            pieces = [(r, b_tiles)] + pieces
+        if t + 1 < row_count:
+            total = step(pieces, total, False)
+        else:
+            total = step(pieces[:-1], total, False)
+            total = step(pieces[-1:], total, True)
     return total
 
 

time: 53.2 us -> 51.8 us (0.974); the launches traced: 53 us -> 51 us
  waiting for transfers between devices: 22.3 us -> 6.27 us
  starting transfers between devices: 21.4 us -> 31.5 us
  local copies, waits for them, and re-layouts: 1.65 us -> 4.95 us
  Pallas kernels: 6.47 us -> 7.08 us
    ppermute x5 -> x6, starting transfers between devices: 6.98 us -> 25.1 us  [exchange(): return lax.ppermute(x, ('row', 'col'), pairs)]
    ppermute x7, waiting for transfers between devices: 13.3 us -> 5.16 us  [swap(): return lax.ppermute(x, axis, [(k, k ^ d) for k in range(n)])]
    ppermute x7, starting transfers between devices: 14.4 us -> 6.36 us  [swap(): return lax.ppermute(x, axis, [(k, k ^ d) for k in range(n)])]
    ppermute x5 -> x6, waiting for transfers between devices: 8.99 us -> 1.12 us  [exchange(): return lax.ppermute(x, ('row', 'col'), pairs)]
    unnamed x10 -> x18, local copies, waits for them, and re-layouts: 1.56 us -> 4.86 us
    pallas_call x3 -> x4, Pallas kernels: 4.52 us -> 5.13 us  [step(): pl.pallas_call(functools.partial(step_kernel, parts, last), out_shape=out...]
  transfers between devices with their start and end apart: 12 -> 13, of which waited for: 4 -> 3; matrix products, arithmetic and copies ran while one was open for 2% -> 2% of each run, Pallas kernels for 9% -> 11%
where the time goes in v5:
time: 51.8 us; the launch traced here: 51 us
  starting transfers between devices  31.5 us (61%)
  Pallas kernels  7.08 us (14%)
  waiting for transfers between devices  6.27 us (12%)
  local copies, waits for them, and re-layouts  4.95 us (10%)
  other arithmetic  0.94 us (2%)
    ppermute x6, starting transfers between devices, exchange(): return lax.ppermute(x, ('row', 'col'), pairs)  25.1 us
    ppermute x7, starting transfers between devices, swap(): return lax.ppermute(x, axis, [(k, k ^ d) for k in range(n)])  6.36 us
    ppermute x7, waiting for transfers between devices, swap(): return lax.ppermute(x, axis, [(k, k ^ d) for k in range(n)])  5.16 us
    pallas_call x4, Pallas kernels, step(): pl.pallas_call(functools.partial(step_kernel, parts, last), out_shape=out...  5.13 us
    unnamed x18, local copies, waits for them, and re-layouts  4.86 us
    pallas_call x1, Pallas kernels, body(): pl.pallas_call(functools.partial(prepare_kernel, row_count, col_count), o...  1.95 us
    ppermute x6, waiting for transfers between devices, exchange(): return lax.ppermute(x, ('row', 'col'), pairs)  1.12 us
  transfers between devices with their start and end apart: 13, of which 3 were waited for; matrix products, arithmetic and copies ran while one was open for 2% of the time, Pallas kernels for 11%

profile of v5, /device:TPU:0, one launch (start us, length us, event | category | flops | bytes accessed | tf_op | source)
XLA Modules:
  0.0 51.0 jit_solution(14964136032454189606)
XLA Ops:
  0.0 5.1 %collective-permute-start.10 = (bf16[2,8,128,128]{3,2,1,0:T(8,128)(2,1)}, bf16[2,8,128,128]{3,2,1,0:T(8,128)(2,1)S(1)}, u32[]{:S(2)}, u32[]{:S(2)}) collective-permute-start(bf16[2,8,128,128]{3,2,1,0:T(8,128)(2,1)} %refs_0_.3), channel_id=1, source_target_pairs={{4,0},{1,1},{6,2},{3,3},{0,4},{9,5},{2,6},{11,7},{12,8},{5,9},{14,... | collective-permute-start | bytes 1572872 | tf_op jit(solution)/shard_map/ppermute | solution.py:104
  5.1 1.7 %collective-permute-start.7 = (bf16[2,8,128,128]{3,2,1,0:T(8,128)(2,1)}, bf16[2,8,128,128]{3,2,1,0:T(8,128)(2,1)S(1)}, u32[]{:S(2)}, u32[]{:S(2)}) collective-permute-start(bf16[2,8,128,128]{3,2,1,0:T(8,128)(2,1)} %refs_0_.3), channel_id=1, source_target_pairs={{0,0},{5,1},{2,2},{7,3},{8,4},{1,5},{10,6},{3,7},{4,8},{13,9},{6,1... | collective-permute-start | bytes 1572872 | tf_op jit(solution)/shard_map/ppermute | solution.py:104
  6.8 1.5 %collective-permute-start.4 = (bf16[2,4,128,128]{3,2,1,0:T(8,128)(2,1)}, bf16[2,4,128,128]{3,2,1,0:T(8,128)(2,1)S(1)}, u32[]{:S(2)}, u32[]{:S(2)}) collective-permute-start(bf16[2,4,128,128]{3,2,1,0:T(8,128)(2,1)} %refs_0_.2), channel_id=1, source_target_pairs={{0,2},{1,3},{2,0},{3,1},{4,6},{5,7},{6,4},{7,5},{8,10},{9,11},{10,... | collective-permute-start | bytes 786440 | tf_op jit(solution)/shard_map/ppermute | solution.py:111
  8.3 0.5 %collective-permute-start = (s32[2,4]{1,0:T(2,128)}, s32[2,4]{1,0:T(2,128)S(1)}, u32[]{:S(2)}, u32[]{:S(2)}) collective-permute-start(s32[2,4]{1,0:T(2,128)} %param.6), channel_id=1, source_target_pairs={{0,2},{1,3},{2,0},{3,1},{4,6},{5,7},{6,4},{7,5},{8,10},{9,11},{10,... | collective-permute-start | bytes 104 | tf_op jit(solution)/shard_map/ppermute | solution.py:111
  8.8 3.4 %collective-permute-start.2 = (s32[2,8]{1,0:T(2,128)}, s32[2,8]{1,0:T(2,128)S(1)}, u32[]{:S(2)}, u32[]{:S(2)}) collective-permute-start(s32[2,8]{1,0:T(2,128)} %param.8), channel_id=1, source_target_pairs={{0,4},{4,0},{8,12},{12,8},{1,5},{5,1},{9,13},{13,9},{2,6},{6,2},{1... | collective-permute-start | bytes 200 | tf_op jit(solution)/shard_map/ppermute | solution.py:111
  12.2 3.8 %collective-permute-done = s32[2,4]{1,0:T(2,128)S(1)} collective-permute-done((s32[2,4]{1,0:T(2,128)}, s32[2,4]{1,0:T(2,128)S(1)}, u32[]{:S(2)}, u32[]{:S(2)}) %collective-permute-start) | collective-permute-done | bytes 64 | tf_op jit(solution)/shard_map/ppermute | solution.py:111
  16.1 0.7 %pad_add_fusion.2 = s32[4,4]{1,0:T(4,128)S(1)} fusion(s32[2,4]{1,0:T(2,128)S(1)} %collective-permute-done, s32[2,4]{1,0:T(2,128)} %param.6), kind=kLoop, calls=%fused_computation.2 | loop fusion | flops 16 | bytes 128 | tf_op jit(solution)/shard_map/concatenate | solution.py:121
  16.7 0.7 %collective-permute-start.11 = (bf16[2,8,128,128]{3,2,1,0:T(8,128)(2,1)S(1)}, bf16[2,8,128,128]{3,2,1,0:T(8,128)(2,1)S(1)}, u32[]{:S(2)}, u32[]{:S(2)}) collective-permute-start(bf16[2,8,128,128]{3,2,1,0:T(8,128)(2,1)S(1)} %collective-permute-done.10.refs_1_), channel_id=1, source_target_pairs={{0,0},{5,1},{2,2},{7,3},{8,4},{1,5},{10,6},{3,7},{4,8},{13,9},{6,1... | collective-permute-start | bytes 1572872 | tf_op jit(solution)/shard_map/ppermute | solution.py:104
  17.5 7.0 %collective-permute-start.8 = (bf16[2,8,128,128]{3,2,1,0:T(8,128)(2,1)S(1)}, bf16[2,8,128,128]{3,2,1,0:T(8,128)(2,1)S(1)}, u32[]{:S(2)}, u32[]{:S(2)}) collective-permute-start(bf16[2,8,128,128]{3,2,1,0:T(8,128)(2,1)S(1)} %collective-permute-done.7.refs_2_), channel_id=1, source_target_pairs={{4,0},{1,1},{6,2},{3,3},{0,4},{9,5},{2,6},{11,7},{12,8},{5,9},{14,... | collective-permute-start | bytes 1572872 | tf_op jit(solution)/shard_map/ppermute | solution.py:104
  24.6 0.1 collective-permute-start.5
  24.6 0.5 collective-permute-start.6
  25.1 0.1 collective-permute-start.1
  25.2 1.3 %collective-permute-done.1 = s32[4,4]{1,0:T(4,128)S(1)} collective-permute-done((s32[4,4]{1,0:T(4,128)S(1)}, s32[4,4]{1,0:T(4,128)S(1)}, u32[]{:S(2)}, u32[]{:S(2)}) %collective-permute-start.1) | collective-permute-done | bytes 96 | tf_op jit(solution)/shard_map/ppermute | solution.py:111
  26.5 0.2 collective-permute-start.3
  26.8 9.9 %collective-permute-start.12 = (bf16[2,8,128,128]{3,2,1,0:T(8,128)(2,1)S(1)}, bf16[2,8,128,128]{3,2,1,0:T(8,128)(2,1)S(1)}, u32[]{:S(2)}, u32[]{:S(2)}) collective-permute-start(bf16[2,8,128,128]{3,2,1,0:T(8,128)(2,1)S(1)} %collective-permute-done.11.refs_0_), channel_id=1, source_target_pairs={{4,0},{1,1},{6,2},{3,3},{0,4},{5,5},{2,6},{7,7},{12,8},{9,9},{14,1... | collective-permute-start | bytes 1572872 | tf_op jit(solution)/shard_map/ppermute | solution.py:104
  36.8 0.7 %copy-done.2 = bf16[2,4,128,128]{3,2,1,0:T(8,128)(2,1)} copy-done((bf16[2,4,128,128]{3,2,1,0:T(8,128)(2,1)}, bf16[2,4,128,128]{3,2,1,0:T(8,128)(2,1)S(1)}, u32[]{:S(2)}) %copy-start.2) | copy-done | bytes 262168
  37.5 0.7 %copy-done.4 = bf16[2,4,128,128]{3,2,1,0:T(8,128)(2,1)} copy-done((bf16[2,4,128,128]{3,2,1,0:T(8,128)(2,1)}, bf16[2,4,128,128]{3,2,1,0:T(8,128)(2,1)S(1)}, u32[]{:S(2)}) %copy-start.4) | copy-done | bytes 262168
  38.2 0.7 %collective-permute-start.9 = (bf16[2,8,128,128]{3,2,1,0:T(8,128)(2,1)S(1)}, bf16[2,8,128,128]{3,2,1,0:T(8,128)(2,1)S(1)}, u32[]{:S(2)}, u32[]{:S(2)}) collective-permute-start(bf16[2,8,128,128]{3,2,1,0:T(8,128)(2,1)S(1)} %collective-permute-done.8.refs_1_), channel_id=1, source_target_pairs={{0,0},{5,1},{2,2},{7,3},{4,4},{1,5},{6,6},{3,7},{8,8},{13,9},{10,1... | collective-permute-start | bytes 1572872 | tf_op jit(solution)/shard_map/ppermute | solution.py:104
  39.0 0.1 stack.60.place
  39.1 0.1 pad_add_fusion.6.place
  39.1 0.1 pad_add_fusion.8.place
  39.2 0.1 pad_add_fusion.4
  39.3 0.6 %copy-done.6 = s32[2,6]{1,0:T(2,128)S(1)} copy-done((s32[2,6]{1,0:T(2,128)S(1)}, s32[2,6]{1,0:T(2,128)}, u32[]{:S(2)}) %copy-start.6) | copy-done | bytes 72
  39.9 0.9 %copy-done.1 = bf16[2,4,128,128]{3,2,1,0:T(8,128)(2,1)S(1)} copy-done((bf16[2,4,128,128]{3,2,1,0:T(8,128)(2,1)S(1)}, bf16[2,4,128,128]{3,2,1,0:T(8,128)(2,1)}, u32[]{:S(2)}) %copy-start.1) | copy-done | bytes 262168
  40.8 0.9 %copy-done.3 = bf16[2,4,128,128]{3,2,1,0:T(8,128)(2,1)S(1)} copy-done((bf16[2,4,128,128]{3,2,1,0:T(8,128)(2,1)S(1)}, bf16[2,4,128,128]{3,2,1,0:T(8,128)(2,1)}, u32[]{:S(2)}) %copy-start.3) | copy-done | bytes 262168
  41.8 0.9 %copy-done.5 = bf16[2,4,128,128]{3,2,1,0:T(8,128)(2,1)S(1)} copy-done((bf16[2,4,128,128]{3,2,1,0:T(8,128)(2,1)S(1)}, bf16[2,4,128,128]{3,2,1,0:T(8,128)(2,1)}, u32[]{:S(2)}) %copy-start.5) | copy-done | bytes 262168
  42.7 2.0 %shard_map.55 = (bf16[2,8,128,128]{3,2,1,0:T(8,128)(2,1)S(1)}, s32[2,48]{1,0:T(2,128)S(1)}) custom-call(s32[2]{0:T(128)S(1)} %pad_add_fusion.6.place, s32[2,6]{1,0:T(2,128)S(1)} %copy-done.6, s32[8,4]{1,0:T(8,128)S(1)} %pad_add_fusion.a_index, s32[8,8]{1,0:T(8,128)S(1)} %pad_add_fusion.1.b_index, bf16[2,4,128,128]{3,2,1,0:T(8,128)(2,1)S(1)} %copy-done.1, ...), custom_call_target="tpu_custom_call" | custom-call | tf_op jit(solution)/shard_map/pallas_call | solution.py:142
  44.7 1.6 %shard_map.56.refs_3_ = f32[2,128,768]{2,1,0:T(8,128)S(1)} custom-call(s32[5]{0:T(128)S(1)} %stack.60.place, s32[2,48]{1,0:T(2,128)S(1)} %get-tuple-element.9.table, bf16[2,8,128,128]{3,2,1,0:T(8,128)(2,1)S(1)} %copy-done, bf16[2,8,128,128]{3,2,1,0:T(8,128)(2,1)S(1)} %collective-permute-done.10.refs_1_, ...), custom_call_target="tpu_custom_call" | custom-call | flops 301989888 | bytes 2097152 | tf_op jit(solution)/shard_map/pallas_call | solution.py:166
  46.3 1.1 %shard_map.57.refs_2_ = f32[2,128,768]{2,1,0:T(8,128)S(1)} custom-call(s32[4]{0:T(128)S(1)} %pad_add_fusion.8.place, s32[2,48]{1,0:T(2,128)S(1)} %get-tuple-element.9.table, bf16[2,8,128,128]{3,2,1,0:T(8,128)(2,1)S(1)} %collective-permute-done.11.refs_0_, bf16[2,8,128,128]{3,2,1,0:T(8,128)(2,1)S(1)} %collective-permute-done.8.refs_1_, ...), custom_call_target="tpu_custom_call" | custom-call | flops 201326592 | bytes 2097152 | tf_op jit(solution)/shard_map/pallas_call | solution.py:166
  47.4 1.1 %collective-permute-done.12.refs_0_ = bf16[2,8,128,128]{3,2,1,0:T(8,128)(2,1)S(1)} collective-permute-done((bf16[2,8,128,128]{3,2,1,0:T(8,128)(2,1)S(1)}, bf16[2,8,128,128]{3,2,1,0:T(8,128)(2,1)S(1)}, u32[]{:S(2)}, u32[]{:S(2)}) %collective-permute-start.12) | collective-permute-done | bytes 524320 | tf_op jit(solution)/shard_map/ppermute | solution.py:104
  48.5 1.1 %shard_map.58.refs_2_ = f32[2,128,768]{2,1,0:T(8,128)S(1)} custom-call(s32[3]{0:T(128)S(1)} %get-tuple-element.14.place, s32[2,48]{1,0:T(2,128)S(1)} %get-tuple-element.9.table, bf16[2,8,128,128]{3,2,1,0:T(8,128)(2,1)S(1)} %collective-permute-done.12.refs_0_, bf16[2,8,128,128]{3,2,1,0:T(8,128)(2,1)S(1)} %get-tuple-element.12.refs_3_.refs_2_.refs_1_, ...), custom_call_target="tpu_custom_call" | custom-call | flops 100663296 | bytes 2097152 | tf_op jit(solution)/shard_map/pallas_call | solution.py:166
  49.6 1.4 %shard_map.59 = bf16[2,6,128,128]{3,2,1,0:T(8,128)(2,1)} custom-call(s32[3]{0:T(128)S(1)} %get-tuple-element.13.place, s32[2,48]{1,0:T(2,128)S(1)} %get-tuple-element.9.table, bf16[2,8,128,128]{3,2,1,0:T(8,128)(2,1)S(1)} %collective-permute-done.9.refs_0_, bf16[2,8,128,128]{3,2,1,0:T(8,128)(2,1)S(1)} %get-tuple-element.12.refs_3_.refs_2_.refs_1_, ...), custom_call_target="tpu_custom_call" | custom-call | flops 100663296 | bytes 2097152 | tf_op jit(solution)/shard_map/pallas_call | solution.py:166
  (25 shorter events, 0.1 us)
Async XLA Ops:
  0.0 17.5 %copy-start.8 = (s32[2,8]{1,0:T(2,128)S(1)}, s32[2,8]{1,0:T(2,128)}, u32[]{:S(2)}) copy-start(s32[2,8]{1,0:T(2,128)} %param.8) | copy-start | bytes 196
  0.0 16.7 %collective-permute-start.10 = (bf16[2,8,128,128]{3,2,1,0:T(8,128)(2,1)}, bf16[2,8,128,128]{3,2,1,0:T(8,128)(2,1)S(1)}, u32[]{:S(2)}, u32[]{:S(2)}) collective-permute-start(bf16[2,8,128,128]{3,2,1,0:T(8,128)(2,1)} %refs_0_.3), channel_id=1, source_target_pairs={{4,0},{1,1},{6,2},{3,3},{0,4},{9,5},{2,6},{11,7},{12,8},{5,9},{14,... | collective-permute-start | bytes 1572872 | tf_op jit(solution)/shard_map/ppermute | solution.py:104
  5.1 12.4 %collective-permute-start.7 = (bf16[2,8,128,128]{3,2,1,0:T(8,128)(2,1)}, bf16[2,8,128,128]{3,2,1,0:T(8,128)(2,1)S(1)}, u32[]{:S(2)}, u32[]{:S(2)}) collective-permute-start(bf16[2,8,128,128]{3,2,1,0:T(8,128)(2,1)} %refs_0_.3), channel_id=1, source_target_pairs={{0,0},{5,1},{2,2},{7,3},{8,4},{1,5},{10,6},{3,7},{4,8},{13,9},{6,1... | collective-permute-start | bytes 1572872 | tf_op jit(solution)/shard_map/ppermute | solution.py:104
  6.8 10.7 %collective-permute-start.4 = (bf16[2,4,128,128]{3,2,1,0:T(8,128)(2,1)}, bf16[2,4,128,128]{3,2,1,0:T(8,128)(2,1)S(1)}, u32[]{:S(2)}, u32[]{:S(2)}) collective-permute-start(bf16[2,4,128,128]{3,2,1,0:T(8,128)(2,1)} %refs_0_.2), channel_id=1, source_target_pairs={{0,2},{1,3},{2,0},{3,1},{4,6},{5,7},{6,4},{7,5},{8,10},{9,11},{10,... | collective-permute-start | bytes 786440 | tf_op jit(solution)/shard_map/ppermute | solution.py:111
  8.3 7.8 %collective-permute-start = (s32[2,4]{1,0:T(2,128)}, s32[2,4]{1,0:T(2,128)S(1)}, u32[]{:S(2)}, u32[]{:S(2)}) collective-permute-start(s32[2,4]{1,0:T(2,128)} %param.6), channel_id=1, source_target_pairs={{0,2},{1,3},{2,0},{3,1},{4,6},{5,7},{6,4},{7,5},{8,10},{9,11},{10,... | collective-permute-start | bytes 104 | tf_op jit(solution)/shard_map/ppermute | solution.py:111
  8.8 8.7 %collective-permute-start.2 = (s32[2,8]{1,0:T(2,128)}, s32[2,8]{1,0:T(2,128)S(1)}, u32[]{:S(2)}, u32[]{:S(2)}) collective-permute-start(s32[2,8]{1,0:T(2,128)} %param.8), channel_id=1, source_target_pairs={{0,4},{4,0},{8,12},{12,8},{1,5},{5,1},{9,13},{13,9},{2,6},{6,2},{1... | collective-permute-start | bytes 200 | tf_op jit(solution)/shard_map/ppermute | solution.py:111
  16.7 10.1 %copy-start.7 = (s32[2,4]{1,0:T(2,128)S(1)}, s32[2,4]{1,0:T(2,128)}, u32[]{:S(2)}) copy-start(s32[2,4]{1,0:T(2,128)} %param.6) | copy-start | bytes 100
  16.7 10.1 %collective-permute-start.11 = (bf16[2,8,128,128]{3,2,1,0:T(8,128)(2,1)S(1)}, bf16[2,8,128,128]{3,2,1,0:T(8,128)(2,1)S(1)}, u32[]{:S(2)}, u32[]{:S(2)}) collective-permute-start(bf16[2,8,128,128]{3,2,1,0:T(8,128)(2,1)S(1)} %collective-permute-done.10.refs_1_), channel_id=1, source_target_pairs={{0,0},{5,1},{2,2},{7,3},{8,4},{1,5},{10,6},{3,7},{4,8},{13,9},{6,1... | collective-permute-start | bytes 1572872 | tf_op jit(solution)/shard_map/ppermute | solution.py:104
  17.5 20.7 %collective-permute-start.8 = (bf16[2,8,128,128]{3,2,1,0:T(8,128)(2,1)S(1)}, bf16[2,8,128,128]{3,2,1,0:T(8,128)(2,1)S(1)}, u32[]{:S(2)}, u32[]{:S(2)}) collective-permute-start(bf16[2,8,128,128]{3,2,1,0:T(8,128)(2,1)S(1)} %collective-permute-done.7.refs_2_), channel_id=1, source_target_pairs={{4,0},{1,1},{6,2},{3,3},{0,4},{9,5},{2,6},{11,7},{12,8},{5,9},{14,... | collective-permute-start | bytes 1572872 | tf_op jit(solution)/shard_map/ppermute | solution.py:104
  24.6 12.2 %collective-permute-start.5 = (bf16[2,4,128,128]{3,2,1,0:T(8,128)(2,1)}, bf16[2,4,128,128]{3,2,1,0:T(8,128)(2,1)S(1)}, u32[]{:S(2)}, u32[]{:S(2)}) collective-permute-start(bf16[2,4,128,128]{3,2,1,0:T(8,128)(2,1)} %refs_0_.2), channel_id=1, source_target_pairs={{0,1},{1,0},{2,3},{3,2},{4,5},{5,4},{6,7},{7,6},{8,9},{9,8},{10,11... | collective-permute-start | bytes 786440 | tf_op jit(solution)/shard_map/ppermute | solution.py:111
  24.6 12.9 %collective-permute-start.6 = (bf16[2,4,128,128]{3,2,1,0:T(8,128)(2,1)S(1)}, bf16[2,4,128,128]{3,2,1,0:T(8,128)(2,1)S(1)}, u32[]{:S(2)}, u32[]{:S(2)}) collective-permute-start(bf16[2,4,128,128]{3,2,1,0:T(8,128)(2,1)S(1)} %collective-permute-done.4.refs_1_), channel_id=1, source_target_pairs={{0,1},{1,0},{2,3},{3,2},{4,5},{5,4},{6,7},{7,6},{8,9},{9,8},{10,11... | collective-permute-start | bytes 786440 | tf_op jit(solution)/shard_map/ppermute | solution.py:111
  25.1 1.4 %collective-permute-start.1 = (s32[4,4]{1,0:T(4,128)S(1)}, s32[4,4]{1,0:T(4,128)S(1)}, u32[]{:S(2)}, u32[]{:S(2)}) collective-permute-start(s32[4,4]{1,0:T(4,128)S(1)} %pad_add_fusion.2), channel_id=1, source_target_pairs={{0,1},{1,0},{2,3},{3,2},{4,5},{5,4},{6,7},{7,6},{8,9},{9,8},{10,11... | collective-permute-start | bytes 200 | tf_op jit(solution)/shard_map/ppermute | solution.py:111
  26.5 10.2 %collective-permute-start.3 = (s32[4,8]{1,0:T(4,128)S(1)}, s32[4,8]{1,0:T(4,128)S(1)}, u32[]{:S(2)}, u32[]{:S(2)}) collective-permute-start(s32[4,8]{1,0:T(4,128)S(1)} %pad_add_fusion.3), channel_id=1, source_target_pairs={{0,8},{4,12},{8,0},{12,4},{1,9},{5,13},{9,1},{13,5},{2,10},{6,14},... | collective-permute-start | bytes 392 | tf_op jit(solution)/shard_map/ppermute | solution.py:111
  26.8 21.7 %collective-permute-start.12 = (bf16[2,8,128,128]{3,2,1,0:T(8,128)(2,1)S(1)}, bf16[2,8,128,128]{3,2,1,0:T(8,128)(2,1)S(1)}, u32[]{:S(2)}, u32[]{:S(2)}) collective-permute-start(bf16[2,8,128,128]{3,2,1,0:T(8,128)(2,1)S(1)} %collective-permute-done.11.refs_0_), channel_id=1, source_target_pairs={{4,0},{1,1},{6,2},{3,3},{0,4},{5,5},{2,6},{7,7},{12,8},{9,9},{14,1... | collective-permute-start | bytes 1572872 | tf_op jit(solution)/shard_map/ppermute | solution.py:104
  36.8 0.7 %copy-start.2 = (bf16[2,4,128,128]{3,2,1,0:T(8,128)(2,1)}, bf16[2,4,128,128]{3,2,1,0:T(8,128)(2,1)S(1)}, u32[]{:S(2)}) copy-start(bf16[2,4,128,128]{3,2,1,0:T(8,128)(2,1)S(1)} %collective-permute-done.5.refs_2_) | copy-start | bytes 786436
  37.5 0.7 %copy-start.4 = (bf16[2,4,128,128]{3,2,1,0:T(8,128)(2,1)}, bf16[2,4,128,128]{3,2,1,0:T(8,128)(2,1)S(1)}, u32[]{:S(2)}) copy-start(bf16[2,4,128,128]{3,2,1,0:T(8,128)(2,1)S(1)} %collective-permute-done.6.refs_3_) | copy-start | bytes 786436
  38.2 11.4 %collective-permute-start.9 = (bf16[2,8,128,128]{3,2,1,0:T(8,128)(2,1)S(1)}, bf16[2,8,128,128]{3,2,1,0:T(8,128)(2,1)S(1)}, u32[]{:S(2)}, u32[]{:S(2)}) collective-permute-start(bf16[2,8,128,128]{3,2,1,0:T(8,128)(2,1)S(1)} %collective-permute-done.8.refs_1_), channel_id=1, source_target_pairs={{0,0},{5,1},{2,2},{7,3},{4,4},{1,5},{6,6},{3,7},{8,8},{13,9},{10,1... | collective-permute-start | bytes 1572872 | tf_op jit(solution)/shard_map/ppermute | solution.py:104
  39.2 0.7 %copy-start.6 = (s32[2,6]{1,0:T(2,128)S(1)}, s32[2,6]{1,0:T(2,128)}, u32[]{:S(2)}) copy-start(s32[2,6]{1,0:T(2,128)} %wanted.1) | copy-start | bytes 148
  39.9 0.9 %copy-start.1 = (bf16[2,4,128,128]{3,2,1,0:T(8,128)(2,1)S(1)}, bf16[2,4,128,128]{3,2,1,0:T(8,128)(2,1)}, u32[]{:S(2)}) copy-start(bf16[2,4,128,128]{3,2,1,0:T(8,128)(2,1)} %refs_0_.2) | copy-start | bytes 786436
  40.8 0.9 %copy-start.3 = (bf16[2,4,128,128]{3,2,1,0:T(8,128)(2,1)S(1)}, bf16[2,4,128,128]{3,2,1,0:T(8,128)(2,1)}, u32[]{:S(2)}) copy-start(bf16[2,4,128,128]{3,2,1,0:T(8,128)(2,1)} %copy-done.2) | copy-start | bytes 786436
  41.8 0.9 %copy-start.5 = (bf16[2,4,128,128]{3,2,1,0:T(8,128)(2,1)S(1)}, bf16[2,4,128,128]{3,2,1,0:T(8,128)(2,1)}, u32[]{:S(2)}) copy-start(bf16[2,4,128,128]{3,2,1,0:T(8,128)(2,1)} %copy-done.4) | copy-start | bytes 786436
  42.7 2.0 %copy-start = (bf16[2,8,128,128]{3,2,1,0:T(8,128)(2,1)S(1)}, bf16[2,8,128,128]{3,2,1,0:T(8,128)(2,1)}, u32[]{:S(2)}) copy-start(bf16[2,8,128,128]{3,2,1,0:T(8,128)(2,1)} %refs_0_.3) | copy-start | bytes 1572868

commit v6 on v0

v6 whole, which is shorter than its diff:
```python
import functools

import jax
import jax.numpy as jnp
from jax import lax
from jax.experimental import pallas as pl
from jax.experimental.pallas import tpu as pltpu
from jax.sharding import PartitionSpec as P

COLS_DEV = 16

SMEM = pl.BlockSpec(memory_space=pltpu.SMEM)
VMEM = pl.BlockSpec(memory_space=pltpu.VMEM)
PARAMS = pltpu.CompilerParams(vmem_limit_bytes=32 * 2**20)


def tail(count):
    return -(-count // 16) * 16


def pack_kernel(index, tiles, out):
    size = tiles.shape[0]
    out[:size, :] = tiles[...]
    row = lax.broadcasted_iota(jnp.int32, (out.shape[0] - size, out.shape[1]), 0)
    found = jnp.zeros(row.shape, jnp.float32)
    slots = index.shape[1]
    for k in range(index.shape[0] * slots):
        found = jnp.where(row == k, index[k // slots, k % slots].astype(jnp.float32), found)
    out[size:, :] = found.astype(out.dtype)


def left_kernel(index, *refs):
    parts, dense = refs[:-1], refs[-1]
    dense[...] = jnp.zeros_like(dense)
    rows, _, block, _ = dense.shape
    slots = index.shape[1] // rows
    for p, part in enumerate(parts):
        for i in range(rows):
            for s in range(slots):
                inner = index[p, i * slots + s]
                start = (i * slots + s) * block

                @pl.when(inner >= 0)
                def _():
                    dense[i, inner] = part[start : start + block, :]


def step_kernel(parts, last, place, wanted, *refs):
    cols, refs = refs[:parts], refs[parts:]
    tiles, refs = refs[:parts], refs[parts:]
    dense, refs = refs[0], refs[1:]
    before, out, right, slot = refs if len(refs) == 4 else (None,) + refs
    first = place[0]
    rows, slots = wanted.shape
    inner_rows, inner_slots, block, _ = tiles[0].shape

    sums = [None if before is None else before[i] for i in range(rows)]
    for p in range(parts):
        for m in range(inner_rows):
            for c in range(COLS_DEV):
                slot[m, c] = -1
            for l in range(inner_slots):
                slot[m, cols[p][m, l] - first] = l
        for i in range(rows):
            for m in range(inner_rows):
                for j in range(slots):
                    l = slot[m, wanted[i, j] - first]
                    tile = tiles[p][m, jnp.maximum(l, 0)]
                    right[i, m * block : (m + 1) * block, j * block : (j + 1) * block] = jnp.where(
                        l >= 0, tile, jnp.zeros_like(tile)
                    )
        for i in range(rows):
            left = jnp.concatenate(
                [dense[i, place[1 + p] * inner_rows + m] for m in range(inner_rows)], axis=1
            )
            product = jnp.dot(left, right[i], preferred_element_type=jnp.float32)
            sums[i] = product if sums[i] is None else sums[i] + product
    for i in range(rows):
        if last:
            for j in range(slots):
                out[i, j] = sums[i][:, j * block : (j + 1) * block].astype(out.dtype)
        else:
            out[i] = sums[i]


def body(row_count, col_count, a_tiles, a_cols, b_tiles, b_cols, c_cols):
    rows, slots = c_cols.shape
    inner_rows = b_tiles.shape[0]
    block = a_tiles.shape[-1]
    dtype = b_tiles.dtype
    r = lax.axis_index("row")
    first = lax.axis_index("col") * COLS_DEV

    def swap(x, axis, n, d):
        return lax.ppermute(x, axis, [(k, k ^ d) for k in range(n)])

    def spans(n):
        while n > 1:
            yield n - 1
            n //= 2

    def pack(index, tiles):
        size = index.size * block
        return pl.pallas_call(
            pack_kernel,
            out_shape=jax.ShapeDtypeStruct((size + tail(index.size), block), dtype),
            in_specs=[SMEM, VMEM],
            out_specs=VMEM,
            compiler_params=PARAMS,
        )(index, tiles.reshape(size, block))

    dists, cols, tiles = [0], [b_cols], [b_tiles]
    a_parts = [pack(a_cols, a_tiles)]
    col_spans = [col_count >> k for k in range(1, col_count.bit_length())]
    for stage, d in enumerate(spans(row_count)):
        if stage == 1:
            tiles.append(swap(b_tiles, "row", row_count, d))
            cols.append(swap(b_cols, "row", row_count, d))
            a_parts.append(swap(a_parts[0], "col", col_count, col_spans[0]))
            cols, tiles, a_parts = lax.optimization_barrier((cols, tiles, a_parts))
            far_tiles, far_cols = tiles[1:2], cols[1:2]
        else:
            far_tiles, far_cols = tiles, cols
        dists = dists + [e ^ d for e in dists]
        tiles = tiles + [swap(x, "row", row_count, d) for x in far_tiles]
        cols = cols + [swap(x, "row", row_count, d) for x in far_cols]
    for d in col_spans[len(a_parts) - 1 :]:
        a_parts = a_parts + [swap(x, "col", col_count, d) for x in a_parts]
    shards = list(zip(dists, cols, tiles))

    size = a_cols.size * block
    a_index = jnp.stack([x[size:, 0][: a_cols.size] for x in a_parts]).astype(jnp.int32)
    dense = pl.pallas_call(
        left_kernel,
        out_shape=jax.ShapeDtypeStruct((rows, inner_rows * row_count, block, block), dtype),
        in_specs=[SMEM] + [VMEM] * col_count,
        out_specs=VMEM,
        compiler_params=PARAMS,
    )(a_index, *a_parts)

    def step(pieces, before, last):
        parts = len(pieces)
        place = jnp.stack([first] + [r ^ d for d, _, _ in pieces]).astype(jnp.int32)
        if last:
            out = jax.ShapeDtypeStruct((rows, slots, block, block), dtype)
        else:
            out = jax.ShapeDtypeStruct((rows, block, slots * block), jnp.float32)
        held = [dense] if before is None else [dense, before]
        return pl.pallas_call(
            functools.partial(step_kernel, parts, last),
            out_shape=out,
            in_specs=[SMEM] * (2 + parts) + [VMEM] * (parts + len(held)),
            out_specs=VMEM,
            scratch_shapes=[
                pltpu.VMEM((rows, inner_rows * block, slots * block), dtype),
                pltpu.SMEM((inner_rows, COLS_DEV), jnp.int32),
            ],
            compiler_params=PARAMS,
            cost_estimate=pl.CostEstimate(
                flops=2 * rows * parts * inner_rows * slots * block**3, bytes_accessed=2**21, transcendentals=0
            ),
        )(place, c_cols, *[c for _, c, _ in pieces], *[x for _, _, x in pieces], *held)

    total = None
    for p in range(0, row_count - 1, 3):
        total = step(shards[p : min(p + 3, row_count - 1)], total, False)
    return step(shards[-1:], total, True)


def solution(mesh):
    return jax.shard_map(
        functools.partial(body, mesh.shape["row"], mesh.shape["col"]),
        mesh=mesh,
        in_specs=(
            P(("groups", "row"), "col", None, None),
            P(("groups", "row"), "col"),
            P(("groups", "row"), "col", None, None),
            P(("groups", "row"), "col"),
            P(("groups", "row"), "col"),
        ),
        out_specs=P(("groups", "row"), "col", None, None),
        check_vma=False,
    )
```

time: 136 us -> 45.2 us (0.33)
  waiting for transfers between devices: 90.2 us -> 27 us
  local copies, waits for them, and re-layouts: 15.5 us -> 1.43 us
  between operations: 13.4 us -> 0.07 us
  starting transfers between devices: 0.04 us -> 11.2 us
  matrix products: 6.96 us -> 0 us
  blocking collectives: 6.25 us -> 0 us
  Pallas kernels: 0 us -> 5.14 us
  other arithmetic: 2.96 us -> 0.17 us
    all_gather x2 -> x0, waiting for transfers between devices: 90.1 us -> none  [the longest x1 80.2 us: body(): slab = lax.all_gather(prepared, 'row', axis=0, tiled=True)]
    ppermute x0 -> x9, waiting for transfers between devices: none -> 27 us  [swap(): return lax.ppermute(x, axis, [(k, k ^ d) for k in range(n)])]
    ppermute x0 -> x9, starting transfers between devices: none -> 11.2 us  [swap(): return lax.ppermute(x, axis, [(k, k ^ d) for k in range(n)])]
    unnamed x5 -> x10, local copies, waits for them, and re-layouts: 8.1 us -> 1.09 us
    dot_general x3 -> x0, matrix products: 6.96 us -> none  [the longest x1 3.47 us: body(): total = jnp.dot(chosen, right, preferred_element_type=jnp.float32)]
    reshape x1 -> x0, local copies, waits for them, and re-layouts: 6.39 us -> none  [body(): right = slab.reshape(count * block, width * block)]
    all_gather x1 -> x0, blocking collectives: 6.25 us -> none  [body(): lax.all_gather(a_cols, 'col', axis=1, tiled=True)]
    pallas_call x0 -> x4, Pallas kernels: none -> 5.14 us  [the longest x2 3.68 us: step(): pl.pallas_call(functools.partial(step_kernel, parts, last), out_shape=out...]
  transfers between devices with their start and end apart: 2 -> 9, of which waited for: 2 -> 3; matrix products, arithmetic and copies ran while one was open for 4% -> 1% of each run, Pallas kernels for 0% -> 7%
where the time goes in v6:
time: 45.2 us; the launch traced here: 45.1 us
  waiting for transfers between devices  27 us (60%)
  starting transfers between devices  11.2 us (25%)
  Pallas kernels  5.14 us (11%)
  local copies, waits for them, and re-layouts  1.43 us (3%)
    ppermute x9, waiting for transfers between devices, swap(): return lax.ppermute(x, axis, [(k, k ^ d) for k in range(n)])  27 us
    ppermute x9, starting transfers between devices, swap(): return lax.ppermute(x, axis, [(k, k ^ d) for k in range(n)])  11.2 us
    pallas_call x2, Pallas kernels, step(): pl.pallas_call(functools.partial(step_kernel, parts, last), out_shape=out...  3.68 us
    unnamed x10, local copies, waits for them, and re-layouts  1.09 us
  transfers between devices with their start and end apart: 9, of which 3 were waited for; matrix products, arithmetic and copies ran while one was open for 1% of the time, Pallas kernels for 7%

profile of v6, /device:TPU:0, one launch (start us, length us, event | category | flops | bytes accessed | tf_op | source)
XLA Modules:
  0.0 45.1 jit_solution(7766348075581987719)
XLA Ops:
  0.0 5.0 %collective-permute-start.2 = (bf16[2,8,128,128]{3,2,1,0:T(8,128)(2,1)}, bf16[2,8,128,128]{3,2,1,0:T(8,128)(2,1)S(1)}, u32[]{:S(2)}, u32[]{:S(2)}) collective-permute-start(bf16[2,8,128,128]{3,2,1,0:T(8,128)(2,1)} %refs_3_), channel_id=1, source_target_pairs={{0,12},{4,8},{8,4},{12,0},{1,13},{5,9},{9,5},{13,1},{2,14},{6,10},... | collective-permute-start | bytes 1572872 | tf_op jit(solution)/shard_map/ppermute | solution.py:95
  5.1 0.0 collective-permute-start.3
  5.1 0.0 copy-done.3
  5.1 0.9 %copy-done.1 = bf16[2,4,128,128]{3,2,1,0:T(8,128)(2,1)S(1)} copy-done((bf16[2,4,128,128]{3,2,1,0:T(8,128)(2,1)S(1)}, bf16[2,4,128,128]{3,2,1,0:T(8,128)(2,1)}, u32[]{:S(2)}) %copy-start.1) | copy-done | bytes 262168
  6.0 0.6 %shard_map.55.refs_0_ = bf16[1040,128]{1,0:T(8,128)(2,1)S(1)} custom-call(s32[2,4]{1,0:T(2,128)S(1)} %copy-done.3, bf16[1024,128]{1,0:T(8,128)(2,1)S(1)} %bitcast.10), custom_call_target="tpu_custom_call" | custom-call | tf_op jit(solution)/shard_map/pallas_call | solution.py:104
  6.6 1.6 %collective-permute-start.4 = (bf16[1040,128]{1,0:T(8,128)(2,1)S(1)}, bf16[1040,128]{1,0:T(8,128)(2,1)S(1)}, u32[]{:S(2)}, u32[]{:S(2)}) collective-permute-start(bf16[1040,128]{1,0:T(8,128)(2,1)S(1)} %shard_map.55.refs_0_), channel_id=1, source_target_pairs={{0,2},{1,3},{2,0},{3,1},{4,6},{5,7},{6,4},{7,5},{8,10},{9,11},{10,... | collective-permute-start | bytes 798728 | tf_op jit(solution)/shard_map/ppermute | solution.py:95
  8.1 0.9 %collective-permute-start = (s32[2,8]{1,0:T(2,128)S(1)}, s32[2,8]{1,0:T(2,128)S(1)}, u32[]{:S(2)}, u32[]{:S(2)}) collective-permute-start(s32[2,8]{1,0:T(2,128)S(1)} %copy-done.4), channel_id=1, source_target_pairs={{0,12},{4,8},{8,4},{12,0},{1,13},{5,9},{9,5},{13,1},{2,14},{6,10},... | collective-permute-start | bytes 200 | tf_op jit(solution)/shard_map/ppermute | solution.py:95
  9.0 1.1 %collective-permute-start.1 = (s32[2,8]{1,0:T(2,128)S(1)}, s32[2,8]{1,0:T(2,128)S(1)}, u32[]{:S(2)}, u32[]{:S(2)}) collective-permute-start(s32[2,8]{1,0:T(2,128)S(1)} %copy-done.4), channel_id=1, source_target_pairs={{0,4},{4,0},{8,12},{12,8},{1,5},{5,1},{9,13},{13,9},{2,6},{6,2},{1... | collective-permute-start | bytes 200 | tf_op jit(solution)/shard_map/ppermute | solution.py:95
  10.2 18.4 %collective-permute-done.refs_1_ = s32[2,8]{1,0:T(2,128)S(1)} collective-permute-done((s32[2,8]{1,0:T(2,128)S(1)}, s32[2,8]{1,0:T(2,128)S(1)}, u32[]{:S(2)}, u32[]{:S(2)}) %collective-permute-start) | collective-permute-done | bytes 96 | tf_op jit(solution)/shard_map/ppermute | solution.py:95
  28.5 0.1 collective-permute-done.1.refs_2_
  28.6 0.0 collective-permute-done.4.refs_1_
  28.6 0.0 collective-permute-done.2.refs_4_
  28.6 0.0 collective-permute-done.3.refs_5_
  28.6 0.1 collective-permute-start.7
  28.7 0.1 pad_add_fusion.place
  28.8 0.5 %collective-permute-start.8 = (bf16[1040,128]{1,0:T(8,128)(2,1)S(1)}, bf16[1040,128]{1,0:T(8,128)(2,1)S(1)}, u32[]{:S(2)}, u32[]{:S(2)}) collective-permute-start(bf16[1040,128]{1,0:T(8,128)(2,1)S(1)} %collective-permute-done.4.refs_1_), channel_id=1, source_target_pairs={{0,1},{1,0},{2,3},{3,2},{4,5},{5,4},{6,7},{7,6},{8,9},{9,8},{10,11... | collective-permute-start | bytes 798728 | tf_op jit(solution)/shard_map/ppermute | solution.py:95
  29.3 1.7 %collective-permute-start.6 = (bf16[2,8,128,128]{3,2,1,0:T(8,128)(2,1)S(1)}, bf16[2,8,128,128]{3,2,1,0:T(8,128)(2,1)S(1)}, u32[]{:S(2)}, u32[]{:S(2)}) collective-permute-start(bf16[2,8,128,128]{3,2,1,0:T(8,128)(2,1)S(1)} %collective-permute-done.2.refs_4_), channel_id=1, source_target_pairs={{0,4},{4,0},{8,12},{12,8},{1,5},{5,1},{9,13},{13,9},{2,6},{6,2},{1... | collective-permute-start | bytes 1572872 | tf_op jit(solution)/shard_map/ppermute | solution.py:95
  31.0 0.1 pad_add_fusion.1.place
  31.0 0.3 collective-permute-start.5
  31.4 0.1 slice_reduce_fusion.2
  31.5 0.0 collective-permute-done.7.refs_2_
  31.5 0.1 slice_reduce_fusion.1
  31.6 0.0 collective-permute-done.8.refs_3_
  31.6 0.1 slice_reduce_fusion
  31.7 0.0 copy-start
  31.8 0.0 copy-start.2
  31.8 0.9 %shard_map.56.refs_6_.refs_2_ = bf16[2,8,128,128]{3,2,1,0:T(8,128)(2,1)S(1)} custom-call(s32[4,8]{1,0:T(4,128)S(1)} %maximum_convert_fusion.index, bf16[1040,128]{1,0:T(8,128)(2,1)S(1)} %shard_map.55.refs_0_, bf16[1040,128]{1,0:T(8,128)(2,1)S(1)} %collective-permute-done.4.refs_1_, bf16[1040,128]{1,0:T(8,128)(2,1)S(1)} %collective-permute-done.7.refs_2_, ...), custom_call_target="tpu_custom_call" | custom-call | tf_op jit(solution)/shard_map/pallas_call | solution.py:133
  32.7 0.1 copy-done
  32.8 1.8 %shard_map.57.refs_3_ = f32[2,128,768]{2,1,0:T(8,128)S(1)} custom-call(s32[4]{0:T(128)S(1)} %pad_add_fusion.1.place, s32[2,6]{1,0:T(2,128)S(1)} %copy-done.2, s32[2,8]{1,0:T(2,128)S(1)} %copy-done.4, s32[2,8]{1,0:T(2,128)S(1)} %collective-permute-done.refs_1_, s32[2,8]{1,0:T(2,128)S(1)} %collective-permute-done.1.refs_2_, ...), custom_call_target="tpu_custom_call" | custom-call | flops 301989888 | bytes 2097152 | tf_op jit(solution)/shard_map/pallas_call | solution.py:149
  34.6 8.6 %collective-permute-done.5.refs_0_ = s32[2,8]{1,0:T(2,128)S(1)} collective-permute-done((s32[2,8]{1,0:T(2,128)S(1)}, s32[2,8]{1,0:T(2,128)S(1)}, u32[]{:S(2)}, u32[]{:S(2)}) %collective-permute-start.5) | collective-permute-done | bytes 96 | tf_op jit(solution)/shard_map/ppermute | solution.py:95
  43.2 0.0 collective-permute-done.6.refs_1_
  43.2 1.8 %shard_map.58 = bf16[2,6,128,128]{3,2,1,0:T(8,128)(2,1)} custom-call(s32[2]{0:T(128)S(1)} %pad_add_fusion.place, s32[2,6]{1,0:T(2,128)S(1)} %copy-done.2, s32[2,8]{1,0:T(2,128)S(1)} %collective-permute-done.5.refs_0_, bf16[2,8,128,128]{3,2,1,0:T(8,128)(2,1)S(1)} %collective-permute-done.6.refs_1_, bf16[2,8,128,128]{3,2,1,0:T(8,128)(2,1)S(1)} %shard_map.56.refs_6_.refs_2_, ...), custom_call_target="tpu_custom_call" | custom-call | flops 100663296 | bytes 2097152 | tf_op jit(solution)/shard_map/pallas_call | solution.py:149
  (6 shorter events, 0.0 us)
Async XLA Ops:
  0.0 5.1 %copy-start.3 = (s32[2,4]{1,0:T(2,128)S(1)}, s32[2,4]{1,0:T(2,128)}, u32[]{:S(2)}) copy-start(s32[2,4]{1,0:T(2,128)} %index.1) | copy-start | bytes 100
  0.0 28.6 %collective-permute-start.2 = (bf16[2,8,128,128]{3,2,1,0:T(8,128)(2,1)}, bf16[2,8,128,128]{3,2,1,0:T(8,128)(2,1)S(1)}, u32[]{:S(2)}, u32[]{:S(2)}) collective-permute-start(bf16[2,8,128,128]{3,2,1,0:T(8,128)(2,1)} %refs_3_), channel_id=1, source_target_pairs={{0,12},{4,8},{8,4},{12,0},{1,13},{5,9},{9,5},{13,1},{2,14},{6,10},... | collective-permute-start | bytes 1572872 | tf_op jit(solution)/shard_map/ppermute | solution.py:95
  5.1 23.6 %collective-permute-start.3 = (bf16[2,8,128,128]{3,2,1,0:T(8,128)(2,1)}, bf16[2,8,128,128]{3,2,1,0:T(8,128)(2,1)S(1)}, u32[]{:S(2)}, u32[]{:S(2)}) collective-permute-start(bf16[2,8,128,128]{3,2,1,0:T(8,128)(2,1)} %refs_3_), channel_id=1, source_target_pairs={{0,4},{4,0},{8,12},{12,8},{1,5},{5,1},{9,13},{13,9},{2,6},{6,2},{1... | collective-permute-start | bytes 1572872 | tf_op jit(solution)/shard_map/ppermute | solution.py:95
  5.1 1.0 %copy-start.1 = (bf16[2,4,128,128]{3,2,1,0:T(8,128)(2,1)S(1)}, bf16[2,4,128,128]{3,2,1,0:T(8,128)(2,1)}, u32[]{:S(2)}) copy-start(bf16[2,4,128,128]{3,2,1,0:T(8,128)(2,1)} %param.5) | copy-start | bytes 786436
  6.0 2.1 %copy-start.4 = (s32[2,8]{1,0:T(2,128)S(1)}, s32[2,8]{1,0:T(2,128)}, u32[]{:S(2)}) copy-start(s32[2,8]{1,0:T(2,128)} %refs_0_) | copy-start | bytes 196
  6.6 22.0 %collective-permute-start.4 = (bf16[1040,128]{1,0:T(8,128)(2,1)S(1)}, bf16[1040,128]{1,0:T(8,128)(2,1)S(1)}, u32[]{:S(2)}, u32[]{:S(2)}) collective-permute-start(bf16[1040,128]{1,0:T(8,128)(2,1)S(1)} %shard_map.55.refs_0_), channel_id=1, source_target_pairs={{0,2},{1,3},{2,0},{3,1},{4,6},{5,7},{6,4},{7,5},{8,10},{9,11},{10,... | collective-permute-start | bytes 798728 | tf_op jit(solution)/shard_map/ppermute | solution.py:95
  8.1 20.4 %collective-permute-start = (s32[2,8]{1,0:T(2,128)S(1)}, s32[2,8]{1,0:T(2,128)S(1)}, u32[]{:S(2)}, u32[]{:S(2)}) collective-permute-start(s32[2,8]{1,0:T(2,128)S(1)} %copy-done.4), channel_id=1, source_target_pairs={{0,12},{4,8},{8,4},{12,0},{1,13},{5,9},{9,5},{13,1},{2,14},{6,10},... | collective-permute-start | bytes 200 | tf_op jit(solution)/shard_map/ppermute | solution.py:95
  9.0 19.6 %collective-permute-start.1 = (s32[2,8]{1,0:T(2,128)S(1)}, s32[2,8]{1,0:T(2,128)S(1)}, u32[]{:S(2)}, u32[]{:S(2)}) collective-permute-start(s32[2,8]{1,0:T(2,128)S(1)} %copy-done.4), channel_id=1, source_target_pairs={{0,4},{4,0},{8,12},{12,8},{1,5},{5,1},{9,13},{13,9},{2,6},{6,2},{1... | collective-permute-start | bytes 200 | tf_op jit(solution)/shard_map/ppermute | solution.py:95
  28.6 2.9 %collective-permute-start.7 = (bf16[1040,128]{1,0:T(8,128)(2,1)S(1)}, bf16[1040,128]{1,0:T(8,128)(2,1)S(1)}, u32[]{:S(2)}, u32[]{:S(2)}) collective-permute-start(bf16[1040,128]{1,0:T(8,128)(2,1)S(1)} %shard_map.55.refs_0_), channel_id=1, source_target_pairs={{0,1},{1,0},{2,3},{3,2},{4,5},{5,4},{6,7},{7,6},{8,9},{9,8},{10,11... | collective-permute-start | bytes 798728 | tf_op jit(solution)/shard_map/ppermute | solution.py:95
  28.8 2.8 %collective-permute-start.8 = (bf16[1040,128]{1,0:T(8,128)(2,1)S(1)}, bf16[1040,128]{1,0:T(8,128)(2,1)S(1)}, u32[]{:S(2)}, u32[]{:S(2)}) collective-permute-start(bf16[1040,128]{1,0:T(8,128)(2,1)S(1)} %collective-permute-done.4.refs_1_), channel_id=1, source_target_pairs={{0,1},{1,0},{2,3},{3,2},{4,5},{5,4},{6,7},{7,6},{8,9},{9,8},{10,11... | collective-permute-start | bytes 798728 | tf_op jit(solution)/shard_map/ppermute | solution.py:95
  29.3 14.0 %collective-permute-start.6 = (bf16[2,8,128,128]{3,2,1,0:T(8,128)(2,1)S(1)}, bf16[2,8,128,128]{3,2,1,0:T(8,128)(2,1)S(1)}, u32[]{:S(2)}, u32[]{:S(2)}) collective-permute-start(bf16[2,8,128,128]{3,2,1,0:T(8,128)(2,1)S(1)} %collective-permute-done.2.refs_4_), channel_id=1, source_target_pairs={{0,4},{4,0},{8,12},{12,8},{1,5},{5,1},{9,13},{13,9},{2,6},{6,2},{1... | collective-permute-start | bytes 1572872 | tf_op jit(solution)/shard_map/ppermute | solution.py:95
  31.0 12.2 %collective-permute-start.5 = (s32[2,8]{1,0:T(2,128)S(1)}, s32[2,8]{1,0:T(2,128)S(1)}, u32[]{:S(2)}, u32[]{:S(2)}) collective-permute-start(s32[2,8]{1,0:T(2,128)S(1)} %collective-permute-done.refs_1_), channel_id=1, source_target_pairs={{0,4},{4,0},{8,12},{12,8},{1,5},{5,1},{9,13},{13,9},{2,6},{6,2},{1... | collective-permute-start | bytes 200 | tf_op jit(solution)/shard_map/ppermute | solution.py:95
  31.7 1.0 %copy-start = (bf16[2,8,128,128]{3,2,1,0:T(8,128)(2,1)S(1)}, bf16[2,8,128,128]{3,2,1,0:T(8,128)(2,1)}, u32[]{:S(2)}) copy-start(bf16[2,8,128,128]{3,2,1,0:T(8,128)(2,1)} %refs_3_) | copy-start | bytes 1572868
  31.8 1.0 %copy-start.2 = (s32[2,6]{1,0:T(2,128)S(1)}, s32[2,6]{1,0:T(2,128)}, u32[]{:S(2)}) copy-start(s32[2,6]{1,0:T(2,128)} %wanted.3) | copy-start | bytes 148

commit v7 on v0

v7 whole, which is shorter than its diff:
```python
import functools

import jax
import jax.numpy as jnp
from jax import lax
from jax.experimental import pallas as pl
from jax.experimental.pallas import tpu as pltpu
from jax.sharding import PartitionSpec as P

COLS_DEV = 16

SMEM = pl.BlockSpec(memory_space=pltpu.SMEM)
VMEM = pl.BlockSpec(memory_space=pltpu.VMEM)
PARAMS = pltpu.CompilerParams(vmem_limit_bytes=32 * 2**20)


def pack_kernel(*refs):
    indices, tiles, out = refs[:-2], refs[-2], refs[-1]
    size = tiles.shape[0]
    out[:size, :] = tiles[...]
    row = lax.broadcasted_iota(jnp.int32, (out.shape[0] - size, out.shape[1]), 0)
    found = jnp.zeros(row.shape, jnp.float32)
    at = 0
    for index in indices:
        for i in range(index.shape[0]):
            for k in range(index.shape[1]):
                found = jnp.where(row == at, index[i, k].astype(jnp.float32), found)
                at += 1
    out[size:, :] = found.astype(out.dtype)


def left_kernel(slots, index, *refs):
    parts, dense = refs[:-1], refs[-1]
    dense[...] = jnp.zeros_like(dense)
    rows, _, block, _ = dense.shape
    for p, part in enumerate(parts):
        for i in range(rows):
            for s in range(slots):
                inner = index[p, i * slots + s]
                start = (i * slots + s) * block

                @pl.when(inner >= 0)
                def _():
                    dense[i, inner] = part[start : start + block, :]


def step_kernel(parts, groups, starts, slots, last, place, *refs):
    wanted, refs = refs[:groups], refs[groups:]
    cols, refs = refs[:parts], refs[parts:]
    tiles, refs = refs[:parts], refs[parts:]
    dense, refs = refs[:groups], refs[groups:]
    before, refs = (refs[:groups], refs[groups:]) if len(refs) > groups + 2 else ([None] * groups, refs)
    outs, right, slot = refs[:groups], refs[groups], refs[groups + 1]
    first = place[0]
    rows = dense[0].shape[0]
    inner_rows, inner_slots, block, _ = tiles[0].shape

    def read(ref, start, i, k, width):
        return ref[i, k] if start is None else ref[0, start + i * width + k]

    sums = [[None if total is None else total[i] for i in range(rows)] for total in before]
    for p in range(parts):
        for m in range(inner_rows):
            for c in range(COLS_DEV):
                slot[m, c] = -1
            for l in range(inner_slots):
                slot[m, read(cols[p], starts[groups + p], m, l, inner_slots) - first] = l
        for g in range(groups):
            for i in range(rows):
                for j in range(slots):
                    column = read(wanted[g], starts[g], i, j, slots) - first
                    for m in range(inner_rows):
                        l = slot[m, column]
                        tile = tiles[p][m, jnp.maximum(l, 0)]
                        right[g, i, m * block : (m + 1) * block, j * block : (j + 1) * block] = jnp.where(
                            l >= 0, tile, jnp.zeros_like(tile)
                        )
            for i in range(rows):
                left = jnp.concatenate(
                    [dense[g][i, place[1 + p] * inner_rows + m] for m in range(inner_rows)], axis=1
                )
                product = jnp.dot(left, right[g, i], preferred_element_type=jnp.float32)
                sums[g][i] = product if sums[g][i] is None else sums[g][i] + product
    for g in range(groups):
        for i in range(rows):
            if last:
                for j in range(slots):
                    outs[g][i, j] = sums[g][i][:, j * block : (j + 1) * block].astype(outs[g].dtype)
            else:
                outs[g][i] = sums[g][i]


def parity(k):
    return bin(k).count("1") % 2


def body(row_count, col_count, a_tiles, a_cols, b_tiles, b_cols, c_cols):
    rows, slots = c_cols.shape
    inner_rows = b_tiles.shape[0]
    block = a_tiles.shape[-1]
    dtype = b_tiles.dtype
    r, q = lax.axis_index("row"), lax.axis_index("col")
    first = q * COLS_DEV
    bits = sum((r >> k) & 1 for k in range(row_count.bit_length()))
    working = (bits + q) % 2 == 0

    def works(k, c):
        return parity(k) == c % 2

    def swap(x, axis, n, d):
        return lax.ppermute(x, axis, [(k, k ^ d) for k in range(n)])

    def permute(x, target):
        pairs = []
        for k in range(row_count):
            for c in range(col_count):
                to, at = target(k, c)
                pairs.append((k * col_count + c, to * col_count + at))
        return lax.ppermute(x, ("row", "col"), pairs)

    def deliver(x, d):
        def target(k, c):
            if parity(d):
                return (k, c ^ 1) if works(k, c) else (k ^ d, c)
            return (k ^ d, c) if works(k, c) else (k, c ^ (col_count // 2))

        return permute(x, target)

    def give_back(x):
        return permute(x, lambda k, c: (k ^ 1, c) if works(k, c) else (k, c ^ 1))

    size = a_cols.size * block
    count = a_cols.size + c_cols.size + b_cols.size
    own = pl.pallas_call(
        pack_kernel,
        out_shape=jax.ShapeDtypeStruct((size + -(-count // 16) * 16, block), dtype),
        in_specs=[SMEM] * 3 + [VMEM],
        out_specs=VMEM,
        compiler_params=PARAMS,
    )(a_cols, c_cols, b_cols, a_tiles.reshape(size, block))
    c_start, b_start = a_cols.size, a_cols.size + c_cols.size

    shards = {d: deliver(b_tiles, d) for d in range(row_count - 1, 1, -1)}
    other = swap(own, "row", row_count, 1)
    shards[1] = deliver(lax.optimization_barrier((b_tiles, own))[0], 1)

    def across(x):
        parts, d = [x], col_count // 2
        while d:
            parts = parts + [swap(part, "col", col_count, d) for part in parts]
            d //= 2
        return parts

    def index_of(packs):
        return jnp.stack([x[size:, 0] for x in packs]).astype(jnp.int32)

    def dense_of(packs):
        return pl.pallas_call(
            functools.partial(left_kernel, a_cols.shape[1]),
            out_shape=jax.ShapeDtypeStruct((rows, inner_rows * row_count, block, block), dtype),
            in_specs=[SMEM] + [VMEM] * len(packs),
            out_specs=VMEM,
            compiler_params=PARAMS,
        )(index_of(packs), *packs)

    own_packs, other_packs = across(own), across(other)
    own_dense, other_dense = dense_of(own_packs), dense_of(other_packs)
    behind = index_of([other])
    late_cols = lax.optimization_barrier((b_cols, other_packs))[0]
    cols = {0: (None, b_cols), 1: (b_start, behind)}
    for d in range(row_count - 1, 1, -1):
        cols[d] = (None, swap(late_cols, "row", row_count, d))
    shards[0] = b_tiles
    own_rows, other_rows = (None, c_cols, own_dense), (c_start, behind, other_dense)

    def step(dists, groups, before, last):
        place = jnp.stack([first] + [r ^ d for d in dists]).astype(jnp.int32)
        parts, count = len(dists), len(groups)
        if last:
            out = jax.ShapeDtypeStruct((rows, slots, block, block), dtype)
        else:
            out = jax.ShapeDtypeStruct((rows, block, slots * block), jnp.float32)
        starts = [start for start, _, _ in groups] + [cols[d][0] for d in dists]
        return pl.pallas_call(
            functools.partial(step_kernel, parts, count, starts, slots, last),
            out_shape=[out] * count,
            in_specs=[SMEM] * (1 + count + parts) + [VMEM] * (parts + count + len(before)),
            out_specs=[VMEM] * count,
            scratch_shapes=[
                pltpu.VMEM((count, rows, inner_rows * block, slots * block), dtype),
                pltpu.SMEM((inner_rows, COLS_DEV), jnp.int32),
            ],
            compiler_params=PARAMS,
            cost_estimate=pl.CostEstimate(
                flops=2 * count * rows * parts * inner_rows * slots * block**3,
                bytes_accessed=2**21,
                transcendentals=0,
            ),
        )(
            place,
            *[x for _, x, _ in groups],
            *[cols[d][1] for d in dists],
            *[shards[d] for d in dists],
            *[x for _, _, x in groups],
            *before,
        )

    order = [0, 1] + list(range(2, row_count))
    totals = step(order[:2], [own_rows, other_rows], [], False)
    for at in range(2, row_count - 2, 2):
        totals = step(order[at : at + 2], [own_rows, other_rows], totals, False)
    final = order[-2:] if row_count > 2 else []
    (given,) = step(final, [other_rows], totals[1:], True)
    given = give_back(given)
    (kept,) = step(final, [own_rows], totals[:1], True)
    return jnp.where(working, kept, given)


def solution(mesh):
    return jax.shard_map(
        functools.partial(body, mesh.shape["row"], mesh.shape["col"]),
        mesh=mesh,
        in_specs=(
            P(("groups", "row"), "col", None, None),
            P(("groups", "row"), "col"),
            P(("groups", "row"), "col", None, None),
            P(("groups", "row"), "col"),
            P(("groups", "row"), "col"),
        ),
        out_specs=P(("groups", "row"), "col", None, None),
        check_vma=False,
    )
```

time: 136 us -> 45 us (0.33)
  waiting for transfers between devices: 90.2 us -> 18.5 us
  starting transfers between devices: 0.04 us -> 13.3 us
  between operations: 13.4 us -> 0.18 us
  local copies, waits for them, and re-layouts: 15.5 us -> 4.45 us
  Pallas kernels: 0 us -> 7.37 us
  matrix products: 6.96 us -> 0 us
  blocking collectives: 6.25 us -> 0 us
  other arithmetic: 2.96 us -> 0.99 us
    all_gather x2 -> x0, waiting for transfers between devices: 90.1 us -> none  [the longest x1 80.2 us: body(): slab = lax.all_gather(prepared, 'row', axis=0, tiled=True)]
    ppermute x0 -> x13, waiting for transfers between devices: none -> 18.5 us  [the longest x9 11.7 us: swap(): return lax.ppermute(x, axis, [(k, k ^ d) for k in range(n)])]
    ppermute x0 -> x13, starting transfers between devices: none -> 13.3 us  [the longest x9 10.5 us: swap(): return lax.ppermute(x, axis, [(k, k ^ d) for k in range(n)])]
    pallas_call x0 -> x6, Pallas kernels: none -> 7.37 us  [the longest x3 4.98 us: step(): pl.pallas_call(functools.partial(step_kernel, parts, count, starts, slots...]
    dot_general x3 -> x0, matrix products: 6.96 us -> none  [the longest x1 3.47 us: body(): total = jnp.dot(chosen, right, preferred_element_type=jnp.float32)]
    reshape x1 -> x0, local copies, waits for them, and re-layouts: 6.39 us -> none  [body(): right = slab.reshape(count * block, width * block)]
    all_gather x1 -> x0, blocking collectives: 6.25 us -> none  [body(): lax.all_gather(a_cols, 'col', axis=1, tiled=True)]
    unnamed x5 -> x14, local copies, waits for them, and re-layouts: 8.1 us -> 3.59 us
  transfers between devices with their start and end apart: 2 -> 13, of which waited for: 2 -> 5; matrix products, arithmetic and copies ran while one was open for 4% -> 2% of each run, Pallas kernels for 0% -> 12%
where the time goes in v7:
time: 45 us; the launch traced here: 44.8 us
  waiting for transfers between devices  18.5 us (41%)
  starting transfers between devices  13.3 us (30%)
  Pallas kernels  7.37 us (16%)
  local copies, waits for them, and re-layouts  4.45 us (10%)
  other arithmetic  0.99 us (2%)
    ppermute x9, waiting for transfers between devices, swap(): return lax.ppermute(x, axis, [(k, k ^ d) for k in range(n)])  11.7 us
    ppermute x9, starting transfers between devices, swap(): return lax.ppermute(x, axis, [(k, k ^ d) for k in range(n)])  10.5 us
    ppermute x4, waiting for transfers between devices, permute(): return lax.ppermute(x, ('row', 'col'), pairs)  6.78 us
    pallas_call x3, Pallas kernels, step(): pl.pallas_call(functools.partial(step_kernel, parts, count, starts, slots...  4.98 us
    unnamed x14, local copies, waits for them, and re-layouts  3.59 us
    ppermute x4, starting transfers between devices, permute(): return lax.ppermute(x, ('row', 'col'), pairs)  2.83 us
    pallas_call x2, Pallas kernels, dense_of(): pl.pallas_call(functools.partial(left_kernel, a_cols.shape[1]), out_shape...  1.79 us
  transfers between devices with their start and end apart: 13, of which 5 were waited for; matrix products, arithmetic and copies ran while one was open for 2% of the time, Pallas kernels for 12%

profile of v7, /device:TPU:0, one launch (start us, length us, event | category | flops | bytes accessed | tf_op | source)
XLA Modules:
  0.0 44.8 jit_solution(12904368370560713940)
XLA Ops:
  0.0 1.0 %copy-done.1 = bf16[2,4,128,128]{3,2,1,0:T(8,128)(2,1)S(1)} copy-done((bf16[2,4,128,128]{3,2,1,0:T(8,128)(2,1)S(1)}, bf16[2,4,128,128]{3,2,1,0:T(8,128)(2,1)}, u32[]{:S(2)}) %copy-start.1) | copy-done | bytes 262168
  1.0 0.7 %copy-done.2 = s32[2,6]{1,0:T(2,128)S(1)} copy-done((s32[2,6]{1,0:T(2,128)S(1)}, s32[2,6]{1,0:T(2,128)}, u32[]{:S(2)}) %copy-start.2) | copy-done | bytes 72
  1.7 0.7 %copy-done.4 = s32[2,8]{1,0:T(2,128)S(1)} copy-done((s32[2,8]{1,0:T(2,128)S(1)}, s32[2,8]{1,0:T(2,128)}, u32[]{:S(2)}) %copy-start.4) | copy-done | bytes 88
  2.4 0.7 %copy-done.6 = s32[2,4]{1,0:T(2,128)S(1)} copy-done((s32[2,4]{1,0:T(2,128)S(1)}, s32[2,4]{1,0:T(2,128)}, u32[]{:S(2)}) %copy-start.6) | copy-done | bytes 56
  3.0 0.6 %shard_map.55.refs_0_ = bf16[1072,128]{1,0:T(8,128)(2,1)S(1)} custom-call(s32[2,4]{1,0:T(2,128)S(1)} %copy-done.6, s32[2,6]{1,0:T(2,128)S(1)} %copy-done.2, s32[2,8]{1,0:T(2,128)S(1)} %copy-done.4, bf16[1024,128]{1,0:T(8,128)(2,1)S(1)} %bitcast.15), custom_call_target="tpu_custom_call" | custom-call | tf_op jit(solution)/shard_map/pallas_call | solution.py:134
  3.7 0.5 %collective-permute-start.9 = (bf16[1072,128]{1,0:T(8,128)(2,1)S(1)}, bf16[1072,128]{1,0:T(8,128)(2,1)S(1)}, u32[]{:S(2)}, u32[]{:S(2)}) collective-permute-start(bf16[1072,128]{1,0:T(8,128)(2,1)S(1)} %shard_map.55.refs_0_), channel_id=1, source_target_pairs={{0,1},{1,0},{2,3},{3,2},{4,5},{5,4},{6,7},{7,6},{8,9},{9,8},{10,11... | collective-permute-start | bytes 823304 | tf_op jit(solution)/shard_map/ppermute | solution.py:111
  4.2 2.6 %collective-permute-start.8 = (bf16[1072,128]{1,0:T(8,128)(2,1)S(1)}, bf16[1072,128]{1,0:T(8,128)(2,1)S(1)}, u32[]{:S(2)}, u32[]{:S(2)}) collective-permute-start(bf16[1072,128]{1,0:T(8,128)(2,1)S(1)} %shard_map.55.refs_0_), channel_id=1, source_target_pairs={{0,2},{1,3},{2,0},{3,1},{4,6},{5,7},{6,4},{7,5},{8,10},{9,11},{10,... | collective-permute-start | bytes 823304 | tf_op jit(solution)/shard_map/ppermute | solution.py:111
  6.7 1.6 %collective-permute-start = (bf16[1072,128]{1,0:T(8,128)(2,1)S(1)}, bf16[1072,128]{1,0:T(8,128)(2,1)S(1)}, u32[]{:S(2)}, u32[]{:S(2)}) collective-permute-start(bf16[1072,128]{1,0:T(8,128)(2,1)S(1)} %shard_map.55.refs_0_), channel_id=1, source_target_pairs={{0,4},{4,0},{8,12},{12,8},{1,5},{5,1},{9,13},{13,9},{2,6},{6,2},{1... | collective-permute-start | bytes 823304 | tf_op jit(solution)/shard_map/ppermute | solution.py:111
  8.3 2.5 %collective-permute-start.7 = (bf16[2,8,128,128]{3,2,1,0:T(8,128)(2,1)S(1)}, bf16[2,8,128,128]{3,2,1,0:T(8,128)(2,1)S(1)}, u32[]{:S(2)}, u32[]{:S(2)}) collective-permute-start(bf16[2,8,128,128]{3,2,1,0:T(8,128)(2,1)S(1)} %copy-done), channel_id=1, source_target_pairs={{0,12},{1,3},{2,14},{3,1},{4,6},{5,9},{6,4},{7,11},{8,10},{9,5},{1... | collective-permute-start | bytes 1572872 | tf_op jit(solution)/shard_map/ppermute | solution.py:119
  11.0 0.1 slice_reduce_fusion.7
  11.1 3.1 %collective-permute-done.8.refs_1_ = bf16[1072,128]{1,0:T(8,128)(2,1)S(1)} collective-permute-done((bf16[1072,128]{1,0:T(8,128)(2,1)S(1)}, bf16[1072,128]{1,0:T(8,128)(2,1)S(1)}, u32[]{:S(2)}, u32[]{:S(2)}) %collective-permute-start.8) | collective-permute-done | bytes 274464 | tf_op jit(solution)/shard_map/ppermute | solution.py:111
  14.2 1.3 %collective-permute-done.refs_0_ = bf16[1072,128]{1,0:T(8,128)(2,1)S(1)} collective-permute-done((bf16[1072,128]{1,0:T(8,128)(2,1)S(1)}, bf16[1072,128]{1,0:T(8,128)(2,1)S(1)}, u32[]{:S(2)}, u32[]{:S(2)}) %collective-permute-start) | collective-permute-done | bytes 274464 | tf_op jit(solution)/shard_map/ppermute | solution.py:111
  15.4 0.1 slice_reduce_fusion.3
  15.6 0.8 %collective-permute-start.1 = (bf16[1072,128]{1,0:T(8,128)(2,1)S(1)}, bf16[1072,128]{1,0:T(8,128)(2,1)S(1)}, u32[]{:S(2)}, u32[]{:S(2)}) collective-permute-start(bf16[1072,128]{1,0:T(8,128)(2,1)S(1)} %collective-permute-done.refs_0_), channel_id=1, source_target_pairs={{0,2},{1,3},{2,0},{3,1},{4,6},{5,7},{6,4},{7,5},{8,10},{9,11},{10,... | collective-permute-start | bytes 823304 | tf_op jit(solution)/shard_map/ppermute | solution.py:111
  16.3 0.1 slice_reduce_fusion.6
  16.4 0.3 collective-permute-start.11
  16.7 0.1 slice_reduce_fusion.5
  16.8 0.9 %collective-permute-start.2 = (bf16[1072,128]{1,0:T(8,128)(2,1)S(1)}, bf16[1072,128]{1,0:T(8,128)(2,1)S(1)}, u32[]{:S(2)}, u32[]{:S(2)}) collective-permute-start(bf16[1072,128]{1,0:T(8,128)(2,1)S(1)} %collective-permute-done.refs_0_), channel_id=1, source_target_pairs={{0,1},{1,0},{2,3},{3,2},{4,5},{5,4},{6,7},{7,6},{8,9},{9,8},{10,11... | collective-permute-start | bytes 823304 | tf_op jit(solution)/shard_map/ppermute | solution.py:111
  17.9 7.3 %collective-permute-done.1.refs_1_ = bf16[1072,128]{1,0:T(8,128)(2,1)S(1)} collective-permute-done((bf16[1072,128]{1,0:T(8,128)(2,1)S(1)}, bf16[1072,128]{1,0:T(8,128)(2,1)S(1)}, u32[]{:S(2)}, u32[]{:S(2)}) %collective-permute-start.1) | collective-permute-done | bytes 274464 | tf_op jit(solution)/shard_map/ppermute | solution.py:111
  25.1 0.4 collective-permute-start.3
  25.5 0.9 %shard_map.56.refs_6_.refs_5_ = bf16[2,8,128,128]{3,2,1,0:T(8,128)(2,1)S(1)} custom-call(s32[4,48]{1,0:T(4,128)S(1)} %maximum_convert_fusion.index, bf16[1072,128]{1,0:T(8,128)(2,1)S(1)} %shard_map.55.refs_0_, bf16[1072,128]{1,0:T(8,128)(2,1)S(1)} %collective-permute-done.8.refs_1_, bf16[1072,128]{1,0:T(8,128)(2,1)S(1)} %collective-permute-done.9.refs_2_, ...), custom_call_target="tpu_custom_call" | custom-call | tf_op jit(solution)/shard_map/pallas_call | solution.py:158
  26.4 0.1 slice_reduce_fusion.2
  26.6 0.1 slice_reduce_fusion.1
  26.7 0.5 %copy-done.5 = s32[2,8]{1,0:T(2,128)S(1)} copy-done((s32[2,8]{1,0:T(2,128)S(1)}, s32[2,8]{1,0:T(2,128)}, u32[]{:S(2)}) %copy-start.5) | copy-done | bytes 88
  27.2 3.8 %collective-permute-start.5 = (s32[2,8]{1,0:T(2,128)S(1)}, s32[2,8]{1,0:T(2,128)S(1)}, u32[]{:S(2)}, u32[]{:S(2)}) collective-permute-start(s32[2,8]{1,0:T(2,128)S(1)} %copy-done.5), channel_id=1, source_target_pairs={{0,12},{4,8},{8,4},{12,0},{1,13},{5,9},{9,5},{13,1},{2,14},{6,10},... | collective-permute-start | bytes 200 | tf_op jit(solution)/shard_map/ppermute | solution.py:111
  31.1 0.9 %shard_map.57.refs_7_.refs_5_ = bf16[2,8,128,128]{3,2,1,0:T(8,128)(2,1)S(1)} custom-call(s32[4,48]{1,0:T(4,128)S(1)} %maximum_convert_fusion.1.index, bf16[1072,128]{1,0:T(8,128)(2,1)S(1)} %collective-permute-done.refs_0_, bf16[1072,128]{1,0:T(8,128)(2,1)S(1)} %collective-permute-done.1.refs_1_, bf16[1072,128]{1,0:T(8,128)(2,1)S(1)} %collective-permute-done.2.refs_2_, ...), custom_call_target="tpu_custom_call" | custom-call | tf_op jit(solution)/shard_map/pallas_call | solution.py:158
  32.0 3.0 %collective-permute-done.11.refs_5_ = bf16[2,8,128,128]{3,2,1,0:T(8,128)(2,1)S(1)} collective-permute-done((bf16[2,8,128,128]{3,2,1,0:T(8,128)(2,1)S(1)}, bf16[2,8,128,128]{3,2,1,0:T(8,128)(2,1)S(1)}, u32[]{:S(2)}, u32[]{:S(2)}) %collective-permute-start.11) | collective-permute-done | bytes 524320 | tf_op jit(solution)/shard_map/ppermute | solution.py:119
  35.0 2.0 %shard_map.58 = (f32[2,128,768]{2,1,0:T(8,128)S(1)}, f32[2,128,768]{2,1,0:T(8,128)S(1)}) custom-call(s32[3]{0:T(128)S(1)} %pad_add_fusion.1.place, s32[2,6]{1,0:T(2,128)S(1)} %copy-done.3, s32[1,48]{1,0:T(1,128)S(1)} %bitcast_convert_fusion.refs_1_.refs_3_.refs_0_, s32[2,8]{1,0:T(2,128)S(1)} %copy-done.5, ...), custom_call_target="tpu_custom_call" | custom-call | flops 402653184 | bytes 2097152 | tf_op jit(solution)/shard_map/pallas_call | solution.py:184
  37.1 1.5 %shard_map.60 = bf16[2,6,128,128]{3,2,1,0:T(8,128)(2,1)S(1)} custom-call(s32[3]{0:T(128)S(1)} %pad_add_fusion.place, s32[1,48]{1,0:T(1,128)S(1)} %bitcast_convert_fusion.refs_1_.refs_3_.refs_0_, s32[2,8]{1,0:T(2,128)S(1)} %collective-permute-done.4.refs_1_, s32[2,8]{1,0:T(2,128)S(1)} %collective-permute-done.5.refs_2_, ...), custom_call_target="tpu_custom_call" | custom-call | flops 201326592 | bytes 2097152 | tf_op jit(solution)/shard_map/pallas_call | solution.py:184
  38.7 1.5 %shard_map.59 = bf16[2,6,128,128]{3,2,1,0:T(8,128)(2,1)S(1)} custom-call(s32[3]{0:T(128)S(1)} %pad_add_fusion.place, s32[2,6]{1,0:T(2,128)S(1)} %copy-done.3, s32[2,8]{1,0:T(2,128)S(1)} %collective-permute-done.4.refs_1_, s32[2,8]{1,0:T(2,128)S(1)} %collective-permute-done.5.refs_2_, bf16[2,8,128,128]{3,2,1,0:T(8,128)(2,1)S(1)} %collective-permute-done.6.refs_3_, ...), custom_call_target="tpu_custom_call" | custom-call | flops 201326592 | bytes 2097152 | tf_op jit(solution)/shard_map/pallas_call | solution.py:184
  40.2 3.8 %collective-permute-done.12 = bf16[2,6,128,128]{3,2,1,0:T(8,128)(2,1)S(1)} collective-permute-done((bf16[2,6,128,128]{3,2,1,0:T(8,128)(2,1)S(1)}, bf16[2,6,128,128]{3,2,1,0:T(8,128)(2,1)S(1)}, u32[]{:S(2)}, u32[]{:S(2)}) %collective-permute-start.12) | collective-permute-done | bytes 393248 | tf_op jit(solution)/shard_map/ppermute | solution.py:119
  44.0 0.8 %broadcast_select_fusion = bf16[2,6,128,128]{3,2,1,0:T(8,128)(2,1)} fusion(bf16[2,6,128,128]{3,2,1,0:T(8,128)(2,1)S(1)} %shard_map.59, bf16[2,6,128,128]{3,2,1,0:T(8,128)(2,1)S(1)} %collective-permute-done.12, pred[]{:T(512)S(6)} %eq.5), kind=kLoop, calls=%fused_computation | loop fusion | flops 196608 | bytes 1179649 | tf_op jit(solution)/shard_map/jit(_where)/select_n | solution.py:216
  (28 shorter events, 0.5 us)
Async XLA Ops:
  0.0 8.3 %copy-start = (bf16[2,8,128,128]{3,2,1,0:T(8,128)(2,1)S(1)}, bf16[2,8,128,128]{3,2,1,0:T(8,128)(2,1)}, u32[]{:S(2)}) copy-start(bf16[2,8,128,128]{3,2,1,0:T(8,128)(2,1)} %refs_4_.1) | copy-start | bytes 1572868
  0.0 1.0 %copy-start.1 = (bf16[2,4,128,128]{3,2,1,0:T(8,128)(2,1)S(1)}, bf16[2,4,128,128]{3,2,1,0:T(8,128)(2,1)}, u32[]{:S(2)}) copy-start(bf16[2,4,128,128]{3,2,1,0:T(8,128)(2,1)} %param.5) | copy-start | bytes 786436
  1.0 0.7 %copy-start.2 = (s32[2,6]{1,0:T(2,128)S(1)}, s32[2,6]{1,0:T(2,128)}, u32[]{:S(2)}) copy-start(s32[2,6]{1,0:T(2,128)} %refs_0_.5) | copy-start | bytes 148
  1.7 0.7 %copy-start.4 = (s32[2,8]{1,0:T(2,128)S(1)}, s32[2,8]{1,0:T(2,128)}, u32[]{:S(2)}) copy-start(s32[2,8]{1,0:T(2,128)} %refs_2_.3) | copy-start | bytes 196
  2.4 0.7 %copy-start.6 = (s32[2,4]{1,0:T(2,128)S(1)}, s32[2,4]{1,0:T(2,128)}, u32[]{:S(2)}) copy-start(s32[2,4]{1,0:T(2,128)} %refs_0_.3) | copy-start | bytes 100
  3.7 12.8 %collective-permute-start.9 = (bf16[1072,128]{1,0:T(8,128)(2,1)S(1)}, bf16[1072,128]{1,0:T(8,128)(2,1)S(1)}, u32[]{:S(2)}, u32[]{:S(2)}) collective-permute-start(bf16[1072,128]{1,0:T(8,128)(2,1)S(1)} %shard_map.55.refs_0_), channel_id=1, source_target_pairs={{0,1},{1,0},{2,3},{3,2},{4,5},{5,4},{6,7},{7,6},{8,9},{9,8},{10,11... | collective-permute-start | bytes 823304 | tf_op jit(solution)/shard_map/ppermute | solution.py:111
  4.2 10.0 %collective-permute-start.8 = (bf16[1072,128]{1,0:T(8,128)(2,1)S(1)}, bf16[1072,128]{1,0:T(8,128)(2,1)S(1)}, u32[]{:S(2)}, u32[]{:S(2)}) collective-permute-start(bf16[1072,128]{1,0:T(8,128)(2,1)S(1)} %shard_map.55.refs_0_), channel_id=1, source_target_pairs={{0,2},{1,3},{2,0},{3,1},{4,6},{5,7},{6,4},{7,5},{8,10},{9,11},{10,... | collective-permute-start | bytes 823304 | tf_op jit(solution)/shard_map/ppermute | solution.py:111
  6.7 8.7 %collective-permute-start = (bf16[1072,128]{1,0:T(8,128)(2,1)S(1)}, bf16[1072,128]{1,0:T(8,128)(2,1)S(1)}, u32[]{:S(2)}, u32[]{:S(2)}) collective-permute-start(bf16[1072,128]{1,0:T(8,128)(2,1)S(1)} %shard_map.55.refs_0_), channel_id=1, source_target_pairs={{0,4},{4,0},{8,12},{12,8},{1,5},{5,1},{9,13},{13,9},{2,6},{6,2},{1... | collective-permute-start | bytes 823304 | tf_op jit(solution)/shard_map/ppermute | solution.py:111
  8.3 28.7 %collective-permute-start.7 = (bf16[2,8,128,128]{3,2,1,0:T(8,128)(2,1)S(1)}, bf16[2,8,128,128]{3,2,1,0:T(8,128)(2,1)S(1)}, u32[]{:S(2)}, u32[]{:S(2)}) collective-permute-start(bf16[2,8,128,128]{3,2,1,0:T(8,128)(2,1)S(1)} %copy-done), channel_id=1, source_target_pairs={{0,12},{1,3},{2,14},{3,1},{4,6},{5,9},{6,4},{7,11},{8,10},{9,5},{1... | collective-permute-start | bytes 1572872 | tf_op jit(solution)/shard_map/ppermute | solution.py:119
  10.8 26.3 %collective-permute-start.6 = (bf16[2,8,128,128]{3,2,1,0:T(8,128)(2,1)S(1)}, bf16[2,8,128,128]{3,2,1,0:T(8,128)(2,1)S(1)}, u32[]{:S(2)}, u32[]{:S(2)}) collective-permute-start(bf16[2,8,128,128]{3,2,1,0:T(8,128)(2,1)S(1)} %copy-done), channel_id=1, source_target_pairs={{0,1},{1,9},{2,3},{3,11},{4,12},{5,4},{6,14},{7,6},{8,0},{9,8},{10... | collective-permute-start | bytes 1572872 | tf_op jit(solution)/shard_map/ppermute | solution.py:119
  14.2 2.7 %collective-permute-start.10 = (bf16[1072,128]{1,0:T(8,128)(2,1)S(1)}, bf16[1072,128]{1,0:T(8,128)(2,1)S(1)}, u32[]{:S(2)}, u32[]{:S(2)}) collective-permute-start(bf16[1072,128]{1,0:T(8,128)(2,1)S(1)} %collective-permute-done.8.refs_1_), channel_id=1, source_target_pairs={{0,1},{1,0},{2,3},{3,2},{4,5},{5,4},{6,7},{7,6},{8,9},{9,8},{10,11... | collective-permute-start | bytes 823304 | tf_op jit(solution)/shard_map/ppermute | solution.py:111
  15.6 9.6 %collective-permute-start.1 = (bf16[1072,128]{1,0:T(8,128)(2,1)S(1)}, bf16[1072,128]{1,0:T(8,128)(2,1)S(1)}, u32[]{:S(2)}, u32[]{:S(2)}) collective-permute-start(bf16[1072,128]{1,0:T(8,128)(2,1)S(1)} %collective-permute-done.refs_0_), channel_id=1, source_target_pairs={{0,2},{1,3},{2,0},{3,1},{4,6},{5,7},{6,4},{7,5},{8,10},{9,11},{10,... | collective-permute-start | bytes 823304 | tf_op jit(solution)/shard_map/ppermute | solution.py:111
  16.4 18.6 %collective-permute-start.11 = (bf16[2,8,128,128]{3,2,1,0:T(8,128)(2,1)S(1)}, bf16[2,8,128,128]{3,2,1,0:T(8,128)(2,1)S(1)}, u32[]{:S(2)}, u32[]{:S(2)}) collective-permute-start(bf16[2,8,128,128]{3,2,1,0:T(8,128)(2,1)S(1)} %copy-done), channel_id=1, source_target_pairs={{0,1},{1,5},{2,3},{3,7},{4,0},{5,4},{6,2},{7,6},{8,12},{9,8},{10,1... | collective-permute-start | bytes 1572872 | tf_op jit(solution)/shard_map/ppermute | solution.py:119
  16.8 9.7 %collective-permute-start.2 = (bf16[1072,128]{1,0:T(8,128)(2,1)S(1)}, bf16[1072,128]{1,0:T(8,128)(2,1)S(1)}, u32[]{:S(2)}, u32[]{:S(2)}) collective-permute-start(bf16[1072,128]{1,0:T(8,128)(2,1)S(1)} %collective-permute-done.refs_0_), channel_id=1, source_target_pairs={{0,1},{1,0},{2,3},{3,2},{4,5},{5,4},{6,7},{7,6},{8,9},{9,8},{10,11... | collective-permute-start | bytes 823304 | tf_op jit(solution)/shard_map/ppermute | solution.py:111
  25.1 1.6 %collective-permute-start.3 = (bf16[1072,128]{1,0:T(8,128)(2,1)S(1)}, bf16[1072,128]{1,0:T(8,128)(2,1)S(1)}, u32[]{:S(2)}, u32[]{:S(2)}) collective-permute-start(bf16[1072,128]{1,0:T(8,128)(2,1)S(1)} %collective-permute-done.1.refs_1_), channel_id=1, source_target_pairs={{0,1},{1,0},{2,3},{3,2},{4,5},{5,4},{6,7},{7,6},{8,9},{9,8},{10,11... | collective-permute-start | bytes 823304 | tf_op jit(solution)/shard_map/ppermute | solution.py:111
  26.5 0.7 %copy-start.5 = (s32[2,8]{1,0:T(2,128)S(1)}, s32[2,8]{1,0:T(2,128)}, u32[]{:S(2)}) copy-start(s32[2,8]{1,0:T(2,128)} %refs_2_.3) | copy-start | bytes 196
  27.2 9.9 %collective-permute-start.5 = (s32[2,8]{1,0:T(2,128)S(1)}, s32[2,8]{1,0:T(2,128)S(1)}, u32[]{:S(2)}, u32[]{:S(2)}) collective-permute-start(s32[2,8]{1,0:T(2,128)S(1)} %copy-done.5), channel_id=1, source_target_pairs={{0,12},{4,8},{8,4},{12,0},{1,13},{5,9},{9,5},{13,1},{2,14},{6,10},... | collective-permute-start | bytes 200 | tf_op jit(solution)/shard_map/ppermute | solution.py:111
  31.0 6.1 %collective-permute-start.4 = (s32[2,8]{1,0:T(2,128)S(1)}, s32[2,8]{1,0:T(2,128)S(1)}, u32[]{:S(2)}, u32[]{:S(2)}) collective-permute-start(s32[2,8]{1,0:T(2,128)S(1)} %copy-done.5), channel_id=1, source_target_pairs={{0,8},{4,12},{8,0},{12,4},{1,9},{5,13},{9,1},{13,5},{2,10},{6,14},... | collective-permute-start | bytes 200 | tf_op jit(solution)/shard_map/ppermute | solution.py:111
  31.1 3.9 %copy-start.3 = (s32[2,6]{1,0:T(2,128)S(1)}, s32[2,6]{1,0:T(2,128)}, u32[]{:S(2)}) copy-start(s32[2,6]{1,0:T(2,128)} %refs_0_.5) | copy-start | bytes 148
  38.6 5.4 %collective-permute-start.12 = (bf16[2,6,128,128]{3,2,1,0:T(8,128)(2,1)S(1)}, bf16[2,6,128,128]{3,2,1,0:T(8,128)(2,1)S(1)}, u32[]{:S(2)}, u32[]{:S(2)}) collective-permute-start(bf16[2,6,128,128]{3,2,1,0:T(8,128)(2,1)S(1)} %shard_map.60), channel_id=1, source_target_pairs={{0,4},{1,0},{2,6},{3,2},{4,5},{5,1},{6,7},{7,3},{8,9},{9,13},{10,1... | collective-permute-start | bytes 1179656 | tf_op jit(solution)/shard_map/ppermute | solution.py:119

commit v8 on v7

--- a/solution.py
+++ b/solution.py
@@ -140,16 +140,26 @@
     )(a_cols, c_cols, b_cols, a_tiles.reshape(size, block))
     c_start, b_start = a_cols.size, a_cols.size + c_cols.size
 
-    shards = {d: deliver(b_tiles, d) for d in range(row_count - 1, 1, -1)}
-    other = swap(own, "row", row_count, 1)
-    shards[1] = deliver(lax.optimization_barrier((b_tiles, own))[0], 1)
-
-    def across(x):
-        parts, d = [x], col_count // 2
+    def across(parts, d):
         while d:
             parts = parts + [swap(part, "col", col_count, d) for part in parts]
             d //= 2
         return parts
+
+    far = col_count // 2
+    shards = {0: b_tiles, row_count - 1: deliver(b_tiles, row_count - 1)}
+    cols = {0: (None, b_cols)}
+    for d in range(row_count - 1, 1, -1):
+        cols[d] = (None, swap(b_cols, "row", row_count, d))
+    own_packs = [own, swap(own, "col", col_count, far)]
+    other = swap(own, "row", row_count, 1)
+    next_tiles = lax.optimization_barrier((b_tiles, own_packs[1]))[0]
+    for d in range(row_count - 2, 1, -1):
+        shards[d] = deliver(next_tiles, d)
+    last_tiles, other, _, _ = lax.optimization_barrier((b_tiles, other, shards[row_count - 1], cols))
+    shards[1] = deliver(last_tiles, 1)
+    own_packs = across(own_packs, far // 2)
+    other_packs = across([other], far)
 
     def index_of(packs):
         return jnp.stack([x[size:, 0] for x in packs]).astype(jnp.int32)
@@ -163,14 +173,9 @@
             compiler_params=PARAMS,
         )(index_of(packs), *packs)
 
-    own_packs, other_packs = across(own), across(other)
     own_dense, other_dense = dense_of(own_packs), dense_of(other_packs)
     behind = index_of([other])
-    late_cols = lax.optimization_barrier((b_cols, other_packs))[0]
-    cols = {0: (None, b_cols), 1: (b_start, behind)}
-    for d in range(row_count - 1, 1, -1):
-        cols[d] = (None, swap(late_cols, "row", row_count, d))
-    shards[0] = b_tiles
+    cols[1] = (b_start, behind)
     own_rows, other_rows = (None, c_cols, own_dense), (c_start, behind, other_dense)
 
     def step(dists, groups, before, last):
@@ -205,14 +210,14 @@
             *before,
         )
 
-    order = [0, 1] + list(range(2, row_count))
-    totals = step(order[:2], [own_rows, other_rows], [], False)
-    for at in range(2, row_count - 2, 2):
-        totals = step(order[at : at + 2], [own_rows, other_rows], totals, False)
-    final = order[-2:] if row_count > 2 else []
-    (given,) = step(final, [other_rows], totals[1:], True)
-    given = give_back(given)
-    (kept,) = step(final, [own_rows], totals[:1], True)
+    def products(group):
+        order, totals = [0] + list(range(row_count - 1, 0, -1)), []
+        for at in range(0, row_count, 2):
+            totals = step(order[at : at + 2], [group], totals, at + 2 >= row_count)
+        return totals[0]
+
+    given = give_back(products(other_rows))
+    kept = products(own_rows)
     return jnp.where(working, kept, given)
 
 

time: 45 us -> 45.6 us (1.013)
  starting transfers between devices: 13.3 us -> 16 us
  waiting for transfers between devices: 18.5 us -> 16.6 us
  local copies, waits for them, and re-layouts: 4.45 us -> 3.18 us
  Pallas kernels: 7.37 us -> 8.61 us
    ppermute x9, waiting for transfers between devices: 11.7 us -> 9 us  [swap(): return lax.ppermute(x, axis, [(k, k ^ d) for k in range(n)])]
    ppermute x4, starting transfers between devices: 2.83 us -> 5.19 us  [permute(): return lax.ppermute(x, ('row', 'col'), pairs)]
    unnamed x14 -> x10, local copies, waits for them, and re-layouts: 3.59 us -> 2.32 us
    pallas_call x3 -> x4, Pallas kernels: 4.98 us -> 6.05 us  [step(): pl.pallas_call(functools.partial(step_kernel, parts, count, starts, slots...]
    ppermute x4, waiting for transfers between devices: 6.78 us -> 7.58 us  [permute(): return lax.ppermute(x, ('row', 'col'), pairs)]
  transfers between devices with their start and end apart: 13 -> 13, of which waited for: 5 -> 8; matrix products, arithmetic and copies ran while one was open for 2% -> 2% of each run, Pallas kernels for 12% -> 19%
where the time goes in v8:
time: 45.6 us; the launch traced here: 45.4 us
  waiting for transfers between devices  16.6 us (36%)
  starting transfers between devices  16 us (35%)
  Pallas kernels  8.61 us (19%)
  local copies, waits for them, and re-layouts  3.18 us (7%)
  other arithmetic  0.9 us (2%)
    ppermute x9, starting transfers between devices, swap(): return lax.ppermute(x, axis, [(k, k ^ d) for k in range(n)])  10.8 us
    ppermute x9, waiting for transfers between devices, swap(): return lax.ppermute(x, axis, [(k, k ^ d) for k in range(n)])  9 us
    ppermute x4, waiting for transfers between devices, permute(): return lax.ppermute(x, ('row', 'col'), pairs)  7.58 us
    pallas_call x4, Pallas kernels, step(): pl.pallas_call(functools.partial(step_kernel, parts, count, starts, slots...  6.05 us
    ppermute x4, starting transfers between devices, permute(): return lax.ppermute(x, ('row', 'col'), pairs)  5.19 us
    unnamed x10, local copies, waits for them, and re-layouts  2.32 us
    pallas_call x2, Pallas kernels, dense_of(): pl.pallas_call(functools.partial(left_kernel, a_cols.shape[1]), out_shape...  1.79 us
  transfers between devices with their start and end apart: 13, of which 8 were waited for; matrix products, arithmetic and copies ran while one was open for 2% of the time, Pallas kernels for 19%

profile of v8, /device:TPU:0, one launch (start us, length us, event | category | flops | bytes accessed | tf_op | source)
XLA Modules:
  0.0 45.4 jit_solution(2971441770257139519)
XLA Ops:
  0.0 5.0 %collective-permute-start.2 = (bf16[2,8,128,128]{3,2,1,0:T(8,128)(2,1)}, bf16[2,8,128,128]{3,2,1,0:T(8,128)(2,1)S(1)}, u32[]{:S(2)}, u32[]{:S(2)}) collective-permute-start(bf16[2,8,128,128]{3,2,1,0:T(8,128)(2,1)} %refs_3_.3), channel_id=1, source_target_pairs={{0,12},{1,3},{2,14},{3,1},{4,6},{5,9},{6,4},{7,11},{8,10},{9,5},{1... | collective-permute-start | bytes 1572872 | tf_op jit(solution)/shard_map/ppermute | solution.py:119
  5.1 0.9 %copy-done.1 = bf16[2,4,128,128]{3,2,1,0:T(8,128)(2,1)S(1)} copy-done((bf16[2,4,128,128]{3,2,1,0:T(8,128)(2,1)S(1)}, bf16[2,4,128,128]{3,2,1,0:T(8,128)(2,1)}, u32[]{:S(2)}) %copy-start.1) | copy-done | bytes 262168
  6.0 0.7 %copy-done.2 = s32[2,6]{1,0:T(2,128)S(1)} copy-done((s32[2,6]{1,0:T(2,128)S(1)}, s32[2,6]{1,0:T(2,128)}, u32[]{:S(2)}) %copy-start.2) | copy-done | bytes 72
  6.7 0.7 %copy-done.4 = s32[2,4]{1,0:T(2,128)S(1)} copy-done((s32[2,4]{1,0:T(2,128)S(1)}, s32[2,4]{1,0:T(2,128)}, u32[]{:S(2)}) %copy-start.4) | copy-done | bytes 56
  7.4 0.8 %shard_map.55.refs_0_ = bf16[1072,128]{1,0:T(8,128)(2,1)S(1)} custom-call(s32[2,4]{1,0:T(2,128)S(1)} %copy-done.4, s32[2,6]{1,0:T(2,128)S(1)} %copy-done.2, s32[2,8]{1,0:T(2,128)} %refs_1_.5, bf16[1024,128]{1,0:T(8,128)(2,1)S(1)} %bitcast.15), custom_call_target="tpu_custom_call" | custom-call | tf_op jit(solution)/shard_map/pallas_call | solution.py:134
  8.2 1.6 %collective-permute-start.4 = (bf16[1072,128]{1,0:T(8,128)(2,1)S(1)}, bf16[1072,128]{1,0:T(8,128)(2,1)S(1)}, u32[]{:S(2)}, u32[]{:S(2)}) collective-permute-start(bf16[1072,128]{1,0:T(8,128)(2,1)S(1)} %shard_map.55.refs_0_), channel_id=1, source_target_pairs={{0,2},{1,3},{2,0},{3,1},{4,6},{5,7},{6,4},{7,5},{8,10},{9,11},{10,... | collective-permute-start | bytes 823304 | tf_op jit(solution)/shard_map/ppermute | solution.py:111
  9.8 0.7 %collective-permute-start = (s32[2,8]{1,0:T(2,128)}, s32[2,8]{1,0:T(2,128)S(1)}, u32[]{:S(2)}, u32[]{:S(2)}) collective-permute-start(s32[2,8]{1,0:T(2,128)} %refs_1_.5), channel_id=1, source_target_pairs={{0,8},{4,12},{8,0},{12,4},{1,9},{5,13},{9,1},{13,5},{2,10},{6,14},... | collective-permute-start | bytes 200 | tf_op jit(solution)/shard_map/ppermute | solution.py:111
  10.5 3.6 %collective-permute-start.3 = (s32[2,8]{1,0:T(2,128)}, s32[2,8]{1,0:T(2,128)S(1)}, u32[]{:S(2)}, u32[]{:S(2)}) collective-permute-start(s32[2,8]{1,0:T(2,128)} %refs_1_.5), channel_id=1, source_target_pairs={{0,12},{4,8},{8,4},{12,0},{1,13},{5,9},{9,5},{13,1},{2,14},{6,10},... | collective-permute-start | bytes 200 | tf_op jit(solution)/shard_map/ppermute | solution.py:111
  14.1 3.9 %collective-permute-done.refs_1_ = s32[2,8]{1,0:T(2,128)S(1)} collective-permute-done((s32[2,8]{1,0:T(2,128)}, s32[2,8]{1,0:T(2,128)S(1)}, u32[]{:S(2)}, u32[]{:S(2)}) %collective-permute-start) | collective-permute-done | bytes 96 | tf_op jit(solution)/shard_map/ppermute | solution.py:111
  17.9 0.5 %collective-permute-done.3.refs_2_ = s32[2,8]{1,0:T(2,128)S(1)} collective-permute-done((s32[2,8]{1,0:T(2,128)}, s32[2,8]{1,0:T(2,128)S(1)}, u32[]{:S(2)}, u32[]{:S(2)}) %collective-permute-start.3) | collective-permute-done | bytes 96 | tf_op jit(solution)/shard_map/ppermute | solution.py:111
  18.5 1.6 %collective-permute-start.9 = (bf16[1072,128]{1,0:T(8,128)(2,1)S(1)}, bf16[1072,128]{1,0:T(8,128)(2,1)S(1)}, u32[]{:S(2)}, u32[]{:S(2)}) collective-permute-start(bf16[1072,128]{1,0:T(8,128)(2,1)S(1)} %collective-permute-done.1.refs_0_), channel_id=1, source_target_pairs={{0,2},{1,3},{2,0},{3,1},{4,6},{5,7},{6,4},{7,5},{8,10},{9,11},{10,... | collective-permute-start | bytes 823304 | tf_op jit(solution)/shard_map/ppermute | solution.py:111
  20.2 0.1 slice_reduce_fusion.6
  20.4 2.6 %collective-permute-start.10 = (bf16[1072,128]{1,0:T(8,128)(2,1)S(1)}, bf16[1072,128]{1,0:T(8,128)(2,1)S(1)}, u32[]{:S(2)}, u32[]{:S(2)}) collective-permute-start(bf16[1072,128]{1,0:T(8,128)(2,1)S(1)} %collective-permute-done.1.refs_0_), channel_id=1, source_target_pairs={{0,1},{1,0},{2,3},{3,2},{4,5},{5,4},{6,7},{7,6},{8,9},{9,8},{10,11... | collective-permute-start | bytes 823304 | tf_op jit(solution)/shard_map/ppermute | solution.py:111
  23.1 0.1 slice_reduce_fusion.7
  23.2 3.8 %collective-permute-done.9.refs_1_ = bf16[1072,128]{1,0:T(8,128)(2,1)S(1)} collective-permute-done((bf16[1072,128]{1,0:T(8,128)(2,1)S(1)}, bf16[1072,128]{1,0:T(8,128)(2,1)S(1)}, u32[]{:S(2)}, u32[]{:S(2)}) %collective-permute-start.9) | collective-permute-done | bytes 274464 | tf_op jit(solution)/shard_map/ppermute | solution.py:111
  27.0 0.1 slice_reduce_fusion.2
  27.1 0.6 %collective-permute-start.8 = (bf16[1072,128]{1,0:T(8,128)(2,1)S(1)}, bf16[1072,128]{1,0:T(8,128)(2,1)S(1)}, u32[]{:S(2)}, u32[]{:S(2)}) collective-permute-start(bf16[1072,128]{1,0:T(8,128)(2,1)S(1)} %collective-permute-done.4.refs_1_), channel_id=1, source_target_pairs={{0,1},{1,0},{2,3},{3,2},{4,5},{5,4},{6,7},{7,6},{8,9},{9,8},{10,11... | collective-permute-start | bytes 823304 | tf_op jit(solution)/shard_map/ppermute | solution.py:111
  27.8 0.7 %collective-permute-done.11.refs_3_ = bf16[1072,128]{1,0:T(8,128)(2,1)S(1)} collective-permute-done((bf16[1072,128]{1,0:T(8,128)(2,1)S(1)}, bf16[1072,128]{1,0:T(8,128)(2,1)S(1)}, u32[]{:S(2)}, u32[]{:S(2)}) %collective-permute-start.11) | collective-permute-done | bytes 274464 | tf_op jit(solution)/shard_map/ppermute | solution.py:111
  28.6 0.1 slice_reduce_fusion
  28.7 0.9 %shard_map.59.refs_5_ = bf16[2,8,128,128]{3,2,1,0:T(8,128)(2,1)S(1)} custom-call(s32[4,48]{1,0:T(4,128)S(1)} %maximum_convert_fusion.1.index, bf16[1072,128]{1,0:T(8,128)(2,1)S(1)} %collective-permute-done.1.refs_0_, bf16[1072,128]{1,0:T(8,128)(2,1)S(1)} %collective-permute-done.9.refs_1_, bf16[1072,128]{1,0:T(8,128)(2,1)S(1)} %collective-permute-done.10.refs_2_, ...), custom_call_target="tpu_custom_call" | custom-call | tf_op jit(solution)/shard_map/pallas_call | solution.py:168
  29.6 1.6 %shard_map.60.refs_6_ = f32[2,128,768]{2,1,0:T(8,128)S(1)} custom-call(s32[3]{0:T(128)S(1)} %get-tuple-element.12.place, s32[1,48]{1,0:T(1,128)S(1)} %bitcast_convert_fusion.refs_2_.refs_0_, s32[2,8]{1,0:T(2,128)} %refs_1_.5, s32[2,8]{1,0:T(2,128)S(1)} %collective-permute-done.3.refs_2_, bf16[2,8,128,128]{3,2,1,0:T(8,128)(2,1)S(1)} %copy-done, ...), custom_call_target="tpu_custom_call" | custom-call | flops 201326592 | bytes 2097152 | tf_op jit(solution)/shard_map/pallas_call | solution.py:189
  31.2 4.8 %collective-permute-done.5.refs_3_ = bf16[2,8,128,128]{3,2,1,0:T(8,128)(2,1)S(1)} collective-permute-done((bf16[2,8,128,128]{3,2,1,0:T(8,128)(2,1)S(1)}, bf16[2,8,128,128]{3,2,1,0:T(8,128)(2,1)S(1)}, u32[]{:S(2)}, u32[]{:S(2)}) %collective-permute-start.5) | collective-permute-done | bytes 524320 | tf_op jit(solution)/shard_map/ppermute | solution.py:119
  35.9 1.8 %collective-permute-done.6.refs_4_ = bf16[2,8,128,128]{3,2,1,0:T(8,128)(2,1)S(1)} collective-permute-done((bf16[2,8,128,128]{3,2,1,0:T(8,128)(2,1)S(1)}, bf16[2,8,128,128]{3,2,1,0:T(8,128)(2,1)S(1)}, u32[]{:S(2)}, u32[]{:S(2)}) %collective-permute-start.6) | collective-permute-done | bytes 524320 | tf_op jit(solution)/shard_map/ppermute | solution.py:119
  37.8 1.5 %shard_map.61 = bf16[2,6,128,128]{3,2,1,0:T(8,128)(2,1)S(1)} custom-call(s32[3]{0:T(128)S(1)} %get-tuple-element.11.place, s32[1,48]{1,0:T(1,128)S(1)} %bitcast_convert_fusion.refs_2_.refs_0_, s32[2,8]{1,0:T(2,128)S(1)} %collective-permute-done.refs_1_, s32[1,48]{1,0:T(1,128)S(1)} %bitcast_convert_fusion.refs_2_.refs_0_, ...), custom_call_target="tpu_custom_call" | custom-call | flops 201326592 | bytes 2097152 | tf_op jit(solution)/shard_map/pallas_call | solution.py:189
  39.3 0.1 slice_reduce_fusion.5
  39.5 0.1 slice_reduce_fusion.4
  39.6 0.1 slice_reduce_fusion.3
  39.7 0.9 %shard_map.56.refs_5_ = bf16[2,8,128,128]{3,2,1,0:T(8,128)(2,1)S(1)} custom-call(s32[4,48]{1,0:T(4,128)S(1)} %maximum_convert_fusion.index, bf16[1072,128]{1,0:T(8,128)(2,1)S(1)} %shard_map.55.refs_0_, bf16[1072,128]{1,0:T(8,128)(2,1)S(1)} %collective-permute-done.4.refs_1_, bf16[1072,128]{1,0:T(8,128)(2,1)S(1)} %collective-permute-done.7.refs_2_, ...), custom_call_target="tpu_custom_call" | custom-call | tf_op jit(solution)/shard_map/pallas_call | solution.py:168
  40.6 1.6 %shard_map.57.refs_6_ = f32[2,128,768]{2,1,0:T(8,128)S(1)} custom-call(s32[3]{0:T(128)S(1)} %get-tuple-element.12.place, s32[2,6]{1,0:T(2,128)S(1)} %copy-done.3, s32[2,8]{1,0:T(2,128)} %refs_1_.5, s32[2,8]{1,0:T(2,128)S(1)} %collective-permute-done.3.refs_2_, bf16[2,8,128,128]{3,2,1,0:T(8,128)(2,1)S(1)} %copy-done, ...), custom_call_target="tpu_custom_call" | custom-call | flops 201326592 | bytes 2097152 | tf_op jit(solution)/shard_map/pallas_call | solution.py:189
  42.2 1.5 %shard_map.58 = bf16[2,6,128,128]{3,2,1,0:T(8,128)(2,1)S(1)} custom-call(s32[3]{0:T(128)S(1)} %get-tuple-element.11.place, s32[2,6]{1,0:T(2,128)S(1)} %copy-done.3, s32[2,8]{1,0:T(2,128)S(1)} %collective-permute-done.refs_1_, s32[1,48]{1,0:T(1,128)S(1)} %bitcast_convert_fusion.refs_2_.refs_0_, bf16[2,8,128,128]{3,2,1,0:T(8,128)(2,1)S(1)} %collective-permute-done.5.refs_3_, ...), custom_call_target="tpu_custom_call" | custom-call | flops 201326592 | bytes 2097152 | tf_op jit(solution)/shard_map/pallas_call | solution.py:189
  43.7 0.9 %collective-permute-done.12 = bf16[2,6,128,128]{3,2,1,0:T(8,128)(2,1)S(1)} collective-permute-done((bf16[2,6,128,128]{3,2,1,0:T(8,128)(2,1)S(1)}, bf16[2,6,128,128]{3,2,1,0:T(8,128)(2,1)S(1)}, u32[]{:S(2)}, u32[]{:S(2)}) %collective-permute-start.12) | collective-permute-done | bytes 393248 | tf_op jit(solution)/shard_map/ppermute | solution.py:119
  44.6 0.8 %broadcast_select_fusion = bf16[2,6,128,128]{3,2,1,0:T(8,128)(2,1)} fusion(bf16[2,6,128,128]{3,2,1,0:T(8,128)(2,1)S(1)} %shard_map.58, bf16[2,6,128,128]{3,2,1,0:T(8,128)(2,1)S(1)} %collective-permute-done.12, pred[]{:T(512)S(6)} %eq.5), kind=kLoop, calls=%fused_computation | loop fusion | flops 196608 | bytes 1179649 | tf_op jit(solution)/shard_map/jit(_where)/select_n | solution.py:221
  (24 shorter events, 0.5 us)
Async XLA Ops:
  0.0 20.4 %copy-start = (bf16[2,8,128,128]{3,2,1,0:T(8,128)(2,1)S(1)}, bf16[2,8,128,128]{3,2,1,0:T(8,128)(2,1)}, u32[]{:S(2)}) copy-start(bf16[2,8,128,128]{3,2,1,0:T(8,128)(2,1)} %refs_3_.3) | copy-start | bytes 1572868
  0.0 18.5 %collective-permute-start.2 = (bf16[2,8,128,128]{3,2,1,0:T(8,128)(2,1)}, bf16[2,8,128,128]{3,2,1,0:T(8,128)(2,1)S(1)}, u32[]{:S(2)}, u32[]{:S(2)}) collective-permute-start(bf16[2,8,128,128]{3,2,1,0:T(8,128)(2,1)} %refs_3_.3), channel_id=1, source_target_pairs={{0,12},{1,3},{2,14},{3,1},{4,6},{5,9},{6,4},{7,11},{8,10},{9,5},{1... | collective-permute-start | bytes 1572872 | tf_op jit(solution)/shard_map/ppermute | solution.py:119
  5.1 0.9 %copy-start.1 = (bf16[2,4,128,128]{3,2,1,0:T(8,128)(2,1)S(1)}, bf16[2,4,128,128]{3,2,1,0:T(8,128)(2,1)}, u32[]{:S(2)}) copy-start(bf16[2,4,128,128]{3,2,1,0:T(8,128)(2,1)} %param.5) | copy-start | bytes 786436
  6.0 0.7 %copy-start.2 = (s32[2,6]{1,0:T(2,128)S(1)}, s32[2,6]{1,0:T(2,128)}, u32[]{:S(2)}) copy-start(s32[2,6]{1,0:T(2,128)} %refs_0_.5) | copy-start | bytes 148
  6.7 0.7 %copy-start.4 = (s32[2,4]{1,0:T(2,128)S(1)}, s32[2,4]{1,0:T(2,128)}, u32[]{:S(2)}) copy-start(s32[2,4]{1,0:T(2,128)} %refs_0_.3) | copy-start | bytes 100
  8.1 10.4 %collective-permute-start.1 = (bf16[1072,128]{1,0:T(8,128)(2,1)S(1)}, bf16[1072,128]{1,0:T(8,128)(2,1)S(1)}, u32[]{:S(2)}, u32[]{:S(2)}) collective-permute-start(bf16[1072,128]{1,0:T(8,128)(2,1)S(1)} %shard_map.55.refs_0_), channel_id=1, source_target_pairs={{0,4},{4,0},{8,12},{12,8},{1,5},{5,1},{9,13},{13,9},{2,6},{6,2},{1... | collective-permute-start | bytes 823304 | tf_op jit(solution)/shard_map/ppermute | solution.py:111
  8.2 12.1 %collective-permute-start.4 = (bf16[1072,128]{1,0:T(8,128)(2,1)S(1)}, bf16[1072,128]{1,0:T(8,128)(2,1)S(1)}, u32[]{:S(2)}, u32[]{:S(2)}) collective-permute-start(bf16[1072,128]{1,0:T(8,128)(2,1)S(1)} %shard_map.55.refs_0_), channel_id=1, source_target_pairs={{0,2},{1,3},{2,0},{3,1},{4,6},{5,7},{6,4},{7,5},{8,10},{9,11},{10,... | collective-permute-start | bytes 823304 | tf_op jit(solution)/shard_map/ppermute | solution.py:111
  9.8 8.2 %collective-permute-start = (s32[2,8]{1,0:T(2,128)}, s32[2,8]{1,0:T(2,128)S(1)}, u32[]{:S(2)}, u32[]{:S(2)}) collective-permute-start(s32[2,8]{1,0:T(2,128)} %refs_1_.5), channel_id=1, source_target_pairs={{0,8},{4,12},{8,0},{12,4},{1,9},{5,13},{9,1},{13,5},{2,10},{6,14},... | collective-permute-start | bytes 200 | tf_op jit(solution)/shard_map/ppermute | solution.py:111
  10.5 8.0 %collective-permute-start.3 = (s32[2,8]{1,0:T(2,128)}, s32[2,8]{1,0:T(2,128)S(1)}, u32[]{:S(2)}, u32[]{:S(2)}) collective-permute-start(s32[2,8]{1,0:T(2,128)} %refs_1_.5), channel_id=1, source_target_pairs={{0,12},{4,8},{8,4},{12,0},{1,13},{5,9},{9,5},{13,1},{2,14},{6,10},... | collective-permute-start | bytes 200 | tf_op jit(solution)/shard_map/ppermute | solution.py:111
  17.9 21.5 %collective-permute-start.7 = (bf16[1072,128]{1,0:T(8,128)(2,1)S(1)}, bf16[1072,128]{1,0:T(8,128)(2,1)S(1)}, u32[]{:S(2)}, u32[]{:S(2)}) collective-permute-start(bf16[1072,128]{1,0:T(8,128)(2,1)S(1)} %shard_map.55.refs_0_), channel_id=1, source_target_pairs={{0,1},{1,0},{2,3},{3,2},{4,5},{5,4},{6,7},{7,6},{8,9},{9,8},{10,11... | collective-permute-start | bytes 823304 | tf_op jit(solution)/shard_map/ppermute | solution.py:111
  18.5 8.5 %collective-permute-start.9 = (bf16[1072,128]{1,0:T(8,128)(2,1)S(1)}, bf16[1072,128]{1,0:T(8,128)(2,1)S(1)}, u32[]{:S(2)}, u32[]{:S(2)}) collective-permute-start(bf16[1072,128]{1,0:T(8,128)(2,1)S(1)} %collective-permute-done.1.refs_0_), channel_id=1, source_target_pairs={{0,2},{1,3},{2,0},{3,1},{4,6},{5,7},{6,4},{7,5},{8,10},{9,11},{10,... | collective-permute-start | bytes 823304 | tf_op jit(solution)/shard_map/ppermute | solution.py:111
  20.4 15.6 %collective-permute-start.5 = (bf16[2,8,128,128]{3,2,1,0:T(8,128)(2,1)S(1)}, bf16[2,8,128,128]{3,2,1,0:T(8,128)(2,1)S(1)}, u32[]{:S(2)}, u32[]{:S(2)}) collective-permute-start(bf16[2,8,128,128]{3,2,1,0:T(8,128)(2,1)S(1)} %copy-done), channel_id=1, source_target_pairs={{0,1},{1,9},{2,3},{3,11},{4,12},{5,4},{6,14},{7,6},{8,0},{9,8},{10... | collective-permute-start | bytes 1572872 | tf_op jit(solution)/shard_map/ppermute | solution.py:119
  20.4 6.7 %collective-permute-start.10 = (bf16[1072,128]{1,0:T(8,128)(2,1)S(1)}, bf16[1072,128]{1,0:T(8,128)(2,1)S(1)}, u32[]{:S(2)}, u32[]{:S(2)}) collective-permute-start(bf16[1072,128]{1,0:T(8,128)(2,1)S(1)} %collective-permute-done.1.refs_0_), channel_id=1, source_target_pairs={{0,1},{1,0},{2,3},{3,2},{4,5},{5,4},{6,7},{7,6},{8,9},{9,8},{10,11... | collective-permute-start | bytes 823304 | tf_op jit(solution)/shard_map/ppermute | solution.py:111
  23.1 14.7 %collective-permute-start.6 = (bf16[2,8,128,128]{3,2,1,0:T(8,128)(2,1)S(1)}, bf16[2,8,128,128]{3,2,1,0:T(8,128)(2,1)S(1)}, u32[]{:S(2)}, u32[]{:S(2)}) collective-permute-start(bf16[2,8,128,128]{3,2,1,0:T(8,128)(2,1)S(1)} %copy-done), channel_id=1, source_target_pairs={{0,1},{1,5},{2,3},{3,7},{4,0},{5,4},{6,2},{7,6},{8,12},{9,8},{10,1... | collective-permute-start | bytes 1572872 | tf_op jit(solution)/shard_map/ppermute | solution.py:119
  27.0 1.6 %collective-permute-start.11 = (bf16[1072,128]{1,0:T(8,128)(2,1)S(1)}, bf16[1072,128]{1,0:T(8,128)(2,1)S(1)}, u32[]{:S(2)}, u32[]{:S(2)}) collective-permute-start(bf16[1072,128]{1,0:T(8,128)(2,1)S(1)} %collective-permute-done.9.refs_1_), channel_id=1, source_target_pairs={{0,1},{1,0},{2,3},{3,2},{4,5},{5,4},{6,7},{7,6},{8,9},{9,8},{10,11... | collective-permute-start | bytes 823304 | tf_op jit(solution)/shard_map/ppermute | solution.py:111
  27.1 12.4 %collective-permute-start.8 = (bf16[1072,128]{1,0:T(8,128)(2,1)S(1)}, bf16[1072,128]{1,0:T(8,128)(2,1)S(1)}, u32[]{:S(2)}, u32[]{:S(2)}) collective-permute-start(bf16[1072,128]{1,0:T(8,128)(2,1)S(1)} %collective-permute-done.4.refs_1_), channel_id=1, source_target_pairs={{0,1},{1,0},{2,3},{3,2},{4,5},{5,4},{6,7},{7,6},{8,9},{9,8},{10,11... | collective-permute-start | bytes 823304 | tf_op jit(solution)/shard_map/ppermute | solution.py:111
  39.3 5.4 %collective-permute-start.12 = (bf16[2,6,128,128]{3,2,1,0:T(8,128)(2,1)S(1)}, bf16[2,6,128,128]{3,2,1,0:T(8,128)(2,1)S(1)}, u32[]{:S(2)}, u32[]{:S(2)}) collective-permute-start(bf16[2,6,128,128]{3,2,1,0:T(8,128)(2,1)S(1)} %shard_map.61), channel_id=1, source_target_pairs={{0,4},{1,0},{2,6},{3,2},{4,5},{5,1},{6,7},{7,3},{8,9},{9,13},{10,1... | collective-permute-start | bytes 1179656 | tf_op jit(solution)/shard_map/ppermute | solution.py:119
  39.7 0.9 %copy-start.3 = (s32[2,6]{1,0:T(2,128)S(1)}, s32[2,6]{1,0:T(2,128)}, u32[]{:S(2)}) copy-start(s32[2,6]{1,0:T(2,128)} %refs_0_.5) | copy-start | bytes 148

commit v9 on v8

v9 whole, which is shorter than its diff:
```python
import functools

import jax
import jax.numpy as jnp
from jax import lax
from jax.experimental import pallas as pl
from jax.experimental.pallas import tpu as pltpu
from jax.sharding import PartitionSpec as P

COLS_DEV = 16

SMEM = pl.BlockSpec(memory_space=pltpu.SMEM)
VMEM = pl.BlockSpec(memory_space=pltpu.VMEM)
PARAMS = pltpu.CompilerParams(vmem_limit_bytes=32 * 2**20)
FREE = pl.CostEstimate(flops=1, bytes_accessed=1, transcendentals=0)


def pack_kernel(*refs):
    indices, tiles, out = refs[:-2], refs[-2], refs[-1]
    size = tiles.shape[0]
    out[:size, :] = tiles[...]
    row = lax.broadcasted_iota(jnp.int32, (out.shape[0] - size, out.shape[1]), 0)
    found = jnp.zeros(row.shape, jnp.float32)
    at = 0
    for index in indices:
        for i in range(index.shape[0]):
            for k in range(index.shape[1]):
                found = jnp.where(row == at, index[i, k].astype(jnp.float32), found)
                at += 1
    out[size:, :] = found.astype(out.dtype)


def left_kernel(slots, index, *refs):
    parts, dense = refs[:-1], refs[-1]
    dense[...] = jnp.zeros_like(dense)
    rows, _, block, _ = dense.shape
    for p, part in enumerate(parts):
        for i in range(rows):
            for s in range(slots):
                inner = index[p, i * slots + s]
                start = (i * slots + s) * block

                @pl.when(inner >= 0)
                def _():
                    dense[i, inner] = part[start : start + block, :]


def step_kernel(starts, span, last, place, *refs):
    parts = len(starts) - 1
    wanted, refs = refs[0], refs[1:]
    cols, refs = refs[:parts], refs[parts:]
    tiles, refs = refs[:parts], refs[parts:]
    dense, refs = refs[0], refs[1:]
    before, out, right, slot = refs if len(refs) == 4 else (None,) + refs
    @pl.when(place[0] >= 0)
    def _():
        first = place[0]
        inner_rows = slot.shape[0]
        block = dense.shape[-1]
        slots = right.shape[2] // block
        inner_slots = tiles[0].shape[0] // block // inner_rows

        def read(ref, start, i, k, width):
            return ref[i, k] if start is None else ref[0, start + i * width + k]

        sums = {i: None if before is None else before[i] for i in span}
        for p in range(parts):
            for m in range(inner_rows):
                for c in range(COLS_DEV):
                    slot[m, c] = -1
                for l in range(inner_slots):
                    slot[m, read(cols[p], starts[1 + p], m, l, inner_slots) - first] = l
            for i in span:
                for j in range(slots):
                    column = read(wanted, starts[0], i, j, slots) - first
                    for m in range(inner_rows):
                        l = slot[m, column]
                        start = pl.multiple_of((m * inner_slots + jnp.maximum(l, 0)) * block, block)
                        tile = tiles[p][pl.ds(start, block), :]
                        right[i, m * block : (m + 1) * block, j * block : (j + 1) * block] = jnp.where(
                            l >= 0, tile, jnp.zeros_like(tile)
                        )
            for i in span:
                left = jnp.concatenate(
                    [dense[i, place[1 + p] * inner_rows + m] for m in range(inner_rows)], axis=1
                )
                product = jnp.dot(left, right[i], preferred_element_type=jnp.float32)
                sums[i] = product if sums[i] is None else sums[i] + product
        for at, i in enumerate(span):
            if last:
                for j in range(slots):
                    out[at, j] = sums[i][:, j * block : (j + 1) * block].astype(out.dtype)
            else:
                out[i] = sums[i]


def parity(k):
    return bin(k).count("1") % 2


def body(row_count, col_count, a_tiles, a_cols, b_tiles, b_cols, c_cols):
    rows, slots = c_cols.shape
    inner_rows = b_tiles.shape[0]
    block = a_tiles.shape[-1]
    dtype = b_tiles.dtype
    r, q = lax.axis_index("row"), lax.axis_index("col")
    first = q * COLS_DEV
    bits = sum((r >> k) & 1 for k in range(row_count.bit_length()))
    working = (bits + q) % 2 == 0

    def works(k, c):
        return parity(k) == c % 2

    def swap(x, axis, n, d):
        return lax.ppermute(x, axis, [(k, k ^ d) for k in range(n)])

    def permute(x, target):
        pairs = []
        for k in range(row_count):
            for c in range(col_count):
                to, at = target(k, c)
                pairs.append((k * col_count + c, to * col_count + at))
        return lax.ppermute(x, ("row", "col"), pairs)

    def deliver(x, d):
        def target(k, c):
            if parity(d):
                return (k, c ^ 1) if works(k, c) else (k ^ d, c)
            return (k ^ d, c) if works(k, c) else (k, c ^ (col_count // 2))

        return permute(x, target)

    def give_back(x):
        return permute(x, lambda k, c: (k ^ 1, c) if works(k, c) else (k, c ^ 1))

    def pack(tiles, *indices):
        size = tiles.size // block
        count = sum(x.size for x in indices)
        return pl.pallas_call(
            pack_kernel,
            out_shape=jax.ShapeDtypeStruct((size + -(-count // 16) * 16, block), dtype),
            in_specs=[SMEM] * len(indices) + [VMEM],
            out_specs=VMEM,
            compiler_params=PARAMS,
            cost_estimate=FREE,
        )(*indices, tiles.reshape(size, block))

    def index_of(packs, tiles):
        return jnp.stack([x[tiles.size // block :, 0] for x in packs]).astype(jnp.int32)

    def across(parts, d):
        while d:
            parts = parts + [swap(part, "col", col_count, d) for part in parts]
            d //= 2
        return parts

    far, end = col_count // 2, row_count - 1
    flat = b_tiles.reshape(-1, block)
    own, packed = pack(a_tiles, a_cols, c_cols), pack(b_tiles, b_cols)
    shards = {0: flat, end: deliver(flat, end)}
    cols = {0: (None, b_cols), end: (None, swap(b_cols, "row", row_count, end))}
    own_packs = [own, swap(own, "col", col_count, far)]
    other = swap(own, "row", row_count, 1)
    ready = lax.optimization_barrier((packed, own_packs[1]))[0]
    for d in range(end - 1, 1, -1):
        shards[d] = deliver(ready, d)
    ready, other, _, _ = lax.optimization_barrier((packed, other, shards[end], cols[end][1]))
    shards[1] = deliver(ready, 1)
    own_packs, other_packs = across(own_packs, far // 2), across([other], far)
    def dense_of(packs):
        return pl.pallas_call(
            functools.partial(left_kernel, a_cols.shape[1]),
            out_shape=jax.ShapeDtypeStruct((rows, inner_rows * row_count, block, block), dtype),
            in_specs=[SMEM] + [VMEM] * len(packs),
            out_specs=VMEM,
            compiler_params=PARAMS,
            cost_estimate=FREE,
        )(index_of(packs, a_tiles), *packs)

    def step(dists, wanted, dense, before, span, last):
        place = jnp.stack([jnp.where(working, first, -1)] + [r ^ d for d in dists]).astype(jnp.int32)
        if last:
            out = jax.ShapeDtypeStruct((len(span), slots, block, block), dtype)
        else:
            out = jax.ShapeDtypeStruct((rows, block, slots * block), jnp.float32)
        held = [dense] if before is None else [dense, before]
        return pl.pallas_call(
            functools.partial(step_kernel, [wanted[0]] + [cols[d][0] for d in dists], span, last),
            out_shape=out,
            in_specs=[SMEM] * (2 + len(dists)) + [VMEM] * (len(dists) + len(held)),
            out_specs=VMEM,
            scratch_shapes=[
                pltpu.VMEM((rows, inner_rows * block, slots * block), dtype),
                pltpu.SMEM((inner_rows, COLS_DEV), jnp.int32),
            ],
            compiler_params=PARAMS,
            cost_estimate=FREE,
        )(place, wanted[1], *[cols[d][1] for d in dists], *[shards[d] for d in dists], *held)

    order, every = list(range(1, end)) + [0, end], list(range(rows))
    early, late = order[:-4], order[-4:]
    for d in range(1, end):
        cols[d] = (0, index_of([shards[d]], b_tiles))

    def products(wanted, packs, spans):
        dense, total = dense_of(packs), None
        for at in range(0, len(early), 4):
            total = step(early[at : at + 4], wanted, dense, total, every, False)
        return [step(late, wanted, dense, total, span, True) for span in spans]

    given = products((a_cols.size, index_of([other], a_tiles)), other_packs, [[i] for i in every])
    given = [give_back(x) for x in given]
    (kept,) = products((None, c_cols), own_packs, [every])
    return jnp.where(working, kept, jnp.concatenate(given, axis=0))


def solution(mesh):
    return jax.shard_map(
        functools.partial(body, mesh.shape["row"], mesh.shape["col"]),
        mesh=mesh,
        in_specs=(
            P(("groups", "row"), "col", None, None),
            P(("groups", "row"), "col"),
            P(("groups", "row"), "col", None, None),
            P(("groups", "row"), "col"),
            P(("groups", "row"), "col"),
        ),
        out_specs=P(("groups", "row"), "col", None, None),
        check_vma=False,
    )
```

time: 45.6 us -> 46.5 us (1.020)
  waiting for transfers between devices: 16.6 us -> 23.2 us
  starting transfers between devices: 16 us -> 10.4 us
  Pallas kernels: 8.61 us -> 8.11 us
    ppermute x9 -> x8, starting transfers between devices: 10.8 us -> 4.72 us  [swap(): return lax.ppermute(x, axis, [(k, k ^ d) for k in range(n)])]
    ppermute x9 -> x8, waiting for transfers between devices: 9 us -> 12.8 us  [swap(): return lax.ppermute(x, axis, [(k, k ^ d) for k in range(n)])]
    ppermute x4 -> x5, waiting for transfers between devices: 7.58 us -> 10.5 us  [permute(): return lax.ppermute(x, ('row', 'col'), pairs)]
    pallas_call x5, Pallas kernels: 6.82 us -> 6.32 us  [the longest x3 5.15 us: step(): pl.pallas_call(functools.partial(step_kernel, [wanted[0]] + [cols[d][0] f...]
    ppermute x4 -> x5, starting transfers between devices: 5.19 us -> 5.68 us  [permute(): return lax.ppermute(x, ('row', 'col'), pairs)]
    unnamed x10 -> x12, local copies, waits for them, and re-layouts: 2.32 us -> 2.32 us
  transfers between devices with their start and end apart: 13 -> 13, of which waited for: 8 -> 6; matrix products, arithmetic and copies ran while one was open for 2% -> 3% of each run, Pallas kernels for 19% -> 18%
where the time goes in v9:
time: 46.5 us; the launch traced here: 46.3 us
  waiting for transfers between devices  23.2 us (50%)
  starting transfers between devices  10.4 us (22%)
  Pallas kernels  8.11 us (17%)
  local copies, waits for them, and re-layouts  3.29 us (7%)
  other arithmetic  1.06 us (2%)
    ppermute x8, waiting for transfers between devices, swap(): return lax.ppermute(x, axis, [(k, k ^ d) for k in range(n)])  12.8 us
    ppermute x5, waiting for transfers between devices, permute(): return lax.ppermute(x, ('row', 'col'), pairs)  10.5 us
    ppermute x5, starting transfers between devices, permute(): return lax.ppermute(x, ('row', 'col'), pairs)  5.68 us
    pallas_call x3, Pallas kernels, step(): pl.pallas_call(functools.partial(step_kernel, [wanted[0]] + [cols[d][0] f...  5.15 us
    ppermute x8, starting transfers between devices, swap(): return lax.ppermute(x, axis, [(k, k ^ d) for k in range(n)])  4.72 us
    unnamed x12, local copies, waits for them, and re-layouts  2.32 us
    pallas_call x2, Pallas kernels, dense_of(): pl.pallas_call(functools.partial(left_kernel, a_cols.shape[1]), out_shape...  1.79 us
    pallas_call x2, Pallas kernels, pack(): pl.pallas_call(pack_kernel, out_shape=jax.ShapeDtypeStruct((size + -(-cou...  1.17 us
  transfers between devices with their start and end apart: 13, of which 6 were waited for; matrix products, arithmetic and copies ran while one was open for 3% of the time, Pallas kernels for 18%

profile of v9, /device:TPU:0, one launch (start us, length us, event | category | flops | bytes accessed | tf_op | source)
XLA Modules:
  0.0 46.3 jit_solution(9639866525242166384)
XLA Ops:
  0.0 5.0 %collective-permute-start.1 = (bf16[2048,128]{1,0:T(8,128)(2,1)}, bf16[2048,128]{1,0:T(8,128)(2,1)S(1)}, u32[]{:S(2)}, u32[]{:S(2)}) collective-permute-start(bf16[2048,128]{1,0:T(8,128)(2,1)} %bitcast.18), channel_id=1, source_target_pairs={{0,12},{1,3},{2,14},{3,1},{4,6},{5,9},{6,4},{7,11},{8,10},{9,5},{1... | collective-permute-start | bytes 1572872 | tf_op jit(solution)/shard_map/ppermute | solution.py:123
  5.1 0.9 %copy-done.1 = bf16[2,4,128,128]{3,2,1,0:T(8,128)(2,1)S(1)} copy-done((bf16[2,4,128,128]{3,2,1,0:T(8,128)(2,1)S(1)}, bf16[2,4,128,128]{3,2,1,0:T(8,128)(2,1)}, u32[]{:S(2)}) %copy-start.1) | copy-done | bytes 262168
  6.0 0.7 %copy-done.3 = s32[2,6]{1,0:T(2,128)S(1)} copy-done((s32[2,6]{1,0:T(2,128)S(1)}, s32[2,6]{1,0:T(2,128)}, u32[]{:S(2)}) %copy-start.3) | copy-done | bytes 72
  6.7 0.7 %copy-done.5 = s32[2,4]{1,0:T(2,128)S(1)} copy-done((s32[2,4]{1,0:T(2,128)S(1)}, s32[2,4]{1,0:T(2,128)}, u32[]{:S(2)}) %copy-start.5) | copy-done | bytes 56
  7.4 0.6 %shard_map.56.refs_0_ = bf16[1056,128]{1,0:T(8,128)(2,1)S(1)} custom-call(s32[2,4]{1,0:T(2,128)S(1)} %copy-done.5, s32[2,6]{1,0:T(2,128)S(1)} %copy-done.3, bf16[1024,128]{1,0:T(8,128)(2,1)S(1)} %bitcast.23), custom_call_target="tpu_custom_call" | custom-call | flops 1 | bytes 1 | tf_op jit(solution)/shard_map/pallas_call | solution.py:139
  8.0 1.6 %collective-permute-start.4 = (bf16[1056,128]{1,0:T(8,128)(2,1)S(1)}, bf16[1056,128]{1,0:T(8,128)(2,1)S(1)}, u32[]{:S(2)}, u32[]{:S(2)}) collective-permute-start(bf16[1056,128]{1,0:T(8,128)(2,1)S(1)} %shard_map.56.refs_0_), channel_id=1, source_target_pairs={{0,2},{1,3},{2,0},{3,1},{4,6},{5,7},{6,4},{7,5},{8,10},{9,11},{10,... | collective-permute-start | bytes 811016 | tf_op jit(solution)/shard_map/ppermute | solution.py:115
  9.5 1.0 %collective-permute-start.2 = (s32[2,8]{1,0:T(2,128)S(1)}, s32[2,8]{1,0:T(2,128)S(1)}, u32[]{:S(2)}, u32[]{:S(2)}) collective-permute-start(s32[2,8]{1,0:T(2,128)S(1)} %copy-done.2), channel_id=1, source_target_pairs={{0,12},{4,8},{8,4},{12,0},{1,13},{5,9},{9,5},{13,1},{2,14},{6,10},... | collective-permute-start | bytes 200 | tf_op jit(solution)/shard_map/ppermute | solution.py:115
  10.5 0.1 slice_reduce_fusion.6
  10.6 0.6 %shard_map.55 = bf16[2064,128]{1,0:T(8,128)(2,1)S(1)} custom-call(s32[2,8]{1,0:T(2,128)S(1)} %copy-done.2, bf16[2048,128]{1,0:T(8,128)(2,1)S(1)} %bitcast.19), custom_call_target="tpu_custom_call" | custom-call | flops 1 | bytes 1 | tf_op jit(solution)/shard_map/pallas_call | solution.py:139
  11.3 4.0 %collective-permute-done.4.refs_1_ = bf16[1056,128]{1,0:T(8,128)(2,1)S(1)} collective-permute-done((bf16[1056,128]{1,0:T(8,128)(2,1)S(1)}, bf16[1056,128]{1,0:T(8,128)(2,1)S(1)}, u32[]{:S(2)}, u32[]{:S(2)}) %collective-permute-start.4) | collective-permute-done | bytes 270368 | tf_op jit(solution)/shard_map/ppermute | solution.py:115
  15.3 0.1 slice_reduce_fusion.5
  15.5 0.1 slice_reduce_fusion.4
  15.6 3.7 %collective-permute-done.2.refs_4_ = s32[2,8]{1,0:T(2,128)S(1)} collective-permute-done((s32[2,8]{1,0:T(2,128)S(1)}, s32[2,8]{1,0:T(2,128)S(1)}, u32[]{:S(2)}, u32[]{:S(2)}) %collective-permute-start.2) | collective-permute-done | bytes 96 | tf_op jit(solution)/shard_map/ppermute | solution.py:115
  19.4 2.0 %collective-permute-start.8 = (bf16[1056,128]{1,0:T(8,128)(2,1)S(1)}, bf16[1056,128]{1,0:T(8,128)(2,1)S(1)}, u32[]{:S(2)}, u32[]{:S(2)}) collective-permute-start(bf16[1056,128]{1,0:T(8,128)(2,1)S(1)} %collective-permute-done.refs_0_), channel_id=1, source_target_pairs={{0,2},{1,3},{2,0},{3,1},{4,6},{5,7},{6,4},{7,5},{8,10},{9,11},{10,... | collective-permute-start | bytes 811016 | tf_op jit(solution)/shard_map/ppermute | solution.py:115
  21.4 0.1 slice_reduce_fusion.7
  21.6 0.5 %collective-permute-start.3 = (bf16[2064,128]{1,0:T(8,128)(2,1)S(1)}, bf16[2064,128]{1,0:T(8,128)(2,1)S(1)}, u32[]{:S(2)}, u32[]{:S(2)}) collective-permute-start(bf16[2064,128]{1,0:T(8,128)(2,1)S(1)} %shard_map.55), channel_id=1, source_target_pairs={{0,1},{1,5},{2,3},{3,7},{4,0},{5,4},{6,2},{7,6},{8,12},{9,8},{10,1... | collective-permute-start | bytes 1585160 | tf_op jit(solution)/shard_map/ppermute | solution.py:123
  22.1 5.0 %collective-permute-done.8.refs_1_ = bf16[1056,128]{1,0:T(8,128)(2,1)S(1)} collective-permute-done((bf16[1056,128]{1,0:T(8,128)(2,1)S(1)}, bf16[1056,128]{1,0:T(8,128)(2,1)S(1)}, u32[]{:S(2)}, u32[]{:S(2)}) %collective-permute-start.8) | collective-permute-done | bytes 270368 | tf_op jit(solution)/shard_map/ppermute | solution.py:115
  27.1 0.1 slice_reduce_fusion.2
  27.2 0.1 slice_reduce_fusion.1
  27.4 4.1 %collective-permute-done.5.refs_6_ = bf16[2064,128]{1,0:T(8,128)(2,1)S(1)} collective-permute-done((bf16[2064,128]{1,0:T(8,128)(2,1)S(1)}, bf16[2064,128]{1,0:T(8,128)(2,1)S(1)}, u32[]{:S(2)}, u32[]{:S(2)}) %collective-permute-start.5) | collective-permute-done | bytes 528416 | tf_op jit(solution)/shard_map/ppermute | solution.py:123
  31.5 0.1 convert_reduce_fusion
  31.6 0.1 slice_reduce_fusion
  31.8 5.9 %collective-permute-done.3.refs_5_ = bf16[2064,128]{1,0:T(8,128)(2,1)S(1)} collective-permute-done((bf16[2064,128]{1,0:T(8,128)(2,1)S(1)}, bf16[2064,128]{1,0:T(8,128)(2,1)S(1)}, u32[]{:S(2)}, u32[]{:S(2)}) %collective-permute-start.3) | collective-permute-done | bytes 528416 | tf_op jit(solution)/shard_map/ppermute | solution.py:123
  37.6 0.1 convert_reduce_fusion.1
  37.7 0.9 %shard_map.59.refs_9_ = bf16[2,8,128,128]{3,2,1,0:T(8,128)(2,1)S(1)} custom-call(s32[4,32]{1,0:T(4,128)S(1)} %maximum_convert_fusion.1.index, bf16[1056,128]{1,0:T(8,128)(2,1)S(1)} %collective-permute-done.refs_0_, bf16[1056,128]{1,0:T(8,128)(2,1)S(1)} %collective-permute-done.8.refs_1_, bf16[1056,128]{1,0:T(8,128)(2,1)S(1)} %collective-permute-done.9.refs_2_, ...), custom_call_target="tpu_custom_call" | custom-call | flops 1 | bytes 1 | tf_op jit(solution)/shard_map/pallas_call | solution.py:171
  38.6 1.5 %shard_map.60 = bf16[1,6,128,128]{3,2,1,0:T(8,128)(2,1)S(1)} custom-call(s32[5]{0:T(128)S(1)} %stack.41.place, s32[1,32]{1,0:T(1,128)S(1)} %bitcast_convert_fusion.refs_0_, s32[1,16]{1,0:T(1,128)S(1)} %bitcast.27, s32[1,16]{1,0:T(1,128)S(1)} %bitcast.24, s32[2,8]{1,0:T(2,128)S(1)} %copy-done.2, s32[2,8]{1,0:T(2,128)S(1)} %collective-permute-done.2.refs_4_, ...), custom_call_target="tpu_custom_call" | custom-call | flops 1 | bytes 1 | tf_op jit(solution)/shard_map/pallas_call | solution.py:187
  40.2 1.5 %shard_map.61 = bf16[1,6,128,128]{3,2,1,0:T(8,128)(2,1)S(1)} custom-call(s32[5]{0:T(128)S(1)} %stack.41.place, s32[1,32]{1,0:T(1,128)S(1)} %bitcast_convert_fusion.refs_0_, s32[1,16]{1,0:T(1,128)S(1)} %bitcast.28, s32[1,16]{1,0:T(1,128)S(1)} %bitcast.25, s32[2,8]{1,0:T(2,128)S(1)} %copy-done.2, s32[2,8]{1,0:T(2,128)S(1)} %collective-permute-done.2.refs_4_, ...), custom_call_target="tpu_custom_call" | custom-call | flops 1 | bytes 1 | tf_op jit(solution)/shard_map/pallas_call | solution.py:187
  41.8 0.1 slice_reduce_fusion.3
  41.9 0.9 %shard_map.57.refs_9_ = bf16[2,8,128,128]{3,2,1,0:T(8,128)(2,1)S(1)} custom-call(s32[4,32]{1,0:T(4,128)S(1)} %maximum_convert_fusion.index, bf16[1056,128]{1,0:T(8,128)(2,1)S(1)} %shard_map.56.refs_0_, bf16[1056,128]{1,0:T(8,128)(2,1)S(1)} %collective-permute-done.4.refs_1_, bf16[1056,128]{1,0:T(8,128)(2,1)S(1)} %collective-permute-done.6.refs_2_, ...), custom_call_target="tpu_custom_call" | custom-call | flops 1 | bytes 1 | tf_op jit(solution)/shard_map/pallas_call | solution.py:171
  42.8 2.2 %shard_map.58 = bf16[2,6,128,128]{3,2,1,0:T(8,128)(2,1)S(1)} custom-call(s32[5]{0:T(128)S(1)} %stack.41.place, s32[2,6]{1,0:T(2,128)S(1)} %copy-done.4, s32[1,16]{1,0:T(1,128)S(1)} %bitcast.29, s32[1,16]{1,0:T(1,128)S(1)} %bitcast.26, s32[2,8]{1,0:T(2,128)S(1)} %copy-done.2, s32[2,8]{1,0:T(2,128)S(1)} %collective-permute-done.2.refs_4_, ...), custom_call_target="tpu_custom_call" | custom-call | flops 1 | bytes 1 | tf_op jit(solution)/shard_map/pallas_call | solution.py:187
  45.0 0.5 collective-permute-done.12
  45.5 0.8 %maximum_select_fusion = bf16[2,6,128,128]{3,2,1,0:T(8,128)(2,1)} fusion(bf16[2,6,128,128]{3,2,1,0:T(8,128)(2,1)S(1)} %shard_map.58, bf16[1,6,128,128]{3,2,1,0:T(8,128)(2,1)S(1)} %collective-permute-done.12, bf16[1,6,128,128]{3,2,1,0:T(8,128)(2,1)S(1)} %collective-permute-done.11, pred[]{:T(512)S(6)} %eq.5), kind=kLoop, calls=%fused_computation | loop fusion | flops 393216 | bytes 1179649 | tf_op jit(solution)/shard_map/jit(_where)/select_n | solution.py:214
  (28 shorter events, 0.4 us)
Async XLA Ops:
  0.0 10.6 %copy-start = (bf16[2,8,128,128]{3,2,1,0:T(8,128)(2,1)S(1)}, bf16[2,8,128,128]{3,2,1,0:T(8,128)(2,1)}, u32[]{:S(2)}) copy-start(bf16[2,8,128,128]{3,2,1,0:T(8,128)(2,1)} %param.7) | copy-start | bytes 1572868
  0.0 19.4 %collective-permute-start.1 = (bf16[2048,128]{1,0:T(8,128)(2,1)}, bf16[2048,128]{1,0:T(8,128)(2,1)S(1)}, u32[]{:S(2)}, u32[]{:S(2)}) collective-permute-start(bf16[2048,128]{1,0:T(8,128)(2,1)} %bitcast.18), channel_id=1, source_target_pairs={{0,12},{1,3},{2,14},{3,1},{4,6},{5,9},{6,4},{7,11},{8,10},{9,5},{1... | collective-permute-start | bytes 1572872 | tf_op jit(solution)/shard_map/ppermute | solution.py:123
  5.1 0.9 %copy-start.1 = (bf16[2,4,128,128]{3,2,1,0:T(8,128)(2,1)S(1)}, bf16[2,4,128,128]{3,2,1,0:T(8,128)(2,1)}, u32[]{:S(2)}) copy-start(bf16[2,4,128,128]{3,2,1,0:T(8,128)(2,1)} %param.5) | copy-start | bytes 786436
  6.0 0.7 %copy-start.3 = (s32[2,6]{1,0:T(2,128)S(1)}, s32[2,6]{1,0:T(2,128)}, u32[]{:S(2)}) copy-start(s32[2,6]{1,0:T(2,128)} %refs_0_.5) | copy-start | bytes 148
  6.7 0.7 %copy-start.5 = (s32[2,4]{1,0:T(2,128)S(1)}, s32[2,4]{1,0:T(2,128)}, u32[]{:S(2)}) copy-start(s32[2,4]{1,0:T(2,128)} %refs_0_.4) | copy-start | bytes 100
  7.4 2.2 %copy-start.2 = (s32[2,8]{1,0:T(2,128)S(1)}, s32[2,8]{1,0:T(2,128)}, u32[]{:S(2)}) copy-start(s32[2,8]{1,0:T(2,128)} %refs_3_.5) | copy-start | bytes 196
  8.0 7.4 %collective-permute-start.4 = (bf16[1056,128]{1,0:T(8,128)(2,1)S(1)}, bf16[1056,128]{1,0:T(8,128)(2,1)S(1)}, u32[]{:S(2)}, u32[]{:S(2)}) collective-permute-start(bf16[1056,128]{1,0:T(8,128)(2,1)S(1)} %shard_map.56.refs_0_), channel_id=1, source_target_pairs={{0,2},{1,3},{2,0},{3,1},{4,6},{5,7},{6,4},{7,5},{8,10},{9,11},{10,... | collective-permute-start | bytes 811016 | tf_op jit(solution)/shard_map/ppermute | solution.py:115
  9.5 5.9 %collective-permute-start.6 = (bf16[1056,128]{1,0:T(8,128)(2,1)S(1)}, bf16[1056,128]{1,0:T(8,128)(2,1)S(1)}, u32[]{:S(2)}, u32[]{:S(2)}) collective-permute-start(bf16[1056,128]{1,0:T(8,128)(2,1)S(1)} %shard_map.56.refs_0_), channel_id=1, source_target_pairs={{0,1},{1,0},{2,3},{3,2},{4,5},{5,4},{6,7},{7,6},{8,9},{9,8},{10,11... | collective-permute-start | bytes 811016 | tf_op jit(solution)/shard_map/ppermute | solution.py:115
  9.5 9.8 %collective-permute-start = (bf16[1056,128]{1,0:T(8,128)(2,1)S(1)}, bf16[1056,128]{1,0:T(8,128)(2,1)S(1)}, u32[]{:S(2)}, u32[]{:S(2)}) collective-permute-start(bf16[1056,128]{1,0:T(8,128)(2,1)S(1)} %shard_map.56.refs_0_), channel_id=1, source_target_pairs={{0,4},{4,0},{8,12},{12,8},{1,5},{5,1},{9,13},{13,9},{2,6},{6,2},{1... | collective-permute-start | bytes 811016 | tf_op jit(solution)/shard_map/ppermute | solution.py:115
  9.5 9.8 %collective-permute-start.2 = (s32[2,8]{1,0:T(2,128)S(1)}, s32[2,8]{1,0:T(2,128)S(1)}, u32[]{:S(2)}, u32[]{:S(2)}) collective-permute-start(s32[2,8]{1,0:T(2,128)S(1)} %copy-done.2), channel_id=1, source_target_pairs={{0,12},{4,8},{8,4},{12,0},{1,13},{5,9},{9,5},{13,1},{2,14},{6,10},... | collective-permute-start | bytes 200 | tf_op jit(solution)/shard_map/ppermute | solution.py:115
  15.3 16.2 %collective-permute-start.5 = (bf16[2064,128]{1,0:T(8,128)(2,1)S(1)}, bf16[2064,128]{1,0:T(8,128)(2,1)S(1)}, u32[]{:S(2)}, u32[]{:S(2)}) collective-permute-start(bf16[2064,128]{1,0:T(8,128)(2,1)S(1)} %shard_map.55), channel_id=1, source_target_pairs={{0,1},{1,9},{2,3},{3,11},{4,12},{5,4},{6,14},{7,6},{8,0},{9,8},{10... | collective-permute-start | bytes 1585160 | tf_op jit(solution)/shard_map/ppermute | solution.py:123
  15.4 26.3 %collective-permute-start.7 = (bf16[1056,128]{1,0:T(8,128)(2,1)S(1)}, bf16[1056,128]{1,0:T(8,128)(2,1)S(1)}, u32[]{:S(2)}, u32[]{:S(2)}) collective-permute-start(bf16[1056,128]{1,0:T(8,128)(2,1)S(1)} %collective-permute-done.4.refs_1_), channel_id=1, source_target_pairs={{0,1},{1,0},{2,3},{3,2},{4,5},{5,4},{6,7},{7,6},{8,9},{9,8},{10,11... | collective-permute-start | bytes 811016 | tf_op jit(solution)/shard_map/ppermute | solution.py:115
  19.4 7.8 %collective-permute-start.8 = (bf16[1056,128]{1,0:T(8,128)(2,1)S(1)}, bf16[1056,128]{1,0:T(8,128)(2,1)S(1)}, u32[]{:S(2)}, u32[]{:S(2)}) collective-permute-start(bf16[1056,128]{1,0:T(8,128)(2,1)S(1)} %collective-permute-done.refs_0_), channel_id=1, source_target_pairs={{0,2},{1,3},{2,0},{3,1},{4,6},{5,7},{6,4},{7,5},{8,10},{9,11},{10,... | collective-permute-start | bytes 811016 | tf_op jit(solution)/shard_map/ppermute | solution.py:115
  21.5 5.7 %collective-permute-start.9 = (bf16[1056,128]{1,0:T(8,128)(2,1)S(1)}, bf16[1056,128]{1,0:T(8,128)(2,1)S(1)}, u32[]{:S(2)}, u32[]{:S(2)}) collective-permute-start(bf16[1056,128]{1,0:T(8,128)(2,1)S(1)} %collective-permute-done.refs_0_), channel_id=1, source_target_pairs={{0,1},{1,0},{2,3},{3,2},{4,5},{5,4},{6,7},{7,6},{8,9},{9,8},{10,11... | collective-permute-start | bytes 811016 | tf_op jit(solution)/shard_map/ppermute | solution.py:115
  21.6 16.0 %collective-permute-start.3 = (bf16[2064,128]{1,0:T(8,128)(2,1)S(1)}, bf16[2064,128]{1,0:T(8,128)(2,1)S(1)}, u32[]{:S(2)}, u32[]{:S(2)}) collective-permute-start(bf16[2064,128]{1,0:T(8,128)(2,1)S(1)} %shard_map.55), channel_id=1, source_target_pairs={{0,1},{1,5},{2,3},{3,7},{4,0},{5,4},{6,2},{7,6},{8,12},{9,8},{10,1... | collective-permute-start | bytes 1585160 | tf_op jit(solution)/shard_map/ppermute | solution.py:123
  27.1 4.5 %collective-permute-start.10 = (bf16[1056,128]{1,0:T(8,128)(2,1)S(1)}, bf16[1056,128]{1,0:T(8,128)(2,1)S(1)}, u32[]{:S(2)}, u32[]{:S(2)}) collective-permute-start(bf16[1056,128]{1,0:T(8,128)(2,1)S(1)} %collective-permute-done.8.refs_1_), channel_id=1, source_target_pairs={{0,1},{1,0},{2,3},{3,2},{4,5},{5,4},{6,7},{7,6},{8,9},{9,8},{10,11... | collective-permute-start | bytes 811016 | tf_op jit(solution)/shard_map/ppermute | solution.py:115
  40.1 4.9 %collective-permute-start.11 = (bf16[1,6,128,128]{3,2,1,0:T(8,128)(2,1)S(1)}, bf16[1,6,128,128]{3,2,1,0:T(8,128)(2,1)S(1)}, u32[]{:S(2)}, u32[]{:S(2)}) collective-permute-start(bf16[1,6,128,128]{3,2,1,0:T(8,128)(2,1)S(1)} %shard_map.60), channel_id=1, source_target_pairs={{0,4},{1,0},{2,6},{3,2},{4,5},{5,1},{6,7},{7,3},{8,9},{9,13},{10,1... | collective-permute-start | bytes 589832 | tf_op jit(solution)/shard_map/ppermute | solution.py:123
  41.7 3.8 %collective-permute-start.12 = (bf16[1,6,128,128]{3,2,1,0:T(8,128)(2,1)S(1)}, bf16[1,6,128,128]{3,2,1,0:T(8,128)(2,1)S(1)}, u32[]{:S(2)}, u32[]{:S(2)}) collective-permute-start(bf16[1,6,128,128]{3,2,1,0:T(8,128)(2,1)S(1)} %shard_map.61), channel_id=1, source_target_pairs={{0,4},{1,0},{2,6},{3,2},{4,5},{5,1},{6,7},{7,3},{8,9},{9,13},{10,1... | collective-permute-start | bytes 589832 | tf_op jit(solution)/shard_map/ppermute | solution.py:123
  41.9 0.9 %copy-start.4 = (s32[2,6]{1,0:T(2,128)S(1)}, s32[2,6]{1,0:T(2,128)}, u32[]{:S(2)}) copy-start(s32[2,6]{1,0:T(2,128)} %refs_0_.5) | copy-start | bytes 148

commit v10 on v9

--- a/solution.py
+++ b/solution.py
@@ -162,10 +162,9 @@
     own_packs = [own, swap(own, "col", col_count, far)]
     other = swap(own, "row", row_count, 1)
     ready = lax.optimization_barrier((packed, own_packs[1]))[0]
-    for d in range(end - 1, 1, -1):
+    for d in range(end - 1, 0, -1):
         shards[d] = deliver(ready, d)
-    ready, other, _, _ = lax.optimization_barrier((packed, other, shards[end], cols[end][1]))
-    shards[1] = deliver(ready, 1)
+    other = lax.optimization_barrier((other, shards[end]))[0]
     own_packs, other_packs = across(own_packs, far // 2), across([other], far)
     def dense_of(packs):
         return pl.pallas_call(

time: 46.5 us -> 40.5 us (0.87)
  waiting for transfers between devices: 23.2 us -> 17.2 us
    ppermute x5, waiting for transfers between devices: 10.5 us -> 3.85 us  [permute(): return lax.ppermute(x, ('row', 'col'), pairs)]
    ppermute x8, waiting for transfers between devices: 12.8 us -> 13.3 us  [swap(): return lax.ppermute(x, axis, [(k, k ^ d) for k in range(n)])]
    ppermute x8, starting transfers between devices: 4.72 us -> 5.22 us  [swap(): return lax.ppermute(x, axis, [(k, k ^ d) for k in range(n)])]
  transfers between devices with their start and end apart: 13 -> 13, of which waited for: 6 -> 5; matrix products, arithmetic and copies ran while one was open for 3% -> 3% of each run, Pallas kernels for 18% -> 20%
where the time goes in v10:
time: 40.5 us; the launch traced here: 40.3 us
  waiting for transfers between devices  17.2 us (42%)
  starting transfers between devices  10.5 us (26%)
  Pallas kernels  8.11 us (20%)
  local copies, waits for them, and re-layouts  3.29 us (8%)
  other arithmetic  1.07 us (3%)
    ppermute x8, waiting for transfers between devices, swap(): return lax.ppermute(x, axis, [(k, k ^ d) for k in range(n)])  13.3 us
    ppermute x5, starting transfers between devices, permute(): return lax.ppermute(x, ('row', 'col'), pairs)  5.25 us
    ppermute x8, starting transfers between devices, swap(): return lax.ppermute(x, axis, [(k, k ^ d) for k in range(n)])  5.22 us
    pallas_call x3, Pallas kernels, step(): pl.pallas_call(functools.partial(step_kernel, [wanted[0]] + [cols[d][0] f...  5.15 us
    ppermute x5, waiting for transfers between devices, permute(): return lax.ppermute(x, ('row', 'col'), pairs)  3.85 us
    unnamed x12, local copies, waits for them, and re-layouts  2.32 us
    pallas_call x2, Pallas kernels, dense_of(): pl.pallas_call(functools.partial(left_kernel, a_cols.shape[1]), out_shape...  1.79 us
    pallas_call x2, Pallas kernels, pack(): pl.pallas_call(pack_kernel, out_shape=jax.ShapeDtypeStruct((size + -(-cou...  1.17 us
  transfers between devices with their start and end apart: 13, of which 5 were waited for; matrix products, arithmetic and copies ran while one was open for 3% of the time, Pallas kernels for 20%

profile of v10, /device:TPU:0, one launch (start us, length us, event | category | flops | bytes accessed | tf_op | source)
XLA Modules:
  0.0 40.3 jit_solution(3864140563525001928)
XLA Ops:
  0.0 5.0 %collective-permute-start.4 = (bf16[2048,128]{1,0:T(8,128)(2,1)}, bf16[2048,128]{1,0:T(8,128)(2,1)S(1)}, u32[]{:S(2)}, u32[]{:S(2)}) collective-permute-start(bf16[2048,128]{1,0:T(8,128)(2,1)} %bitcast.18), channel_id=1, source_target_pairs={{0,12},{1,3},{2,14},{3,1},{4,6},{5,9},{6,4},{7,11},{8,10},{9,5},{1... | collective-permute-start | bytes 1572872 | tf_op jit(solution)/shard_map/ppermute | solution.py:123
  5.1 0.9 %copy-done.1 = bf16[2,4,128,128]{3,2,1,0:T(8,128)(2,1)S(1)} copy-done((bf16[2,4,128,128]{3,2,1,0:T(8,128)(2,1)S(1)}, bf16[2,4,128,128]{3,2,1,0:T(8,128)(2,1)}, u32[]{:S(2)}) %copy-start.1) | copy-done | bytes 262168
  6.0 0.7 %copy-done.3 = s32[2,6]{1,0:T(2,128)S(1)} copy-done((s32[2,6]{1,0:T(2,128)S(1)}, s32[2,6]{1,0:T(2,128)}, u32[]{:S(2)}) %copy-start.3) | copy-done | bytes 72
  6.7 0.7 %copy-done.5 = s32[2,4]{1,0:T(2,128)S(1)} copy-done((s32[2,4]{1,0:T(2,128)S(1)}, s32[2,4]{1,0:T(2,128)}, u32[]{:S(2)}) %copy-start.5) | copy-done | bytes 56
  7.4 0.6 %shard_map.56.refs_0_ = bf16[1056,128]{1,0:T(8,128)(2,1)S(1)} custom-call(s32[2,4]{1,0:T(2,128)S(1)} %copy-done.5, s32[2,6]{1,0:T(2,128)S(1)} %copy-done.3, bf16[1024,128]{1,0:T(8,128)(2,1)S(1)} %bitcast.23), custom_call_target="tpu_custom_call" | custom-call | flops 1 | bytes 1 | tf_op jit(solution)/shard_map/pallas_call | solution.py:139
  8.0 1.6 %collective-permute-start = (bf16[1056,128]{1,0:T(8,128)(2,1)S(1)}, bf16[1056,128]{1,0:T(8,128)(2,1)S(1)}, u32[]{:S(2)}, u32[]{:S(2)}) collective-permute-start(bf16[1056,128]{1,0:T(8,128)(2,1)S(1)} %shard_map.56.refs_0_), channel_id=1, source_target_pairs={{0,2},{1,3},{2,0},{3,1},{4,6},{5,7},{6,4},{7,5},{8,10},{9,11},{10,... | collective-permute-start | bytes 811016 | tf_op jit(solution)/shard_map/ppermute | solution.py:115
  9.5 1.0 %collective-permute-start.3 = (s32[2,8]{1,0:T(2,128)S(1)}, s32[2,8]{1,0:T(2,128)S(1)}, u32[]{:S(2)}, u32[]{:S(2)}) collective-permute-start(s32[2,8]{1,0:T(2,128)S(1)} %copy-done.2), channel_id=1, source_target_pairs={{0,12},{4,8},{8,4},{12,0},{1,13},{5,9},{9,5},{13,1},{2,14},{6,10},... | collective-permute-start | bytes 200 | tf_op jit(solution)/shard_map/ppermute | solution.py:115
  10.5 0.1 slice_reduce_fusion.6
  10.6 0.6 %shard_map.55 = bf16[2064,128]{1,0:T(8,128)(2,1)S(1)} custom-call(s32[2,8]{1,0:T(2,128)S(1)} %copy-done.2, bf16[2048,128]{1,0:T(8,128)(2,1)S(1)} %bitcast.19), custom_call_target="tpu_custom_call" | custom-call | flops 1 | bytes 1 | tf_op jit(solution)/shard_map/pallas_call | solution.py:139
  11.2 0.1 stack.41.place
  11.3 4.0 %collective-permute-done.refs_1_ = bf16[1056,128]{1,0:T(8,128)(2,1)S(1)} collective-permute-done((bf16[1056,128]{1,0:T(8,128)(2,1)S(1)}, bf16[1056,128]{1,0:T(8,128)(2,1)S(1)}, u32[]{:S(2)}, u32[]{:S(2)}) %collective-permute-start) | collective-permute-done | bytes 270368 | tf_op jit(solution)/shard_map/ppermute | solution.py:115
  15.3 0.1 slice_reduce_fusion.5
  15.5 0.1 slice_reduce_fusion.4
  15.6 3.7 %collective-permute-done.7.refs_0_ = bf16[1056,128]{1,0:T(8,128)(2,1)S(1)} collective-permute-done((bf16[1056,128]{1,0:T(8,128)(2,1)S(1)}, bf16[1056,128]{1,0:T(8,128)(2,1)S(1)}, u32[]{:S(2)}, u32[]{:S(2)}) %collective-permute-start.7) | collective-permute-done | bytes 270368 | tf_op jit(solution)/shard_map/ppermute | solution.py:115
  19.3 2.0 %collective-permute-start.8 = (bf16[1056,128]{1,0:T(8,128)(2,1)S(1)}, bf16[1056,128]{1,0:T(8,128)(2,1)S(1)}, u32[]{:S(2)}, u32[]{:S(2)}) collective-permute-start(bf16[1056,128]{1,0:T(8,128)(2,1)S(1)} %collective-permute-done.7.refs_0_), channel_id=1, source_target_pairs={{0,2},{1,3},{2,0},{3,1},{4,6},{5,7},{6,4},{7,5},{8,10},{9,11},{10,... | collective-permute-start | bytes 811016 | tf_op jit(solution)/shard_map/ppermute | solution.py:115
  21.4 0.1 slice_reduce_fusion.7
  21.6 5.6 %collective-permute-done.8.refs_1_ = bf16[1056,128]{1,0:T(8,128)(2,1)S(1)} collective-permute-done((bf16[1056,128]{1,0:T(8,128)(2,1)S(1)}, bf16[1056,128]{1,0:T(8,128)(2,1)S(1)}, u32[]{:S(2)}, u32[]{:S(2)}) %collective-permute-start.8) | collective-permute-done | bytes 270368 | tf_op jit(solution)/shard_map/ppermute | solution.py:115
  27.2 0.1 slice_reduce_fusion.2
  27.3 0.6 %collective-permute-start.6 = (bf16[1056,128]{1,0:T(8,128)(2,1)S(1)}, bf16[1056,128]{1,0:T(8,128)(2,1)S(1)}, u32[]{:S(2)}, u32[]{:S(2)}) collective-permute-start(bf16[1056,128]{1,0:T(8,128)(2,1)S(1)} %collective-permute-done.refs_1_), channel_id=1, source_target_pairs={{0,1},{1,0},{2,3},{3,2},{4,5},{5,4},{6,7},{7,6},{8,9},{9,8},{10,11... | collective-permute-start | bytes 811016 | tf_op jit(solution)/shard_map/ppermute | solution.py:115
  27.9 0.1 slice_reduce_fusion.1
  28.0 3.4 %collective-permute-done.2.refs_6_ = bf16[2064,128]{1,0:T(8,128)(2,1)S(1)} collective-permute-done((bf16[2064,128]{1,0:T(8,128)(2,1)S(1)}, bf16[2064,128]{1,0:T(8,128)(2,1)S(1)}, u32[]{:S(2)}, u32[]{:S(2)}) %collective-permute-start.2) | collective-permute-done | bytes 528416 | tf_op jit(solution)/shard_map/ppermute | solution.py:123
  31.4 0.1 convert_reduce_fusion
  31.5 0.1 slice_reduce_fusion
  31.7 0.1 convert_reduce_fusion.1
  31.8 0.9 %shard_map.59.refs_9_ = bf16[2,8,128,128]{3,2,1,0:T(8,128)(2,1)S(1)} custom-call(s32[4,32]{1,0:T(4,128)S(1)} %maximum_convert_fusion.1.index, bf16[1056,128]{1,0:T(8,128)(2,1)S(1)} %collective-permute-done.7.refs_0_, bf16[1056,128]{1,0:T(8,128)(2,1)S(1)} %collective-permute-done.8.refs_1_, bf16[1056,128]{1,0:T(8,128)(2,1)S(1)} %collective-permute-done.9.refs_2_, ...), custom_call_target="tpu_custom_call" | custom-call | flops 1 | bytes 1 | tf_op jit(solution)/shard_map/pallas_call | solution.py:170
  32.7 1.5 %shard_map.60 = bf16[1,6,128,128]{3,2,1,0:T(8,128)(2,1)S(1)} custom-call(s32[5]{0:T(128)S(1)} %stack.41.place, s32[1,32]{1,0:T(1,128)S(1)} %bitcast_convert_fusion.refs_0_, s32[1,16]{1,0:T(1,128)S(1)} %bitcast.27, s32[1,16]{1,0:T(1,128)S(1)} %bitcast.24, s32[2,8]{1,0:T(2,128)S(1)} %copy-done.2, s32[2,8]{1,0:T(2,128)S(1)} %collective-permute-done.3.refs_4_, ...), custom_call_target="tpu_custom_call" | custom-call | flops 1 | bytes 1 | tf_op jit(solution)/shard_map/pallas_call | solution.py:186
  34.3 1.5 %shard_map.61 = bf16[1,6,128,128]{3,2,1,0:T(8,128)(2,1)S(1)} custom-call(s32[5]{0:T(128)S(1)} %stack.41.place, s32[1,32]{1,0:T(1,128)S(1)} %bitcast_convert_fusion.refs_0_, s32[1,16]{1,0:T(1,128)S(1)} %bitcast.28, s32[1,16]{1,0:T(1,128)S(1)} %bitcast.25, s32[2,8]{1,0:T(2,128)S(1)} %copy-done.2, s32[2,8]{1,0:T(2,128)S(1)} %collective-permute-done.3.refs_4_, ...), custom_call_target="tpu_custom_call" | custom-call | flops 1 | bytes 1 | tf_op jit(solution)/shard_map/pallas_call | solution.py:186
  35.8 0.1 slice_reduce_fusion.3
  36.0 0.9 %shard_map.57.refs_9_ = bf16[2,8,128,128]{3,2,1,0:T(8,128)(2,1)S(1)} custom-call(s32[4,32]{1,0:T(4,128)S(1)} %maximum_convert_fusion.index, bf16[1056,128]{1,0:T(8,128)(2,1)S(1)} %shard_map.56.refs_0_, bf16[1056,128]{1,0:T(8,128)(2,1)S(1)} %collective-permute-done.refs_1_, bf16[1056,128]{1,0:T(8,128)(2,1)S(1)} %collective-permute-done.5.refs_2_, ...), custom_call_target="tpu_custom_call" | custom-call | flops 1 | bytes 1 | tf_op jit(solution)/shard_map/pallas_call | solution.py:170
  36.9 2.2 %shard_map.58 = bf16[2,6,128,128]{3,2,1,0:T(8,128)(2,1)S(1)} custom-call(s32[5]{0:T(128)S(1)} %stack.41.place, s32[2,6]{1,0:T(2,128)S(1)} %copy-done.4, s32[1,16]{1,0:T(1,128)S(1)} %bitcast.29, s32[1,16]{1,0:T(1,128)S(1)} %bitcast.26, s32[2,8]{1,0:T(2,128)S(1)} %copy-done.2, s32[2,8]{1,0:T(2,128)S(1)} %collective-permute-done.3.refs_4_, ...), custom_call_target="tpu_custom_call" | custom-call | flops 1 | bytes 1 | tf_op jit(solution)/shard_map/pallas_call | solution.py:186
  39.1 0.5 %collective-permute-done.12 = bf16[1,6,128,128]{3,2,1,0:T(8,128)(2,1)S(1)} collective-permute-done((bf16[1,6,128,128]{3,2,1,0:T(8,128)(2,1)S(1)}, bf16[1,6,128,128]{3,2,1,0:T(8,128)(2,1)S(1)}, u32[]{:S(2)}, u32[]{:S(2)}) %collective-permute-start.12) | collective-permute-done | bytes 196640 | tf_op jit(solution)/shard_map/ppermute | solution.py:123
  39.5 0.8 %maximum_select_fusion = bf16[2,6,128,128]{3,2,1,0:T(8,128)(2,1)} fusion(bf16[2,6,128,128]{3,2,1,0:T(8,128)(2,1)S(1)} %shard_map.58, bf16[1,6,128,128]{3,2,1,0:T(8,128)(2,1)S(1)} %collective-permute-done.12, bf16[1,6,128,128]{3,2,1,0:T(8,128)(2,1)S(1)} %collective-permute-done.11, pred[]{:T(512)S(6)} %eq.5), kind=kLoop, calls=%fused_computation | loop fusion | flops 393216 | bytes 1179649 | tf_op jit(solution)/shard_map/jit(_where)/select_n | solution.py:213
  (28 shorter events, 0.4 us)
Async XLA Ops:
  0.0 10.6 %copy-start = (bf16[2,8,128,128]{3,2,1,0:T(8,128)(2,1)S(1)}, bf16[2,8,128,128]{3,2,1,0:T(8,128)(2,1)}, u32[]{:S(2)}) copy-start(bf16[2,8,128,128]{3,2,1,0:T(8,128)(2,1)} %param.7) | copy-start | bytes 1572868
  0.0 19.3 %collective-permute-start.4 = (bf16[2048,128]{1,0:T(8,128)(2,1)}, bf16[2048,128]{1,0:T(8,128)(2,1)S(1)}, u32[]{:S(2)}, u32[]{:S(2)}) collective-permute-start(bf16[2048,128]{1,0:T(8,128)(2,1)} %bitcast.18), channel_id=1, source_target_pairs={{0,12},{1,3},{2,14},{3,1},{4,6},{5,9},{6,4},{7,11},{8,10},{9,5},{1... | collective-permute-start | bytes 1572872 | tf_op jit(solution)/shard_map/ppermute | solution.py:123
  5.1 0.9 %copy-start.1 = (bf16[2,4,128,128]{3,2,1,0:T(8,128)(2,1)S(1)}, bf16[2,4,128,128]{3,2,1,0:T(8,128)(2,1)}, u32[]{:S(2)}) copy-start(bf16[2,4,128,128]{3,2,1,0:T(8,128)(2,1)} %param.5) | copy-start | bytes 786436
  6.0 0.7 %copy-start.3 = (s32[2,6]{1,0:T(2,128)S(1)}, s32[2,6]{1,0:T(2,128)}, u32[]{:S(2)}) copy-start(s32[2,6]{1,0:T(2,128)} %refs_0_.5) | copy-start | bytes 148
  6.7 0.7 %copy-start.5 = (s32[2,4]{1,0:T(2,128)S(1)}, s32[2,4]{1,0:T(2,128)}, u32[]{:S(2)}) copy-start(s32[2,4]{1,0:T(2,128)} %refs_0_.4) | copy-start | bytes 100
  7.4 2.2 %copy-start.2 = (s32[2,8]{1,0:T(2,128)S(1)}, s32[2,8]{1,0:T(2,128)}, u32[]{:S(2)}) copy-start(s32[2,8]{1,0:T(2,128)} %refs_3_.5) | copy-start | bytes 196
  8.0 7.4 %collective-permute-start = (bf16[1056,128]{1,0:T(8,128)(2,1)S(1)}, bf16[1056,128]{1,0:T(8,128)(2,1)S(1)}, u32[]{:S(2)}, u32[]{:S(2)}) collective-permute-start(bf16[1056,128]{1,0:T(8,128)(2,1)S(1)} %shard_map.56.refs_0_), channel_id=1, source_target_pairs={{0,2},{1,3},{2,0},{3,1},{4,6},{5,7},{6,4},{7,5},{8,10},{9,11},{10,... | collective-permute-start | bytes 811016 | tf_op jit(solution)/shard_map/ppermute | solution.py:115
  9.5 5.9 %collective-permute-start.5 = (bf16[1056,128]{1,0:T(8,128)(2,1)S(1)}, bf16[1056,128]{1,0:T(8,128)(2,1)S(1)}, u32[]{:S(2)}, u32[]{:S(2)}) collective-permute-start(bf16[1056,128]{1,0:T(8,128)(2,1)S(1)} %shard_map.56.refs_0_), channel_id=1, source_target_pairs={{0,1},{1,0},{2,3},{3,2},{4,5},{5,4},{6,7},{7,6},{8,9},{9,8},{10,11... | collective-permute-start | bytes 811016 | tf_op jit(solution)/shard_map/ppermute | solution.py:115
  9.5 9.8 %collective-permute-start.7 = (bf16[1056,128]{1,0:T(8,128)(2,1)S(1)}, bf16[1056,128]{1,0:T(8,128)(2,1)S(1)}, u32[]{:S(2)}, u32[]{:S(2)}) collective-permute-start(bf16[1056,128]{1,0:T(8,128)(2,1)S(1)} %shard_map.56.refs_0_), channel_id=1, source_target_pairs={{0,4},{4,0},{8,12},{12,8},{1,5},{5,1},{9,13},{13,9},{2,6},{6,2},{1... | collective-permute-start | bytes 811016 | tf_op jit(solution)/shard_map/ppermute | solution.py:115
  9.5 23.2 %collective-permute-start.3 = (s32[2,8]{1,0:T(2,128)S(1)}, s32[2,8]{1,0:T(2,128)S(1)}, u32[]{:S(2)}, u32[]{:S(2)}) collective-permute-start(s32[2,8]{1,0:T(2,128)S(1)} %copy-done.2), channel_id=1, source_target_pairs={{0,12},{4,8},{8,4},{12,0},{1,13},{5,9},{9,5},{13,1},{2,14},{6,10},... | collective-permute-start | bytes 200 | tf_op jit(solution)/shard_map/ppermute | solution.py:115
  15.3 16.1 %collective-permute-start.2 = (bf16[2064,128]{1,0:T(8,128)(2,1)S(1)}, bf16[2064,128]{1,0:T(8,128)(2,1)S(1)}, u32[]{:S(2)}, u32[]{:S(2)}) collective-permute-start(bf16[2064,128]{1,0:T(8,128)(2,1)S(1)} %shard_map.55), channel_id=1, source_target_pairs={{0,1},{1,9},{2,3},{3,11},{4,12},{5,4},{6,14},{7,6},{8,0},{9,8},{10... | collective-permute-start | bytes 1585160 | tf_op jit(solution)/shard_map/ppermute | solution.py:123
  15.4 16.2 %collective-permute-start.1 = (bf16[2064,128]{1,0:T(8,128)(2,1)S(1)}, bf16[2064,128]{1,0:T(8,128)(2,1)S(1)}, u32[]{:S(2)}, u32[]{:S(2)}) collective-permute-start(bf16[2064,128]{1,0:T(8,128)(2,1)S(1)} %shard_map.55), channel_id=1, source_target_pairs={{0,1},{1,5},{2,3},{3,7},{4,0},{5,4},{6,2},{7,6},{8,12},{9,8},{10,1... | collective-permute-start | bytes 1585160 | tf_op jit(solution)/shard_map/ppermute | solution.py:123
  19.3 7.9 %collective-permute-start.8 = (bf16[1056,128]{1,0:T(8,128)(2,1)S(1)}, bf16[1056,128]{1,0:T(8,128)(2,1)S(1)}, u32[]{:S(2)}, u32[]{:S(2)}) collective-permute-start(bf16[1056,128]{1,0:T(8,128)(2,1)S(1)} %collective-permute-done.7.refs_0_), channel_id=1, source_target_pairs={{0,2},{1,3},{2,0},{3,1},{4,6},{5,7},{6,4},{7,5},{8,10},{9,11},{10,... | collective-permute-start | bytes 811016 | tf_op jit(solution)/shard_map/ppermute | solution.py:115
  21.5 5.8 %collective-permute-start.9 = (bf16[1056,128]{1,0:T(8,128)(2,1)S(1)}, bf16[1056,128]{1,0:T(8,128)(2,1)S(1)}, u32[]{:S(2)}, u32[]{:S(2)}) collective-permute-start(bf16[1056,128]{1,0:T(8,128)(2,1)S(1)} %collective-permute-done.7.refs_0_), channel_id=1, source_target_pairs={{0,1},{1,0},{2,3},{3,2},{4,5},{5,4},{6,7},{7,6},{8,9},{9,8},{10,11... | collective-permute-start | bytes 811016 | tf_op jit(solution)/shard_map/ppermute | solution.py:115
  27.2 4.3 %collective-permute-start.10 = (bf16[1056,128]{1,0:T(8,128)(2,1)S(1)}, bf16[1056,128]{1,0:T(8,128)(2,1)S(1)}, u32[]{:S(2)}, u32[]{:S(2)}) collective-permute-start(bf16[1056,128]{1,0:T(8,128)(2,1)S(1)} %collective-permute-done.8.refs_1_), channel_id=1, source_target_pairs={{0,1},{1,0},{2,3},{3,2},{4,5},{5,4},{6,7},{7,6},{8,9},{9,8},{10,11... | collective-permute-start | bytes 811016 | tf_op jit(solution)/shard_map/ppermute | solution.py:115
  27.3 8.5 %collective-permute-start.6 = (bf16[1056,128]{1,0:T(8,128)(2,1)S(1)}, bf16[1056,128]{1,0:T(8,128)(2,1)S(1)}, u32[]{:S(2)}, u32[]{:S(2)}) collective-permute-start(bf16[1056,128]{1,0:T(8,128)(2,1)S(1)} %collective-permute-done.refs_1_), channel_id=1, source_target_pairs={{0,1},{1,0},{2,3},{3,2},{4,5},{5,4},{6,7},{7,6},{8,9},{9,8},{10,11... | collective-permute-start | bytes 811016 | tf_op jit(solution)/shard_map/ppermute | solution.py:115
  34.2 4.9 %collective-permute-start.11 = (bf16[1,6,128,128]{3,2,1,0:T(8,128)(2,1)S(1)}, bf16[1,6,128,128]{3,2,1,0:T(8,128)(2,1)S(1)}, u32[]{:S(2)}, u32[]{:S(2)}) collective-permute-start(bf16[1,6,128,128]{3,2,1,0:T(8,128)(2,1)S(1)} %shard_map.60), channel_id=1, source_target_pairs={{0,4},{1,0},{2,6},{3,2},{4,5},{5,1},{6,7},{7,3},{8,9},{9,13},{10,1... | collective-permute-start | bytes 589832 | tf_op jit(solution)/shard_map/ppermute | solution.py:123
  35.7 3.8 %collective-permute-start.12 = (bf16[1,6,128,128]{3,2,1,0:T(8,128)(2,1)S(1)}, bf16[1,6,128,128]{3,2,1,0:T(8,128)(2,1)S(1)}, u32[]{:S(2)}, u32[]{:S(2)}) collective-permute-start(bf16[1,6,128,128]{3,2,1,0:T(8,128)(2,1)S(1)} %shard_map.61), channel_id=1, source_target_pairs={{0,4},{1,0},{2,6},{3,2},{4,5},{5,1},{6,7},{7,3},{8,9},{9,13},{10,1... | collective-permute-start | bytes 589832 | tf_op jit(solution)/shard_map/ppermute | solution.py:123
  36.0 0.9 %copy-start.4 = (s32[2,6]{1,0:T(2,128)S(1)}, s32[2,6]{1,0:T(2,128)}, u32[]{:S(2)}) copy-start(s32[2,6]{1,0:T(2,128)} %refs_0_.5) | copy-start | bytes 148

commit v11 on v10

--- a/solution.py
+++ b/solution.py
@@ -158,10 +158,11 @@
     flat = b_tiles.reshape(-1, block)
     own, packed = pack(a_tiles, a_cols, c_cols), pack(b_tiles, b_cols)
     shards = {0: flat, end: deliver(flat, end)}
-    cols = {0: (None, b_cols), end: (None, swap(b_cols, "row", row_count, end))}
     own_packs = [own, swap(own, "col", col_count, far)]
+    late_cols = lax.optimization_barrier((b_cols, own_packs[1]))[0]
+    cols = {0: (None, b_cols), end: (None, swap(late_cols, "row", row_count, end))}
     other = swap(own, "row", row_count, 1)
-    ready = lax.optimization_barrier((packed, own_packs[1]))[0]
+    ready = packed
     for d in range(end - 1, 0, -1):
         shards[d] = deliver(ready, d)
     other = lax.optimization_barrier((other, shards[end]))[0]
@@ -197,12 +198,16 @@
         )(place, wanted[1], *[cols[d][1] for d in dists], *[shards[d] for d in dists], *held)
 
     order, every = list(range(1, end)) + [0, end], list(range(rows))
-    early, late = order[:-4], order[-4:]
+    order = order[-2:] + order[:-2]
+    early, late = order[:-2], order[-2:]
     for d in range(1, end):
-        cols[d] = (0, index_of([shards[d]], b_tiles))
+        cols[d] = None
 
     def products(wanted, packs, spans):
         dense, total = dense_of(packs), None
+        for d in range(1, end):
+            if cols[d] is None:
+                cols[d] = (0, index_of(lax.optimization_barrier(([shards[d]], dense))[0], b_tiles))
         for at in range(0, len(early), 4):
             total = step(early[at : at + 4], wanted, dense, total, every, False)
         return [step(late, wanted, dense, total, span, True) for span in spans]

time: 40.5 us -> 45.2 us (1.12)
  starting transfers between devices: 10.5 us -> 15.1 us
  Pallas kernels: 8.11 us -> 9.64 us
  waiting for transfers between devices: 17.2 us -> 15.7 us
    ppermute x5, starting transfers between devices: 5.25 us -> 9.93 us  [permute(): return lax.ppermute(x, ('row', 'col'), pairs)]
    ppermute x5, waiting for transfers between devices: 3.85 us -> 0.31 us  [permute(): return lax.ppermute(x, ('row', 'col'), pairs)]
    ppermute x8, waiting for transfers between devices: 13.3 us -> 15.4 us  [swap(): return lax.ppermute(x, axis, [(k, k ^ d) for k in range(n)])]
    pallas_call x3 -> x5, Pallas kernels: 5.15 us -> 6.68 us  [step(): pl.pallas_call(functools.partial(step_kernel, [wanted[0]] + [cols[d][0] f...]
  transfers between devices with their start and end apart: 13 -> 13, of which waited for: 5 -> 4; matrix products, arithmetic and copies ran while one was open for 3% -> 3% of each run, Pallas kernels for 20% -> 21%
where the time goes in v11:
time: 45.2 us; the launch traced here: 45 us
  waiting for transfers between devices  15.7 us (35%)
  starting transfers between devices  15.1 us (33%)
  Pallas kernels  9.64 us (21%)
  local copies, waits for them, and re-layouts  3.21 us (7%)
  other arithmetic  1.14 us (3%)
    ppermute x8, waiting for transfers between devices, swap(): return lax.ppermute(x, axis, [(k, k ^ d) for k in range(n)])  15.4 us
    ppermute x5, starting transfers between devices, permute(): return lax.ppermute(x, ('row', 'col'), pairs)  9.93 us
    pallas_call x5, Pallas kernels, step(): pl.pallas_call(functools.partial(step_kernel, [wanted[0]] + [cols[d][0] f...  6.68 us
    ppermute x8, starting transfers between devices, swap(): return lax.ppermute(x, axis, [(k, k ^ d) for k in range(n)])  5.15 us
    unnamed x12, local copies, waits for them, and re-layouts  2.32 us
    pallas_call x2, Pallas kernels, dense_of(): pl.pallas_call(functools.partial(left_kernel, a_cols.shape[1]), out_shape...  1.79 us
    pallas_call x2, Pallas kernels, pack(): pl.pallas_call(pack_kernel, out_shape=jax.ShapeDtypeStruct((size + -(-cou...  1.17 us
  transfers between devices with their start and end apart: 13, of which 4 were waited for; matrix products, arithmetic and copies ran while one was open for 3% of the time, Pallas kernels for 21%

profile of v11, /device:TPU:0, one launch (start us, length us, event | category | flops | bytes accessed | tf_op | source)
XLA Modules:
  0.0 45.0 jit_solution(12577582276656546465)
XLA Ops:
  0.0 5.0 %collective-permute-start.2 = (bf16[2048,128]{1,0:T(8,128)(2,1)}, bf16[2048,128]{1,0:T(8,128)(2,1)S(1)}, u32[]{:S(2)}, u32[]{:S(2)}) collective-permute-start(bf16[2048,128]{1,0:T(8,128)(2,1)} %bitcast.18), channel_id=1, source_target_pairs={{0,12},{1,3},{2,14},{3,1},{4,6},{5,9},{6,4},{7,11},{8,10},{9,5},{1... | collective-permute-start | bytes 1572872 | tf_op jit(solution)/shard_map/ppermute | solution.py:123
  5.1 0.9 %copy-done.1 = bf16[2,4,128,128]{3,2,1,0:T(8,128)(2,1)S(1)} copy-done((bf16[2,4,128,128]{3,2,1,0:T(8,128)(2,1)S(1)}, bf16[2,4,128,128]{3,2,1,0:T(8,128)(2,1)}, u32[]{:S(2)}) %copy-start.1) | copy-done | bytes 262168
  6.0 0.7 %copy-done.3 = s32[2,6]{1,0:T(2,128)S(1)} copy-done((s32[2,6]{1,0:T(2,128)S(1)}, s32[2,6]{1,0:T(2,128)}, u32[]{:S(2)}) %copy-start.3) | copy-done | bytes 72
  6.7 0.7 %copy-done.5 = s32[2,4]{1,0:T(2,128)S(1)} copy-done((s32[2,4]{1,0:T(2,128)S(1)}, s32[2,4]{1,0:T(2,128)}, u32[]{:S(2)}) %copy-start.5) | copy-done | bytes 56
  7.4 0.6 %shard_map.56.refs_0_ = bf16[1056,128]{1,0:T(8,128)(2,1)S(1)} custom-call(s32[2,4]{1,0:T(2,128)S(1)} %copy-done.5, s32[2,6]{1,0:T(2,128)S(1)} %copy-done.3, bf16[1024,128]{1,0:T(8,128)(2,1)S(1)} %bitcast.22), custom_call_target="tpu_custom_call" | custom-call | flops 1 | bytes 1 | tf_op jit(solution)/shard_map/pallas_call | solution.py:139
  8.0 1.6 %collective-permute-start.7 = (bf16[1056,128]{1,0:T(8,128)(2,1)S(1)}, bf16[1056,128]{1,0:T(8,128)(2,1)S(1)}, u32[]{:S(2)}, u32[]{:S(2)}) collective-permute-start(bf16[1056,128]{1,0:T(8,128)(2,1)S(1)} %shard_map.56.refs_0_), channel_id=1, source_target_pairs={{0,2},{1,3},{2,0},{3,1},{4,6},{5,7},{6,4},{7,5},{8,10},{9,11},{10,... | collective-permute-start | bytes 811016 | tf_op jit(solution)/shard_map/ppermute | solution.py:115
  9.6 0.6 %shard_map.55 = bf16[2064,128]{1,0:T(8,128)(2,1)S(1)} custom-call(s32[2,8]{1,0:T(2,128)S(1)} %copy-done.2, bf16[2048,128]{1,0:T(8,128)(2,1)S(1)} %bitcast.19), custom_call_target="tpu_custom_call" | custom-call | flops 1 | bytes 1 | tf_op jit(solution)/shard_map/pallas_call | solution.py:139
  10.2 0.6 %collective-permute-start.6 = (bf16[2064,128]{1,0:T(8,128)(2,1)S(1)}, bf16[2064,128]{1,0:T(8,128)(2,1)S(1)}, u32[]{:S(2)}, u32[]{:S(2)}) collective-permute-start(bf16[2064,128]{1,0:T(8,128)(2,1)S(1)} %shard_map.55), channel_id=1, source_target_pairs={{0,1},{1,9},{2,3},{3,11},{4,12},{5,4},{6,14},{7,6},{8,0},{9,8},{10... | collective-permute-start | bytes 1585160 | tf_op jit(solution)/shard_map/ppermute | solution.py:123
  10.8 0.1 slice_reduce_fusion.3
  10.9 11.6 %collective-permute-done.1.refs_0_ = bf16[1056,128]{1,0:T(8,128)(2,1)S(1)} collective-permute-done((bf16[1056,128]{1,0:T(8,128)(2,1)S(1)}, bf16[1056,128]{1,0:T(8,128)(2,1)S(1)}, u32[]{:S(2)}, u32[]{:S(2)}) %collective-permute-start.1) | collective-permute-done | bytes 270368 | tf_op jit(solution)/shard_map/ppermute | solution.py:115
  22.5 1.5 %collective-permute-start.3 = (bf16[1056,128]{1,0:T(8,128)(2,1)S(1)}, bf16[1056,128]{1,0:T(8,128)(2,1)S(1)}, u32[]{:S(2)}, u32[]{:S(2)}) collective-permute-start(bf16[1056,128]{1,0:T(8,128)(2,1)S(1)} %collective-permute-done.1.refs_0_), channel_id=1, source_target_pairs={{0,2},{1,3},{2,0},{3,1},{4,6},{5,7},{6,4},{7,5},{8,10},{9,11},{10,... | collective-permute-start | bytes 811016 | tf_op jit(solution)/shard_map/ppermute | solution.py:115
  24.1 1.4 %collective-permute-start.10 = (s32[2,8]{1,0:T(2,128)S(1)}, s32[2,8]{1,0:T(2,128)S(1)}, u32[]{:S(2)}, u32[]{:S(2)}) collective-permute-start(s32[2,8]{1,0:T(2,128)S(1)} %copy-done.2), channel_id=1, source_target_pairs={{0,12},{4,8},{8,4},{12,0},{1,13},{5,9},{9,5},{13,1},{2,14},{6,10},... | collective-permute-start | bytes 200 | tf_op jit(solution)/shard_map/ppermute | solution.py:115
  25.7 0.1 slice_reduce_fusion.1
  25.8 3.2 %collective-permute-done.3.refs_1_ = bf16[1056,128]{1,0:T(8,128)(2,1)S(1)} collective-permute-done((bf16[1056,128]{1,0:T(8,128)(2,1)S(1)}, bf16[1056,128]{1,0:T(8,128)(2,1)S(1)}, u32[]{:S(2)}, u32[]{:S(2)}) %collective-permute-start.3) | collective-permute-done | bytes 270368 | tf_op jit(solution)/shard_map/ppermute | solution.py:115
  29.0 0.1 slice_reduce_fusion.7
  29.1 0.1 slice_reduce_fusion.6
  29.2 0.6 %collective-permute-start.9 = (bf16[1056,128]{1,0:T(8,128)(2,1)S(1)}, bf16[1056,128]{1,0:T(8,128)(2,1)S(1)}, u32[]{:S(2)}, u32[]{:S(2)}) collective-permute-start(bf16[1056,128]{1,0:T(8,128)(2,1)S(1)} %collective-permute-done.7.refs_1_), channel_id=1, source_target_pairs={{0,1},{1,0},{2,3},{3,2},{4,5},{5,4},{6,7},{7,6},{8,9},{9,8},{10,11... | collective-permute-start | bytes 811016 | tf_op jit(solution)/shard_map/ppermute | solution.py:115
  29.9 0.6 %collective-permute-done.5.refs_3_ = bf16[1056,128]{1,0:T(8,128)(2,1)S(1)} collective-permute-done((bf16[1056,128]{1,0:T(8,128)(2,1)S(1)}, bf16[1056,128]{1,0:T(8,128)(2,1)S(1)}, u32[]{:S(2)}, u32[]{:S(2)}) %collective-permute-start.5) | collective-permute-done | bytes 270368 | tf_op jit(solution)/shard_map/ppermute | solution.py:115
  30.5 0.1 slice_reduce_fusion.4
  30.7 0.9 %shard_map.57.refs_5_ = bf16[2,8,128,128]{3,2,1,0:T(8,128)(2,1)S(1)} custom-call(s32[4,32]{1,0:T(4,128)S(1)} %maximum_convert_fusion.index, bf16[1056,128]{1,0:T(8,128)(2,1)S(1)} %collective-permute-done.1.refs_0_, bf16[1056,128]{1,0:T(8,128)(2,1)S(1)} %collective-permute-done.3.refs_1_, bf16[1056,128]{1,0:T(8,128)(2,1)S(1)} %collective-permute-done.4.refs_2_, ...), custom_call_target="tpu_custom_call" | custom-call | flops 1 | bytes 1 | tf_op jit(solution)/shard_map/pallas_call | solution.py:171
  31.6 1.5 %shard_map.61.refs_6_ = f32[2,128,768]{2,1,0:T(8,128)S(1)} custom-call(s32[3]{0:T(128)S(1)} %get-tuple-element.14.place, s32[1,32]{1,0:T(1,128)S(1)} %bitcast_convert_fusion.refs_0_, s32[2,8]{1,0:T(2,128)S(1)} %copy-done.2, s32[2,8]{1,0:T(2,128)S(1)} %collective-permute-done.10.refs_2_, bf16[2048,128]{1,0:T(8,128)(2,1)S(1)} %bitcast.20, ...), custom_call_target="tpu_custom_call" | custom-call | flops 1 | bytes 1 | tf_op jit(solution)/shard_map/pallas_call | solution.py:187
  33.0 0.3 collective-permute-done.refs_3_
  33.3 0.1 convert_reduce_fusion
  33.5 0.1 convert_reduce_fusion.1
  33.6 1.1 %shard_map.62 = bf16[1,6,128,128]{3,2,1,0:T(8,128)(2,1)S(1)} custom-call(s32[3]{0:T(128)S(1)} %get-tuple-element.13.place, s32[1,32]{1,0:T(1,128)S(1)} %bitcast_convert_fusion.refs_0_, s32[1,16]{1,0:T(1,128)S(1)} %bitcast.26, s32[1,16]{1,0:T(1,128)S(1)} %bitcast.23, bf16[2064,128]{1,0:T(8,128)(2,1)S(1)} %collective-permute-done.refs_3_, ...), custom_call_target="tpu_custom_call" | custom-call | flops 1 | bytes 1 | tf_op jit(solution)/shard_map/pallas_call | solution.py:187
  34.7 3.3 %collective-permute-start.11 = (bf16[1,6,128,128]{3,2,1,0:T(8,128)(2,1)S(1)}, bf16[1,6,128,128]{3,2,1,0:T(8,128)(2,1)S(1)}, u32[]{:S(2)}, u32[]{:S(2)}) collective-permute-start(bf16[1,6,128,128]{3,2,1,0:T(8,128)(2,1)S(1)} %shard_map.62), channel_id=1, source_target_pairs={{0,4},{1,0},{2,6},{3,2},{4,5},{5,1},{6,7},{7,3},{8,9},{9,13},{10,1... | collective-permute-start | bytes 589832 | tf_op jit(solution)/shard_map/ppermute | solution.py:123
  38.0 1.1 %shard_map.63 = bf16[1,6,128,128]{3,2,1,0:T(8,128)(2,1)S(1)} custom-call(s32[3]{0:T(128)S(1)} %get-tuple-element.13.place, s32[1,32]{1,0:T(1,128)S(1)} %bitcast_convert_fusion.refs_0_, s32[1,16]{1,0:T(1,128)S(1)} %bitcast.27, s32[1,16]{1,0:T(1,128)S(1)} %bitcast.24, bf16[2064,128]{1,0:T(8,128)(2,1)S(1)} %collective-permute-done.refs_3_, ...), custom_call_target="tpu_custom_call" | custom-call | flops 1 | bytes 1 | tf_op jit(solution)/shard_map/pallas_call | solution.py:187
  39.1 1.1 %collective-permute-start.12 = (bf16[1,6,128,128]{3,2,1,0:T(8,128)(2,1)S(1)}, bf16[1,6,128,128]{3,2,1,0:T(8,128)(2,1)S(1)}, u32[]{:S(2)}, u32[]{:S(2)}) collective-permute-start(bf16[1,6,128,128]{3,2,1,0:T(8,128)(2,1)S(1)} %shard_map.63), channel_id=1, source_target_pairs={{0,4},{1,0},{2,6},{3,2},{4,5},{5,1},{6,7},{7,3},{8,9},{9,13},{10,1... | collective-permute-start | bytes 589832 | tf_op jit(solution)/shard_map/ppermute | solution.py:123
  40.3 0.9 %shard_map.58.refs_5_ = bf16[2,8,128,128]{3,2,1,0:T(8,128)(2,1)S(1)} custom-call(s32[4,32]{1,0:T(4,128)S(1)} %maximum_convert_fusion.1.index, bf16[1056,128]{1,0:T(8,128)(2,1)S(1)} %shard_map.56.refs_0_, bf16[1056,128]{1,0:T(8,128)(2,1)S(1)} %collective-permute-done.7.refs_1_, bf16[1056,128]{1,0:T(8,128)(2,1)S(1)} %collective-permute-done.8.refs_2_, ...), custom_call_target="tpu_custom_call" | custom-call | flops 1 | bytes 1 | tf_op jit(solution)/shard_map/pallas_call | solution.py:171
  41.2 1.5 %shard_map.59.refs_6_ = f32[2,128,768]{2,1,0:T(8,128)S(1)} custom-call(s32[3]{0:T(128)S(1)} %get-tuple-element.14.place, s32[2,6]{1,0:T(2,128)S(1)} %copy-done.4, s32[2,8]{1,0:T(2,128)S(1)} %copy-done.2, s32[2,8]{1,0:T(2,128)S(1)} %collective-permute-done.10.refs_2_, bf16[2048,128]{1,0:T(8,128)(2,1)S(1)} %bitcast.21, ...), custom_call_target="tpu_custom_call" | custom-call | flops 1 | bytes 1 | tf_op jit(solution)/shard_map/pallas_call | solution.py:187
  42.7 1.5 %shard_map.60 = bf16[2,6,128,128]{3,2,1,0:T(8,128)(2,1)S(1)} custom-call(s32[3]{0:T(128)S(1)} %get-tuple-element.13.place, s32[2,6]{1,0:T(2,128)S(1)} %copy-done.4, s32[1,16]{1,0:T(1,128)S(1)} %bitcast.28, s32[1,16]{1,0:T(1,128)S(1)} %bitcast.25, bf16[2064,128]{1,0:T(8,128)(2,1)S(1)} %collective-permute-done.refs_3_, ...), custom_call_target="tpu_custom_call" | custom-call | flops 1 | bytes 1 | tf_op jit(solution)/shard_map/pallas_call | solution.py:187
  44.2 0.8 %maximum_select_fusion = bf16[2,6,128,128]{3,2,1,0:T(8,128)(2,1)} fusion(bf16[2,6,128,128]{3,2,1,0:T(8,128)(2,1)S(1)} %shard_map.60, bf16[1,6,128,128]{3,2,1,0:T(8,128)(2,1)S(1)} %collective-permute-done.12, bf16[1,6,128,128]{3,2,1,0:T(8,128)(2,1)S(1)} %collective-permute-done.11, pred[]{:T(512)S(6)} %eq.5), kind=kLoop, calls=%fused_computation | loop fusion | flops 393216 | bytes 1179649 | tf_op jit(solution)/shard_map/jit(_where)/select_n | solution.py:218
  (30 shorter events, 0.6 us)
Async XLA Ops:
  0.0 9.6 %copy-start = (bf16[2,8,128,128]{3,2,1,0:T(8,128)(2,1)S(1)}, bf16[2,8,128,128]{3,2,1,0:T(8,128)(2,1)}, u32[]{:S(2)}) copy-start(bf16[2,8,128,128]{3,2,1,0:T(8,128)(2,1)} %param.7) | copy-start | bytes 1572868
  0.0 22.5 %collective-permute-start.2 = (bf16[2048,128]{1,0:T(8,128)(2,1)}, bf16[2048,128]{1,0:T(8,128)(2,1)S(1)}, u32[]{:S(2)}, u32[]{:S(2)}) collective-permute-start(bf16[2048,128]{1,0:T(8,128)(2,1)} %bitcast.18), channel_id=1, source_target_pairs={{0,12},{1,3},{2,14},{3,1},{4,6},{5,9},{6,4},{7,11},{8,10},{9,5},{1... | collective-permute-start | bytes 1572872 | tf_op jit(solution)/shard_map/ppermute | solution.py:123
  5.1 0.9 %copy-start.1 = (bf16[2,4,128,128]{3,2,1,0:T(8,128)(2,1)S(1)}, bf16[2,4,128,128]{3,2,1,0:T(8,128)(2,1)}, u32[]{:S(2)}) copy-start(bf16[2,4,128,128]{3,2,1,0:T(8,128)(2,1)} %param.5) | copy-start | bytes 786436
  6.0 0.7 %copy-start.3 = (s32[2,6]{1,0:T(2,128)S(1)}, s32[2,6]{1,0:T(2,128)}, u32[]{:S(2)}) copy-start(s32[2,6]{1,0:T(2,128)} %refs_0_.7) | copy-start | bytes 148
  6.7 0.7 %copy-start.5 = (s32[2,4]{1,0:T(2,128)S(1)}, s32[2,4]{1,0:T(2,128)}, u32[]{:S(2)}) copy-start(s32[2,4]{1,0:T(2,128)} %refs_0_.5) | copy-start | bytes 100
  7.4 2.2 %copy-start.2 = (s32[2,8]{1,0:T(2,128)S(1)}, s32[2,8]{1,0:T(2,128)}, u32[]{:S(2)}) copy-start(s32[2,8]{1,0:T(2,128)} %refs_1_.5) | copy-start | bytes 196
  8.0 14.5 %collective-permute-start.1 = (bf16[1056,128]{1,0:T(8,128)(2,1)S(1)}, bf16[1056,128]{1,0:T(8,128)(2,1)S(1)}, u32[]{:S(2)}, u32[]{:S(2)}) collective-permute-start(bf16[1056,128]{1,0:T(8,128)(2,1)S(1)} %shard_map.56.refs_0_), channel_id=1, source_target_pairs={{0,4},{4,0},{8,12},{12,8},{1,5},{5,1},{9,13},{13,9},{2,6},{6,2},{1... | collective-permute-start | bytes 811016 | tf_op jit(solution)/shard_map/ppermute | solution.py:115
  8.0 16.0 %collective-permute-start.7 = (bf16[1056,128]{1,0:T(8,128)(2,1)S(1)}, bf16[1056,128]{1,0:T(8,128)(2,1)S(1)}, u32[]{:S(2)}, u32[]{:S(2)}) collective-permute-start(bf16[1056,128]{1,0:T(8,128)(2,1)S(1)} %shard_map.56.refs_0_), channel_id=1, source_target_pairs={{0,2},{1,3},{2,0},{3,1},{4,6},{5,7},{6,4},{7,5},{8,10},{9,11},{10,... | collective-permute-start | bytes 811016 | tf_op jit(solution)/shard_map/ppermute | solution.py:115
  9.6 16.0 %collective-permute-start.8 = (bf16[1056,128]{1,0:T(8,128)(2,1)S(1)}, bf16[1056,128]{1,0:T(8,128)(2,1)S(1)}, u32[]{:S(2)}, u32[]{:S(2)}) collective-permute-start(bf16[1056,128]{1,0:T(8,128)(2,1)S(1)} %shard_map.56.refs_0_), channel_id=1, source_target_pairs={{0,1},{1,0},{2,3},{3,2},{4,5},{5,4},{6,7},{7,6},{8,9},{9,8},{10,11... | collective-permute-start | bytes 811016 | tf_op jit(solution)/shard_map/ppermute | solution.py:115
  10.2 22.8 %collective-permute-start.6 = (bf16[2064,128]{1,0:T(8,128)(2,1)S(1)}, bf16[2064,128]{1,0:T(8,128)(2,1)S(1)}, u32[]{:S(2)}, u32[]{:S(2)}) collective-permute-start(bf16[2064,128]{1,0:T(8,128)(2,1)S(1)} %shard_map.55), channel_id=1, source_target_pairs={{0,1},{1,9},{2,3},{3,11},{4,12},{5,4},{6,14},{7,6},{8,0},{9,8},{10... | collective-permute-start | bytes 1585160 | tf_op jit(solution)/shard_map/ppermute | solution.py:123
  22.5 10.8 %collective-permute-start = (bf16[2064,128]{1,0:T(8,128)(2,1)S(1)}, bf16[2064,128]{1,0:T(8,128)(2,1)S(1)}, u32[]{:S(2)}, u32[]{:S(2)}) collective-permute-start(bf16[2064,128]{1,0:T(8,128)(2,1)S(1)} %shard_map.55), channel_id=1, source_target_pairs={{0,1},{1,5},{2,3},{3,7},{4,0},{5,4},{6,2},{7,6},{8,12},{9,8},{10,1... | collective-permute-start | bytes 1585160 | tf_op jit(solution)/shard_map/ppermute | solution.py:123
  22.5 6.5 %collective-permute-start.3 = (bf16[1056,128]{1,0:T(8,128)(2,1)S(1)}, bf16[1056,128]{1,0:T(8,128)(2,1)S(1)}, u32[]{:S(2)}, u32[]{:S(2)}) collective-permute-start(bf16[1056,128]{1,0:T(8,128)(2,1)S(1)} %collective-permute-done.1.refs_0_), channel_id=1, source_target_pairs={{0,2},{1,3},{2,0},{3,1},{4,6},{5,7},{6,4},{7,5},{8,10},{9,11},{10,... | collective-permute-start | bytes 811016 | tf_op jit(solution)/shard_map/ppermute | solution.py:115
  24.1 7.5 %collective-permute-start.10 = (s32[2,8]{1,0:T(2,128)S(1)}, s32[2,8]{1,0:T(2,128)S(1)}, u32[]{:S(2)}, u32[]{:S(2)}) collective-permute-start(s32[2,8]{1,0:T(2,128)S(1)} %copy-done.2), channel_id=1, source_target_pairs={{0,12},{4,8},{8,4},{12,0},{1,13},{5,9},{9,5},{13,1},{2,14},{6,10},... | collective-permute-start | bytes 200 | tf_op jit(solution)/shard_map/ppermute | solution.py:115
  25.6 3.6 %collective-permute-start.4 = (bf16[1056,128]{1,0:T(8,128)(2,1)S(1)}, bf16[1056,128]{1,0:T(8,128)(2,1)S(1)}, u32[]{:S(2)}, u32[]{:S(2)}) collective-permute-start(bf16[1056,128]{1,0:T(8,128)(2,1)S(1)} %collective-permute-done.1.refs_0_), channel_id=1, source_target_pairs={{0,1},{1,0},{2,3},{3,2},{4,5},{5,4},{6,7},{7,6},{8,9},{9,8},{10,11... | collective-permute-start | bytes 811016 | tf_op jit(solution)/shard_map/ppermute | solution.py:115
  29.0 1.5 %collective-permute-start.5 = (bf16[1056,128]{1,0:T(8,128)(2,1)S(1)}, bf16[1056,128]{1,0:T(8,128)(2,1)S(1)}, u32[]{:S(2)}, u32[]{:S(2)}) collective-permute-start(bf16[1056,128]{1,0:T(8,128)(2,1)S(1)} %collective-permute-done.3.refs_1_), channel_id=1, source_target_pairs={{0,1},{1,0},{2,3},{3,2},{4,5},{5,4},{6,7},{7,6},{8,9},{9,8},{10,11... | collective-permute-start | bytes 811016 | tf_op jit(solution)/shard_map/ppermute | solution.py:115
  29.2 11.0 %collective-permute-start.9 = (bf16[1056,128]{1,0:T(8,128)(2,1)S(1)}, bf16[1056,128]{1,0:T(8,128)(2,1)S(1)}, u32[]{:S(2)}, u32[]{:S(2)}) collective-permute-start(bf16[1056,128]{1,0:T(8,128)(2,1)S(1)} %collective-permute-done.7.refs_1_), channel_id=1, source_target_pairs={{0,1},{1,0},{2,3},{3,2},{4,5},{5,4},{6,7},{7,6},{8,9},{9,8},{10,11... | collective-permute-start | bytes 811016 | tf_op jit(solution)/shard_map/ppermute | solution.py:115
  34.7 9.5 %collective-permute-start.11 = (bf16[1,6,128,128]{3,2,1,0:T(8,128)(2,1)S(1)}, bf16[1,6,128,128]{3,2,1,0:T(8,128)(2,1)S(1)}, u32[]{:S(2)}, u32[]{:S(2)}) collective-permute-start(bf16[1,6,128,128]{3,2,1,0:T(8,128)(2,1)S(1)} %shard_map.62), channel_id=1, source_target_pairs={{0,4},{1,0},{2,6},{3,2},{4,5},{5,1},{6,7},{7,3},{8,9},{9,13},{10,1... | collective-permute-start | bytes 589832 | tf_op jit(solution)/shard_map/ppermute | solution.py:123
  39.1 5.1 %collective-permute-start.12 = (bf16[1,6,128,128]{3,2,1,0:T(8,128)(2,1)S(1)}, bf16[1,6,128,128]{3,2,1,0:T(8,128)(2,1)S(1)}, u32[]{:S(2)}, u32[]{:S(2)}) collective-permute-start(bf16[1,6,128,128]{3,2,1,0:T(8,128)(2,1)S(1)} %shard_map.63), channel_id=1, source_target_pairs={{0,4},{1,0},{2,6},{3,2},{4,5},{5,1},{6,7},{7,3},{8,9},{9,13},{10,1... | collective-permute-start | bytes 589832 | tf_op jit(solution)/shard_map/ppermute | solution.py:123
  40.3 0.9 %copy-start.4 = (s32[2,6]{1,0:T(2,128)S(1)}, s32[2,6]{1,0:T(2,128)}, u32[]{:S(2)}) copy-start(s32[2,6]{1,0:T(2,128)} %refs_0_.7) | copy-start | bytes 148

commit v12 on v10

--- a/solution.py
+++ b/solution.py
@@ -122,8 +122,9 @@
                 pairs.append((k * col_count + c, to * col_count + at))
         return lax.ppermute(x, ("row", "col"), pairs)
 
-    def deliver(x, d):
+    def deliver(x, dists):
         def target(k, c):
+            d = dists[c % 2]
             if parity(d):
                 return (k, c ^ 1) if works(k, c) else (k ^ d, c)
             return (k ^ d, c) if works(k, c) else (k, c ^ (col_count // 2))
@@ -154,18 +155,22 @@
             d //= 2
         return parts
 
-    far, end = col_count // 2, row_count - 1
+    odd = [d for d in range(1, row_count) if parity(d)]
+    deliveries = [(d, e) for d, e in zip(reversed(odd), odd)]
+    deliveries[1:1] = [(d, d) for d in range(row_count - 1, 0, -1) if not parity(d)]
+    start, far = deliveries[0], col_count // 2
     flat = b_tiles.reshape(-1, block)
     own, packed = pack(a_tiles, a_cols, c_cols), pack(b_tiles, b_cols)
-    shards = {0: flat, end: deliver(flat, end)}
-    cols = {0: (None, b_cols), end: (None, swap(b_cols, "row", row_count, end))}
+    shards = {(0, 0): flat, start: deliver(flat, start)}
     own_packs = [own, swap(own, "col", col_count, far)]
+    late_cols = lax.optimization_barrier((b_cols, own_packs[1]))[0]
+    cols = {(0, 0): (None, b_cols), start: (None, deliver(late_cols, start))}
     other = swap(own, "row", row_count, 1)
-    ready = lax.optimization_barrier((packed, own_packs[1]))[0]
-    for d in range(end - 1, 0, -1):
-        shards[d] = deliver(ready, d)
-    other = lax.optimization_barrier((other, shards[end]))[0]
+    for dists in deliveries[1:]:
+        shards[dists] = deliver(packed, dists)
+    other = lax.optimization_barrier((other, shards[start]))[0]
     own_packs, other_packs = across(own_packs, far // 2), across([other], far)
+
     def dense_of(packs):
         return pl.pallas_call(
             functools.partial(left_kernel, a_cols.shape[1]),
@@ -177,7 +182,8 @@
         )(index_of(packs, a_tiles), *packs)
 
     def step(dists, wanted, dense, before, span, last):
-        place = jnp.stack([jnp.where(working, first, -1)] + [r ^ d for d in dists]).astype(jnp.int32)
+        sources = [r ^ jnp.where(q % 2 == 0, d, e) for d, e in dists]
+        place = jnp.stack([jnp.where(working, first, -1)] + sources).astype(jnp.int32)
         if last:
             out = jax.ShapeDtypeStruct((len(span), slots, block, block), dtype)
         else:
@@ -196,15 +202,17 @@
             cost_estimate=FREE,
         )(place, wanted[1], *[cols[d][1] for d in dists], *[shards[d] for d in dists], *held)
 
-    order, every = list(range(1, end)) + [0, end], list(range(rows))
-    early, late = order[:-4], order[-4:]
-    for d in range(1, end):
-        cols[d] = (0, index_of([shards[d]], b_tiles))
+    order, every = [(0, 0)] + deliveries, list(range(rows))
+    early, late = order[:-2], order[-2:]
 
     def products(wanted, packs, spans):
         dense, total = dense_of(packs), None
-        for at in range(0, len(early), 4):
-            total = step(early[at : at + 4], wanted, dense, total, every, False)
+        for d in deliveries:
+            if d not in cols:
+                x = lax.optimization_barrier((shards[d], dense))[0] if d in late else shards[d]
+                cols[d] = (0, index_of([x], b_tiles))
+        for at in range(0, len(early), 2):
+            total = step(early[at : at + 2], wanted, dense, total, every, False)
         return [step(late, wanted, dense, total, span, True) for span in spans]
 
     given = products((a_cols.size, index_of([other], a_tiles)), other_packs, [[i] for i in every])

time: 40.5 us -> 44.3 us (1.094)
  starting transfers between devices: 10.5 us -> 15.8 us
  waiting for transfers between devices: 17.2 us -> 14.2 us
  Pallas kernels: 8.11 us -> 9.64 us
    ppermute x5 -> x6, waiting for transfers between devices: 3.85 us -> 0.02 us  [permute(): return lax.ppermute(x, ('row', 'col'), pairs)]
    ppermute x8 -> x7, starting transfers between devices: 5.22 us -> 8.96 us  [swap(): return lax.ppermute(x, axis, [(k, k ^ d) for k in range(n)])]
    ppermute x5 -> x6, starting transfers between devices: 5.25 us -> 6.81 us  [permute(): return lax.ppermute(x, ('row', 'col'), pairs)]
    pallas_call x3 -> x5, Pallas kernels: 5.15 us -> 6.68 us  [step(): pl.pallas_call(functools.partial(step_kernel, [wanted[0]] + [cols[d][0] f...]
    ppermute x8 -> x7, waiting for transfers between devices: 13.3 us -> 14.2 us  [swap(): return lax.ppermute(x, axis, [(k, k ^ d) for k in range(n)])]
  transfers between devices with their start and end apart: 13 -> 13, of which waited for: 5 -> 3; matrix products, arithmetic and copies ran while one was open for 3% -> 3% of each run, Pallas kernels for 20% -> 22%
where the time goes in v12:
time: 44.3 us; the launch traced here: 44.2 us
  starting transfers between devices  15.8 us (36%)
  waiting for transfers between devices  14.2 us (32%)
  Pallas kernels  9.64 us (22%)
  local copies, waits for them, and re-layouts  3.21 us (7%)
  other arithmetic  1.14 us (3%)
    ppermute x7, waiting for transfers between devices, swap(): return lax.ppermute(x, axis, [(k, k ^ d) for k in range(n)])  14.2 us
    ppermute x7, starting transfers between devices, swap(): return lax.ppermute(x, axis, [(k, k ^ d) for k in range(n)])  8.96 us
    ppermute x6, starting transfers between devices, permute(): return lax.ppermute(x, ('row', 'col'), pairs)  6.81 us
    pallas_call x5, Pallas kernels, step(): pl.pallas_call(functools.partial(step_kernel, [wanted[0]] + [cols[d][0] f...  6.68 us
    unnamed x12, local copies, waits for them, and re-layouts  2.32 us
    pallas_call x2, Pallas kernels, dense_of(): pl.pallas_call(functools.partial(left_kernel, a_cols.shape[1]), out_shape...  1.79 us
    pallas_call x2, Pallas kernels, pack(): pl.pallas_call(pack_kernel, out_shape=jax.ShapeDtypeStruct((size + -(-cou...  1.17 us
  transfers between devices with their start and end apart: 13, of which 3 were waited for; matrix products, arithmetic and copies ran while one was open for 3% of the time, Pallas kernels for 22%

profile of v12, /device:TPU:0, one launch (start us, length us, event | category | flops | bytes accessed | tf_op | source)
XLA Modules:
  0.0 44.2 jit_solution(4987303900937749699)
XLA Ops:
  0.0 0.5 %collective-permute-start.2 = (bf16[2048,128]{1,0:T(8,128)(2,1)}, bf16[2048,128]{1,0:T(8,128)(2,1)S(1)}, u32[]{:S(2)}, u32[]{:S(2)}) collective-permute-start(bf16[2048,128]{1,0:T(8,128)(2,1)} %bitcast.18), channel_id=1, source_target_pairs={{0,1},{1,5},{2,3},{3,7},{4,12},{5,4},{6,14},{7,6},{8,0},{9,8},{10,... | collective-permute-start | bytes 1572872 | tf_op jit(solution)/shard_map/ppermute | solution.py:123
  0.5 0.9 %copy-done.1 = bf16[2,4,128,128]{3,2,1,0:T(8,128)(2,1)S(1)} copy-done((bf16[2,4,128,128]{3,2,1,0:T(8,128)(2,1)S(1)}, bf16[2,4,128,128]{3,2,1,0:T(8,128)(2,1)}, u32[]{:S(2)}) %copy-start.1) | copy-done | bytes 262168
  1.4 0.7 %copy-done.3 = s32[2,6]{1,0:T(2,128)S(1)} copy-done((s32[2,6]{1,0:T(2,128)S(1)}, s32[2,6]{1,0:T(2,128)}, u32[]{:S(2)}) %copy-start.3) | copy-done | bytes 72
  2.1 0.7 %copy-done.5 = s32[2,4]{1,0:T(2,128)S(1)} copy-done((s32[2,4]{1,0:T(2,128)S(1)}, s32[2,4]{1,0:T(2,128)}, u32[]{:S(2)}) %copy-start.5) | copy-done | bytes 56
  2.8 0.6 %shard_map.56.refs_0_ = bf16[1056,128]{1,0:T(8,128)(2,1)S(1)} custom-call(s32[2,4]{1,0:T(2,128)S(1)} %copy-done.5, s32[2,6]{1,0:T(2,128)S(1)} %copy-done.3, bf16[1024,128]{1,0:T(8,128)(2,1)S(1)} %bitcast.22), custom_call_target="tpu_custom_call" | custom-call | flops 1 | bytes 1 | tf_op jit(solution)/shard_map/pallas_call | solution.py:140
  3.4 5.2 %collective-permute-start.1 = (bf16[1056,128]{1,0:T(8,128)(2,1)S(1)}, bf16[1056,128]{1,0:T(8,128)(2,1)S(1)}, u32[]{:S(2)}, u32[]{:S(2)}) collective-permute-start(bf16[1056,128]{1,0:T(8,128)(2,1)S(1)} %shard_map.56.refs_0_), channel_id=1, source_target_pairs={{0,4},{4,0},{8,12},{12,8},{1,5},{5,1},{9,13},{13,9},{2,6},{6,2},{1... | collective-permute-start | bytes 811016 | tf_op jit(solution)/shard_map/ppermute | solution.py:115
  8.6 1.5 %collective-permute-start.7 = (bf16[1056,128]{1,0:T(8,128)(2,1)S(1)}, bf16[1056,128]{1,0:T(8,128)(2,1)S(1)}, u32[]{:S(2)}, u32[]{:S(2)}) collective-permute-start(bf16[1056,128]{1,0:T(8,128)(2,1)S(1)} %shard_map.56.refs_0_), channel_id=1, source_target_pairs={{0,2},{1,3},{2,0},{3,1},{4,6},{5,7},{6,4},{7,5},{8,10},{9,11},{10,... | collective-permute-start | bytes 811016 | tf_op jit(solution)/shard_map/ppermute | solution.py:115
  10.1 0.6 %shard_map.55 = bf16[2064,128]{1,0:T(8,128)(2,1)S(1)} custom-call(s32[2,8]{1,0:T(2,128)S(1)} %copy-done.2, bf16[2048,128]{1,0:T(8,128)(2,1)S(1)} %bitcast.19), custom_call_target="tpu_custom_call" | custom-call | flops 1 | bytes 1 | tf_op jit(solution)/shard_map/pallas_call | solution.py:140
  10.7 0.6 %collective-permute-start.6 = (bf16[2064,128]{1,0:T(8,128)(2,1)S(1)}, bf16[2064,128]{1,0:T(8,128)(2,1)S(1)}, u32[]{:S(2)}, u32[]{:S(2)}) collective-permute-start(bf16[2064,128]{1,0:T(8,128)(2,1)S(1)} %shard_map.55), channel_id=1, source_target_pairs={{0,1},{1,9},{2,3},{3,11},{4,0},{5,4},{6,2},{7,6},{8,12},{9,8},{10,... | collective-permute-start | bytes 1585160 | tf_op jit(solution)/shard_map/ppermute | solution.py:123
  11.2 0.1 slice_reduce_fusion.3
  11.4 5.9 %collective-permute-done.1.refs_0_ = bf16[1056,128]{1,0:T(8,128)(2,1)S(1)} collective-permute-done((bf16[1056,128]{1,0:T(8,128)(2,1)S(1)}, bf16[1056,128]{1,0:T(8,128)(2,1)S(1)}, u32[]{:S(2)}, u32[]{:S(2)}) %collective-permute-start.1) | collective-permute-done | bytes 270368 | tf_op jit(solution)/shard_map/ppermute | solution.py:115
  17.3 3.9 %collective-permute-start = (bf16[2064,128]{1,0:T(8,128)(2,1)S(1)}, bf16[2064,128]{1,0:T(8,128)(2,1)S(1)}, u32[]{:S(2)}, u32[]{:S(2)}) collective-permute-start(bf16[2064,128]{1,0:T(8,128)(2,1)S(1)} %shard_map.55), channel_id=1, source_target_pairs={{0,12},{1,3},{2,14},{3,1},{4,6},{5,9},{6,4},{7,11},{8,10},{9,5},{1... | collective-permute-start | bytes 1585160 | tf_op jit(solution)/shard_map/ppermute | solution.py:123
  21.1 1.5 %collective-permute-start.3 = (bf16[1056,128]{1,0:T(8,128)(2,1)S(1)}, bf16[1056,128]{1,0:T(8,128)(2,1)S(1)}, u32[]{:S(2)}, u32[]{:S(2)}) collective-permute-start(bf16[1056,128]{1,0:T(8,128)(2,1)S(1)} %collective-permute-done.1.refs_0_), channel_id=1, source_target_pairs={{0,2},{1,3},{2,0},{3,1},{4,6},{5,7},{6,4},{7,5},{8,10},{9,11},{10,... | collective-permute-start | bytes 811016 | tf_op jit(solution)/shard_map/ppermute | solution.py:115
  22.7 0.1 slice_reduce_fusion.2
  22.9 0.1 slice_reduce_fusion.1
  23.0 7.5 %collective-permute-done.3.refs_1_ = bf16[1056,128]{1,0:T(8,128)(2,1)S(1)} collective-permute-done((bf16[1056,128]{1,0:T(8,128)(2,1)S(1)}, bf16[1056,128]{1,0:T(8,128)(2,1)S(1)}, u32[]{:S(2)}, u32[]{:S(2)}) %collective-permute-start.3) | collective-permute-done | bytes 270368 | tf_op jit(solution)/shard_map/ppermute | solution.py:115
  30.6 0.6 %collective-permute-start.5 = (bf16[1056,128]{1,0:T(8,128)(2,1)S(1)}, bf16[1056,128]{1,0:T(8,128)(2,1)S(1)}, u32[]{:S(2)}, u32[]{:S(2)}) collective-permute-start(bf16[1056,128]{1,0:T(8,128)(2,1)S(1)} %collective-permute-done.3.refs_1_), channel_id=1, source_target_pairs={{0,1},{1,0},{2,3},{3,2},{4,5},{5,4},{6,7},{7,6},{8,9},{9,8},{10,11... | collective-permute-start | bytes 811016 | tf_op jit(solution)/shard_map/ppermute | solution.py:115
  31.3 0.1 slice_reduce_fusion.6
  31.5 0.1 slice_reduce_fusion.5
  31.6 0.7 %collective-permute-done.5.refs_3_ = bf16[1056,128]{1,0:T(8,128)(2,1)S(1)} collective-permute-done((bf16[1056,128]{1,0:T(8,128)(2,1)S(1)}, bf16[1056,128]{1,0:T(8,128)(2,1)S(1)}, u32[]{:S(2)}, u32[]{:S(2)}) %collective-permute-start.5) | collective-permute-done | bytes 270368 | tf_op jit(solution)/shard_map/ppermute | solution.py:115
  32.5 0.9 %shard_map.57.refs_5_ = bf16[2,8,128,128]{3,2,1,0:T(8,128)(2,1)S(1)} custom-call(s32[4,32]{1,0:T(4,128)S(1)} %maximum_convert_fusion.index, bf16[1056,128]{1,0:T(8,128)(2,1)S(1)} %collective-permute-done.1.refs_0_, bf16[1056,128]{1,0:T(8,128)(2,1)S(1)} %collective-permute-done.3.refs_1_, bf16[1056,128]{1,0:T(8,128)(2,1)S(1)} %collective-permute-done.4.refs_2_, ...), custom_call_target="tpu_custom_call" | custom-call | flops 1 | bytes 1 | tf_op jit(solution)/shard_map/pallas_call | solution.py:175
  33.4 1.5 %shard_map.61.refs_6_ = f32[2,128,768]{2,1,0:T(8,128)S(1)} custom-call(s32[3]{0:T(128)S(1)} %get-tuple-element.14.place, s32[1,32]{1,0:T(1,128)S(1)} %bitcast_convert_fusion.refs_0_, s32[2,8]{1,0:T(2,128)S(1)} %copy-done.2, s32[2,8]{1,0:T(2,128)S(1)} %collective-permute-done.10.refs_2_, bf16[2048,128]{1,0:T(8,128)(2,1)S(1)} %bitcast.20, ...), custom_call_target="tpu_custom_call" | custom-call | flops 1 | bytes 1 | tf_op jit(solution)/shard_map/pallas_call | solution.py:192
  34.9 0.1 convert_reduce_fusion
  35.0 0.1 convert_reduce_fusion.1
  35.1 1.1 %shard_map.62 = bf16[1,6,128,128]{3,2,1,0:T(8,128)(2,1)S(1)} custom-call(s32[3]{0:T(128)S(1)} %get-tuple-element.13.place, s32[1,32]{1,0:T(1,128)S(1)} %bitcast_convert_fusion.refs_0_, s32[1,16]{1,0:T(1,128)S(1)} %bitcast.26, s32[1,16]{1,0:T(1,128)S(1)} %bitcast.23, bf16[2064,128]{1,0:T(8,128)(2,1)S(1)} %collective-permute-done.refs_3_, ...), custom_call_target="tpu_custom_call" | custom-call | flops 1 | bytes 1 | tf_op jit(solution)/shard_map/pallas_call | solution.py:192
  36.3 0.9 %collective-permute-start.11 = (bf16[1,6,128,128]{3,2,1,0:T(8,128)(2,1)S(1)}, bf16[1,6,128,128]{3,2,1,0:T(8,128)(2,1)S(1)}, u32[]{:S(2)}, u32[]{:S(2)}) collective-permute-start(bf16[1,6,128,128]{3,2,1,0:T(8,128)(2,1)S(1)} %shard_map.62), channel_id=1, source_target_pairs={{0,4},{1,0},{2,6},{3,2},{4,5},{5,1},{6,7},{7,3},{8,9},{9,13},{10,1... | collective-permute-start | bytes 589832 | tf_op jit(solution)/shard_map/ppermute | solution.py:123
  37.1 1.1 %shard_map.63 = bf16[1,6,128,128]{3,2,1,0:T(8,128)(2,1)S(1)} custom-call(s32[3]{0:T(128)S(1)} %get-tuple-element.13.place, s32[1,32]{1,0:T(1,128)S(1)} %bitcast_convert_fusion.refs_0_, s32[1,16]{1,0:T(1,128)S(1)} %bitcast.27, s32[1,16]{1,0:T(1,128)S(1)} %bitcast.24, bf16[2064,128]{1,0:T(8,128)(2,1)S(1)} %collective-permute-done.refs_3_, ...), custom_call_target="tpu_custom_call" | custom-call | flops 1 | bytes 1 | tf_op jit(solution)/shard_map/pallas_call | solution.py:192
  38.3 1.1 %collective-permute-start.12 = (bf16[1,6,128,128]{3,2,1,0:T(8,128)(2,1)S(1)}, bf16[1,6,128,128]{3,2,1,0:T(8,128)(2,1)S(1)}, u32[]{:S(2)}, u32[]{:S(2)}) collective-permute-start(bf16[1,6,128,128]{3,2,1,0:T(8,128)(2,1)S(1)} %shard_map.63), channel_id=1, source_target_pairs={{0,4},{1,0},{2,6},{3,2},{4,5},{5,1},{6,7},{7,3},{8,9},{9,13},{10,1... | collective-permute-start | bytes 589832 | tf_op jit(solution)/shard_map/ppermute | solution.py:123
  39.5 0.9 %shard_map.58.refs_5_ = bf16[2,8,128,128]{3,2,1,0:T(8,128)(2,1)S(1)} custom-call(s32[4,32]{1,0:T(4,128)S(1)} %maximum_convert_fusion.1.index, bf16[1056,128]{1,0:T(8,128)(2,1)S(1)} %shard_map.56.refs_0_, bf16[1056,128]{1,0:T(8,128)(2,1)S(1)} %collective-permute-done.7.refs_1_, bf16[1056,128]{1,0:T(8,128)(2,1)S(1)} %collective-permute-done.8.refs_2_, ...), custom_call_target="tpu_custom_call" | custom-call | flops 1 | bytes 1 | tf_op jit(solution)/shard_map/pallas_call | solution.py:175
  40.4 1.5 %shard_map.59.refs_6_ = f32[2,128,768]{2,1,0:T(8,128)S(1)} custom-call(s32[3]{0:T(128)S(1)} %get-tuple-element.14.place, s32[2,6]{1,0:T(2,128)S(1)} %copy-done.4, s32[2,8]{1,0:T(2,128)S(1)} %copy-done.2, s32[2,8]{1,0:T(2,128)S(1)} %collective-permute-done.10.refs_2_, bf16[2048,128]{1,0:T(8,128)(2,1)S(1)} %bitcast.21, ...), custom_call_target="tpu_custom_call" | custom-call | flops 1 | bytes 1 | tf_op jit(solution)/shard_map/pallas_call | solution.py:192
  41.9 1.5 %shard_map.60 = bf16[2,6,128,128]{3,2,1,0:T(8,128)(2,1)S(1)} custom-call(s32[3]{0:T(128)S(1)} %get-tuple-element.13.place, s32[2,6]{1,0:T(2,128)S(1)} %copy-done.4, s32[1,16]{1,0:T(1,128)S(1)} %bitcast.28, s32[1,16]{1,0:T(1,128)S(1)} %bitcast.25, bf16[2064,128]{1,0:T(8,128)(2,1)S(1)} %collective-permute-done.refs_3_, ...), custom_call_target="tpu_custom_call" | custom-call | flops 1 | bytes 1 | tf_op jit(solution)/shard_map/pallas_call | solution.py:192
  43.4 0.8 %maximum_select_fusion = bf16[2,6,128,128]{3,2,1,0:T(8,128)(2,1)} fusion(bf16[2,6,128,128]{3,2,1,0:T(8,128)(2,1)S(1)} %shard_map.60, bf16[1,6,128,128]{3,2,1,0:T(8,128)(2,1)S(1)} %collective-permute-done.12, bf16[1,6,128,128]{3,2,1,0:T(8,128)(2,1)S(1)} %collective-permute-done.11, pred[]{:T(512)S(6)} %eq.27), kind=kLoop, calls=%fused_computation | loop fusion | flops 393216 | bytes 1179649 | tf_op jit(solution)/shard_map/jit(_where)/select_n | solution.py:221
  (30 shorter events, 0.6 us)
Async XLA Ops:
  0.0 10.1 %copy-start = (bf16[2,8,128,128]{3,2,1,0:T(8,128)(2,1)S(1)}, bf16[2,8,128,128]{3,2,1,0:T(8,128)(2,1)}, u32[]{:S(2)}) copy-start(bf16[2,8,128,128]{3,2,1,0:T(8,128)(2,1)} %param.7) | copy-start | bytes 1572868
  0.0 21.1 %collective-permute-start.2 = (bf16[2048,128]{1,0:T(8,128)(2,1)}, bf16[2048,128]{1,0:T(8,128)(2,1)S(1)}, u32[]{:S(2)}, u32[]{:S(2)}) collective-permute-start(bf16[2048,128]{1,0:T(8,128)(2,1)} %bitcast.18), channel_id=1, source_target_pairs={{0,1},{1,5},{2,3},{3,7},{4,12},{5,4},{6,14},{7,6},{8,0},{9,8},{10,... | collective-permute-start | bytes 1572872 | tf_op jit(solution)/shard_map/ppermute | solution.py:123
  0.5 0.9 %copy-start.1 = (bf16[2,4,128,128]{3,2,1,0:T(8,128)(2,1)S(1)}, bf16[2,4,128,128]{3,2,1,0:T(8,128)(2,1)}, u32[]{:S(2)}) copy-start(bf16[2,4,128,128]{3,2,1,0:T(8,128)(2,1)} %param.5) | copy-start | bytes 786436
  1.4 0.7 %copy-start.3 = (s32[2,6]{1,0:T(2,128)S(1)}, s32[2,6]{1,0:T(2,128)}, u32[]{:S(2)}) copy-start(s32[2,6]{1,0:T(2,128)} %refs_0_.7) | copy-start | bytes 148
  2.1 0.7 %copy-start.5 = (s32[2,4]{1,0:T(2,128)S(1)}, s32[2,4]{1,0:T(2,128)}, u32[]{:S(2)}) copy-start(s32[2,4]{1,0:T(2,128)} %refs_0_.5) | copy-start | bytes 100
  2.8 7.3 %copy-start.2 = (s32[2,8]{1,0:T(2,128)S(1)}, s32[2,8]{1,0:T(2,128)}, u32[]{:S(2)}) copy-start(s32[2,8]{1,0:T(2,128)} %refs_1_.5) | copy-start | bytes 196
  3.4 13.9 %collective-permute-start.1 = (bf16[1056,128]{1,0:T(8,128)(2,1)S(1)}, bf16[1056,128]{1,0:T(8,128)(2,1)S(1)}, u32[]{:S(2)}, u32[]{:S(2)}) collective-permute-start(bf16[1056,128]{1,0:T(8,128)(2,1)S(1)} %shard_map.56.refs_0_), channel_id=1, source_target_pairs={{0,4},{4,0},{8,12},{12,8},{1,5},{5,1},{9,13},{13,9},{2,6},{6,2},{1... | collective-permute-start | bytes 811016 | tf_op jit(solution)/shard_map/ppermute | solution.py:115
  8.6 14.1 %collective-permute-start.7 = (bf16[1056,128]{1,0:T(8,128)(2,1)S(1)}, bf16[1056,128]{1,0:T(8,128)(2,1)S(1)}, u32[]{:S(2)}, u32[]{:S(2)}) collective-permute-start(bf16[1056,128]{1,0:T(8,128)(2,1)S(1)} %shard_map.56.refs_0_), channel_id=1, source_target_pairs={{0,2},{1,3},{2,0},{3,1},{4,6},{5,7},{6,4},{7,5},{8,10},{9,11},{10,... | collective-permute-start | bytes 811016 | tf_op jit(solution)/shard_map/ppermute | solution.py:115
  10.1 12.8 %collective-permute-start.8 = (bf16[1056,128]{1,0:T(8,128)(2,1)S(1)}, bf16[1056,128]{1,0:T(8,128)(2,1)S(1)}, u32[]{:S(2)}, u32[]{:S(2)}) collective-permute-start(bf16[1056,128]{1,0:T(8,128)(2,1)S(1)} %shard_map.56.refs_0_), channel_id=1, source_target_pairs={{0,1},{1,0},{2,3},{3,2},{4,5},{5,4},{6,7},{7,6},{8,9},{9,8},{10,11... | collective-permute-start | bytes 811016 | tf_op jit(solution)/shard_map/ppermute | solution.py:115
  10.7 24.2 %collective-permute-start.6 = (bf16[2064,128]{1,0:T(8,128)(2,1)S(1)}, bf16[2064,128]{1,0:T(8,128)(2,1)S(1)}, u32[]{:S(2)}, u32[]{:S(2)}) collective-permute-start(bf16[2064,128]{1,0:T(8,128)(2,1)S(1)} %shard_map.55), channel_id=1, source_target_pairs={{0,1},{1,9},{2,3},{3,11},{4,0},{5,4},{6,2},{7,6},{8,12},{9,8},{10,... | collective-permute-start | bytes 1585160 | tf_op jit(solution)/shard_map/ppermute | solution.py:123
  17.3 17.6 %collective-permute-start = (bf16[2064,128]{1,0:T(8,128)(2,1)S(1)}, bf16[2064,128]{1,0:T(8,128)(2,1)S(1)}, u32[]{:S(2)}, u32[]{:S(2)}) collective-permute-start(bf16[2064,128]{1,0:T(8,128)(2,1)S(1)} %shard_map.55), channel_id=1, source_target_pairs={{0,12},{1,3},{2,14},{3,1},{4,6},{5,9},{6,4},{7,11},{8,10},{9,5},{1... | collective-permute-start | bytes 1585160 | tf_op jit(solution)/shard_map/ppermute | solution.py:123
  21.1 9.4 %collective-permute-start.3 = (bf16[1056,128]{1,0:T(8,128)(2,1)S(1)}, bf16[1056,128]{1,0:T(8,128)(2,1)S(1)}, u32[]{:S(2)}, u32[]{:S(2)}) collective-permute-start(bf16[1056,128]{1,0:T(8,128)(2,1)S(1)} %collective-permute-done.1.refs_0_), channel_id=1, source_target_pairs={{0,2},{1,3},{2,0},{3,1},{4,6},{5,7},{6,4},{7,5},{8,10},{9,11},{10,... | collective-permute-start | bytes 811016 | tf_op jit(solution)/shard_map/ppermute | solution.py:115
  22.7 10.7 %collective-permute-start.10 = (s32[2,8]{1,0:T(2,128)S(1)}, s32[2,8]{1,0:T(2,128)S(1)}, u32[]{:S(2)}, u32[]{:S(2)}) collective-permute-start(s32[2,8]{1,0:T(2,128)S(1)} %copy-done.2), channel_id=1, source_target_pairs={{0,1},{1,5},{2,3},{3,7},{4,12},{5,4},{6,14},{7,6},{8,0},{9,8},{10,... | collective-permute-start | bytes 200 | tf_op jit(solution)/shard_map/ppermute | solution.py:123
  22.9 8.5 %collective-permute-start.4 = (bf16[1056,128]{1,0:T(8,128)(2,1)S(1)}, bf16[1056,128]{1,0:T(8,128)(2,1)S(1)}, u32[]{:S(2)}, u32[]{:S(2)}) collective-permute-start(bf16[1056,128]{1,0:T(8,128)(2,1)S(1)} %collective-permute-done.1.refs_0_), channel_id=1, source_target_pairs={{0,1},{1,0},{2,3},{3,2},{4,5},{5,4},{6,7},{7,6},{8,9},{9,8},{10,11... | collective-permute-start | bytes 811016 | tf_op jit(solution)/shard_map/ppermute | solution.py:115
  30.6 1.8 %collective-permute-start.5 = (bf16[1056,128]{1,0:T(8,128)(2,1)S(1)}, bf16[1056,128]{1,0:T(8,128)(2,1)S(1)}, u32[]{:S(2)}, u32[]{:S(2)}) collective-permute-start(bf16[1056,128]{1,0:T(8,128)(2,1)S(1)} %collective-permute-done.3.refs_1_), channel_id=1, source_target_pairs={{0,1},{1,0},{2,3},{3,2},{4,5},{5,4},{6,7},{7,6},{8,9},{9,8},{10,11... | collective-permute-start | bytes 811016 | tf_op jit(solution)/shard_map/ppermute | solution.py:115
  31.4 7.9 %collective-permute-start.9 = (bf16[1056,128]{1,0:T(8,128)(2,1)S(1)}, bf16[1056,128]{1,0:T(8,128)(2,1)S(1)}, u32[]{:S(2)}, u32[]{:S(2)}) collective-permute-start(bf16[1056,128]{1,0:T(8,128)(2,1)S(1)} %collective-permute-done.7.refs_1_), channel_id=1, source_target_pairs={{0,1},{1,0},{2,3},{3,2},{4,5},{5,4},{6,7},{7,6},{8,9},{9,8},{10,11... | collective-permute-start | bytes 811016 | tf_op jit(solution)/shard_map/ppermute | solution.py:115
  36.3 7.1 %collective-permute-start.11 = (bf16[1,6,128,128]{3,2,1,0:T(8,128)(2,1)S(1)}, bf16[1,6,128,128]{3,2,1,0:T(8,128)(2,1)S(1)}, u32[]{:S(2)}, u32[]{:S(2)}) collective-permute-start(bf16[1,6,128,128]{3,2,1,0:T(8,128)(2,1)S(1)} %shard_map.62), channel_id=1, source_target_pairs={{0,4},{1,0},{2,6},{3,2},{4,5},{5,1},{6,7},{7,3},{8,9},{9,13},{10,1... | collective-permute-start | bytes 589832 | tf_op jit(solution)/shard_map/ppermute | solution.py:123
  38.3 5.1 %collective-permute-start.12 = (bf16[1,6,128,128]{3,2,1,0:T(8,128)(2,1)S(1)}, bf16[1,6,128,128]{3,2,1,0:T(8,128)(2,1)S(1)}, u32[]{:S(2)}, u32[]{:S(2)}) collective-permute-start(bf16[1,6,128,128]{3,2,1,0:T(8,128)(2,1)S(1)} %shard_map.63), channel_id=1, source_target_pairs={{0,4},{1,0},{2,6},{3,2},{4,5},{5,1},{6,7},{7,3},{8,9},{9,13},{10,1... | collective-permute-start | bytes 589832 | tf_op jit(solution)/shard_map/ppermute | solution.py:123
  39.5 0.9 %copy-start.4 = (s32[2,6]{1,0:T(2,128)S(1)}, s32[2,6]{1,0:T(2,128)}, u32[]{:S(2)}) copy-start(s32[2,6]{1,0:T(2,128)} %refs_0_.7) | copy-start | bytes 148

commit v13 on v10

--- a/solution.py
+++ b/solution.py
@@ -30,19 +30,18 @@
     out[size:, :] = found.astype(out.dtype)
 
 
-def left_kernel(slots, index, *refs):
+def left_kernel(group, index, *refs):
     parts, dense = refs[:-1], refs[-1]
     dense[...] = jnp.zeros_like(dense)
-    rows, _, block, _ = dense.shape
+    rows, slots = parts[0].shape[:2]
     for p, part in enumerate(parts):
         for i in range(rows):
             for s in range(slots):
-                inner = index[p, i * slots + s]
-                start = (i * slots + s) * block
+                inner = index[(2 * p + group) * rows + i, s]
 
                 @pl.when(inner >= 0)
                 def _():
-                    dense[i, inner] = part[start : start + block, :]
+                    dense[i, inner] = part[i, s]
 
 
 def step_kernel(starts, span, last, place, *refs):
@@ -61,7 +60,7 @@
         inner_slots = tiles[0].shape[0] // block // inner_rows
 
         def read(ref, start, i, k, width):
-            return ref[i, k] if start is None else ref[0, start + i * width + k]
+            return ref[start[0] + i, start[1] + k] if isinstance(start, tuple) else ref[0, start + i * width + k]
 
         sums = {i: None if before is None else before[i] for i in span}
         for p in range(parts):
@@ -155,26 +154,33 @@
         return parts
 
     far, end = col_count // 2, row_count - 1
-    flat = b_tiles.reshape(-1, block)
-    own, packed = pack(a_tiles, a_cols, c_cols), pack(b_tiles, b_cols)
+    flat, packed = b_tiles.reshape(-1, block), pack(b_tiles, b_cols)
+    index = jnp.concatenate([a_cols, c_cols], axis=1)
+    index = jnp.concatenate([index, swap(index, "row", row_count, 1)], axis=0)
+    other = swap(a_tiles, "row", row_count, 1)
     shards = {0: flat, end: deliver(flat, end)}
-    cols = {0: (None, b_cols), end: (None, swap(b_cols, "row", row_count, end))}
-    own_packs = [own, swap(own, "col", col_count, far)]
-    other = swap(own, "row", row_count, 1)
-    ready = lax.optimization_barrier((packed, own_packs[1]))[0]
+    late_a, late_cols = lax.optimization_barrier((a_tiles, b_cols, other))[:2]
+    cols = {0: ((0, 0), b_cols), end: ((0, 0), swap(late_cols, "row", row_count, end))}
     for d in range(end - 1, 0, -1):
-        shards[d] = deliver(ready, d)
-    other = lax.optimization_barrier((other, shards[end]))[0]
-    own_packs, other_packs = across(own_packs, far // 2), across([other], far)
-    def dense_of(packs):
+        shards[d] = deliver(packed, d)
+    own_parts = across([late_a], far)
+    other_parts = [other, swap(other, "col", col_count, far)]
+    other_parts = list(lax.optimization_barrier((other_parts, shards[end]))[0])
+    other_parts = across(other_parts, far // 2)
+    around, d = index, far
+    while d:
+        around = jnp.concatenate([around, swap(around, "col", col_count, d)], axis=0)
+        d //= 2
+
+    def dense_of(group, parts):
         return pl.pallas_call(
-            functools.partial(left_kernel, a_cols.shape[1]),
+            functools.partial(left_kernel, group),
             out_shape=jax.ShapeDtypeStruct((rows, inner_rows * row_count, block, block), dtype),
-            in_specs=[SMEM] + [VMEM] * len(packs),
+            in_specs=[SMEM] + [VMEM] * len(parts),
             out_specs=VMEM,
             compiler_params=PARAMS,
             cost_estimate=FREE,
-        )(index_of(packs, a_tiles), *packs)
+        )(around, *parts)
 
     def step(dists, wanted, dense, before, span, last):
         place = jnp.stack([jnp.where(working, first, -1)] + [r ^ d for d in dists]).astype(jnp.int32)
@@ -196,20 +202,22 @@
             cost_estimate=FREE,
         )(place, wanted[1], *[cols[d][1] for d in dists], *[shards[d] for d in dists], *held)
 
-    order, every = list(range(1, end)) + [0, end], list(range(rows))
-    early, late = order[:-4], order[-4:]
-    for d in range(1, end):
-        cols[d] = (0, index_of([shards[d]], b_tiles))
-
-    def products(wanted, packs, spans):
-        dense, total = dense_of(packs), None
-        for at in range(0, len(early), 4):
-            total = step(early[at : at + 4], wanted, dense, total, every, False)
+    order, every = [0] + list(range(end, 0, -1)), list(range(rows))
+    early, late = order[:-2], order[-2:]
+
+    def products(wanted, dense, spans):
+        total = None
+        for d in range(1, end):
+            if d not in cols:
+                x = lax.optimization_barrier((shards[d], dense))[0] if d in late else shards[d]
+                cols[d] = (0, index_of([x], b_tiles))
+        for at in range(0, len(early), 2):
+            total = step(early[at : at + 2], wanted, dense, total, every, False)
         return [step(late, wanted, dense, total, span, True) for span in spans]
 
-    given = products((a_cols.size, index_of([other], a_tiles)), other_packs, [[i] for i in every])
+    given = products(((rows, a_cols.shape[1]), index), dense_of(1, other_parts), [[i] for i in every])
     given = [give_back(x) for x in given]
-    (kept,) = products((None, c_cols), own_packs, [every])
+    (kept,) = products(((0, 0), c_cols), dense_of(0, own_parts), [every])
     return jnp.where(working, kept, jnp.concatenate(given, axis=0))
 
 

time: 40.5 us -> 51 us (1.26)
  starting transfers between devices: 10.5 us -> 16.7 us
  waiting for transfers between devices: 17.2 us -> 21.9 us
  local copies, waits for them, and re-layouts: 3.29 us -> 1.09 us
  Pallas kernels: 8.11 us -> 9.61 us
    ppermute x8 -> x11, starting transfers between devices: 5.22 us -> 14 us  [swap(): return lax.ppermute(x, axis, [(k, k ^ d) for k in range(n)])]
    ppermute x8 -> x11, waiting for transfers between devices: 13.3 us -> 21.9 us  [swap(): return lax.ppermute(x, axis, [(k, k ^ d) for k in range(n)])]
    ppermute x5, waiting for transfers between devices: 3.85 us -> 0.06 us  [permute(): return lax.ppermute(x, ('row', 'col'), pairs)]
    ppermute x5, starting transfers between devices: 5.25 us -> 2.68 us  [permute(): return lax.ppermute(x, ('row', 'col'), pairs)]
    pallas_call x3 -> x5, Pallas kernels: 5.15 us -> 6.74 us  [step(): pl.pallas_call(functools.partial(step_kernel, [wanted[0]] + [cols[d][0] f...]
    unnamed x12, local copies, waits for them, and re-layouts: 2.32 us -> 1.09 us
    slice x8 -> x0, local copies, waits for them, and re-layouts: 0.89 us -> none  [index_of(): x[tiles.size // block:, 0]]
    pallas_call x2 -> x1, Pallas kernels: 1.17 us -> 0.58 us  [pack(): pl.pallas_call(pack_kernel, out_shape=jax.ShapeDtypeStruct((size + -(-cou...]
  transfers between devices with their start and end apart: 13 -> 16, of which waited for: 5 -> 5; matrix products, arithmetic and copies ran while one was open for 3% -> 1% of each run, Pallas kernels for 20% -> 19%
where the time goes in v13:
time: 51 us; the launch traced here: 50.8 us
  waiting for transfers between devices  21.9 us (43%)
  starting transfers between devices  16.7 us (33%)
  Pallas kernels  9.61 us (19%)
  other arithmetic  1.41 us (3%)
  local copies, waits for them, and re-layouts  1.09 us (2%)
    ppermute x11, waiting for transfers between devices, swap(): return lax.ppermute(x, axis, [(k, k ^ d) for k in range(n)])  21.9 us
    ppermute x11, starting transfers between devices, swap(): return lax.ppermute(x, axis, [(k, k ^ d) for k in range(n)])  14 us
    pallas_call x5, Pallas kernels, step(): pl.pallas_call(functools.partial(step_kernel, [wanted[0]] + [cols[d][0] f...  6.74 us
    ppermute x5, starting transfers between devices, permute(): return lax.ppermute(x, ('row', 'col'), pairs)  2.68 us
    pallas_call x2, Pallas kernels, dense_of(): pl.pallas_call(functools.partial(left_kernel, group), out_shape=jax.Shape...  2.28 us
    unnamed x12, local copies, waits for them, and re-layouts  1.09 us
  transfers between devices with their start and end apart: 16, of which 5 were waited for; matrix products, arithmetic and copies ran while one was open for 1% of the time, Pallas kernels for 19%

profile of v13, /device:TPU:0, one launch (start us, length us, event | category | flops | bytes accessed | tf_op | source)
XLA Modules:
  0.0 50.8 jit_solution(12504118880064101887)
XLA Ops:
  0.0 3.0 %collective-permute-start.4 = (bf16[2,4,128,128]{3,2,1,0:T(8,128)(2,1)}, bf16[2,4,128,128]{3,2,1,0:T(8,128)(2,1)S(1)}, u32[]{:S(2)}, u32[]{:S(2)}) collective-permute-start(bf16[2,4,128,128]{3,2,1,0:T(8,128)(2,1)} %refs_0_.4), channel_id=1, source_target_pairs={{0,4},{4,0},{8,12},{12,8},{1,5},{5,1},{9,13},{13,9},{2,6},{6,2},{1... | collective-permute-start | bytes 786440 | tf_op jit(solution)/shard_map/ppermute | solution.py:114
  3.0 2.5 %collective-permute-start.6 = (bf16[2048,128]{1,0:T(8,128)(2,1)}, bf16[2048,128]{1,0:T(8,128)(2,1)S(1)}, u32[]{:S(2)}, u32[]{:S(2)}) collective-permute-start(bf16[2048,128]{1,0:T(8,128)(2,1)} %bitcast.8), channel_id=1, source_target_pairs={{0,12},{1,3},{2,14},{3,1},{4,6},{5,9},{6,4},{7,11},{8,10},{9,5},{1... | collective-permute-start | bytes 1572872 | tf_op jit(solution)/shard_map/ppermute | solution.py:122
  5.5 1.1 %copy-done = bf16[2,8,128,128]{3,2,1,0:T(8,128)(2,1)S(1)} copy-done((bf16[2,8,128,128]{3,2,1,0:T(8,128)(2,1)S(1)}, bf16[2,8,128,128]{3,2,1,0:T(8,128)(2,1)}, u32[]{:S(2)}) %copy-start) | copy-done | bytes 524312
  6.6 0.6 %shard_map.55 = bf16[2064,128]{1,0:T(8,128)(2,1)S(1)} custom-call(s32[2,8]{1,0:T(2,128)S(1)} %copy-done.4, bf16[2048,128]{1,0:T(8,128)(2,1)S(1)} %bitcast.9), custom_call_target="tpu_custom_call" | custom-call | flops 1 | bytes 1 | tf_op jit(solution)/shard_map/pallas_call | solution.py:138
  7.3 2.8 %collective-permute-done.4.refs_0_ = bf16[2,4,128,128]{3,2,1,0:T(8,128)(2,1)S(1)} collective-permute-done((bf16[2,4,128,128]{3,2,1,0:T(8,128)(2,1)}, bf16[2,4,128,128]{3,2,1,0:T(8,128)(2,1)S(1)}, u32[]{:S(2)}, u32[]{:S(2)}) %collective-permute-start.4) | collective-permute-done | bytes 262176 | tf_op jit(solution)/shard_map/ppermute | solution.py:114
  10.1 1.5 %collective-permute-start.5 = (bf16[2,4,128,128]{3,2,1,0:T(8,128)(2,1)S(1)}, bf16[2,4,128,128]{3,2,1,0:T(8,128)(2,1)S(1)}, u32[]{:S(2)}, u32[]{:S(2)}) collective-permute-start(bf16[2,4,128,128]{3,2,1,0:T(8,128)(2,1)S(1)} %collective-permute-done.4.refs_0_), channel_id=1, source_target_pairs={{0,2},{1,3},{2,0},{3,1},{4,6},{5,7},{6,4},{7,5},{8,10},{9,11},{10,... | collective-permute-start | bytes 786440 | tf_op jit(solution)/shard_map/ppermute | solution.py:114
  11.6 0.1 pad_add_fusion.3
  11.6 2.4 %collective-permute-start.1 = (s32[2,10]{1,0:T(2,128)S(1)}, s32[2,10]{1,0:T(2,128)S(1)}, u32[]{:S(2)}, u32[]{:S(2)}) collective-permute-start(s32[2,10]{1,0:T(2,128)S(1)} %pad_add_fusion.3), channel_id=1, source_target_pairs={{0,4},{4,0},{8,12},{12,8},{1,5},{5,1},{9,13},{13,9},{2,6},{6,2},{1... | collective-permute-start | bytes 248 | tf_op jit(solution)/shard_map/ppermute | solution.py:114
  14.0 9.5 %collective-permute-done.1 = s32[2,10]{1,0:T(2,128)S(1)} collective-permute-done((s32[2,10]{1,0:T(2,128)S(1)}, s32[2,10]{1,0:T(2,128)S(1)}, u32[]{:S(2)}, u32[]{:S(2)}) %collective-permute-start.1) | collective-permute-done | bytes 112 | tf_op jit(solution)/shard_map/ppermute | solution.py:114
  23.5 0.1 pad_add_fusion.2.refs_0_
  23.6 2.3 %collective-permute-start.2 = (s32[4,10]{1,0:T(4,128)S(1)}, s32[4,10]{1,0:T(4,128)S(1)}, u32[]{:S(2)}, u32[]{:S(2)}) collective-permute-start(s32[4,10]{1,0:T(4,128)S(1)} %pad_add_fusion.2.refs_0_), channel_id=1, source_target_pairs={{0,2},{1,3},{2,0},{3,1},{4,6},{5,7},{6,4},{7,5},{8,10},{9,11},{10,... | collective-permute-start | bytes 488 | tf_op jit(solution)/shard_map/ppermute | solution.py:114
  25.9 1.6 %collective-permute-done.2 = s32[4,10]{1,0:T(4,128)S(1)} collective-permute-done((s32[4,10]{1,0:T(4,128)S(1)}, s32[4,10]{1,0:T(4,128)S(1)}, u32[]{:S(2)}, u32[]{:S(2)}) %collective-permute-start.2) | collective-permute-done | bytes 192 | tf_op jit(solution)/shard_map/ppermute | solution.py:114
  27.5 0.1 pad_add_fusion.1
  27.6 2.1 %collective-permute-start.10 = (bf16[2,4,128,128]{3,2,1,0:T(8,128)(2,1)S(1)}, bf16[2,4,128,128]{3,2,1,0:T(8,128)(2,1)S(1)}, u32[]{:S(2)}, u32[]{:S(2)}) collective-permute-start(bf16[2,4,128,128]{3,2,1,0:T(8,128)(2,1)S(1)} %copy-done.2), channel_id=1, source_target_pairs={{0,2},{1,3},{2,0},{3,1},{4,6},{5,7},{6,4},{7,5},{8,10},{9,11},{10,... | collective-permute-start | bytes 786440 | tf_op jit(solution)/shard_map/ppermute | solution.py:114
  29.7 0.2 collective-permute-start.7
  29.8 0.4 collective-permute-start.8
  30.2 0.1 pad_add_fusion.4
  30.2 0.1 pad_add_fusion.index
  30.3 6.2 %collective-permute-done.10.refs_1_ = bf16[2,4,128,128]{3,2,1,0:T(8,128)(2,1)S(1)} collective-permute-done((bf16[2,4,128,128]{3,2,1,0:T(8,128)(2,1)S(1)}, bf16[2,4,128,128]{3,2,1,0:T(8,128)(2,1)S(1)}, u32[]{:S(2)}, u32[]{:S(2)}) %collective-permute-start.10) | collective-permute-done | bytes 262176 | tf_op jit(solution)/shard_map/ppermute | solution.py:114
  36.5 1.9 %collective-permute-start.13 = (s32[2,8]{1,0:T(2,128)S(1)}, s32[2,8]{1,0:T(2,128)S(1)}, u32[]{:S(2)}, u32[]{:S(2)}) collective-permute-start(s32[2,8]{1,0:T(2,128)S(1)} %copy-done.4), channel_id=1, source_target_pairs={{0,12},{4,8},{8,4},{12,0},{1,13},{5,9},{9,5},{13,1},{2,14},{6,10},... | collective-permute-start | bytes 200 | tf_op jit(solution)/shard_map/ppermute | solution.py:114
  38.5 0.2 collective-permute-start.12
  38.7 1.3 %shard_map.56.refs_5_ = bf16[2,8,128,128]{3,2,1,0:T(8,128)(2,1)S(1)} custom-call(s32[16,10]{1,0:T(8,128)S(1)} %pad_add_fusion.index, bf16[2,4,128,128]{3,2,1,0:T(8,128)(2,1)S(1)} %collective-permute-done.4.refs_0_, bf16[2,4,128,128]{3,2,1,0:T(8,128)(2,1)S(1)} %collective-permute-done.5.refs_1_, bf16[2,4,128,128]{3,2,1,0:T(8,128)(2,1)S(1)} %collective-permute-done.7.refs_2_, ...), custom_call_target="tpu_custom_call" | custom-call | flops 1 | bytes 1 | tf_op jit(solution)/shard_map/pallas_call | solution.py:176
  40.0 0.1 convert_reduce_fusion
  40.1 1.8 %collective-permute-done.13.refs_2_ = s32[2,8]{1,0:T(2,128)S(1)} collective-permute-done((s32[2,8]{1,0:T(2,128)S(1)}, s32[2,8]{1,0:T(2,128)S(1)}, u32[]{:S(2)}, u32[]{:S(2)}) %collective-permute-start.13) | collective-permute-done | bytes 96 | tf_op jit(solution)/shard_map/ppermute | solution.py:114
  41.9 1.5 %shard_map.60.refs_6_ = f32[2,128,768]{2,1,0:T(8,128)S(1)} custom-call(s32[3]{0:T(128)S(1)} %get-tuple-element.18.place, s32[4,10]{1,0:T(4,128)S(1)} %pad_add_fusion.2.refs_0_, s32[2,8]{1,0:T(2,128)S(1)} %copy-done.4, s32[2,8]{1,0:T(2,128)S(1)} %collective-permute-done.13.refs_2_, bf16[2048,128]{1,0:T(8,128)(2,1)S(1)} %bitcast.10, ...), custom_call_target="tpu_custom_call" | custom-call | flops 1 | bytes 1 | tf_op jit(solution)/shard_map/pallas_call | solution.py:192
  43.4 0.1 convert_reduce_fusion.1
  43.5 1.2 %shard_map.61 = bf16[1,6,128,128]{3,2,1,0:T(8,128)(2,1)S(1)} custom-call(s32[3]{0:T(128)S(1)} %get-tuple-element.17.place, s32[4,10]{1,0:T(4,128)S(1)} %pad_add_fusion.2.refs_0_, s32[1,16]{1,0:T(1,128)S(1)} %bitcast.15, s32[1,16]{1,0:T(1,128)S(1)} %bitcast.12, bf16[2064,128]{1,0:T(8,128)(2,1)S(1)} %collective-permute-done.refs_3_, ...), custom_call_target="tpu_custom_call" | custom-call | flops 1 | bytes 1 | tf_op jit(solution)/shard_map/pallas_call | solution.py:192
  44.8 1.2 %shard_map.62 = bf16[1,6,128,128]{3,2,1,0:T(8,128)(2,1)S(1)} custom-call(s32[3]{0:T(128)S(1)} %get-tuple-element.17.place, s32[4,10]{1,0:T(4,128)S(1)} %pad_add_fusion.2.refs_0_, s32[1,16]{1,0:T(1,128)S(1)} %bitcast.16, s32[1,16]{1,0:T(1,128)S(1)} %bitcast.13, bf16[2064,128]{1,0:T(8,128)(2,1)S(1)} %collective-permute-done.refs_3_, ...), custom_call_target="tpu_custom_call" | custom-call | flops 1 | bytes 1 | tf_op jit(solution)/shard_map/pallas_call | solution.py:192
  46.0 1.0 %shard_map.57.refs_5_ = bf16[2,8,128,128]{3,2,1,0:T(8,128)(2,1)S(1)} custom-call(s32[16,10]{1,0:T(8,128)S(1)} %pad_add_fusion.index, bf16[2,4,128,128]{3,2,1,0:T(8,128)(2,1)S(1)} %copy-done.2, bf16[2,4,128,128]{3,2,1,0:T(8,128)(2,1)S(1)} %collective-permute-done.10.refs_1_, bf16[2,4,128,128]{3,2,1,0:T(8,128)(2,1)S(1)} %collective-permute-done.11.refs_2_, ...), custom_call_target="tpu_custom_call" | custom-call | flops 1 | bytes 1 | tf_op jit(solution)/shard_map/pallas_call | solution.py:176
  47.0 1.5 %shard_map.58.refs_6_ = f32[2,128,768]{2,1,0:T(8,128)S(1)} custom-call(s32[3]{0:T(128)S(1)} %get-tuple-element.18.place, s32[2,6]{1,0:T(2,128)S(1)} %copy-done.3, s32[2,8]{1,0:T(2,128)S(1)} %copy-done.4, s32[2,8]{1,0:T(2,128)S(1)} %collective-permute-done.13.refs_2_, bf16[2048,128]{1,0:T(8,128)(2,1)S(1)} %bitcast.11, ...), custom_call_target="tpu_custom_call" | custom-call | flops 1 | bytes 1 | tf_op jit(solution)/shard_map/pallas_call | solution.py:192
  48.5 1.5 %shard_map.59 = bf16[2,6,128,128]{3,2,1,0:T(8,128)(2,1)S(1)} custom-call(s32[3]{0:T(128)S(1)} %get-tuple-element.17.place, s32[2,6]{1,0:T(2,128)S(1)} %copy-done.3, s32[1,16]{1,0:T(1,128)S(1)} %bitcast.17, s32[1,16]{1,0:T(1,128)S(1)} %bitcast.14, bf16[2064,128]{1,0:T(8,128)(2,1)S(1)} %collective-permute-done.refs_3_, ...), custom_call_target="tpu_custom_call" | custom-call | flops 1 | bytes 1 | tf_op jit(solution)/shard_map/pallas_call | solution.py:192
  50.0 0.8 %maximum_select_fusion = bf16[2,6,128,128]{3,2,1,0:T(8,128)(2,1)} fusion(bf16[2,6,128,128]{3,2,1,0:T(8,128)(2,1)S(1)} %shard_map.59, bf16[1,6,128,128]{3,2,1,0:T(8,128)(2,1)S(1)} %collective-permute-done.15, bf16[1,6,128,128]{3,2,1,0:T(8,128)(2,1)S(1)} %collective-permute-done.14, pred[]{:T(512)S(6)} %eq.5), kind=kLoop, calls=%fused_computation | loop fusion | flops 393216 | bytes 1179649 | tf_op jit(solution)/shard_map/jit(_where)/select_n | solution.py:221
  (28 shorter events, 0.3 us)
Async XLA Ops:
  0.0 5.5 %copy-start.4 = (s32[2,8]{1,0:T(2,128)S(1)}, s32[2,8]{1,0:T(2,128)}, u32[]{:S(2)}) copy-start(s32[2,8]{1,0:T(2,128)} %refs_1_.3) | copy-start | bytes 196
  0.0 10.1 %collective-permute-start.4 = (bf16[2,4,128,128]{3,2,1,0:T(8,128)(2,1)}, bf16[2,4,128,128]{3,2,1,0:T(8,128)(2,1)S(1)}, u32[]{:S(2)}, u32[]{:S(2)}) collective-permute-start(bf16[2,4,128,128]{3,2,1,0:T(8,128)(2,1)} %refs_0_.4), channel_id=1, source_target_pairs={{0,4},{4,0},{8,12},{12,8},{1,5},{5,1},{9,13},{13,9},{2,6},{6,2},{1... | collective-permute-start | bytes 786440 | tf_op jit(solution)/shard_map/ppermute | solution.py:114
  3.0 24.5 %collective-permute-start.6 = (bf16[2048,128]{1,0:T(8,128)(2,1)}, bf16[2048,128]{1,0:T(8,128)(2,1)S(1)}, u32[]{:S(2)}, u32[]{:S(2)}) collective-permute-start(bf16[2048,128]{1,0:T(8,128)(2,1)} %bitcast.8), channel_id=1, source_target_pairs={{0,12},{1,3},{2,14},{3,1},{4,6},{5,9},{6,4},{7,11},{8,10},{9,5},{1... | collective-permute-start | bytes 1572872 | tf_op jit(solution)/shard_map/ppermute | solution.py:122
  5.5 1.1 %copy-start = (bf16[2,8,128,128]{3,2,1,0:T(8,128)(2,1)S(1)}, bf16[2,8,128,128]{3,2,1,0:T(8,128)(2,1)}, u32[]{:S(2)}) copy-start(bf16[2,8,128,128]{3,2,1,0:T(8,128)(2,1)} %param.7) | copy-start | bytes 1572868
  6.6 5.0 %copy-start.3 = (s32[2,6]{1,0:T(2,128)S(1)}, s32[2,6]{1,0:T(2,128)}, u32[]{:S(2)}) copy-start(s32[2,6]{1,0:T(2,128)} %refs_0_.6) | copy-start | bytes 148
  6.6 5.0 %copy-start.5 = (s32[2,4]{1,0:T(2,128)S(1)}, s32[2,4]{1,0:T(2,128)}, u32[]{:S(2)}) copy-start(s32[2,4]{1,0:T(2,128)} %param.6) | copy-start | bytes 100
  6.6 21.0 %copy-start.2 = (bf16[2,4,128,128]{3,2,1,0:T(8,128)(2,1)S(1)}, bf16[2,4,128,128]{3,2,1,0:T(8,128)(2,1)}, u32[]{:S(2)}) copy-start(bf16[2,4,128,128]{3,2,1,0:T(8,128)(2,1)} %refs_0_.4) | copy-start | bytes 786436
  7.2 32.8 %collective-permute-start.9 = (bf16[2064,128]{1,0:T(8,128)(2,1)S(1)}, bf16[2064,128]{1,0:T(8,128)(2,1)S(1)}, u32[]{:S(2)}, u32[]{:S(2)}) collective-permute-start(bf16[2064,128]{1,0:T(8,128)(2,1)S(1)} %shard_map.55), channel_id=1, source_target_pairs={{0,1},{1,5},{2,3},{3,7},{4,0},{5,4},{6,2},{7,6},{8,12},{9,8},{10,1... | collective-permute-start | bytes 1585160 | tf_op jit(solution)/shard_map/ppermute | solution.py:122
  10.1 19.6 %collective-permute-start.5 = (bf16[2,4,128,128]{3,2,1,0:T(8,128)(2,1)S(1)}, bf16[2,4,128,128]{3,2,1,0:T(8,128)(2,1)S(1)}, u32[]{:S(2)}, u32[]{:S(2)}) collective-permute-start(bf16[2,4,128,128]{3,2,1,0:T(8,128)(2,1)S(1)} %collective-permute-done.4.refs_0_), channel_id=1, source_target_pairs={{0,2},{1,3},{2,0},{3,1},{4,6},{5,7},{6,4},{7,5},{8,10},{9,11},{10,... | collective-permute-start | bytes 786440 | tf_op jit(solution)/shard_map/ppermute | solution.py:114
  11.6 11.9 %collective-permute-start.1 = (s32[2,10]{1,0:T(2,128)S(1)}, s32[2,10]{1,0:T(2,128)S(1)}, u32[]{:S(2)}, u32[]{:S(2)}) collective-permute-start(s32[2,10]{1,0:T(2,128)S(1)} %pad_add_fusion.3), channel_id=1, source_target_pairs={{0,4},{4,0},{8,12},{12,8},{1,5},{5,1},{9,13},{13,9},{2,6},{6,2},{1... | collective-permute-start | bytes 248 | tf_op jit(solution)/shard_map/ppermute | solution.py:114
  14.0 26.1 %collective-permute-start = (bf16[2064,128]{1,0:T(8,128)(2,1)S(1)}, bf16[2064,128]{1,0:T(8,128)(2,1)S(1)}, u32[]{:S(2)}, u32[]{:S(2)}) collective-permute-start(bf16[2064,128]{1,0:T(8,128)(2,1)S(1)} %shard_map.55), channel_id=1, source_target_pairs={{0,1},{1,9},{2,3},{3,11},{4,12},{5,4},{6,14},{7,6},{8,0},{9,8},{10... | collective-permute-start | bytes 1585160 | tf_op jit(solution)/shard_map/ppermute | solution.py:122
  23.6 3.9 %collective-permute-start.2 = (s32[4,10]{1,0:T(4,128)S(1)}, s32[4,10]{1,0:T(4,128)S(1)}, u32[]{:S(2)}, u32[]{:S(2)}) collective-permute-start(s32[4,10]{1,0:T(4,128)S(1)} %pad_add_fusion.2.refs_0_), channel_id=1, source_target_pairs={{0,2},{1,3},{2,0},{3,1},{4,6},{5,7},{6,4},{7,5},{8,10},{9,11},{10,... | collective-permute-start | bytes 488 | tf_op jit(solution)/shard_map/ppermute | solution.py:114
  27.5 2.3 %collective-permute-start.3 = (s32[8,10]{1,0:T(8,128)S(1)}, s32[8,10]{1,0:T(8,128)S(1)}, u32[]{:S(2)}, u32[]{:S(2)}) collective-permute-start(s32[8,10]{1,0:T(8,128)S(1)} %pad_add_fusion.1), channel_id=1, source_target_pairs={{0,1},{1,0},{2,3},{3,2},{4,5},{5,4},{6,7},{7,6},{8,9},{9,8},{10,11... | collective-permute-start | bytes 968 | tf_op jit(solution)/shard_map/ppermute | solution.py:114
  27.6 9.0 %collective-permute-start.10 = (bf16[2,4,128,128]{3,2,1,0:T(8,128)(2,1)S(1)}, bf16[2,4,128,128]{3,2,1,0:T(8,128)(2,1)S(1)}, u32[]{:S(2)}, u32[]{:S(2)}) collective-permute-start(bf16[2,4,128,128]{3,2,1,0:T(8,128)(2,1)S(1)} %copy-done.2), channel_id=1, source_target_pairs={{0,2},{1,3},{2,0},{3,1},{4,6},{5,7},{6,4},{7,5},{8,10},{9,11},{10,... | collective-permute-start | bytes 786440 | tf_op jit(solution)/shard_map/ppermute | solution.py:114
  29.7 6.9 %collective-permute-start.7 = (bf16[2,4,128,128]{3,2,1,0:T(8,128)(2,1)S(1)}, bf16[2,4,128,128]{3,2,1,0:T(8,128)(2,1)S(1)}, u32[]{:S(2)}, u32[]{:S(2)}) collective-permute-start(bf16[2,4,128,128]{3,2,1,0:T(8,128)(2,1)S(1)} %collective-permute-done.4.refs_0_), channel_id=1, source_target_pairs={{0,1},{1,0},{2,3},{3,2},{4,5},{5,4},{6,7},{7,6},{8,9},{9,8},{10,11... | collective-permute-start | bytes 786440 | tf_op jit(solution)/shard_map/ppermute | solution.py:114
  29.8 8.7 %collective-permute-start.8 = (bf16[2,4,128,128]{3,2,1,0:T(8,128)(2,1)S(1)}, bf16[2,4,128,128]{3,2,1,0:T(8,128)(2,1)}, u32[]{:S(2)}, u32[]{:S(2)}) collective-permute-start(bf16[2,4,128,128]{3,2,1,0:T(8,128)(2,1)S(1)} %collective-permute-done.5.refs_1_), channel_id=1, source_target_pairs={{0,1},{1,0},{2,3},{3,2},{4,5},{5,4},{6,7},{7,6},{8,9},{9,8},{10,11... | collective-permute-start | bytes 786440 | tf_op jit(solution)/shard_map/ppermute | solution.py:114
  30.3 11.6 %copy-start.1 = (bf16[2,8,128,128]{3,2,1,0:T(8,128)(2,1)S(1)}, bf16[2,8,128,128]{3,2,1,0:T(8,128)(2,1)}, u32[]{:S(2)}) copy-start(bf16[2,8,128,128]{3,2,1,0:T(8,128)(2,1)} %param.7) | copy-start | bytes 1572868
  36.5 9.5 %collective-permute-start.11 = (bf16[2,4,128,128]{3,2,1,0:T(8,128)(2,1)S(1)}, bf16[2,4,128,128]{3,2,1,0:T(8,128)(2,1)S(1)}, u32[]{:S(2)}, u32[]{:S(2)}) collective-permute-start(bf16[2,4,128,128]{3,2,1,0:T(8,128)(2,1)S(1)} %copy-done.2), channel_id=1, source_target_pairs={{0,1},{1,0},{2,3},{3,2},{4,5},{5,4},{6,7},{7,6},{8,9},{9,8},{10,11... | collective-permute-start | bytes 786440 | tf_op jit(solution)/shard_map/ppermute | solution.py:114
  36.5 5.4 %collective-permute-start.13 = (s32[2,8]{1,0:T(2,128)S(1)}, s32[2,8]{1,0:T(2,128)S(1)}, u32[]{:S(2)}, u32[]{:S(2)}) collective-permute-start(s32[2,8]{1,0:T(2,128)S(1)} %copy-done.4), channel_id=1, source_target_pairs={{0,12},{4,8},{8,4},{12,0},{1,13},{5,9},{9,5},{13,1},{2,14},{6,10},... | collective-permute-start | bytes 200 | tf_op jit(solution)/shard_map/ppermute | solution.py:114
  38.5 7.5 %collective-permute-start.12 = (bf16[2,4,128,128]{3,2,1,0:T(8,128)(2,1)S(1)}, bf16[2,4,128,128]{3,2,1,0:T(8,128)(2,1)S(1)}, u32[]{:S(2)}, u32[]{:S(2)}) collective-permute-start(bf16[2,4,128,128]{3,2,1,0:T(8,128)(2,1)S(1)} %collective-permute-done.10.refs_1_), channel_id=1, source_target_pairs={{0,1},{1,0},{2,3},{3,2},{4,5},{5,4},{6,7},{7,6},{8,9},{9,8},{10,11... | collective-permute-start | bytes 786440 | tf_op jit(solution)/shard_map/ppermute | solution.py:114
  44.7 5.3 %collective-permute-start.14 = (bf16[1,6,128,128]{3,2,1,0:T(8,128)(2,1)S(1)}, bf16[1,6,128,128]{3,2,1,0:T(8,128)(2,1)S(1)}, u32[]{:S(2)}, u32[]{:S(2)}) collective-permute-start(bf16[1,6,128,128]{3,2,1,0:T(8,128)(2,1)S(1)} %shard_map.61), channel_id=1, source_target_pairs={{0,4},{1,0},{2,6},{3,2},{4,5},{5,1},{6,7},{7,3},{8,9},{9,13},{10,1... | collective-permute-start | bytes 589832 | tf_op jit(solution)/shard_map/ppermute | solution.py:122
  45.9 4.1 %collective-permute-start.15 = (bf16[1,6,128,128]{3,2,1,0:T(8,128)(2,1)S(1)}, bf16[1,6,128,128]{3,2,1,0:T(8,128)(2,1)S(1)}, u32[]{:S(2)}, u32[]{:S(2)}) collective-permute-start(bf16[1,6,128,128]{3,2,1,0:T(8,128)(2,1)S(1)} %shard_map.62), channel_id=1, source_target_pairs={{0,4},{1,0},{2,6},{3,2},{4,5},{5,1},{6,7},{7,3},{8,9},{9,13},{10,1... | collective-permute-start | bytes 589832 | tf_op jit(solution)/shard_map/ppermute | solution.py:122

commit v14 on v10

--- a/solution.py
+++ b/solution.py
@@ -9,25 +9,37 @@
 
 COLS_DEV = 16
 
+ANY = pl.BlockSpec(memory_space=pl.ANY)
 SMEM = pl.BlockSpec(memory_space=pltpu.SMEM)
 VMEM = pl.BlockSpec(memory_space=pltpu.VMEM)
 PARAMS = pltpu.CompilerParams(vmem_limit_bytes=32 * 2**20)
 FREE = pl.CostEstimate(flops=1, bytes_accessed=1, transcendentals=0)
 
 
-def pack_kernel(*refs):
-    indices, tiles, out = refs[:-2], refs[-2], refs[-1]
-    size = tiles.shape[0]
-    out[:size, :] = tiles[...]
-    row = lax.broadcasted_iota(jnp.int32, (out.shape[0] - size, out.shape[1]), 0)
-    found = jnp.zeros(row.shape, jnp.float32)
-    at = 0
-    for index in indices:
-        for i in range(index.shape[0]):
-            for k in range(index.shape[1]):
-                found = jnp.where(row == at, index[i, k].astype(jnp.float32), found)
-                at += 1
-    out[size:, :] = found.astype(out.dtype)
+def pack_kernel(counts, *refs):
+    groups = len(counts)
+    indices, refs = refs[: sum(counts)], refs[sum(counts) :]
+    tiles, outs, rows, sems = refs[:groups], refs[groups : 2 * groups], refs[2 * groups : 3 * groups], refs[3 * groups]
+    copies = [
+        pltpu.make_async_copy(x, out.at[: x.shape[0]], sems.at[2 * g]) for g, (x, out) in enumerate(zip(tiles, outs))
+    ]
+    for copy in copies:
+        copy.start()
+    for g, count in enumerate(counts):
+        row = lax.broadcasted_iota(jnp.int32, rows[g].shape, 0)
+        found, at = jnp.zeros(row.shape, jnp.float32), 0
+        for index in indices[:count]:
+            for i in range(index.shape[0]):
+                for k in range(index.shape[1]):
+                    found = jnp.where(row == at, index[i, k].astype(jnp.float32), found)
+                    at += 1
+        indices = indices[count:]
+        rows[g][...] = found.astype(rows[g].dtype)
+        copy = pltpu.make_async_copy(rows[g], outs[g].at[tiles[g].shape[0] :], sems.at[2 * g + 1])
+        copy.start()
+        copies.append(copy)
+    for copy in copies:
+        copy.wait()
 
 
 def left_kernel(slots, index, *refs):
@@ -133,17 +145,22 @@
     def give_back(x):
         return permute(x, lambda k, c: (k ^ 1, c) if works(k, c) else (k, c ^ 1))
 
-    def pack(tiles, *indices):
-        size = tiles.size // block
-        count = sum(x.size for x in indices)
+    def pack(*groups):
+        flat = [x.reshape(-1, block) for x, _ in groups]
+        counts = [len(indices) for _, indices in groups]
+        tails = [-(-sum(x.size for x in indices) // 16) * 16 for _, indices in groups]
         return pl.pallas_call(
-            pack_kernel,
-            out_shape=jax.ShapeDtypeStruct((size + -(-count // 16) * 16, block), dtype),
-            in_specs=[SMEM] * len(indices) + [VMEM],
-            out_specs=VMEM,
-            compiler_params=PARAMS,
+            functools.partial(pack_kernel, counts),
+            out_shape=[
+                jax.ShapeDtypeStruct((x.shape[0] + more, block), dtype) for x, more in zip(flat, tails)
+            ],
+            in_specs=[SMEM] * sum(counts) + [ANY] * len(groups),
+            out_specs=[ANY] * len(groups),
+            scratch_shapes=[pltpu.VMEM((more, block), dtype) for more in tails]
+            + [pltpu.SemaphoreType.DMA((2 * len(groups),))],
+            compiler_params=pltpu.CompilerParams(vmem_limit_bytes=66 * 10**6),
             cost_estimate=FREE,
-        )(*indices, tiles.reshape(size, block))
+        )(*[x for _, indices in groups for x in indices], *flat)
 
     def index_of(packs, tiles):
         return jnp.stack([x[tiles.size // block :, 0] for x in packs]).astype(jnp.int32)
@@ -155,17 +172,16 @@
         return parts
 
     far, end = col_count // 2, row_count - 1
-    flat = b_tiles.reshape(-1, block)
-    own, packed = pack(a_tiles, a_cols, c_cols), pack(b_tiles, b_cols)
-    shards = {0: flat, end: deliver(flat, end)}
-    cols = {0: (None, b_cols), end: (None, swap(b_cols, "row", row_count, end))}
-    own_packs = [own, swap(own, "col", col_count, far)]
+    own, packed = pack((a_tiles, (a_cols, c_cols)), (b_tiles, (b_cols,)))
     other = swap(own, "row", row_count, 1)
-    ready = lax.optimization_barrier((packed, own_packs[1]))[0]
-    for d in range(end - 1, 0, -1):
-        shards[d] = deliver(ready, d)
-    other = lax.optimization_barrier((other, shards[end]))[0]
-    own_packs, other_packs = across(own_packs, far // 2), across([other], far)
+    shards, cols = {0: b_tiles.reshape(-1, block)}, {0: (None, b_cols)}
+    for d in range(end, 0, -1):
+        shards[d] = deliver(packed, d)
+    other_packs = [other, swap(other, "col", col_count, far)]
+    late = lax.optimization_barrier((own, other_packs[1]))[0]
+    own_packs = across([late], far)
+    other_packs = across(other_packs, far // 2)
+
     def dense_of(packs):
         return pl.pallas_call(
             functools.partial(left_kernel, a_cols.shape[1]),
@@ -196,15 +212,20 @@
             cost_estimate=FREE,
         )(place, wanted[1], *[cols[d][1] for d in dists], *[shards[d] for d in dists], *held)
 
-    order, every = list(range(1, end)) + [0, end], list(range(rows))
-    early, late = order[:-4], order[-4:]
-    for d in range(1, end):
-        cols[d] = (0, index_of([shards[d]], b_tiles))
+    order, every = [0] + list(range(end, 0, -1)), list(range(rows))
+    early, late = order[:-3], order[-3:]
 
     def products(wanted, packs, spans):
         dense, total = dense_of(packs), None
-        for at in range(0, len(early), 4):
-            total = step(early[at : at + 4], wanted, dense, total, every, False)
+        for d in early[1:]:
+            if d not in cols:
+                cols[d] = (0, index_of([shards[d]], b_tiles))
+        for at in range(0, len(early), 2):
+            total = step(early[at : at + 2], wanted, dense, total, every, False)
+        for d in late:
+            if d not in cols:
+                x = lax.optimization_barrier((shards[d], total))[0]
+                cols[d] = (0, index_of([x], b_tiles))
         return [step(late, wanted, dense, total, span, True) for span in spans]
 
     given = products((a_cols.size, index_of([other], a_tiles)), other_packs, [[i] for i in every])

time: 40.5 us -> 65.7 us (1.62); the launches traced: 40.3 us -> 64.5 us
  Pallas kernels: 8.11 us -> 34.1 us
  local copies, waits for them, and re-layouts: 3.29 us -> 1.63 us
    pallas_call x2 -> x1, Pallas kernels: 1.17 us -> 25.7 us  [pack(): pl.pallas_call(functools.partial(pack_kernel, counts), out_shape=[jax.Sha...]
    unnamed x12 -> x8, local copies, waits for them, and re-layouts: 2.32 us -> 0.04 us
    ppermute x5, starting transfers between devices: 5.25 us -> 3.46 us  [permute(): return lax.ppermute(x, ('row', 'col'), pairs)]
    ppermute x8 -> x7, waiting for transfers between devices: 13.3 us -> 11.7 us  [swap(): return lax.ppermute(x, axis, [(k, k ^ d) for k in range(n)])]
    ppermute x8 -> x7, starting transfers between devices: 5.22 us -> 6.82 us  [swap(): return lax.ppermute(x, axis, [(k, k ^ d) for k in range(n)])]
    pallas_call x3 -> x5, Pallas kernels: 5.15 us -> 6.63 us  [step(): pl.pallas_call(functools.partial(step_kernel, [wanted[0]] + [cols[d][0] f...]
    ppermute x5, waiting for transfers between devices: 3.85 us -> 5.3 us  [permute(): return lax.ppermute(x, ('row', 'col'), pairs)]
    slice x8, local copies, waits for them, and re-layouts: 0.89 us -> 1.59 us  [index_of(): x[tiles.size // block:, 0]]
  transfers between devices with their start and end apart: 13 -> 12, of which waited for: 5 -> 3; matrix products, arithmetic and copies ran while one was open for 3% -> 3% of each run, Pallas kernels for 20% -> 13%
where the time goes in v14:
time: 65.7 us; the launch traced here: 64.5 us
  Pallas kernels  34.1 us (52%)
  waiting for transfers between devices  17 us (26%)
  starting transfers between devices  10.3 us (16%)
  local copies, waits for them, and re-layouts  1.63 us (2%)
  other arithmetic  1.33 us (2%)
    pallas_call x1, Pallas kernels, pack(): pl.pallas_call(functools.partial(pack_kernel, counts), out_shape=[jax.Sha...  25.7 us
    ppermute x7, waiting for transfers between devices, swap(): return lax.ppermute(x, axis, [(k, k ^ d) for k in range(n)])  11.7 us
    ppermute x7, starting transfers between devices, swap(): return lax.ppermute(x, axis, [(k, k ^ d) for k in range(n)])  6.82 us
    pallas_call x5, Pallas kernels, step(): pl.pallas_call(functools.partial(step_kernel, [wanted[0]] + [cols[d][0] f...  6.63 us
    ppermute x5, waiting for transfers between devices, permute(): return lax.ppermute(x, ('row', 'col'), pairs)  5.3 us
    ppermute x5, starting transfers between devices, permute(): return lax.ppermute(x, ('row', 'col'), pairs)  3.46 us
    pallas_call x2, Pallas kernels, dense_of(): pl.pallas_call(functools.partial(left_kernel, a_cols.shape[1]), out_shape...  1.79 us
    slice x8, local copies, waits for them, and re-layouts, index_of(): x[tiles.size // block:, 0]  1.59 us
  transfers between devices with their start and end apart: 12, of which 3 were waited for; matrix products, arithmetic and copies ran while one was open for 3% of the time, Pallas kernels for 13%

profile of v14, /device:TPU:0, one launch (start us, length us, event | category | flops | bytes accessed | tf_op | source)
XLA Modules:
  0.0 64.5 jit_solution(15054855520123849565)
XLA Ops:
  0.0 25.7 %shard_map.55 = (bf16[1056,128]{1,0:T(8,128)(2,1)}, bf16[2064,128]{1,0:T(8,128)(2,1)}) custom-call(s32[2,4]{1,0:T(2,128)} %refs_0_.3, s32[2,6]{1,0:T(2,128)} %refs_0_.5, s32[2,8]{1,0:T(2,128)} %refs_1_.5, bf16[1024,128]{1,0:T(8,128)(2,1)} %bitcast.31, bf16[2048,128]{1,0:T(8,128)(2,1)} %bitcast.19), custom_call_target="tpu_custom_call" | custom-call | flops 1 | bytes 1 | tf_op jit(solution)/shard_map/pallas_call | solution.py:152
  25.7 3.1 %collective-permute-start.1 = (bf16[1056,128]{1,0:T(8,128)(2,1)}, bf16[1056,128]{1,0:T(8,128)(2,1)S(1)}, u32[]{:S(2)}, u32[]{:S(2)}) collective-permute-start(bf16[1056,128]{1,0:T(8,128)(2,1)} %get-tuple-element.16.refs_0_), channel_id=1, source_target_pairs={{0,4},{4,0},{8,12},{12,8},{1,5},{5,1},{9,13},{13,9},{2,6},{6,2},{1... | collective-permute-start | bytes 811016 | tf_op jit(solution)/shard_map/ppermute | solution.py:127
  28.8 3.3 %collective-permute-start = (bf16[2064,128]{1,0:T(8,128)(2,1)}, bf16[2064,128]{1,0:T(8,128)(2,1)S(1)}, u32[]{:S(2)}, u32[]{:S(2)}) collective-permute-start(bf16[2064,128]{1,0:T(8,128)(2,1)} %get-tuple-element.11), channel_id=1, source_target_pairs={{0,12},{1,3},{2,14},{3,1},{4,6},{5,9},{6,4},{7,11},{8,10},{9,5},{1... | collective-permute-start | bytes 1585160 | tf_op jit(solution)/shard_map/ppermute | solution.py:135
  32.1 5.2 %collective-permute-done.1.refs_0_ = bf16[1056,128]{1,0:T(8,128)(2,1)S(1)} collective-permute-done((bf16[1056,128]{1,0:T(8,128)(2,1)}, bf16[1056,128]{1,0:T(8,128)(2,1)S(1)}, u32[]{:S(2)}, u32[]{:S(2)}) %collective-permute-start.1) | collective-permute-done | bytes 270368 | tf_op jit(solution)/shard_map/ppermute | solution.py:127
  37.3 1.8 %collective-permute-start.2 = (bf16[1056,128]{1,0:T(8,128)(2,1)S(1)}, bf16[1056,128]{1,0:T(8,128)(2,1)S(1)}, u32[]{:S(2)}, u32[]{:S(2)}) collective-permute-start(bf16[1056,128]{1,0:T(8,128)(2,1)S(1)} %collective-permute-done.1.refs_0_), channel_id=1, source_target_pairs={{0,2},{1,3},{2,0},{3,1},{4,6},{5,7},{6,4},{7,5},{8,10},{9,11},{10,... | collective-permute-start | bytes 811016 | tf_op jit(solution)/shard_map/ppermute | solution.py:127
  39.2 0.1 pad_add_fusion.1.place
  39.2 0.1 pad_add_fusion.place
  39.3 0.1 slice_reduce_fusion.6
  39.4 6.4 %collective-permute-done.2.refs_1_ = bf16[1056,128]{1,0:T(8,128)(2,1)S(1)} collective-permute-done((bf16[1056,128]{1,0:T(8,128)(2,1)S(1)}, bf16[1056,128]{1,0:T(8,128)(2,1)S(1)}, u32[]{:S(2)}, u32[]{:S(2)}) %collective-permute-start.2) | collective-permute-done | bytes 270368 | tf_op jit(solution)/shard_map/ppermute | solution.py:127
  45.9 0.1 slice_reduce_fusion.5
  46.0 1.6 %collective-permute-start.7 = (bf16[1056,128]{1,0:T(8,128)(2,1)}, bf16[1056,128]{1,0:T(8,128)(2,1)S(1)}, u32[]{:S(2)}, u32[]{:S(2)}) collective-permute-start(bf16[1056,128]{1,0:T(8,128)(2,1)} %get-tuple-element.16.refs_0_), channel_id=1, source_target_pairs={{0,2},{1,3},{2,0},{3,1},{4,6},{5,7},{6,4},{7,5},{8,10},{9,11},{10,... | collective-permute-start | bytes 811016 | tf_op jit(solution)/shard_map/ppermute | solution.py:127
  47.5 0.1 slice_reduce_fusion.4
  47.7 0.1 slice_reduce_fusion.3
  47.8 0.8 %slice_reduce_fusion.7 = bf16[32]{0:T(256)(128)(2,1)S(1)} fusion(bf16[1056,128]{1,0:T(8,128)(2,1)} %get-tuple-element.16.refs_0_), kind=kLoop, calls=%fused_computation.11 | loop fusion | bytes 128 | tf_op jit(solution)/shard_map/slice | solution.py:166
  48.6 0.9 %shard_map.56.refs_3_.refs_7_ = bf16[2,8,128,128]{3,2,1,0:T(8,128)(2,1)S(1)} custom-call(s32[4,32]{1,0:T(4,128)S(1)} %maximum_convert_fusion.index, bf16[1056,128]{1,0:T(8,128)(2,1)S(1)} %collective-permute-done.1.refs_0_, bf16[1056,128]{1,0:T(8,128)(2,1)S(1)} %collective-permute-done.2.refs_1_, bf16[1056,128]{1,0:T(8,128)(2,1)S(1)} %collective-permute-done.3.refs_2_, ...), custom_call_target="tpu_custom_call" | custom-call | flops 1 | bytes 1 | tf_op jit(solution)/shard_map/pallas_call | solution.py:186
  49.6 0.3 collective-permute-start.8
  49.8 1.1 %shard_map.57.refs_8_ = f32[2,128,768]{2,1,0:T(8,128)S(1)} custom-call(s32[2]{0:T(128)S(1)} %pad_add_fusion.1.place, s32[1,32]{1,0:T(1,128)S(1)} %bitcast_convert_fusion.refs_0_, s32[2,8]{1,0:T(2,128)S(1)} %copy-done.2, bf16[2048,128]{1,0:T(8,128)(2,1)S(1)} %bitcast.20, bf16[2,8,128,128]{3,2,1,0:T(8,128)(2,1)S(1)} %shard_map.56.refs_3_.refs_7_), custom_call_target="tpu_custom_call" | custom-call | flops 1 | bytes 1 | tf_op jit(solution)/shard_map/pallas_call | solution.py:202
  50.9 5.3 %collective-permute-done.5.refs_5_ = bf16[2064,128]{1,0:T(8,128)(2,1)S(1)} collective-permute-done((bf16[2064,128]{1,0:T(8,128)(2,1)}, bf16[2064,128]{1,0:T(8,128)(2,1)S(1)}, u32[]{:S(2)}, u32[]{:S(2)}) %collective-permute-start.5) | collective-permute-done | bytes 528416 | tf_op jit(solution)/shard_map/ppermute | solution.py:135
  56.2 0.1 convert_reduce_fusion.2
  56.3 0.1 convert_reduce_fusion.1
  56.5 0.1 collective-permute-start.9
  56.5 0.1 convert_reduce_fusion
  56.7 1.3 %shard_map.61 = bf16[1,6,128,128]{3,2,1,0:T(8,128)(2,1)S(1)} custom-call(s32[4]{0:T(128)S(1)} %pad_add_fusion.place, s32[1,32]{1,0:T(1,128)S(1)} %bitcast_convert_fusion.refs_0_, s32[1,16]{1,0:T(1,128)S(1)} %bitcast.22, s32[1,16]{1,0:T(1,128)S(1)} %bitcast.25, s32[1,16]{1,0:T(1,128)S(1)} %bitcast.28, bf16[2064,128]{1,0:T(8,128)(2,1)S(1)} %collective-permute-done.refs_4_, ...), custom_call_target="tpu_custom_call" | custom-call | flops 1 | bytes 1 | tf_op jit(solution)/shard_map/pallas_call | solution.py:202
  58.0 0.1 collective-permute-start.10
  58.1 1.3 %shard_map.62 = bf16[1,6,128,128]{3,2,1,0:T(8,128)(2,1)S(1)} custom-call(s32[4]{0:T(128)S(1)} %pad_add_fusion.place, s32[1,32]{1,0:T(1,128)S(1)} %bitcast_convert_fusion.refs_0_, s32[1,16]{1,0:T(1,128)S(1)} %bitcast.23, s32[1,16]{1,0:T(1,128)S(1)} %bitcast.26, s32[1,16]{1,0:T(1,128)S(1)} %bitcast.29, bf16[2064,128]{1,0:T(8,128)(2,1)S(1)} %collective-permute-done.refs_4_, ...), custom_call_target="tpu_custom_call" | custom-call | flops 1 | bytes 1 | tf_op jit(solution)/shard_map/pallas_call | solution.py:202
  59.5 0.1 slice_reduce_fusion.2
  59.6 0.1 slice_reduce_fusion.1
  59.7 0.1 slice_reduce_fusion
  59.8 0.9 %shard_map.58.refs_3_.refs_7_ = bf16[2,8,128,128]{3,2,1,0:T(8,128)(2,1)S(1)} custom-call(s32[4,32]{1,0:T(4,128)S(1)} %maximum_convert_fusion.1.index, bf16[1056,128]{1,0:T(8,128)(2,1)S(1)} %copy-done.1, bf16[1056,128]{1,0:T(8,128)(2,1)S(1)} %collective-permute-done.7.refs_1_, bf16[1056,128]{1,0:T(8,128)(2,1)S(1)} %collective-permute-done.8.refs_2_, ...), custom_call_target="tpu_custom_call" | custom-call | flops 1 | bytes 1 | tf_op jit(solution)/shard_map/pallas_call | solution.py:186
  60.8 1.1 %shard_map.59.refs_8_ = f32[2,128,768]{2,1,0:T(8,128)S(1)} custom-call(s32[2]{0:T(128)S(1)} %pad_add_fusion.1.place, s32[2,6]{1,0:T(2,128)S(1)} %copy-done.3, s32[2,8]{1,0:T(2,128)S(1)} %copy-done.2, bf16[2048,128]{1,0:T(8,128)(2,1)S(1)} %bitcast.21, bf16[2,8,128,128]{3,2,1,0:T(8,128)(2,1)S(1)} %shard_map.58.refs_3_.refs_7_), custom_call_target="tpu_custom_call" | custom-call | flops 1 | bytes 1 | tf_op jit(solution)/shard_map/pallas_call | solution.py:202
  61.8 1.8 %shard_map.60 = bf16[2,6,128,128]{3,2,1,0:T(8,128)(2,1)S(1)} custom-call(s32[4]{0:T(128)S(1)} %pad_add_fusion.place, s32[2,6]{1,0:T(2,128)S(1)} %copy-done.3, s32[1,16]{1,0:T(1,128)S(1)} %bitcast.24, s32[1,16]{1,0:T(1,128)S(1)} %bitcast.27, s32[1,16]{1,0:T(1,128)S(1)} %bitcast.30, bf16[2064,128]{1,0:T(8,128)(2,1)S(1)} %collective-permute-done.refs_4_, ...), custom_call_target="tpu_custom_call" | custom-call | flops 1 | bytes 1 | tf_op jit(solution)/shard_map/pallas_call | solution.py:202
  63.7 0.8 %maximum_select_fusion = bf16[2,6,128,128]{3,2,1,0:T(8,128)(2,1)} fusion(bf16[2,6,128,128]{3,2,1,0:T(8,128)(2,1)S(1)} %shard_map.60, bf16[1,6,128,128]{3,2,1,0:T(8,128)(2,1)S(1)} %collective-permute-done.11, bf16[1,6,128,128]{3,2,1,0:T(8,128)(2,1)S(1)} %collective-permute-done.10, pred[]{:T(512)S(6)} %eq.5), kind=kLoop, calls=%fused_computation | loop fusion | flops 393216 | bytes 1179649 | tf_op jit(solution)/shard_map/jit(_where)/select_n | solution.py:234
  (25 shorter events, 0.2 us)
Async XLA Ops:
  25.7 11.6 %collective-permute-start.1 = (bf16[1056,128]{1,0:T(8,128)(2,1)}, bf16[1056,128]{1,0:T(8,128)(2,1)S(1)}, u32[]{:S(2)}, u32[]{:S(2)}) collective-permute-start(bf16[1056,128]{1,0:T(8,128)(2,1)} %get-tuple-element.16.refs_0_), channel_id=1, source_target_pairs={{0,4},{4,0},{8,12},{12,8},{1,5},{5,1},{9,13},{13,9},{2,6},{6,2},{1... | collective-permute-start | bytes 811016 | tf_op jit(solution)/shard_map/ppermute | solution.py:127
  28.8 27.7 %collective-permute-start.6 = (bf16[2064,128]{1,0:T(8,128)(2,1)}, bf16[2064,128]{1,0:T(8,128)(2,1)S(1)}, u32[]{:S(2)}, u32[]{:S(2)}) collective-permute-start(bf16[2064,128]{1,0:T(8,128)(2,1)} %get-tuple-element.11), channel_id=1, source_target_pairs={{0,1},{1,5},{2,3},{3,7},{4,0},{5,4},{6,2},{7,6},{8,12},{9,8},{10,1... | collective-permute-start | bytes 1585160 | tf_op jit(solution)/shard_map/ppermute | solution.py:135
  28.8 27.4 %collective-permute-start.5 = (bf16[2064,128]{1,0:T(8,128)(2,1)}, bf16[2064,128]{1,0:T(8,128)(2,1)S(1)}, u32[]{:S(2)}, u32[]{:S(2)}) collective-permute-start(bf16[2064,128]{1,0:T(8,128)(2,1)} %get-tuple-element.11), channel_id=1, source_target_pairs={{0,1},{1,9},{2,3},{3,11},{4,12},{5,4},{6,14},{7,6},{8,0},{9,8},{10... | collective-permute-start | bytes 1585160 | tf_op jit(solution)/shard_map/ppermute | solution.py:135
  28.8 27.4 %collective-permute-start = (bf16[2064,128]{1,0:T(8,128)(2,1)}, bf16[2064,128]{1,0:T(8,128)(2,1)S(1)}, u32[]{:S(2)}, u32[]{:S(2)}) collective-permute-start(bf16[2064,128]{1,0:T(8,128)(2,1)} %get-tuple-element.11), channel_id=1, source_target_pairs={{0,12},{1,3},{2,14},{3,1},{4,6},{5,9},{6,4},{7,11},{8,10},{9,5},{1... | collective-permute-start | bytes 1585160 | tf_op jit(solution)/shard_map/ppermute | solution.py:135
  37.3 8.5 %collective-permute-start.2 = (bf16[1056,128]{1,0:T(8,128)(2,1)S(1)}, bf16[1056,128]{1,0:T(8,128)(2,1)S(1)}, u32[]{:S(2)}, u32[]{:S(2)}) collective-permute-start(bf16[1056,128]{1,0:T(8,128)(2,1)S(1)} %collective-permute-done.1.refs_0_), channel_id=1, source_target_pairs={{0,2},{1,3},{2,0},{3,1},{4,6},{5,7},{6,4},{7,5},{8,10},{9,11},{10,... | collective-permute-start | bytes 811016 | tf_op jit(solution)/shard_map/ppermute | solution.py:127
  39.3 6.7 %collective-permute-start.3 = (bf16[1056,128]{1,0:T(8,128)(2,1)S(1)}, bf16[1056,128]{1,0:T(8,128)(2,1)S(1)}, u32[]{:S(2)}, u32[]{:S(2)}) collective-permute-start(bf16[1056,128]{1,0:T(8,128)(2,1)S(1)} %collective-permute-done.1.refs_0_), channel_id=1, source_target_pairs={{0,1},{1,0},{2,3},{3,2},{4,5},{5,4},{6,7},{7,6},{8,9},{9,8},{10,11... | collective-permute-start | bytes 811016 | tf_op jit(solution)/shard_map/ppermute | solution.py:127
  45.9 1.8 %collective-permute-start.4 = (bf16[1056,128]{1,0:T(8,128)(2,1)S(1)}, bf16[1056,128]{1,0:T(8,128)(2,1)S(1)}, u32[]{:S(2)}, u32[]{:S(2)}) collective-permute-start(bf16[1056,128]{1,0:T(8,128)(2,1)S(1)} %collective-permute-done.2.refs_1_), channel_id=1, source_target_pairs={{0,1},{1,0},{2,3},{3,2},{4,5},{5,4},{6,7},{7,6},{8,9},{9,8},{10,11... | collective-permute-start | bytes 811016 | tf_op jit(solution)/shard_map/ppermute | solution.py:127
  46.0 10.5 %collective-permute-start.7 = (bf16[1056,128]{1,0:T(8,128)(2,1)}, bf16[1056,128]{1,0:T(8,128)(2,1)S(1)}, u32[]{:S(2)}, u32[]{:S(2)}) collective-permute-start(bf16[1056,128]{1,0:T(8,128)(2,1)} %get-tuple-element.16.refs_0_), channel_id=1, source_target_pairs={{0,2},{1,3},{2,0},{3,1},{4,6},{5,7},{6,4},{7,5},{8,10},{9,11},{10,... | collective-permute-start | bytes 811016 | tf_op jit(solution)/shard_map/ppermute | solution.py:127
  48.6 1.0 %copy-start.1 = (bf16[1056,128]{1,0:T(8,128)(2,1)S(1)}, bf16[1056,128]{1,0:T(8,128)(2,1)}, u32[]{:S(2)}) copy-start(bf16[1056,128]{1,0:T(8,128)(2,1)} %get-tuple-element.16.refs_0_) | copy-start | bytes 811012
  48.6 1.2 %copy-start = (bf16[2,8,128,128]{3,2,1,0:T(8,128)(2,1)S(1)}, bf16[2,8,128,128]{3,2,1,0:T(8,128)(2,1)}, u32[]{:S(2)}) copy-start(bf16[2,8,128,128]{3,2,1,0:T(8,128)(2,1)} %param.7) | copy-start | bytes 1572868
  48.6 1.2 %copy-start.2 = (s32[2,8]{1,0:T(2,128)S(1)}, s32[2,8]{1,0:T(2,128)}, u32[]{:S(2)}) copy-start(s32[2,8]{1,0:T(2,128)} %refs_1_.5) | copy-start | bytes 196
  49.6 10.0 %collective-permute-start.8 = (bf16[1056,128]{1,0:T(8,128)(2,1)S(1)}, bf16[1056,128]{1,0:T(8,128)(2,1)S(1)}, u32[]{:S(2)}, u32[]{:S(2)}) collective-permute-start(bf16[1056,128]{1,0:T(8,128)(2,1)S(1)} %copy-done.1), channel_id=1, source_target_pairs={{0,1},{1,0},{2,3},{3,2},{4,5},{5,4},{6,7},{7,6},{8,9},{9,8},{10,11... | collective-permute-start | bytes 811016 | tf_op jit(solution)/shard_map/ppermute | solution.py:127
  56.5 3.2 %collective-permute-start.9 = (bf16[1056,128]{1,0:T(8,128)(2,1)S(1)}, bf16[1056,128]{1,0:T(8,128)(2,1)S(1)}, u32[]{:S(2)}, u32[]{:S(2)}) collective-permute-start(bf16[1056,128]{1,0:T(8,128)(2,1)S(1)} %collective-permute-done.7.refs_1_), channel_id=1, source_target_pairs={{0,1},{1,0},{2,3},{3,2},{4,5},{5,4},{6,7},{7,6},{8,9},{9,8},{10,11... | collective-permute-start | bytes 811016 | tf_op jit(solution)/shard_map/ppermute | solution.py:127
  58.0 5.7 %collective-permute-start.10 = (bf16[1,6,128,128]{3,2,1,0:T(8,128)(2,1)S(1)}, bf16[1,6,128,128]{3,2,1,0:T(8,128)(2,1)S(1)}, u32[]{:S(2)}, u32[]{:S(2)}) collective-permute-start(bf16[1,6,128,128]{3,2,1,0:T(8,128)(2,1)S(1)} %shard_map.61), channel_id=1, source_target_pairs={{0,4},{1,0},{2,6},{3,2},{4,5},{5,1},{6,7},{7,3},{8,9},{9,13},{10,1... | collective-permute-start | bytes 589832 | tf_op jit(solution)/shard_map/ppermute | solution.py:135
  59.4 4.3 %collective-permute-start.11 = (bf16[1,6,128,128]{3,2,1,0:T(8,128)(2,1)S(1)}, bf16[1,6,128,128]{3,2,1,0:T(8,128)(2,1)S(1)}, u32[]{:S(2)}, u32[]{:S(2)}) collective-permute-start(bf16[1,6,128,128]{3,2,1,0:T(8,128)(2,1)S(1)} %shard_map.62), channel_id=1, source_target_pairs={{0,4},{1,0},{2,6},{3,2},{4,5},{5,1},{6,7},{7,3},{8,9},{9,13},{10,1... | collective-permute-start | bytes 589832 | tf_op jit(solution)/shard_map/ppermute | solution.py:135
  59.8 0.9 %copy-start.3 = (s32[2,6]{1,0:T(2,128)S(1)}, s32[2,6]{1,0:T(2,128)}, u32[]{:S(2)}) copy-start(s32[2,6]{1,0:T(2,128)} %refs_0_.5) | copy-start | bytes 148

commit v15 on v11

--- a/solution.py
+++ b/solution.py
@@ -158,9 +158,8 @@
     flat = b_tiles.reshape(-1, block)
     own, packed = pack(a_tiles, a_cols, c_cols), pack(b_tiles, b_cols)
     shards = {0: flat, end: deliver(flat, end)}
+    cols = {0: (None, b_cols), end: (None, swap(b_cols, "row", row_count, end))}
     own_packs = [own, swap(own, "col", col_count, far)]
-    late_cols = lax.optimization_barrier((b_cols, own_packs[1]))[0]
-    cols = {0: (None, b_cols), end: (None, swap(late_cols, "row", row_count, end))}
     other = swap(own, "row", row_count, 1)
     ready = packed
     for d in range(end - 1, 0, -1):

time: 45.2 us -> 44.8 us (level)
  starting transfers between devices: 15.1 us -> 11.9 us
  waiting for transfers between devices: 15.7 us -> 18.6 us
    ppermute x5, waiting for transfers between devices: 0.31 us -> 5.57 us  [permute(): return lax.ppermute(x, ('row', 'col'), pairs)]
    ppermute x5, starting transfers between devices: 9.93 us -> 6.24 us  [permute(): return lax.ppermute(x, ('row', 'col'), pairs)]
    ppermute x8, waiting for transfers between devices: 15.4 us -> 13 us  [swap(): return lax.ppermute(x, axis, [(k, k ^ d) for k in range(n)])]
    ppermute x8, starting transfers between devices: 5.15 us -> 5.65 us  [swap(): return lax.ppermute(x, axis, [(k, k ^ d) for k in range(n)])]
  transfers between devices with their start and end apart: 13 -> 13, of which waited for: 4 -> 5; matrix products, arithmetic and copies ran while one was open for 3% -> 3% of each run, Pallas kernels for 21% -> 22%
where the time goes in v15:
time: 44.8 us; the launch traced here: 44.6 us
  waiting for transfers between devices  18.6 us (42%)
  starting transfers between devices  11.9 us (27%)
  Pallas kernels  9.62 us (21%)
  local copies, waits for them, and re-layouts  3.21 us (7%)
  other arithmetic  1.14 us (3%)
    ppermute x8, waiting for transfers between devices, swap(): return lax.ppermute(x, axis, [(k, k ^ d) for k in range(n)])  13 us
    pallas_call x5, Pallas kernels, step(): pl.pallas_call(functools.partial(step_kernel, [wanted[0]] + [cols[d][0] f...  6.65 us
    ppermute x5, starting transfers between devices, permute(): return lax.ppermute(x, ('row', 'col'), pairs)  6.24 us
    ppermute x8, starting transfers between devices, swap(): return lax.ppermute(x, axis, [(k, k ^ d) for k in range(n)])  5.65 us
    ppermute x5, waiting for transfers between devices, permute(): return lax.ppermute(x, ('row', 'col'), pairs)  5.57 us
    unnamed x12, local copies, waits for them, and re-layouts  2.32 us
    pallas_call x2, Pallas kernels, dense_of(): pl.pallas_call(functools.partial(left_kernel, a_cols.shape[1]), out_shape...  1.79 us
    pallas_call x2, Pallas kernels, pack(): pl.pallas_call(pack_kernel, out_shape=jax.ShapeDtypeStruct((size + -(-cou...  1.17 us
  transfers between devices with their start and end apart: 13, of which 5 were waited for; matrix products, arithmetic and copies ran while one was open for 3% of the time, Pallas kernels for 22%

profile of v15, /device:TPU:0, one launch (start us, length us, event | category | flops | bytes accessed | tf_op | source)
XLA Modules:
  0.0 44.6 jit_solution(13361018137705409313)
XLA Ops:
  0.0 5.0 %collective-permute-start.2 = (bf16[2048,128]{1,0:T(8,128)(2,1)}, bf16[2048,128]{1,0:T(8,128)(2,1)S(1)}, u32[]{:S(2)}, u32[]{:S(2)}) collective-permute-start(bf16[2048,128]{1,0:T(8,128)(2,1)} %bitcast.18), channel_id=1, source_target_pairs={{0,12},{1,3},{2,14},{3,1},{4,6},{5,9},{6,4},{7,11},{8,10},{9,5},{1... | collective-permute-start | bytes 1572872 | tf_op jit(solution)/shard_map/ppermute | solution.py:123
  5.1 0.9 %copy-done.1 = bf16[2,4,128,128]{3,2,1,0:T(8,128)(2,1)S(1)} copy-done((bf16[2,4,128,128]{3,2,1,0:T(8,128)(2,1)S(1)}, bf16[2,4,128,128]{3,2,1,0:T(8,128)(2,1)}, u32[]{:S(2)}) %copy-start.1) | copy-done | bytes 262168
  6.0 0.7 %copy-done.3 = s32[2,6]{1,0:T(2,128)S(1)} copy-done((s32[2,6]{1,0:T(2,128)S(1)}, s32[2,6]{1,0:T(2,128)}, u32[]{:S(2)}) %copy-start.3) | copy-done | bytes 72
  6.7 0.7 %copy-done.5 = s32[2,4]{1,0:T(2,128)S(1)} copy-done((s32[2,4]{1,0:T(2,128)S(1)}, s32[2,4]{1,0:T(2,128)}, u32[]{:S(2)}) %copy-start.5) | copy-done | bytes 56
  7.4 0.6 %shard_map.56.refs_0_ = bf16[1056,128]{1,0:T(8,128)(2,1)S(1)} custom-call(s32[2,4]{1,0:T(2,128)S(1)} %copy-done.5, s32[2,6]{1,0:T(2,128)S(1)} %copy-done.3, bf16[1024,128]{1,0:T(8,128)(2,1)S(1)} %bitcast.22), custom_call_target="tpu_custom_call" | custom-call | flops 1 | bytes 1 | tf_op jit(solution)/shard_map/pallas_call | solution.py:139
  8.0 1.6 %collective-permute-start.7 = (bf16[1056,128]{1,0:T(8,128)(2,1)S(1)}, bf16[1056,128]{1,0:T(8,128)(2,1)S(1)}, u32[]{:S(2)}, u32[]{:S(2)}) collective-permute-start(bf16[1056,128]{1,0:T(8,128)(2,1)S(1)} %shard_map.56.refs_0_), channel_id=1, source_target_pairs={{0,2},{1,3},{2,0},{3,1},{4,6},{5,7},{6,4},{7,5},{8,10},{9,11},{10,... | collective-permute-start | bytes 811016 | tf_op jit(solution)/shard_map/ppermute | solution.py:115
  9.6 0.9 %collective-permute-start.10 = (s32[2,8]{1,0:T(2,128)S(1)}, s32[2,8]{1,0:T(2,128)S(1)}, u32[]{:S(2)}, u32[]{:S(2)}) collective-permute-start(s32[2,8]{1,0:T(2,128)S(1)} %copy-done.2), channel_id=1, source_target_pairs={{0,12},{4,8},{8,4},{12,0},{1,13},{5,9},{9,5},{13,1},{2,14},{6,10},... | collective-permute-start | bytes 200 | tf_op jit(solution)/shard_map/ppermute | solution.py:115
  10.5 0.1 slice_reduce_fusion.3
  10.6 0.6 %shard_map.55 = bf16[2064,128]{1,0:T(8,128)(2,1)S(1)} custom-call(s32[2,8]{1,0:T(2,128)S(1)} %copy-done.2, bf16[2048,128]{1,0:T(8,128)(2,1)S(1)} %bitcast.19), custom_call_target="tpu_custom_call" | custom-call | flops 1 | bytes 1 | tf_op jit(solution)/shard_map/pallas_call | solution.py:139
  11.2 7.2 %collective-permute-done.1.refs_0_ = bf16[1056,128]{1,0:T(8,128)(2,1)S(1)} collective-permute-done((bf16[1056,128]{1,0:T(8,128)(2,1)S(1)}, bf16[1056,128]{1,0:T(8,128)(2,1)S(1)}, u32[]{:S(2)}, u32[]{:S(2)}) %collective-permute-start.1) | collective-permute-done | bytes 270368 | tf_op jit(solution)/shard_map/ppermute | solution.py:115
  18.4 1.6 %collective-permute-start.3 = (bf16[1056,128]{1,0:T(8,128)(2,1)S(1)}, bf16[1056,128]{1,0:T(8,128)(2,1)S(1)}, u32[]{:S(2)}, u32[]{:S(2)}) collective-permute-start(bf16[1056,128]{1,0:T(8,128)(2,1)S(1)} %collective-permute-done.1.refs_0_), channel_id=1, source_target_pairs={{0,2},{1,3},{2,0},{3,1},{4,6},{5,7},{6,4},{7,5},{8,10},{9,11},{10,... | collective-permute-start | bytes 811016 | tf_op jit(solution)/shard_map/ppermute | solution.py:115
  20.1 1.1 %collective-permute-start = (bf16[2064,128]{1,0:T(8,128)(2,1)S(1)}, bf16[2064,128]{1,0:T(8,128)(2,1)S(1)}, u32[]{:S(2)}, u32[]{:S(2)}) collective-permute-start(bf16[2064,128]{1,0:T(8,128)(2,1)S(1)} %shard_map.55), channel_id=1, source_target_pairs={{0,1},{1,5},{2,3},{3,7},{4,0},{5,4},{6,2},{7,6},{8,12},{9,8},{10,1... | collective-permute-start | bytes 1585160 | tf_op jit(solution)/shard_map/ppermute | solution.py:123
  21.2 0.1 slice_reduce_fusion.2
  21.3 0.6 %collective-permute-start.4 = (bf16[1056,128]{1,0:T(8,128)(2,1)S(1)}, bf16[1056,128]{1,0:T(8,128)(2,1)S(1)}, u32[]{:S(2)}, u32[]{:S(2)}) collective-permute-start(bf16[1056,128]{1,0:T(8,128)(2,1)S(1)} %collective-permute-done.1.refs_0_), channel_id=1, source_target_pairs={{0,1},{1,0},{2,3},{3,2},{4,5},{5,4},{6,7},{7,6},{8,9},{9,8},{10,11... | collective-permute-start | bytes 811016 | tf_op jit(solution)/shard_map/ppermute | solution.py:115
  22.1 5.1 %collective-permute-done.3.refs_1_ = bf16[1056,128]{1,0:T(8,128)(2,1)S(1)} collective-permute-done((bf16[1056,128]{1,0:T(8,128)(2,1)S(1)}, bf16[1056,128]{1,0:T(8,128)(2,1)S(1)}, u32[]{:S(2)}, u32[]{:S(2)}) %collective-permute-start.3) | collective-permute-done | bytes 270368 | tf_op jit(solution)/shard_map/ppermute | solution.py:115
  27.1 0.8 %collective-permute-start.5 = (bf16[1056,128]{1,0:T(8,128)(2,1)S(1)}, bf16[1056,128]{1,0:T(8,128)(2,1)S(1)}, u32[]{:S(2)}, u32[]{:S(2)}) collective-permute-start(bf16[1056,128]{1,0:T(8,128)(2,1)S(1)} %collective-permute-done.3.refs_1_), channel_id=1, source_target_pairs={{0,1},{1,0},{2,3},{3,2},{4,5},{5,4},{6,7},{7,6},{8,9},{9,8},{10,11... | collective-permute-start | bytes 811016 | tf_op jit(solution)/shard_map/ppermute | solution.py:115
  27.9 0.1 slice_reduce_fusion.7
  28.2 0.1 slice_reduce_fusion.5
  28.3 0.7 %collective-permute-done.5.refs_3_ = bf16[1056,128]{1,0:T(8,128)(2,1)S(1)} collective-permute-done((bf16[1056,128]{1,0:T(8,128)(2,1)S(1)}, bf16[1056,128]{1,0:T(8,128)(2,1)S(1)}, u32[]{:S(2)}, u32[]{:S(2)}) %collective-permute-start.5) | collective-permute-done | bytes 270368 | tf_op jit(solution)/shard_map/ppermute | solution.py:115
  29.2 0.9 %shard_map.57.refs_5_ = bf16[2,8,128,128]{3,2,1,0:T(8,128)(2,1)S(1)} custom-call(s32[4,32]{1,0:T(4,128)S(1)} %maximum_convert_fusion.index, bf16[1056,128]{1,0:T(8,128)(2,1)S(1)} %collective-permute-done.1.refs_0_, bf16[1056,128]{1,0:T(8,128)(2,1)S(1)} %collective-permute-done.3.refs_1_, bf16[1056,128]{1,0:T(8,128)(2,1)S(1)} %collective-permute-done.4.refs_2_, ...), custom_call_target="tpu_custom_call" | custom-call | flops 1 | bytes 1 | tf_op jit(solution)/shard_map/pallas_call | solution.py:170
  30.1 1.4 %shard_map.61.refs_6_ = f32[2,128,768]{2,1,0:T(8,128)S(1)} custom-call(s32[3]{0:T(128)S(1)} %get-tuple-element.12.place, s32[1,32]{1,0:T(1,128)S(1)} %bitcast_convert_fusion.refs_0_, s32[2,8]{1,0:T(2,128)S(1)} %copy-done.2, s32[2,8]{1,0:T(2,128)S(1)} %collective-permute-done.10.refs_2_, bf16[2048,128]{1,0:T(8,128)(2,1)S(1)} %bitcast.20, ...), custom_call_target="tpu_custom_call" | custom-call | flops 1 | bytes 1 | tf_op jit(solution)/shard_map/pallas_call | solution.py:186
  31.6 2.7 %collective-permute-done.6.refs_4_ = bf16[2064,128]{1,0:T(8,128)(2,1)S(1)} collective-permute-done((bf16[2064,128]{1,0:T(8,128)(2,1)S(1)}, bf16[2064,128]{1,0:T(8,128)(2,1)S(1)}, u32[]{:S(2)}, u32[]{:S(2)}) %collective-permute-start.6) | collective-permute-done | bytes 528416 | tf_op jit(solution)/shard_map/ppermute | solution.py:123
  34.3 2.8 %collective-permute-done.refs_3_ = bf16[2064,128]{1,0:T(8,128)(2,1)S(1)} collective-permute-done((bf16[2064,128]{1,0:T(8,128)(2,1)S(1)}, bf16[2064,128]{1,0:T(8,128)(2,1)S(1)}, u32[]{:S(2)}, u32[]{:S(2)}) %collective-permute-start) | collective-permute-done | bytes 528416 | tf_op jit(solution)/shard_map/ppermute | solution.py:123
  37.1 0.1 convert_reduce_fusion
  37.2 0.1 convert_reduce_fusion.1
  37.3 1.1 %shard_map.62 = bf16[1,6,128,128]{3,2,1,0:T(8,128)(2,1)S(1)} custom-call(s32[3]{0:T(128)S(1)} %get-tuple-element.11.place, s32[1,32]{1,0:T(1,128)S(1)} %bitcast_convert_fusion.refs_0_, s32[1,16]{1,0:T(1,128)S(1)} %bitcast.26, s32[1,16]{1,0:T(1,128)S(1)} %bitcast.23, bf16[2064,128]{1,0:T(8,128)(2,1)S(1)} %collective-permute-done.refs_3_, ...), custom_call_target="tpu_custom_call" | custom-call | flops 1 | bytes 1 | tf_op jit(solution)/shard_map/pallas_call | solution.py:186
  38.5 1.1 %shard_map.63 = bf16[1,6,128,128]{3,2,1,0:T(8,128)(2,1)S(1)} custom-call(s32[3]{0:T(128)S(1)} %get-tuple-element.11.place, s32[1,32]{1,0:T(1,128)S(1)} %bitcast_convert_fusion.refs_0_, s32[1,16]{1,0:T(1,128)S(1)} %bitcast.27, s32[1,16]{1,0:T(1,128)S(1)} %bitcast.24, bf16[2064,128]{1,0:T(8,128)(2,1)S(1)} %collective-permute-done.refs_3_, ...), custom_call_target="tpu_custom_call" | custom-call | flops 1 | bytes 1 | tf_op jit(solution)/shard_map/pallas_call | solution.py:186
  39.8 0.1 slice_reduce_fusion
  39.9 0.9 %shard_map.58.refs_5_ = bf16[2,8,128,128]{3,2,1,0:T(8,128)(2,1)S(1)} custom-call(s32[4,32]{1,0:T(4,128)S(1)} %maximum_convert_fusion.1.index, bf16[1056,128]{1,0:T(8,128)(2,1)S(1)} %shard_map.56.refs_0_, bf16[1056,128]{1,0:T(8,128)(2,1)S(1)} %collective-permute-done.7.refs_1_, bf16[1056,128]{1,0:T(8,128)(2,1)S(1)} %collective-permute-done.8.refs_2_, ...), custom_call_target="tpu_custom_call" | custom-call | flops 1 | bytes 1 | tf_op jit(solution)/shard_map/pallas_call | solution.py:170
  40.8 1.4 %shard_map.59.refs_6_ = f32[2,128,768]{2,1,0:T(8,128)S(1)} custom-call(s32[3]{0:T(128)S(1)} %get-tuple-element.12.place, s32[2,6]{1,0:T(2,128)S(1)} %copy-done.4, s32[2,8]{1,0:T(2,128)S(1)} %copy-done.2, s32[2,8]{1,0:T(2,128)S(1)} %collective-permute-done.10.refs_2_, bf16[2048,128]{1,0:T(8,128)(2,1)S(1)} %bitcast.21, ...), custom_call_target="tpu_custom_call" | custom-call | flops 1 | bytes 1 | tf_op jit(solution)/shard_map/pallas_call | solution.py:186
  42.3 1.5 %shard_map.60 = bf16[2,6,128,128]{3,2,1,0:T(8,128)(2,1)S(1)} custom-call(s32[3]{0:T(128)S(1)} %get-tuple-element.11.place, s32[2,6]{1,0:T(2,128)S(1)} %copy-done.4, s32[1,16]{1,0:T(1,128)S(1)} %bitcast.28, s32[1,16]{1,0:T(1,128)S(1)} %bitcast.25, bf16[2064,128]{1,0:T(8,128)(2,1)S(1)} %collective-permute-done.refs_3_, ...), custom_call_target="tpu_custom_call" | custom-call | flops 1 | bytes 1 | tf_op jit(solution)/shard_map/pallas_call | solution.py:186
  43.8 0.8 %maximum_select_fusion = bf16[2,6,128,128]{3,2,1,0:T(8,128)(2,1)} fusion(bf16[2,6,128,128]{3,2,1,0:T(8,128)(2,1)S(1)} %shard_map.60, bf16[1,6,128,128]{3,2,1,0:T(8,128)(2,1)S(1)} %collective-permute-done.12, bf16[1,6,128,128]{3,2,1,0:T(8,128)(2,1)S(1)} %collective-permute-done.11, pred[]{:T(512)S(6)} %eq.5), kind=kLoop, calls=%fused_computation | loop fusion | flops 393216 | bytes 1179649 | tf_op jit(solution)/shard_map/jit(_where)/select_n | solution.py:217
  (30 shorter events, 0.8 us)
Async XLA Ops:
  0.0 10.6 %copy-start = (bf16[2,8,128,128]{3,2,1,0:T(8,128)(2,1)S(1)}, bf16[2,8,128,128]{3,2,1,0:T(8,128)(2,1)}, u32[]{:S(2)}) copy-start(bf16[2,8,128,128]{3,2,1,0:T(8,128)(2,1)} %param.7) | copy-start | bytes 1572868
  0.0 18.4 %collective-permute-start.2 = (bf16[2048,128]{1,0:T(8,128)(2,1)}, bf16[2048,128]{1,0:T(8,128)(2,1)S(1)}, u32[]{:S(2)}, u32[]{:S(2)}) collective-permute-start(bf16[2048,128]{1,0:T(8,128)(2,1)} %bitcast.18), channel_id=1, source_target_pairs={{0,12},{1,3},{2,14},{3,1},{4,6},{5,9},{6,4},{7,11},{8,10},{9,5},{1... | collective-permute-start | bytes 1572872 | tf_op jit(solution)/shard_map/ppermute | solution.py:123
  5.1 0.9 %copy-start.1 = (bf16[2,4,128,128]{3,2,1,0:T(8,128)(2,1)S(1)}, bf16[2,4,128,128]{3,2,1,0:T(8,128)(2,1)}, u32[]{:S(2)}) copy-start(bf16[2,4,128,128]{3,2,1,0:T(8,128)(2,1)} %param.5) | copy-start | bytes 786436
  6.0 0.7 %copy-start.3 = (s32[2,6]{1,0:T(2,128)S(1)}, s32[2,6]{1,0:T(2,128)}, u32[]{:S(2)}) copy-start(s32[2,6]{1,0:T(2,128)} %refs_0_.7) | copy-start | bytes 148
  6.7 0.7 %copy-start.5 = (s32[2,4]{1,0:T(2,128)S(1)}, s32[2,4]{1,0:T(2,128)}, u32[]{:S(2)}) copy-start(s32[2,4]{1,0:T(2,128)} %refs_0_.5) | copy-start | bytes 100
  7.4 2.2 %copy-start.2 = (s32[2,8]{1,0:T(2,128)S(1)}, s32[2,8]{1,0:T(2,128)}, u32[]{:S(2)}) copy-start(s32[2,8]{1,0:T(2,128)} %refs_1_.5) | copy-start | bytes 196
  8.0 10.5 %collective-permute-start.1 = (bf16[1056,128]{1,0:T(8,128)(2,1)S(1)}, bf16[1056,128]{1,0:T(8,128)(2,1)S(1)}, u32[]{:S(2)}, u32[]{:S(2)}) collective-permute-start(bf16[1056,128]{1,0:T(8,128)(2,1)S(1)} %shard_map.56.refs_0_), channel_id=1, source_target_pairs={{0,4},{4,0},{8,12},{12,8},{1,5},{5,1},{9,13},{13,9},{2,6},{6,2},{1... | collective-permute-start | bytes 811016 | tf_op jit(solution)/shard_map/ppermute | solution.py:115
  8.0 12.1 %collective-permute-start.7 = (bf16[1056,128]{1,0:T(8,128)(2,1)S(1)}, bf16[1056,128]{1,0:T(8,128)(2,1)S(1)}, u32[]{:S(2)}, u32[]{:S(2)}) collective-permute-start(bf16[1056,128]{1,0:T(8,128)(2,1)S(1)} %shard_map.56.refs_0_), channel_id=1, source_target_pairs={{0,2},{1,3},{2,0},{3,1},{4,6},{5,7},{6,4},{7,5},{8,10},{9,11},{10,... | collective-permute-start | bytes 811016 | tf_op jit(solution)/shard_map/ppermute | solution.py:115
  9.6 11.7 %collective-permute-start.8 = (bf16[1056,128]{1,0:T(8,128)(2,1)S(1)}, bf16[1056,128]{1,0:T(8,128)(2,1)S(1)}, u32[]{:S(2)}, u32[]{:S(2)}) collective-permute-start(bf16[1056,128]{1,0:T(8,128)(2,1)S(1)} %shard_map.56.refs_0_), channel_id=1, source_target_pairs={{0,1},{1,0},{2,3},{3,2},{4,5},{5,4},{6,7},{7,6},{8,9},{9,8},{10,11... | collective-permute-start | bytes 811016 | tf_op jit(solution)/shard_map/ppermute | solution.py:115
  9.6 20.5 %collective-permute-start.10 = (s32[2,8]{1,0:T(2,128)S(1)}, s32[2,8]{1,0:T(2,128)S(1)}, u32[]{:S(2)}, u32[]{:S(2)}) collective-permute-start(s32[2,8]{1,0:T(2,128)S(1)} %copy-done.2), channel_id=1, source_target_pairs={{0,12},{4,8},{8,4},{12,0},{1,13},{5,9},{9,5},{13,1},{2,14},{6,10},... | collective-permute-start | bytes 200 | tf_op jit(solution)/shard_map/ppermute | solution.py:115
  18.4 15.9 %collective-permute-start.6 = (bf16[2064,128]{1,0:T(8,128)(2,1)S(1)}, bf16[2064,128]{1,0:T(8,128)(2,1)S(1)}, u32[]{:S(2)}, u32[]{:S(2)}) collective-permute-start(bf16[2064,128]{1,0:T(8,128)(2,1)S(1)} %shard_map.55), channel_id=1, source_target_pairs={{0,1},{1,9},{2,3},{3,11},{4,12},{5,4},{6,14},{7,6},{8,0},{9,8},{10... | collective-permute-start | bytes 1585160 | tf_op jit(solution)/shard_map/ppermute | solution.py:123
  18.4 8.7 %collective-permute-start.3 = (bf16[1056,128]{1,0:T(8,128)(2,1)S(1)}, bf16[1056,128]{1,0:T(8,128)(2,1)S(1)}, u32[]{:S(2)}, u32[]{:S(2)}) collective-permute-start(bf16[1056,128]{1,0:T(8,128)(2,1)S(1)} %collective-permute-done.1.refs_0_), channel_id=1, source_target_pairs={{0,2},{1,3},{2,0},{3,1},{4,6},{5,7},{6,4},{7,5},{8,10},{9,11},{10,... | collective-permute-start | bytes 811016 | tf_op jit(solution)/shard_map/ppermute | solution.py:115
  20.1 17.0 %collective-permute-start = (bf16[2064,128]{1,0:T(8,128)(2,1)S(1)}, bf16[2064,128]{1,0:T(8,128)(2,1)S(1)}, u32[]{:S(2)}, u32[]{:S(2)}) collective-permute-start(bf16[2064,128]{1,0:T(8,128)(2,1)S(1)} %shard_map.55), channel_id=1, source_target_pairs={{0,1},{1,5},{2,3},{3,7},{4,0},{5,4},{6,2},{7,6},{8,12},{9,8},{10,1... | collective-permute-start | bytes 1585160 | tf_op jit(solution)/shard_map/ppermute | solution.py:123
  21.3 6.8 %collective-permute-start.4 = (bf16[1056,128]{1,0:T(8,128)(2,1)S(1)}, bf16[1056,128]{1,0:T(8,128)(2,1)S(1)}, u32[]{:S(2)}, u32[]{:S(2)}) collective-permute-start(bf16[1056,128]{1,0:T(8,128)(2,1)S(1)} %collective-permute-done.1.refs_0_), channel_id=1, source_target_pairs={{0,1},{1,0},{2,3},{3,2},{4,5},{5,4},{6,7},{7,6},{8,9},{9,8},{10,11... | collective-permute-start | bytes 811016 | tf_op jit(solution)/shard_map/ppermute | solution.py:115
  27.1 1.9 %collective-permute-start.5 = (bf16[1056,128]{1,0:T(8,128)(2,1)S(1)}, bf16[1056,128]{1,0:T(8,128)(2,1)S(1)}, u32[]{:S(2)}, u32[]{:S(2)}) collective-permute-start(bf16[1056,128]{1,0:T(8,128)(2,1)S(1)} %collective-permute-done.3.refs_1_), channel_id=1, source_target_pairs={{0,1},{1,0},{2,3},{3,2},{4,5},{5,4},{6,7},{7,6},{8,9},{9,8},{10,11... | collective-permute-start | bytes 811016 | tf_op jit(solution)/shard_map/ppermute | solution.py:115
  28.1 11.6 %collective-permute-start.9 = (bf16[1056,128]{1,0:T(8,128)(2,1)S(1)}, bf16[1056,128]{1,0:T(8,128)(2,1)S(1)}, u32[]{:S(2)}, u32[]{:S(2)}) collective-permute-start(bf16[1056,128]{1,0:T(8,128)(2,1)S(1)} %collective-permute-done.7.refs_1_), channel_id=1, source_target_pairs={{0,1},{1,0},{2,3},{3,2},{4,5},{5,4},{6,7},{7,6},{8,9},{9,8},{10,11... | collective-permute-start | bytes 811016 | tf_op jit(solution)/shard_map/ppermute | solution.py:115
  38.5 5.3 %collective-permute-start.11 = (bf16[1,6,128,128]{3,2,1,0:T(8,128)(2,1)S(1)}, bf16[1,6,128,128]{3,2,1,0:T(8,128)(2,1)S(1)}, u32[]{:S(2)}, u32[]{:S(2)}) collective-permute-start(bf16[1,6,128,128]{3,2,1,0:T(8,128)(2,1)S(1)} %shard_map.62), channel_id=1, source_target_pairs={{0,4},{1,0},{2,6},{3,2},{4,5},{5,1},{6,7},{7,3},{8,9},{9,13},{10,1... | collective-permute-start | bytes 589832 | tf_op jit(solution)/shard_map/ppermute | solution.py:123
  39.7 4.1 %collective-permute-start.12 = (bf16[1,6,128,128]{3,2,1,0:T(8,128)(2,1)S(1)}, bf16[1,6,128,128]{3,2,1,0:T(8,128)(2,1)S(1)}, u32[]{:S(2)}, u32[]{:S(2)}) collective-permute-start(bf16[1,6,128,128]{3,2,1,0:T(8,128)(2,1)S(1)} %shard_map.63), channel_id=1, source_target_pairs={{0,4},{1,0},{2,6},{3,2},{4,5},{5,1},{6,7},{7,3},{8,9},{9,13},{10,1... | collective-permute-start | bytes 589832 | tf_op jit(solution)/shard_map/ppermute | solution.py:123
  39.9 0.9 %copy-start.4 = (s32[2,6]{1,0:T(2,128)S(1)}, s32[2,6]{1,0:T(2,128)}, u32[]{:S(2)}) copy-start(s32[2,6]{1,0:T(2,128)} %refs_0_.7) | copy-start | bytes 148

commit v16 on v10

--- a/solution.py
+++ b/solution.py
@@ -158,12 +158,13 @@
     flat = b_tiles.reshape(-1, block)
     own, packed = pack(a_tiles, a_cols, c_cols), pack(b_tiles, b_cols)
     shards = {0: flat, end: deliver(flat, end)}
-    cols = {0: (None, b_cols), end: (None, swap(b_cols, "row", row_count, end))}
     own_packs = [own, swap(own, "col", col_count, far)]
+    late_cols = lax.optimization_barrier((b_cols, own_packs[1]))[0]
+    cols = {0: (None, b_cols), end: (None, swap(late_cols, "row", row_count, end))}
     other = swap(own, "row", row_count, 1)
     ready = lax.optimization_barrier((packed, own_packs[1]))[0]
     for d in range(end - 1, 0, -1):
-        shards[d] = deliver(ready, d)
+        shards[d] = deliver(ready if d > 1 else packed, d)
     other = lax.optimization_barrier((other, shards[end]))[0]
     own_packs, other_packs = across(own_packs, far // 2), across([other], far)
     def dense_of(packs):

time: 40.5 us -> 42.4 us (1.047)
  starting transfers between devices: 10.5 us -> 13.5 us
  waiting for transfers between devices: 17.2 us -> 16 us
    ppermute x8, waiting for transfers between devices: 13.3 us -> 7.01 us  [swap(): return lax.ppermute(x, axis, [(k, k ^ d) for k in range(n)])]
    ppermute x5, waiting for transfers between devices: 3.85 us -> 9.03 us  [permute(): return lax.ppermute(x, ('row', 'col'), pairs)]
    ppermute x5, starting transfers between devices: 5.25 us -> 7.24 us  [permute(): return lax.ppermute(x, ('row', 'col'), pairs)]
    ppermute x8, starting transfers between devices: 5.22 us -> 6.26 us  [swap(): return lax.ppermute(x, axis, [(k, k ^ d) for k in range(n)])]
  transfers between devices with their start and end apart: 13 -> 13, of which waited for: 5 -> 7; matrix products, arithmetic and copies ran while one was open for 3% -> 3% of each run, Pallas kernels for 20% -> 19%
where the time goes in v16:
time: 42.4 us; the launch traced here: 42.2 us
  waiting for transfers between devices  16 us (38%)
  starting transfers between devices  13.5 us (32%)
  Pallas kernels  8.12 us (19%)
  local copies, waits for them, and re-layouts  3.29 us (8%)
  other arithmetic  1.06 us (2%)
    ppermute x5, waiting for transfers between devices, permute(): return lax.ppermute(x, ('row', 'col'), pairs)  9.03 us
    ppermute x5, starting transfers between devices, permute(): return lax.ppermute(x, ('row', 'col'), pairs)  7.24 us
    ppermute x8, waiting for transfers between devices, swap(): return lax.ppermute(x, axis, [(k, k ^ d) for k in range(n)])  7.01 us
    ppermute x8, starting transfers between devices, swap(): return lax.ppermute(x, axis, [(k, k ^ d) for k in range(n)])  6.26 us
    pallas_call x3, Pallas kernels, step(): pl.pallas_call(functools.partial(step_kernel, [wanted[0]] + [cols[d][0] f...  5.16 us
    unnamed x12, local copies, waits for them, and re-layouts  2.32 us
    pallas_call x2, Pallas kernels, dense_of(): pl.pallas_call(functools.partial(left_kernel, a_cols.shape[1]), out_shape...  1.79 us
    pallas_call x2, Pallas kernels, pack(): pl.pallas_call(pack_kernel, out_shape=jax.ShapeDtypeStruct((size + -(-cou...  1.17 us
  transfers between devices with their start and end apart: 13, of which 7 were waited for; matrix products, arithmetic and copies ran while one was open for 3% of the time, Pallas kernels for 19%

profile of v16, /device:TPU:0, one launch (start us, length us, event | category | flops | bytes accessed | tf_op | source)
XLA Modules:
  0.0 42.2 jit_solution(17046709599037194829)
XLA Ops:
  0.0 5.0 %collective-permute-start.4 = (bf16[2048,128]{1,0:T(8,128)(2,1)}, bf16[2048,128]{1,0:T(8,128)(2,1)S(1)}, u32[]{:S(2)}, u32[]{:S(2)}) collective-permute-start(bf16[2048,128]{1,0:T(8,128)(2,1)} %bitcast.18), channel_id=1, source_target_pairs={{0,12},{1,3},{2,14},{3,1},{4,6},{5,9},{6,4},{7,11},{8,10},{9,5},{1... | collective-permute-start | bytes 1572872 | tf_op jit(solution)/shard_map/ppermute | solution.py:123
  5.1 0.9 %copy-done.1 = bf16[2,4,128,128]{3,2,1,0:T(8,128)(2,1)S(1)} copy-done((bf16[2,4,128,128]{3,2,1,0:T(8,128)(2,1)S(1)}, bf16[2,4,128,128]{3,2,1,0:T(8,128)(2,1)}, u32[]{:S(2)}) %copy-start.1) | copy-done | bytes 262168
  6.0 0.7 %copy-done.3 = s32[2,6]{1,0:T(2,128)S(1)} copy-done((s32[2,6]{1,0:T(2,128)S(1)}, s32[2,6]{1,0:T(2,128)}, u32[]{:S(2)}) %copy-start.3) | copy-done | bytes 72
  6.7 0.7 %copy-done.5 = s32[2,4]{1,0:T(2,128)S(1)} copy-done((s32[2,4]{1,0:T(2,128)S(1)}, s32[2,4]{1,0:T(2,128)}, u32[]{:S(2)}) %copy-start.5) | copy-done | bytes 56
  7.4 0.6 %shard_map.56.refs_0_ = bf16[1056,128]{1,0:T(8,128)(2,1)S(1)} custom-call(s32[2,4]{1,0:T(2,128)S(1)} %copy-done.5, s32[2,6]{1,0:T(2,128)S(1)} %copy-done.3, bf16[1024,128]{1,0:T(8,128)(2,1)S(1)} %bitcast.23), custom_call_target="tpu_custom_call" | custom-call | flops 1 | bytes 1 | tf_op jit(solution)/shard_map/pallas_call | solution.py:139
  8.0 1.6 %collective-permute-start.1 = (bf16[1056,128]{1,0:T(8,128)(2,1)S(1)}, bf16[1056,128]{1,0:T(8,128)(2,1)S(1)}, u32[]{:S(2)}, u32[]{:S(2)}) collective-permute-start(bf16[1056,128]{1,0:T(8,128)(2,1)S(1)} %shard_map.56.refs_0_), channel_id=1, source_target_pairs={{0,2},{1,3},{2,0},{3,1},{4,6},{5,7},{6,4},{7,5},{8,10},{9,11},{10,... | collective-permute-start | bytes 811016 | tf_op jit(solution)/shard_map/ppermute | solution.py:115
  9.5 0.6 %shard_map.55 = bf16[2064,128]{1,0:T(8,128)(2,1)S(1)} custom-call(s32[2,8]{1,0:T(2,128)S(1)} %copy-done.2, bf16[2048,128]{1,0:T(8,128)(2,1)S(1)} %bitcast.19), custom_call_target="tpu_custom_call" | custom-call | flops 1 | bytes 1 | tf_op jit(solution)/shard_map/pallas_call | solution.py:139
  10.1 0.6 %collective-permute-start = (bf16[2064,128]{1,0:T(8,128)(2,1)S(1)}, bf16[2064,128]{1,0:T(8,128)(2,1)S(1)}, u32[]{:S(2)}, u32[]{:S(2)}) collective-permute-start(bf16[2064,128]{1,0:T(8,128)(2,1)S(1)} %shard_map.55), channel_id=1, source_target_pairs={{0,1},{1,5},{2,3},{3,7},{4,0},{5,4},{6,2},{7,6},{8,12},{9,8},{10,1... | collective-permute-start | bytes 1585160 | tf_op jit(solution)/shard_map/ppermute | solution.py:123
  10.7 0.1 slice_reduce_fusion.6
  10.9 4.4 %collective-permute-done.1.refs_1_ = bf16[1056,128]{1,0:T(8,128)(2,1)S(1)} collective-permute-done((bf16[1056,128]{1,0:T(8,128)(2,1)S(1)}, bf16[1056,128]{1,0:T(8,128)(2,1)S(1)}, u32[]{:S(2)}, u32[]{:S(2)}) %collective-permute-start.1) | collective-permute-done | bytes 270368 | tf_op jit(solution)/shard_map/ppermute | solution.py:115
  15.3 2.2 %collective-permute-start.3 = (s32[2,8]{1,0:T(2,128)S(1)}, s32[2,8]{1,0:T(2,128)S(1)}, u32[]{:S(2)}, u32[]{:S(2)}) collective-permute-start(s32[2,8]{1,0:T(2,128)S(1)} %copy-done.2), channel_id=1, source_target_pairs={{0,12},{4,8},{8,4},{12,0},{1,13},{5,9},{9,5},{13,1},{2,14},{6,10},... | collective-permute-start | bytes 200 | tf_op jit(solution)/shard_map/ppermute | solution.py:115
  17.5 0.1 slice_reduce_fusion.5
  17.6 1.5 %collective-permute-start.2 = (bf16[2064,128]{1,0:T(8,128)(2,1)S(1)}, bf16[2064,128]{1,0:T(8,128)(2,1)S(1)}, u32[]{:S(2)}, u32[]{:S(2)}) collective-permute-start(bf16[2064,128]{1,0:T(8,128)(2,1)S(1)} %shard_map.55), channel_id=1, source_target_pairs={{0,1},{1,9},{2,3},{3,11},{4,12},{5,4},{6,14},{7,6},{8,0},{9,8},{10... | collective-permute-start | bytes 1585160 | tf_op jit(solution)/shard_map/ppermute | solution.py:123
  19.1 0.1 slice_reduce_fusion.4
  19.3 2.4 %collective-permute-start.8 = (bf16[1056,128]{1,0:T(8,128)(2,1)S(1)}, bf16[1056,128]{1,0:T(8,128)(2,1)S(1)}, u32[]{:S(2)}, u32[]{:S(2)}) collective-permute-start(bf16[1056,128]{1,0:T(8,128)(2,1)S(1)} %collective-permute-done.7.refs_0_), channel_id=1, source_target_pairs={{0,2},{1,3},{2,0},{3,1},{4,6},{5,7},{6,4},{7,5},{8,10},{9,11},{10,... | collective-permute-start | bytes 811016 | tf_op jit(solution)/shard_map/ppermute | solution.py:115
  21.8 0.1 slice_reduce_fusion.7
  22.0 4.4 %collective-permute-done.refs_5_ = bf16[2064,128]{1,0:T(8,128)(2,1)S(1)} collective-permute-done((bf16[2064,128]{1,0:T(8,128)(2,1)S(1)}, bf16[2064,128]{1,0:T(8,128)(2,1)S(1)}, u32[]{:S(2)}, u32[]{:S(2)}) %collective-permute-start) | collective-permute-done | bytes 528416 | tf_op jit(solution)/shard_map/ppermute | solution.py:123
  26.4 1.3 %collective-permute-done.8.refs_1_ = bf16[1056,128]{1,0:T(8,128)(2,1)S(1)} collective-permute-done((bf16[1056,128]{1,0:T(8,128)(2,1)S(1)}, bf16[1056,128]{1,0:T(8,128)(2,1)S(1)}, u32[]{:S(2)}, u32[]{:S(2)}) %collective-permute-start.8) | collective-permute-done | bytes 270368 | tf_op jit(solution)/shard_map/ppermute | solution.py:115
  27.7 0.1 convert_reduce_fusion.1
  27.8 0.1 slice_reduce_fusion.2
  28.0 0.1 slice_reduce_fusion.1
  28.1 1.2 %collective-permute-done.10.refs_3_ = bf16[1056,128]{1,0:T(8,128)(2,1)S(1)} collective-permute-done((bf16[1056,128]{1,0:T(8,128)(2,1)S(1)}, bf16[1056,128]{1,0:T(8,128)(2,1)S(1)}, u32[]{:S(2)}, u32[]{:S(2)}) %collective-permute-start.10) | collective-permute-done | bytes 270368 | tf_op jit(solution)/shard_map/ppermute | solution.py:115
  29.4 4.1 %collective-permute-done.2.refs_6_ = bf16[2064,128]{1,0:T(8,128)(2,1)S(1)} collective-permute-done((bf16[2064,128]{1,0:T(8,128)(2,1)S(1)}, bf16[2064,128]{1,0:T(8,128)(2,1)S(1)}, u32[]{:S(2)}, u32[]{:S(2)}) %collective-permute-start.2) | collective-permute-done | bytes 528416 | tf_op jit(solution)/shard_map/ppermute | solution.py:123
  33.5 0.1 convert_reduce_fusion
  33.6 0.9 %shard_map.59.refs_9_ = bf16[2,8,128,128]{3,2,1,0:T(8,128)(2,1)S(1)} custom-call(s32[4,32]{1,0:T(4,128)S(1)} %maximum_convert_fusion.1.index, bf16[1056,128]{1,0:T(8,128)(2,1)S(1)} %collective-permute-done.7.refs_0_, bf16[1056,128]{1,0:T(8,128)(2,1)S(1)} %collective-permute-done.8.refs_1_, bf16[1056,128]{1,0:T(8,128)(2,1)S(1)} %collective-permute-done.9.refs_2_, ...), custom_call_target="tpu_custom_call" | custom-call | flops 1 | bytes 1 | tf_op jit(solution)/shard_map/pallas_call | solution.py:171
  34.6 1.5 %shard_map.60 = bf16[1,6,128,128]{3,2,1,0:T(8,128)(2,1)S(1)} custom-call(s32[5]{0:T(128)S(1)} %stack.41.place, s32[1,32]{1,0:T(1,128)S(1)} %bitcast_convert_fusion.refs_0_, s32[1,16]{1,0:T(1,128)S(1)} %bitcast.24, s32[1,16]{1,0:T(1,128)S(1)} %bitcast.27, s32[2,8]{1,0:T(2,128)S(1)} %copy-done.2, s32[2,8]{1,0:T(2,128)S(1)} %collective-permute-done.3.refs_4_, ...), custom_call_target="tpu_custom_call" | custom-call | flops 1 | bytes 1 | tf_op jit(solution)/shard_map/pallas_call | solution.py:187
  36.1 1.5 %shard_map.61 = bf16[1,6,128,128]{3,2,1,0:T(8,128)(2,1)S(1)} custom-call(s32[5]{0:T(128)S(1)} %stack.41.place, s32[1,32]{1,0:T(1,128)S(1)} %bitcast_convert_fusion.refs_0_, s32[1,16]{1,0:T(1,128)S(1)} %bitcast.25, s32[1,16]{1,0:T(1,128)S(1)} %bitcast.28, s32[2,8]{1,0:T(2,128)S(1)} %copy-done.2, s32[2,8]{1,0:T(2,128)S(1)} %collective-permute-done.3.refs_4_, ...), custom_call_target="tpu_custom_call" | custom-call | flops 1 | bytes 1 | tf_op jit(solution)/shard_map/pallas_call | solution.py:187
  37.7 0.1 slice_reduce_fusion.3
  37.9 0.9 %shard_map.57.refs_9_ = bf16[2,8,128,128]{3,2,1,0:T(8,128)(2,1)S(1)} custom-call(s32[4,32]{1,0:T(4,128)S(1)} %maximum_convert_fusion.index, bf16[1056,128]{1,0:T(8,128)(2,1)S(1)} %shard_map.56.refs_0_, bf16[1056,128]{1,0:T(8,128)(2,1)S(1)} %collective-permute-done.1.refs_1_, bf16[1056,128]{1,0:T(8,128)(2,1)S(1)} %collective-permute-done.5.refs_2_, ...), custom_call_target="tpu_custom_call" | custom-call | flops 1 | bytes 1 | tf_op jit(solution)/shard_map/pallas_call | solution.py:171
  38.8 2.2 %shard_map.58 = bf16[2,6,128,128]{3,2,1,0:T(8,128)(2,1)S(1)} custom-call(s32[5]{0:T(128)S(1)} %stack.41.place, s32[2,6]{1,0:T(2,128)S(1)} %copy-done.4, s32[1,16]{1,0:T(1,128)S(1)} %bitcast.26, s32[1,16]{1,0:T(1,128)S(1)} %bitcast.29, s32[2,8]{1,0:T(2,128)S(1)} %copy-done.2, s32[2,8]{1,0:T(2,128)S(1)} %collective-permute-done.3.refs_4_, ...), custom_call_target="tpu_custom_call" | custom-call | flops 1 | bytes 1 | tf_op jit(solution)/shard_map/pallas_call | solution.py:187
  41.0 0.4 %collective-permute-done.12 = bf16[1,6,128,128]{3,2,1,0:T(8,128)(2,1)S(1)} collective-permute-done((bf16[1,6,128,128]{3,2,1,0:T(8,128)(2,1)S(1)}, bf16[1,6,128,128]{3,2,1,0:T(8,128)(2,1)S(1)}, u32[]{:S(2)}, u32[]{:S(2)}) %collective-permute-start.12) | collective-permute-done | bytes 196640 | tf_op jit(solution)/shard_map/ppermute | solution.py:123
  41.4 0.8 %maximum_select_fusion = bf16[2,6,128,128]{3,2,1,0:T(8,128)(2,1)} fusion(bf16[2,6,128,128]{3,2,1,0:T(8,128)(2,1)S(1)} %shard_map.58, bf16[1,6,128,128]{3,2,1,0:T(8,128)(2,1)S(1)} %collective-permute-done.12, bf16[1,6,128,128]{3,2,1,0:T(8,128)(2,1)S(1)} %collective-permute-done.11, pred[]{:T(512)S(6)} %eq.5), kind=kLoop, calls=%fused_computation | loop fusion | flops 393216 | bytes 1179649 | tf_op jit(solution)/shard_map/jit(_where)/select_n | solution.py:214
  (28 shorter events, 0.6 us)
Async XLA Ops:
  0.0 9.5 %copy-start = (bf16[2,8,128,128]{3,2,1,0:T(8,128)(2,1)S(1)}, bf16[2,8,128,128]{3,2,1,0:T(8,128)(2,1)}, u32[]{:S(2)}) copy-start(bf16[2,8,128,128]{3,2,1,0:T(8,128)(2,1)} %param.7) | copy-start | bytes 1572868
  0.0 19.3 %collective-permute-start.4 = (bf16[2048,128]{1,0:T(8,128)(2,1)}, bf16[2048,128]{1,0:T(8,128)(2,1)S(1)}, u32[]{:S(2)}, u32[]{:S(2)}) collective-permute-start(bf16[2048,128]{1,0:T(8,128)(2,1)} %bitcast.18), channel_id=1, source_target_pairs={{0,12},{1,3},{2,14},{3,1},{4,6},{5,9},{6,4},{7,11},{8,10},{9,5},{1... | collective-permute-start | bytes 1572872 | tf_op jit(solution)/shard_map/ppermute | solution.py:123
  5.1 0.9 %copy-start.1 = (bf16[2,4,128,128]{3,2,1,0:T(8,128)(2,1)S(1)}, bf16[2,4,128,128]{3,2,1,0:T(8,128)(2,1)}, u32[]{:S(2)}) copy-start(bf16[2,4,128,128]{3,2,1,0:T(8,128)(2,1)} %param.5) | copy-start | bytes 786436
  6.0 0.7 %copy-start.3 = (s32[2,6]{1,0:T(2,128)S(1)}, s32[2,6]{1,0:T(2,128)}, u32[]{:S(2)}) copy-start(s32[2,6]{1,0:T(2,128)} %refs_0_.5) | copy-start | bytes 148
  6.7 0.7 %copy-start.5 = (s32[2,4]{1,0:T(2,128)S(1)}, s32[2,4]{1,0:T(2,128)}, u32[]{:S(2)}) copy-start(s32[2,4]{1,0:T(2,128)} %refs_0_.4) | copy-start | bytes 100
  7.4 2.2 %copy-start.2 = (s32[2,8]{1,0:T(2,128)S(1)}, s32[2,8]{1,0:T(2,128)}, u32[]{:S(2)}) copy-start(s32[2,8]{1,0:T(2,128)} %refs_3_.5) | copy-start | bytes 196
  8.0 7.4 %collective-permute-start.1 = (bf16[1056,128]{1,0:T(8,128)(2,1)S(1)}, bf16[1056,128]{1,0:T(8,128)(2,1)S(1)}, u32[]{:S(2)}, u32[]{:S(2)}) collective-permute-start(bf16[1056,128]{1,0:T(8,128)(2,1)S(1)} %shard_map.56.refs_0_), channel_id=1, source_target_pairs={{0,2},{1,3},{2,0},{3,1},{4,6},{5,7},{6,4},{7,5},{8,10},{9,11},{10,... | collective-permute-start | bytes 811016 | tf_op jit(solution)/shard_map/ppermute | solution.py:115
  9.5 8.1 %collective-permute-start.5 = (bf16[1056,128]{1,0:T(8,128)(2,1)S(1)}, bf16[1056,128]{1,0:T(8,128)(2,1)S(1)}, u32[]{:S(2)}, u32[]{:S(2)}) collective-permute-start(bf16[1056,128]{1,0:T(8,128)(2,1)S(1)} %shard_map.56.refs_0_), channel_id=1, source_target_pairs={{0,1},{1,0},{2,3},{3,2},{4,5},{5,4},{6,7},{7,6},{8,9},{9,8},{10,11... | collective-permute-start | bytes 811016 | tf_op jit(solution)/shard_map/ppermute | solution.py:115
  9.5 9.8 %collective-permute-start.7 = (bf16[1056,128]{1,0:T(8,128)(2,1)S(1)}, bf16[1056,128]{1,0:T(8,128)(2,1)S(1)}, u32[]{:S(2)}, u32[]{:S(2)}) collective-permute-start(bf16[1056,128]{1,0:T(8,128)(2,1)S(1)} %shard_map.56.refs_0_), channel_id=1, source_target_pairs={{0,4},{4,0},{8,12},{12,8},{1,5},{5,1},{9,13},{13,9},{2,6},{6,2},{1... | collective-permute-start | bytes 811016 | tf_op jit(solution)/shard_map/ppermute | solution.py:115
  10.1 16.3 %collective-permute-start = (bf16[2064,128]{1,0:T(8,128)(2,1)S(1)}, bf16[2064,128]{1,0:T(8,128)(2,1)S(1)}, u32[]{:S(2)}, u32[]{:S(2)}) collective-permute-start(bf16[2064,128]{1,0:T(8,128)(2,1)S(1)} %shard_map.55), channel_id=1, source_target_pairs={{0,1},{1,5},{2,3},{3,7},{4,0},{5,4},{6,2},{7,6},{8,12},{9,8},{10,1... | collective-permute-start | bytes 1585160 | tf_op jit(solution)/shard_map/ppermute | solution.py:123
  15.3 19.2 %collective-permute-start.3 = (s32[2,8]{1,0:T(2,128)S(1)}, s32[2,8]{1,0:T(2,128)S(1)}, u32[]{:S(2)}, u32[]{:S(2)}) collective-permute-start(s32[2,8]{1,0:T(2,128)S(1)} %copy-done.2), channel_id=1, source_target_pairs={{0,12},{4,8},{8,4},{12,0},{1,13},{5,9},{9,5},{13,1},{2,14},{6,10},... | collective-permute-start | bytes 200 | tf_op jit(solution)/shard_map/ppermute | solution.py:115
  17.6 15.9 %collective-permute-start.2 = (bf16[2064,128]{1,0:T(8,128)(2,1)S(1)}, bf16[2064,128]{1,0:T(8,128)(2,1)S(1)}, u32[]{:S(2)}, u32[]{:S(2)}) collective-permute-start(bf16[2064,128]{1,0:T(8,128)(2,1)S(1)} %shard_map.55), channel_id=1, source_target_pairs={{0,1},{1,9},{2,3},{3,11},{4,12},{5,4},{6,14},{7,6},{8,0},{9,8},{10... | collective-permute-start | bytes 1585160 | tf_op jit(solution)/shard_map/ppermute | solution.py:123
  19.3 8.4 %collective-permute-start.8 = (bf16[1056,128]{1,0:T(8,128)(2,1)S(1)}, bf16[1056,128]{1,0:T(8,128)(2,1)S(1)}, u32[]{:S(2)}, u32[]{:S(2)}) collective-permute-start(bf16[1056,128]{1,0:T(8,128)(2,1)S(1)} %collective-permute-done.7.refs_0_), channel_id=1, source_target_pairs={{0,2},{1,3},{2,0},{3,1},{4,6},{5,7},{6,4},{7,5},{8,10},{9,11},{10,... | collective-permute-start | bytes 811016 | tf_op jit(solution)/shard_map/ppermute | solution.py:115
  21.9 6.1 %collective-permute-start.9 = (bf16[1056,128]{1,0:T(8,128)(2,1)S(1)}, bf16[1056,128]{1,0:T(8,128)(2,1)S(1)}, u32[]{:S(2)}, u32[]{:S(2)}) collective-permute-start(bf16[1056,128]{1,0:T(8,128)(2,1)S(1)} %collective-permute-done.7.refs_0_), channel_id=1, source_target_pairs={{0,1},{1,0},{2,3},{3,2},{4,5},{5,4},{6,7},{7,6},{8,9},{9,8},{10,11... | collective-permute-start | bytes 811016 | tf_op jit(solution)/shard_map/ppermute | solution.py:115
  26.4 11.3 %collective-permute-start.6 = (bf16[1056,128]{1,0:T(8,128)(2,1)S(1)}, bf16[1056,128]{1,0:T(8,128)(2,1)S(1)}, u32[]{:S(2)}, u32[]{:S(2)}) collective-permute-start(bf16[1056,128]{1,0:T(8,128)(2,1)S(1)} %collective-permute-done.1.refs_1_), channel_id=1, source_target_pairs={{0,1},{1,0},{2,3},{3,2},{4,5},{5,4},{6,7},{7,6},{8,9},{9,8},{10,11... | collective-permute-start | bytes 811016 | tf_op jit(solution)/shard_map/ppermute | solution.py:115
  27.7 1.5 %collective-permute-start.10 = (bf16[1056,128]{1,0:T(8,128)(2,1)S(1)}, bf16[1056,128]{1,0:T(8,128)(2,1)S(1)}, u32[]{:S(2)}, u32[]{:S(2)}) collective-permute-start(bf16[1056,128]{1,0:T(8,128)(2,1)S(1)} %collective-permute-done.8.refs_1_), channel_id=1, source_target_pairs={{0,1},{1,0},{2,3},{3,2},{4,5},{5,4},{6,7},{7,6},{8,9},{9,8},{10,11... | collective-permute-start | bytes 811016 | tf_op jit(solution)/shard_map/ppermute | solution.py:115
  36.0 4.9 %collective-permute-start.11 = (bf16[1,6,128,128]{3,2,1,0:T(8,128)(2,1)S(1)}, bf16[1,6,128,128]{3,2,1,0:T(8,128)(2,1)S(1)}, u32[]{:S(2)}, u32[]{:S(2)}) collective-permute-start(bf16[1,6,128,128]{3,2,1,0:T(8,128)(2,1)S(1)} %shard_map.60), channel_id=1, source_target_pairs={{0,4},{1,0},{2,6},{3,2},{4,5},{5,1},{6,7},{7,3},{8,9},{9,13},{10,1... | collective-permute-start | bytes 589832 | tf_op jit(solution)/shard_map/ppermute | solution.py:123
  37.6 3.8 %collective-permute-start.12 = (bf16[1,6,128,128]{3,2,1,0:T(8,128)(2,1)S(1)}, bf16[1,6,128,128]{3,2,1,0:T(8,128)(2,1)S(1)}, u32[]{:S(2)}, u32[]{:S(2)}) collective-permute-start(bf16[1,6,128,128]{3,2,1,0:T(8,128)(2,1)S(1)} %shard_map.61), channel_id=1, source_target_pairs={{0,4},{1,0},{2,6},{3,2},{4,5},{5,1},{6,7},{7,3},{8,9},{9,13},{10,1... | collective-permute-start | bytes 589832 | tf_op jit(solution)/shard_map/ppermute | solution.py:123
  37.8 0.9 %copy-start.4 = (s32[2,6]{1,0:T(2,128)S(1)}, s32[2,6]{1,0:T(2,128)}, u32[]{:S(2)}) copy-start(s32[2,6]{1,0:T(2,128)} %refs_0_.5) | copy-start | bytes 148

commit v17 on v10

--- a/solution.py
+++ b/solution.py
@@ -30,28 +30,11 @@
     out[size:, :] = found.astype(out.dtype)
 
 
-def left_kernel(slots, index, *refs):
-    parts, dense = refs[:-1], refs[-1]
-    dense[...] = jnp.zeros_like(dense)
-    rows, _, block, _ = dense.shape
-    for p, part in enumerate(parts):
-        for i in range(rows):
-            for s in range(slots):
-                inner = index[p, i * slots + s]
-                start = (i * slots + s) * block
-
-                @pl.when(inner >= 0)
-                def _():
-                    dense[i, inner] = part[start : start + block, :]
-
-
-def step_kernel(starts, span, last, place, *refs):
-    parts = len(starts) - 1
-    wanted, refs = refs[0], refs[1:]
+def product_kernel(starts, span, parts, place, left_index, wanted, *refs):
     cols, refs = refs[:parts], refs[parts:]
     tiles, refs = refs[:parts], refs[parts:]
-    dense, refs = refs[0], refs[1:]
-    before, out, right, slot = refs if len(refs) == 4 else (None,) + refs
+    packs, (out, dense, right, slot) = refs[:-4], refs[-4:]
+
     @pl.when(place[0] >= 0)
     def _():
         first = place[0]
@@ -59,39 +42,51 @@
         block = dense.shape[-1]
         slots = right.shape[2] // block
         inner_slots = tiles[0].shape[0] // block // inner_rows
+        rows = right.shape[0]
+        left_slots = (packs[0].shape[0] // block) // rows
 
         def read(ref, start, i, k, width):
             return ref[i, k] if start is None else ref[0, start + i * width + k]
 
-        sums = {i: None if before is None else before[i] for i in span}
+        for i in span:
+            dense[i] = jnp.zeros_like(dense[i])
+            for p, pack in enumerate(packs):
+                for s in range(left_slots):
+                    inner = left_index[p, i * left_slots + s]
+                    begin = (i * left_slots + s) * block
+
+                    @pl.when(inner >= 0)
+                    def _():
+                        dense[i, inner] = pack[begin : begin + block, :]
+
+        for m in range(inner_rows):
+            for c in range(COLS_DEV):
+                slot[m, c] = 0
+        sums = {}
         for p in range(parts):
             for m in range(inner_rows):
-                for c in range(COLS_DEV):
-                    slot[m, c] = -1
                 for l in range(inner_slots):
                     slot[m, read(cols[p], starts[1 + p], m, l, inner_slots) - first] = l
             for i in span:
                 for j in range(slots):
-                    column = read(wanted, starts[0], i, j, slots) - first
+                    column = read(wanted, starts[0], i, j, slots)
                     for m in range(inner_rows):
-                        l = slot[m, column]
-                        start = pl.multiple_of((m * inner_slots + jnp.maximum(l, 0)) * block, block)
-                        tile = tiles[p][pl.ds(start, block), :]
+                        l = slot[m, column - first]
+                        hit = read(cols[p], starts[1 + p], m, l, inner_slots) == column
+                        begin = pl.multiple_of((m * inner_slots + l) * block, block)
+                        tile = tiles[p][pl.ds(begin, block), :]
                         right[i, m * block : (m + 1) * block, j * block : (j + 1) * block] = jnp.where(
-                            l >= 0, tile, jnp.zeros_like(tile)
+                            hit, tile, jnp.zeros_like(tile)
                         )
             for i in span:
                 left = jnp.concatenate(
                     [dense[i, place[1 + p] * inner_rows + m] for m in range(inner_rows)], axis=1
                 )
                 product = jnp.dot(left, right[i], preferred_element_type=jnp.float32)
-                sums[i] = product if sums[i] is None else sums[i] + product
+                sums[i] = sums[i] + product if i in sums else product
         for at, i in enumerate(span):
-            if last:
-                for j in range(slots):
-                    out[at, j] = sums[i][:, j * block : (j + 1) * block].astype(out.dtype)
-            else:
-                out[i] = sums[i]
+            for j in range(slots):
+                out[at, j] = sums[i][:, j * block : (j + 1) * block].astype(out.dtype)
 
 
 def parity(k):
@@ -162,50 +157,39 @@
     own_packs = [own, swap(own, "col", col_count, far)]
     other = swap(own, "row", row_count, 1)
     ready = lax.optimization_barrier((packed, own_packs[1]))[0]
+    near = [swap(own, "col", col_count, d) for d in [far // 2] if d]
     for d in range(end - 1, 0, -1):
+        if d == 1:
+            ready = lax.optimization_barrier((ready, near))[0]
         shards[d] = deliver(ready, d)
     other = lax.optimization_barrier((other, shards[end]))[0]
-    own_packs, other_packs = across(own_packs, far // 2), across([other], far)
-    def dense_of(packs):
-        return pl.pallas_call(
-            functools.partial(left_kernel, a_cols.shape[1]),
-            out_shape=jax.ShapeDtypeStruct((rows, inner_rows * row_count, block, block), dtype),
-            in_specs=[SMEM] + [VMEM] * len(packs),
-            out_specs=VMEM,
-            compiler_params=PARAMS,
-            cost_estimate=FREE,
-        )(index_of(packs, a_tiles), *packs)
-
-    def step(dists, wanted, dense, before, span, last):
-        place = jnp.stack([jnp.where(working, first, -1)] + [r ^ d for d in dists]).astype(jnp.int32)
-        if last:
-            out = jax.ShapeDtypeStruct((len(span), slots, block, block), dtype)
-        else:
-            out = jax.ShapeDtypeStruct((rows, block, slots * block), jnp.float32)
-        held = [dense] if before is None else [dense, before]
-        return pl.pallas_call(
-            functools.partial(step_kernel, [wanted[0]] + [cols[d][0] for d in dists], span, last),
-            out_shape=out,
-            in_specs=[SMEM] * (2 + len(dists)) + [VMEM] * (len(dists) + len(held)),
-            out_specs=VMEM,
-            scratch_shapes=[
-                pltpu.VMEM((rows, inner_rows * block, slots * block), dtype),
-                pltpu.SMEM((inner_rows, COLS_DEV), jnp.int32),
-            ],
-            compiler_params=PARAMS,
-            cost_estimate=FREE,
-        )(place, wanted[1], *[cols[d][1] for d in dists], *[shards[d] for d in dists], *held)
-
+    own_packs = own_packs + near + [swap(own_packs[1], "col", col_count, d) for d in [far // 2] if d]
+    own_packs = across(own_packs, far // 4)
+    other_packs = across([other], far)
     order, every = list(range(1, end)) + [0, end], list(range(rows))
-    early, late = order[:-4], order[-4:]
     for d in range(1, end):
         cols[d] = (0, index_of([shards[d]], b_tiles))
+    place = jnp.stack([jnp.where(working, first, -1)] + [r ^ d for d in order]).astype(jnp.int32)
 
     def products(wanted, packs, spans):
-        dense, total = dense_of(packs), None
-        for at in range(0, len(early), 4):
-            total = step(early[at : at + 4], wanted, dense, total, every, False)
-        return [step(late, wanted, dense, total, span, True) for span in spans]
+        index = index_of(packs, a_tiles)
+        starts = [wanted[0]] + [cols[d][0] for d in order]
+        return [
+            pl.pallas_call(
+                functools.partial(product_kernel, starts, span, len(order)),
+                out_shape=jax.ShapeDtypeStruct((len(span), slots, block, block), dtype),
+                in_specs=[SMEM] * (3 + len(order)) + [VMEM] * (len(order) + len(packs)),
+                out_specs=VMEM,
+                scratch_shapes=[
+                    pltpu.VMEM((rows, inner_rows * row_count, block, block), dtype),
+                    pltpu.VMEM((rows, inner_rows * block, slots * block), dtype),
+                    pltpu.SMEM((inner_rows, COLS_DEV), jnp.int32),
+                ],
+                compiler_params=PARAMS,
+                cost_estimate=FREE,
+            )(place, index, wanted[1], *[cols[d][1] for d in order], *[shards[d] for d in order], *packs)
+            for span in spans
+        ]
 
     given = products((a_cols.size, index_of([other], a_tiles)), other_packs, [[i] for i in every])
     given = [give_back(x) for x in given]

time: 40.5 us -> 39.7 us (0.980)
  Pallas kernels: 8.11 us -> 7.03 us
  local copies, waits for them, and re-layouts: 3.29 us -> 3.94 us
    pallas_call x5 -> x3, Pallas kernels: 6.94 us -> 5.85 us  [products(): pl.pallas_call(functools.partial(product_kernel, starts, span, len(order)...]
    unnamed x12, local copies, waits for them, and re-layouts: 2.32 us -> 2.97 us
  transfers between devices with their start and end apart: 13 -> 13, of which waited for: 5 -> 5; matrix products, arithmetic and copies ran while one was open for 3% -> 3% of each run, Pallas kernels for 20% -> 18%
where the time goes in v17:
time: 39.7 us; the launch traced here: 39.5 us
  waiting for transfers between devices  16.9 us (43%)
  starting transfers between devices  10.3 us (26%)
  Pallas kernels  7.03 us (18%)
  local copies, waits for them, and re-layouts  3.94 us (10%)
  other arithmetic  1.07 us (3%)
    ppermute x8, waiting for transfers between devices, swap(): return lax.ppermute(x, axis, [(k, k ^ d) for k in range(n)])  13.4 us
    pallas_call x3, Pallas kernels, products(): pl.pallas_call(functools.partial(product_kernel, starts, span, len(order)...  5.85 us
    ppermute x5, starting transfers between devices, permute(): return lax.ppermute(x, ('row', 'col'), pairs)  5.19 us
    ppermute x8, starting transfers between devices, swap(): return lax.ppermute(x, axis, [(k, k ^ d) for k in range(n)])  5.15 us
    ppermute x5, waiting for transfers between devices, permute(): return lax.ppermute(x, ('row', 'col'), pairs)  3.52 us
    unnamed x12, local copies, waits for them, and re-layouts  2.97 us
    pallas_call x2, Pallas kernels, pack(): pl.pallas_call(pack_kernel, out_shape=jax.ShapeDtypeStruct((size + -(-cou...  1.17 us
    slice x8, local copies, waits for them, and re-layouts, index_of(): x[tiles.size // block:, 0]  0.89 us
  transfers between devices with their start and end apart: 13, of which 5 were waited for; matrix products, arithmetic and copies ran while one was open for 3% of the time, Pallas kernels for 18%

profile of v17, /device:TPU:0, one launch (start us, length us, event | category | flops | bytes accessed | tf_op | source)
XLA Modules:
  0.0 39.5 jit_solution(10656954671189866184)
XLA Ops:
  0.0 5.0 %collective-permute-start.6 = (bf16[2048,128]{1,0:T(8,128)(2,1)}, bf16[2048,128]{1,0:T(8,128)(2,1)S(1)}, u32[]{:S(2)}, u32[]{:S(2)}) collective-permute-start(bf16[2048,128]{1,0:T(8,128)(2,1)} %bitcast.18), channel_id=1, source_target_pairs={{0,12},{1,3},{2,14},{3,1},{4,6},{5,9},{6,4},{7,11},{8,10},{9,5},{1... | collective-permute-start | bytes 1572872 | tf_op jit(solution)/shard_map/ppermute | solution.py:118
  5.1 0.9 %copy-done.1 = bf16[2,4,128,128]{3,2,1,0:T(8,128)(2,1)S(1)} copy-done((bf16[2,4,128,128]{3,2,1,0:T(8,128)(2,1)S(1)}, bf16[2,4,128,128]{3,2,1,0:T(8,128)(2,1)}, u32[]{:S(2)}) %copy-start.1) | copy-done | bytes 262168
  6.0 0.7 %copy-done.3 = s32[2,6]{1,0:T(2,128)S(1)} copy-done((s32[2,6]{1,0:T(2,128)S(1)}, s32[2,6]{1,0:T(2,128)}, u32[]{:S(2)}) %copy-start.3) | copy-done | bytes 72
  6.7 0.7 %copy-done.5 = s32[2,4]{1,0:T(2,128)S(1)} copy-done((s32[2,4]{1,0:T(2,128)S(1)}, s32[2,4]{1,0:T(2,128)}, u32[]{:S(2)}) %copy-start.5) | copy-done | bytes 56
  7.4 0.6 %shard_map.55.refs_8_ = bf16[1056,128]{1,0:T(8,128)(2,1)S(1)} custom-call(s32[2,4]{1,0:T(2,128)S(1)} %copy-done.5, s32[2,6]{1,0:T(2,128)S(1)} %copy-done.3, bf16[1024,128]{1,0:T(8,128)(2,1)S(1)} %bitcast.23), custom_call_target="tpu_custom_call" | custom-call | flops 1 | bytes 1 | tf_op jit(solution)/shard_map/pallas_call | solution.py:134
  8.0 1.6 %collective-permute-start = (bf16[1056,128]{1,0:T(8,128)(2,1)S(1)}, bf16[1056,128]{1,0:T(8,128)(2,1)S(1)}, u32[]{:S(2)}, u32[]{:S(2)}) collective-permute-start(bf16[1056,128]{1,0:T(8,128)(2,1)S(1)} %shard_map.55.refs_8_), channel_id=1, source_target_pairs={{0,2},{1,3},{2,0},{3,1},{4,6},{5,7},{6,4},{7,5},{8,10},{9,11},{10,... | collective-permute-start | bytes 811016 | tf_op jit(solution)/shard_map/ppermute | solution.py:110
  9.5 1.0 %collective-permute-start.5 = (s32[2,8]{1,0:T(2,128)S(1)}, s32[2,8]{1,0:T(2,128)S(1)}, u32[]{:S(2)}, u32[]{:S(2)}) collective-permute-start(s32[2,8]{1,0:T(2,128)S(1)} %copy-done.2), channel_id=1, source_target_pairs={{0,12},{4,8},{8,4},{12,0},{1,13},{5,9},{9,5},{13,1},{2,14},{6,10},... | collective-permute-start | bytes 200 | tf_op jit(solution)/shard_map/ppermute | solution.py:110
  10.5 0.1 slice_reduce_fusion.6
  10.6 0.6 %shard_map.56 = bf16[2064,128]{1,0:T(8,128)(2,1)S(1)} custom-call(s32[2,8]{1,0:T(2,128)S(1)} %copy-done.2, bf16[2048,128]{1,0:T(8,128)(2,1)S(1)} %bitcast.19), custom_call_target="tpu_custom_call" | custom-call | flops 1 | bytes 1 | tf_op jit(solution)/shard_map/pallas_call | solution.py:134
  11.2 0.1 stack.29.place
  11.3 4.0 %collective-permute-done.refs_9_ = bf16[1056,128]{1,0:T(8,128)(2,1)S(1)} collective-permute-done((bf16[1056,128]{1,0:T(8,128)(2,1)S(1)}, bf16[1056,128]{1,0:T(8,128)(2,1)S(1)}, u32[]{:S(2)}, u32[]{:S(2)}) %collective-permute-start) | collective-permute-done | bytes 270368 | tf_op jit(solution)/shard_map/ppermute | solution.py:110
  15.3 0.1 slice_reduce_fusion.4
  15.4 0.1 slice_reduce_fusion.5
  15.6 3.8 %collective-permute-done.7.refs_8_ = bf16[1056,128]{1,0:T(8,128)(2,1)S(1)} collective-permute-done((bf16[1056,128]{1,0:T(8,128)(2,1)S(1)}, bf16[1056,128]{1,0:T(8,128)(2,1)S(1)}, u32[]{:S(2)}, u32[]{:S(2)}) %collective-permute-start.7) | collective-permute-done | bytes 270368 | tf_op jit(solution)/shard_map/ppermute | solution.py:110
  19.3 2.0 %collective-permute-start.8 = (bf16[1056,128]{1,0:T(8,128)(2,1)S(1)}, bf16[1056,128]{1,0:T(8,128)(2,1)S(1)}, u32[]{:S(2)}, u32[]{:S(2)}) collective-permute-start(bf16[1056,128]{1,0:T(8,128)(2,1)S(1)} %collective-permute-done.7.refs_8_), channel_id=1, source_target_pairs={{0,2},{1,3},{2,0},{3,1},{4,6},{5,7},{6,4},{7,5},{8,10},{9,11},{10,... | collective-permute-start | bytes 811016 | tf_op jit(solution)/shard_map/ppermute | solution.py:110
  21.4 0.1 slice_reduce_fusion.7
  21.5 5.7 %collective-permute-done.8.refs_9_ = bf16[1056,128]{1,0:T(8,128)(2,1)S(1)} collective-permute-done((bf16[1056,128]{1,0:T(8,128)(2,1)S(1)}, bf16[1056,128]{1,0:T(8,128)(2,1)S(1)}, u32[]{:S(2)}, u32[]{:S(2)}) %collective-permute-start.8) | collective-permute-done | bytes 270368 | tf_op jit(solution)/shard_map/ppermute | solution.py:110
  27.1 0.1 slice_reduce_fusion.2
  27.3 0.6 %collective-permute-start.10 = (bf16[1056,128]{1,0:T(8,128)(2,1)S(1)}, bf16[1056,128]{1,0:T(8,128)(2,1)S(1)}, u32[]{:S(2)}, u32[]{:S(2)}) collective-permute-start(bf16[1056,128]{1,0:T(8,128)(2,1)S(1)} %collective-permute-done.8.refs_9_), channel_id=1, source_target_pairs={{0,1},{1,0},{2,3},{3,2},{4,5},{5,4},{6,7},{7,6},{8,9},{9,8},{10,11... | collective-permute-start | bytes 811016 | tf_op jit(solution)/shard_map/ppermute | solution.py:110
  27.8 0.1 slice_reduce_fusion.1
  28.0 0.1 convert_reduce_fusion.1
  28.1 3.3 %collective-permute-done.4.refs_5_ = bf16[2064,128]{1,0:T(8,128)(2,1)S(1)} collective-permute-done((bf16[2064,128]{1,0:T(8,128)(2,1)S(1)}, bf16[2064,128]{1,0:T(8,128)(2,1)S(1)}, u32[]{:S(2)}, u32[]{:S(2)}) %collective-permute-start.4) | collective-permute-done | bytes 528416 | tf_op jit(solution)/shard_map/ppermute | solution.py:118
  31.4 0.1 convert_reduce_fusion
  31.5 0.1 slice_reduce_fusion
  31.7 1.7 %shard_map.59 = bf16[1,6,128,128]{3,2,1,0:T(8,128)(2,1)S(1)} custom-call(s32[5]{0:T(128)S(1)} %stack.29.place, s32[4,32]{1,0:T(4,128)S(1)} %maximum_convert_fusion.1.left_index, s32[1,32]{1,0:T(1,128)S(1)} %bitcast_convert_fusion.wanted, s32[1,16]{1,0:T(1,128)S(1)} %bitcast.24, s32[1,16]{1,0:T(1,128)S(1)} %bitcast.27, s32[2,8]{1,0:T(2,128)S(1)} %copy-done.2, ...), custom_call_target="tpu_custom_call" | custom-call | flops 1 | bytes 1 | tf_op jit(solution)/shard_map/pallas_call | solution.py:178
  33.3 0.1 collective-permute-start.12
  33.4 1.7 %shard_map.58 = bf16[1,6,128,128]{3,2,1,0:T(8,128)(2,1)S(1)} custom-call(s32[5]{0:T(128)S(1)} %stack.29.place, s32[4,32]{1,0:T(4,128)S(1)} %maximum_convert_fusion.1.left_index, s32[1,32]{1,0:T(1,128)S(1)} %bitcast_convert_fusion.wanted, s32[1,16]{1,0:T(1,128)S(1)} %bitcast.25, s32[1,16]{1,0:T(1,128)S(1)} %bitcast.28, s32[2,8]{1,0:T(2,128)S(1)} %copy-done.2, ...), custom_call_target="tpu_custom_call" | custom-call | flops 1 | bytes 1 | tf_op jit(solution)/shard_map/pallas_call | solution.py:178
  35.2 0.1 slice_reduce_fusion.3
  35.3 0.7 %copy-done.4 = s32[2,6]{1,0:T(2,128)S(1)} copy-done((s32[2,6]{1,0:T(2,128)S(1)}, s32[2,6]{1,0:T(2,128)}, u32[]{:S(2)}) %copy-start.4) | copy-done | bytes 72
  36.0 2.5 %shard_map.57 = bf16[2,6,128,128]{3,2,1,0:T(8,128)(2,1)S(1)} custom-call(s32[5]{0:T(128)S(1)} %stack.29.place, s32[4,32]{1,0:T(4,128)S(1)} %maximum_convert_fusion.left_index, s32[2,6]{1,0:T(2,128)S(1)} %copy-done.4, s32[1,16]{1,0:T(1,128)S(1)} %bitcast.26, s32[1,16]{1,0:T(1,128)S(1)} %bitcast.29, s32[2,8]{1,0:T(2,128)S(1)} %copy-done.2, ...), custom_call_target="tpu_custom_call" | custom-call | flops 1 | bytes 1 | tf_op jit(solution)/shard_map/pallas_call | solution.py:178
  38.5 0.2 collective-permute-done.11
  38.7 0.8 %maximum_select_fusion = bf16[2,6,128,128]{3,2,1,0:T(8,128)(2,1)} fusion(bf16[2,6,128,128]{3,2,1,0:T(8,128)(2,1)S(1)} %shard_map.57, bf16[1,6,128,128]{3,2,1,0:T(8,128)(2,1)S(1)} %collective-permute-done.12, bf16[1,6,128,128]{3,2,1,0:T(8,128)(2,1)S(1)} %collective-permute-done.11, pred[]{:T(512)S(6)} %eq.5), kind=kLoop, calls=%fused_computation | loop fusion | flops 393216 | bytes 1179649 | tf_op jit(solution)/shard_map/jit(_where)/select_n | solution.py:197
  (26 shorter events, 0.2 us)
Async XLA Ops:
  0.0 10.6 %copy-start = (bf16[2,8,128,128]{3,2,1,0:T(8,128)(2,1)S(1)}, bf16[2,8,128,128]{3,2,1,0:T(8,128)(2,1)}, u32[]{:S(2)}) copy-start(bf16[2,8,128,128]{3,2,1,0:T(8,128)(2,1)} %param.7) | copy-start | bytes 1572868
  0.0 19.3 %collective-permute-start.6 = (bf16[2048,128]{1,0:T(8,128)(2,1)}, bf16[2048,128]{1,0:T(8,128)(2,1)S(1)}, u32[]{:S(2)}, u32[]{:S(2)}) collective-permute-start(bf16[2048,128]{1,0:T(8,128)(2,1)} %bitcast.18), channel_id=1, source_target_pairs={{0,12},{1,3},{2,14},{3,1},{4,6},{5,9},{6,4},{7,11},{8,10},{9,5},{1... | collective-permute-start | bytes 1572872 | tf_op jit(solution)/shard_map/ppermute | solution.py:118
  5.1 0.9 %copy-start.1 = (bf16[2,4,128,128]{3,2,1,0:T(8,128)(2,1)S(1)}, bf16[2,4,128,128]{3,2,1,0:T(8,128)(2,1)}, u32[]{:S(2)}) copy-start(bf16[2,4,128,128]{3,2,1,0:T(8,128)(2,1)} %param.5) | copy-start | bytes 786436
  6.0 0.7 %copy-start.3 = (s32[2,6]{1,0:T(2,128)S(1)}, s32[2,6]{1,0:T(2,128)}, u32[]{:S(2)}) copy-start(s32[2,6]{1,0:T(2,128)} %wanted.1) | copy-start | bytes 148
  6.7 0.7 %copy-start.5 = (s32[2,4]{1,0:T(2,128)S(1)}, s32[2,4]{1,0:T(2,128)}, u32[]{:S(2)}) copy-start(s32[2,4]{1,0:T(2,128)} %refs_0_.2) | copy-start | bytes 100
  7.4 2.2 %copy-start.2 = (s32[2,8]{1,0:T(2,128)S(1)}, s32[2,8]{1,0:T(2,128)}, u32[]{:S(2)}) copy-start(s32[2,8]{1,0:T(2,128)} %refs_2_.5) | copy-start | bytes 196
  8.0 7.4 %collective-permute-start = (bf16[1056,128]{1,0:T(8,128)(2,1)S(1)}, bf16[1056,128]{1,0:T(8,128)(2,1)S(1)}, u32[]{:S(2)}, u32[]{:S(2)}) collective-permute-start(bf16[1056,128]{1,0:T(8,128)(2,1)S(1)} %shard_map.55.refs_8_), channel_id=1, source_target_pairs={{0,2},{1,3},{2,0},{3,1},{4,6},{5,7},{6,4},{7,5},{8,10},{9,11},{10,... | collective-permute-start | bytes 811016 | tf_op jit(solution)/shard_map/ppermute | solution.py:110
  9.5 5.8 %collective-permute-start.1 = (bf16[1056,128]{1,0:T(8,128)(2,1)S(1)}, bf16[1056,128]{1,0:T(8,128)(2,1)S(1)}, u32[]{:S(2)}, u32[]{:S(2)}) collective-permute-start(bf16[1056,128]{1,0:T(8,128)(2,1)S(1)} %shard_map.55.refs_8_), channel_id=1, source_target_pairs={{0,1},{1,0},{2,3},{3,2},{4,5},{5,4},{6,7},{7,6},{8,9},{9,8},{10,11... | collective-permute-start | bytes 811016 | tf_op jit(solution)/shard_map/ppermute | solution.py:110
  9.5 9.8 %collective-permute-start.7 = (bf16[1056,128]{1,0:T(8,128)(2,1)S(1)}, bf16[1056,128]{1,0:T(8,128)(2,1)S(1)}, u32[]{:S(2)}, u32[]{:S(2)}) collective-permute-start(bf16[1056,128]{1,0:T(8,128)(2,1)S(1)} %shard_map.55.refs_8_), channel_id=1, source_target_pairs={{0,4},{4,0},{8,12},{12,8},{1,5},{5,1},{9,13},{13,9},{2,6},{6,2},{1... | collective-permute-start | bytes 811016 | tf_op jit(solution)/shard_map/ppermute | solution.py:110
  9.5 22.1 %collective-permute-start.5 = (s32[2,8]{1,0:T(2,128)S(1)}, s32[2,8]{1,0:T(2,128)S(1)}, u32[]{:S(2)}, u32[]{:S(2)}) collective-permute-start(s32[2,8]{1,0:T(2,128)S(1)} %copy-done.2), channel_id=1, source_target_pairs={{0,12},{4,8},{8,4},{12,0},{1,13},{5,9},{9,5},{13,1},{2,14},{6,10},... | collective-permute-start | bytes 200 | tf_op jit(solution)/shard_map/ppermute | solution.py:110
  15.3 16.1 %collective-permute-start.4 = (bf16[2064,128]{1,0:T(8,128)(2,1)S(1)}, bf16[2064,128]{1,0:T(8,128)(2,1)S(1)}, u32[]{:S(2)}, u32[]{:S(2)}) collective-permute-start(bf16[2064,128]{1,0:T(8,128)(2,1)S(1)} %shard_map.56), channel_id=1, source_target_pairs={{0,1},{1,9},{2,3},{3,11},{4,12},{5,4},{6,14},{7,6},{8,0},{9,8},{10... | collective-permute-start | bytes 1585160 | tf_op jit(solution)/shard_map/ppermute | solution.py:118
  15.3 12.6 %collective-permute-start.3 = (bf16[2064,128]{1,0:T(8,128)(2,1)S(1)}, bf16[2064,128]{1,0:T(8,128)(2,1)S(1)}, u32[]{:S(2)}, u32[]{:S(2)}) collective-permute-start(bf16[2064,128]{1,0:T(8,128)(2,1)S(1)} %shard_map.56), channel_id=1, source_target_pairs={{0,1},{1,5},{2,3},{3,7},{4,0},{5,4},{6,2},{7,6},{8,12},{9,8},{10,1... | collective-permute-start | bytes 1585160 | tf_op jit(solution)/shard_map/ppermute | solution.py:118
  19.3 7.8 %collective-permute-start.8 = (bf16[1056,128]{1,0:T(8,128)(2,1)S(1)}, bf16[1056,128]{1,0:T(8,128)(2,1)S(1)}, u32[]{:S(2)}, u32[]{:S(2)}) collective-permute-start(bf16[1056,128]{1,0:T(8,128)(2,1)S(1)} %collective-permute-done.7.refs_8_), channel_id=1, source_target_pairs={{0,2},{1,3},{2,0},{3,1},{4,6},{5,7},{6,4},{7,5},{8,10},{9,11},{10,... | collective-permute-start | bytes 811016 | tf_op jit(solution)/shard_map/ppermute | solution.py:110
  21.4 5.9 %collective-permute-start.9 = (bf16[1056,128]{1,0:T(8,128)(2,1)S(1)}, bf16[1056,128]{1,0:T(8,128)(2,1)S(1)}, u32[]{:S(2)}, u32[]{:S(2)}) collective-permute-start(bf16[1056,128]{1,0:T(8,128)(2,1)S(1)} %collective-permute-done.7.refs_8_), channel_id=1, source_target_pairs={{0,1},{1,0},{2,3},{3,2},{4,5},{5,4},{6,7},{7,6},{8,9},{9,8},{10,11... | collective-permute-start | bytes 811016 | tf_op jit(solution)/shard_map/ppermute | solution.py:110
  27.1 8.0 %collective-permute-start.2 = (bf16[1056,128]{1,0:T(8,128)(2,1)S(1)}, bf16[1056,128]{1,0:T(8,128)(2,1)S(1)}, u32[]{:S(2)}, u32[]{:S(2)}) collective-permute-start(bf16[1056,128]{1,0:T(8,128)(2,1)S(1)} %collective-permute-done.refs_9_), channel_id=1, source_target_pairs={{0,1},{1,0},{2,3},{3,2},{4,5},{5,4},{6,7},{7,6},{8,9},{9,8},{10,11... | collective-permute-start | bytes 811016 | tf_op jit(solution)/shard_map/ppermute | solution.py:110
  27.3 4.2 %collective-permute-start.10 = (bf16[1056,128]{1,0:T(8,128)(2,1)S(1)}, bf16[1056,128]{1,0:T(8,128)(2,1)S(1)}, u32[]{:S(2)}, u32[]{:S(2)}) collective-permute-start(bf16[1056,128]{1,0:T(8,128)(2,1)S(1)} %collective-permute-done.8.refs_9_), channel_id=1, source_target_pairs={{0,1},{1,0},{2,3},{3,2},{4,5},{5,4},{6,7},{7,6},{8,9},{9,8},{10,11... | collective-permute-start | bytes 811016 | tf_op jit(solution)/shard_map/ppermute | solution.py:110
  33.3 5.2 %collective-permute-start.12 = (bf16[1,6,128,128]{3,2,1,0:T(8,128)(2,1)S(1)}, bf16[1,6,128,128]{3,2,1,0:T(8,128)(2,1)S(1)}, u32[]{:S(2)}, u32[]{:S(2)}) collective-permute-start(bf16[1,6,128,128]{3,2,1,0:T(8,128)(2,1)S(1)} %shard_map.59), channel_id=1, source_target_pairs={{0,4},{1,0},{2,6},{3,2},{4,5},{5,1},{6,7},{7,3},{8,9},{9,13},{10,1... | collective-permute-start | bytes 589832 | tf_op jit(solution)/shard_map/ppermute | solution.py:118
  35.1 3.6 %collective-permute-start.11 = (bf16[1,6,128,128]{3,2,1,0:T(8,128)(2,1)S(1)}, bf16[1,6,128,128]{3,2,1,0:T(8,128)(2,1)S(1)}, u32[]{:S(2)}, u32[]{:S(2)}) collective-permute-start(bf16[1,6,128,128]{3,2,1,0:T(8,128)(2,1)S(1)} %shard_map.58), channel_id=1, source_target_pairs={{0,4},{1,0},{2,6},{3,2},{4,5},{5,1},{6,7},{7,3},{8,9},{9,13},{10,1... | collective-permute-start | bytes 589832 | tf_op jit(solution)/shard_map/ppermute | solution.py:118
  35.3 0.7 %copy-start.4 = (s32[2,6]{1,0:T(2,128)S(1)}, s32[2,6]{1,0:T(2,128)}, u32[]{:S(2)}) copy-start(s32[2,6]{1,0:T(2,128)} %wanted.1) | copy-start | bytes 148

commit v18 on v17

--- a/solution.py
+++ b/solution.py
@@ -38,11 +38,11 @@
     @pl.when(place[0] >= 0)
     def _():
         first = place[0]
-        inner_rows = slot.shape[0]
+        inner_rows = slot.shape[0] // parts
         block = dense.shape[-1]
-        slots = right.shape[2] // block
+        slots = right.shape[3] // block
         inner_slots = tiles[0].shape[0] // block // inner_rows
-        rows = right.shape[0]
+        rows = right.shape[1]
         left_slots = (packs[0].shape[0] // block) // rows
 
         def read(ref, start, i, k, width):
@@ -59,30 +59,31 @@
                     def _():
                         dense[i, inner] = pack[begin : begin + block, :]
 
-        for m in range(inner_rows):
-            for c in range(COLS_DEV):
-                slot[m, c] = 0
-        sums = {}
+        for p in range(parts):
+            for m in range(inner_rows):
+                for c in range(COLS_DEV):
+                    slot[p * inner_rows + m, c] = -1
         for p in range(parts):
             for m in range(inner_rows):
                 for l in range(inner_slots):
-                    slot[m, read(cols[p], starts[1 + p], m, l, inner_slots) - first] = l
+                    slot[p * inner_rows + m, read(cols[p], starts[1 + p], m, l, inner_slots) - first] = l
+        sums = {}
+        for p in range(parts):
             for i in span:
                 for j in range(slots):
-                    column = read(wanted, starts[0], i, j, slots)
+                    column = read(wanted, starts[0], i, j, slots) - first
                     for m in range(inner_rows):
-                        l = slot[m, column - first]
-                        hit = read(cols[p], starts[1 + p], m, l, inner_slots) == column
-                        begin = pl.multiple_of((m * inner_slots + l) * block, block)
+                        l = slot[p * inner_rows + m, column]
+                        begin = pl.multiple_of((m * inner_slots + jnp.maximum(l, 0)) * block, block)
                         tile = tiles[p][pl.ds(begin, block), :]
-                        right[i, m * block : (m + 1) * block, j * block : (j + 1) * block] = jnp.where(
-                            hit, tile, jnp.zeros_like(tile)
+                        right[p % 2, i, m * block : (m + 1) * block, j * block : (j + 1) * block] = jnp.where(
+                            l >= 0, tile, jnp.zeros_like(tile)
                         )
             for i in span:
                 left = jnp.concatenate(
                     [dense[i, place[1 + p] * inner_rows + m] for m in range(inner_rows)], axis=1
                 )
-                product = jnp.dot(left, right[i], preferred_element_type=jnp.float32)
+                product = jnp.dot(left, right[p % 2, i], preferred_element_type=jnp.float32)
                 sums[i] = sums[i] + product if i in sums else product
         for at, i in enumerate(span):
             for j in range(slots):
@@ -151,7 +152,7 @@
 
     far, end = col_count // 2, row_count - 1
     flat = b_tiles.reshape(-1, block)
-    own, packed = pack(a_tiles, a_cols, c_cols), pack(b_tiles, b_cols)
+    own, packed = pack(a_tiles, a_cols), pack(b_tiles, b_cols, c_cols)
     shards = {0: flat, end: deliver(flat, end)}
     cols = {0: (None, b_cols), end: (None, swap(b_cols, "row", row_count, end))}
     own_packs = [own, swap(own, "col", col_count, far)]
@@ -182,8 +183,8 @@
                 out_specs=VMEM,
                 scratch_shapes=[
                     pltpu.VMEM((rows, inner_rows * row_count, block, block), dtype),
-                    pltpu.VMEM((rows, inner_rows * block, slots * block), dtype),
-                    pltpu.SMEM((inner_rows, COLS_DEV), jnp.int32),
+                    pltpu.VMEM((2, rows, inner_rows * block, slots * block), dtype),
+                    pltpu.SMEM((len(order) * inner_rows, COLS_DEV), jnp.int32),
                 ],
                 compiler_params=PARAMS,
                 cost_estimate=FREE,
@@ -191,7 +192,7 @@
             for span in spans
         ]
 
-    given = products((a_cols.size, index_of([other], a_tiles)), other_packs, [[i] for i in every])
+    given = products((b_cols.size, cols[1][1]), other_packs, [[i] for i in every])
     given = [give_back(x) for x in given]
     (kept,) = products((None, c_cols), own_packs, [every])
     return jnp.where(working, kept, jnp.concatenate(given, axis=0))

time: 39.7 us -> 39.8 us (level)
  local copies, waits for them, and re-layouts: 3.94 us -> 2.63 us
  waiting for transfers between devices: 16.9 us -> 17.9 us
    unnamed x12 -> x10, local copies, waits for them, and re-layouts: 2.97 us -> 1.64 us
    ppermute x5, waiting for transfers between devices: 3.52 us -> 4.16 us  [permute(): return lax.ppermute(x, ('row', 'col'), pairs)]
  transfers between devices with their start and end apart: 13 -> 13, of which waited for: 5 -> 5; matrix products, arithmetic and copies ran while one was open for 3% -> 3% of each run, Pallas kernels for 18% -> 19%
where the time goes in v18:
time: 39.8 us; the launch traced here: 39.6 us
  waiting for transfers between devices  17.9 us (45%)
  starting transfers between devices  10.5 us (26%)
  Pallas kernels  7.37 us (19%)
  local copies, waits for them, and re-layouts  2.63 us (7%)
  other arithmetic  1.05 us (3%)
    ppermute x8, waiting for transfers between devices, swap(): return lax.ppermute(x, axis, [(k, k ^ d) for k in range(n)])  13.8 us
    pallas_call x3, Pallas kernels, products(): pl.pallas_call(functools.partial(product_kernel, starts, span, len(order)...  6.21 us
    ppermute x8, starting transfers between devices, swap(): return lax.ppermute(x, axis, [(k, k ^ d) for k in range(n)])  5.27 us
    ppermute x5, starting transfers between devices, permute(): return lax.ppermute(x, ('row', 'col'), pairs)  5.19 us
    ppermute x5, waiting for transfers between devices, permute(): return lax.ppermute(x, ('row', 'col'), pairs)  4.16 us
    unnamed x10, local copies, waits for them, and re-layouts  1.64 us
    pallas_call x2, Pallas kernels, pack(): pl.pallas_call(pack_kernel, out_shape=jax.ShapeDtypeStruct((size + -(-cou...  1.17 us
    slice x8, local copies, waits for them, and re-layouts, index_of(): x[tiles.size // block:, 0]  0.91 us
  transfers between devices with their start and end apart: 13, of which 5 were waited for; matrix products, arithmetic and copies ran while one was open for 3% of the time, Pallas kernels for 19%

profile of v18, /device:TPU:0, one launch (start us, length us, event | category | flops | bytes accessed | tf_op | source)
XLA Modules:
  0.0 39.6 jit_solution(6753031420593584993)
XLA Ops:
  0.0 5.0 %collective-permute-start.6 = (bf16[2048,128]{1,0:T(8,128)(2,1)}, bf16[2048,128]{1,0:T(8,128)(2,1)S(1)}, u32[]{:S(2)}, u32[]{:S(2)}) collective-permute-start(bf16[2048,128]{1,0:T(8,128)(2,1)} %bitcast.17), channel_id=1, source_target_pairs={{0,12},{1,3},{2,14},{3,1},{4,6},{5,9},{6,4},{7,11},{8,10},{9,5},{1... | collective-permute-start | bytes 1572872 | tf_op jit(solution)/shard_map/ppermute | solution.py:119
  5.1 0.9 %copy-done.1 = bf16[2,4,128,128]{3,2,1,0:T(8,128)(2,1)S(1)} copy-done((bf16[2,4,128,128]{3,2,1,0:T(8,128)(2,1)S(1)}, bf16[2,4,128,128]{3,2,1,0:T(8,128)(2,1)}, u32[]{:S(2)}) %copy-start.1) | copy-done | bytes 262168
  6.0 0.7 %copy-done.4 = s32[2,4]{1,0:T(2,128)S(1)} copy-done((s32[2,4]{1,0:T(2,128)S(1)}, s32[2,4]{1,0:T(2,128)}, u32[]{:S(2)}) %copy-start.4) | copy-done | bytes 56
  6.7 0.6 %shard_map.55.refs_8_ = bf16[1040,128]{1,0:T(8,128)(2,1)S(1)} custom-call(s32[2,4]{1,0:T(2,128)S(1)} %copy-done.4, bf16[1024,128]{1,0:T(8,128)(2,1)S(1)} %bitcast.22), custom_call_target="tpu_custom_call" | custom-call | flops 1 | bytes 1 | tf_op jit(solution)/shard_map/pallas_call | solution.py:135
  7.3 1.6 %collective-permute-start = (bf16[1040,128]{1,0:T(8,128)(2,1)S(1)}, bf16[1040,128]{1,0:T(8,128)(2,1)S(1)}, u32[]{:S(2)}, u32[]{:S(2)}) collective-permute-start(bf16[1040,128]{1,0:T(8,128)(2,1)S(1)} %shard_map.55.refs_8_), channel_id=1, source_target_pairs={{0,2},{1,3},{2,0},{3,1},{4,6},{5,7},{6,4},{7,5},{8,10},{9,11},{10,... | collective-permute-start | bytes 798728 | tf_op jit(solution)/shard_map/ppermute | solution.py:111
  8.8 1.0 %collective-permute-start.5 = (s32[2,8]{1,0:T(2,128)S(1)}, s32[2,8]{1,0:T(2,128)S(1)}, u32[]{:S(2)}, u32[]{:S(2)}) collective-permute-start(s32[2,8]{1,0:T(2,128)S(1)} %copy-done.2), channel_id=1, source_target_pairs={{0,12},{4,8},{8,4},{12,0},{1,13},{5,9},{9,5},{13,1},{2,14},{6,10},... | collective-permute-start | bytes 200 | tf_op jit(solution)/shard_map/ppermute | solution.py:111
  9.8 0.6 %shard_map.56 = bf16[2080,128]{1,0:T(8,128)(2,1)S(1)} custom-call(s32[2,8]{1,0:T(2,128)S(1)} %copy-done.2, s32[2,6]{1,0:T(2,128)S(1)} %copy-done.3, bf16[2048,128]{1,0:T(8,128)(2,1)S(1)} %bitcast.18), custom_call_target="tpu_custom_call" | custom-call | flops 1 | bytes 1 | tf_op jit(solution)/shard_map/pallas_call | solution.py:135
  10.4 0.1 stack.29.place
  10.5 0.1 slice_reduce_fusion.6
  10.6 4.6 %collective-permute-done.refs_9_ = bf16[1040,128]{1,0:T(8,128)(2,1)S(1)} collective-permute-done((bf16[1040,128]{1,0:T(8,128)(2,1)S(1)}, bf16[1040,128]{1,0:T(8,128)(2,1)S(1)}, u32[]{:S(2)}, u32[]{:S(2)}) %collective-permute-start) | collective-permute-done | bytes 266272 | tf_op jit(solution)/shard_map/ppermute | solution.py:111
  15.2 4.7 %collective-permute-done.7.refs_8_ = bf16[1040,128]{1,0:T(8,128)(2,1)S(1)} collective-permute-done((bf16[1040,128]{1,0:T(8,128)(2,1)S(1)}, bf16[1040,128]{1,0:T(8,128)(2,1)S(1)}, u32[]{:S(2)}, u32[]{:S(2)}) %collective-permute-start.7) | collective-permute-done | bytes 266272 | tf_op jit(solution)/shard_map/ppermute | solution.py:111
  19.9 2.1 %collective-permute-start.8 = (bf16[1040,128]{1,0:T(8,128)(2,1)S(1)}, bf16[1040,128]{1,0:T(8,128)(2,1)S(1)}, u32[]{:S(2)}, u32[]{:S(2)}) collective-permute-start(bf16[1040,128]{1,0:T(8,128)(2,1)S(1)} %collective-permute-done.7.refs_8_), channel_id=1, source_target_pairs={{0,2},{1,3},{2,0},{3,1},{4,6},{5,7},{6,4},{7,5},{8,10},{9,11},{10,... | collective-permute-start | bytes 798728 | tf_op jit(solution)/shard_map/ppermute | solution.py:111
  22.0 0.1 slice_reduce_fusion.4
  22.1 0.1 collective-permute-start.9
  22.2 0.1 slice_reduce_fusion.5
  22.3 0.1 slice_reduce_fusion.7
  22.4 4.5 %collective-permute-done.8.refs_9_ = bf16[1040,128]{1,0:T(8,128)(2,1)S(1)} collective-permute-done((bf16[1040,128]{1,0:T(8,128)(2,1)S(1)}, bf16[1040,128]{1,0:T(8,128)(2,1)S(1)}, u32[]{:S(2)}, u32[]{:S(2)}) %collective-permute-start.8) | collective-permute-done | bytes 266272 | tf_op jit(solution)/shard_map/ppermute | solution.py:111
  26.9 0.1 slice_reduce_fusion.2
  27.1 0.6 %collective-permute-start.10 = (bf16[1040,128]{1,0:T(8,128)(2,1)S(1)}, bf16[1040,128]{1,0:T(8,128)(2,1)S(1)}, u32[]{:S(2)}, u32[]{:S(2)}) collective-permute-start(bf16[1040,128]{1,0:T(8,128)(2,1)S(1)} %collective-permute-done.8.refs_9_), channel_id=1, source_target_pairs={{0,1},{1,0},{2,3},{3,2},{4,5},{5,4},{6,7},{7,6},{8,9},{9,8},{10,11... | collective-permute-start | bytes 798728 | tf_op jit(solution)/shard_map/ppermute | solution.py:111
  27.6 0.1 slice_reduce_fusion.1
  27.8 0.1 convert_reduce_fusion.1
  27.9 3.5 %collective-permute-done.4.refs_5_ = bf16[2080,128]{1,0:T(8,128)(2,1)S(1)} collective-permute-done((bf16[2080,128]{1,0:T(8,128)(2,1)S(1)}, bf16[2080,128]{1,0:T(8,128)(2,1)S(1)}, u32[]{:S(2)}, u32[]{:S(2)}) %collective-permute-start.4) | collective-permute-done | bytes 532512 | tf_op jit(solution)/shard_map/ppermute | solution.py:119
  31.4 0.1 convert_reduce_fusion
  31.5 0.1 slice_reduce_fusion
  31.7 1.8 %shard_map.59 = bf16[1,6,128,128]{3,2,1,0:T(8,128)(2,1)S(1)} custom-call(s32[5]{0:T(128)S(1)} %stack.29.place, s32[4,16]{1,0:T(4,128)S(1)} %maximum_convert_fusion.1.left_index, s32[1,32]{1,0:T(1,128)S(1)} %bitcast.23, s32[1,32]{1,0:T(1,128)S(1)} %bitcast.24, s32[1,32]{1,0:T(1,128)S(1)} %bitcast.28, s32[2,8]{1,0:T(2,128)S(1)} %copy-done.2, ...), custom_call_target="tpu_custom_call" | custom-call | flops 1 | bytes 1 | tf_op jit(solution)/shard_map/pallas_call | solution.py:179
  33.5 0.1 collective-permute-start.12
  33.5 1.8 %shard_map.58 = bf16[1,6,128,128]{3,2,1,0:T(8,128)(2,1)S(1)} custom-call(s32[5]{0:T(128)S(1)} %stack.29.place, s32[4,16]{1,0:T(4,128)S(1)} %maximum_convert_fusion.1.left_index, s32[1,32]{1,0:T(1,128)S(1)} %bitcast.25, s32[1,32]{1,0:T(1,128)S(1)} %bitcast.26, s32[1,32]{1,0:T(1,128)S(1)} %bitcast.29, s32[2,8]{1,0:T(2,128)S(1)} %copy-done.2, ...), custom_call_target="tpu_custom_call" | custom-call | flops 1 | bytes 1 | tf_op jit(solution)/shard_map/pallas_call | solution.py:179
  35.3 0.1 collective-permute-start.11
  35.4 0.1 slice_reduce_fusion.3
  35.5 2.6 %shard_map.57 = bf16[2,6,128,128]{3,2,1,0:T(8,128)(2,1)S(1)} custom-call(s32[5]{0:T(128)S(1)} %stack.29.place, s32[4,16]{1,0:T(4,128)S(1)} %maximum_convert_fusion.left_index, s32[2,6]{1,0:T(2,128)S(1)} %copy-done.3, s32[1,32]{1,0:T(1,128)S(1)} %bitcast.27, s32[1,32]{1,0:T(1,128)S(1)} %bitcast.30, s32[2,8]{1,0:T(2,128)S(1)} %copy-done.2, ...), custom_call_target="tpu_custom_call" | custom-call | flops 1 | bytes 1 | tf_op jit(solution)/shard_map/pallas_call | solution.py:179
  38.2 0.6 %collective-permute-done.11 = bf16[1,6,128,128]{3,2,1,0:T(8,128)(2,1)S(1)} collective-permute-done((bf16[1,6,128,128]{3,2,1,0:T(8,128)(2,1)S(1)}, bf16[1,6,128,128]{3,2,1,0:T(8,128)(2,1)S(1)}, u32[]{:S(2)}, u32[]{:S(2)}) %collective-permute-start.11) | collective-permute-done | bytes 196640 | tf_op jit(solution)/shard_map/ppermute | solution.py:119
  38.8 0.8 %maximum_select_fusion = bf16[2,6,128,128]{3,2,1,0:T(8,128)(2,1)} fusion(bf16[2,6,128,128]{3,2,1,0:T(8,128)(2,1)S(1)} %shard_map.57, bf16[1,6,128,128]{3,2,1,0:T(8,128)(2,1)S(1)} %collective-permute-done.12, bf16[1,6,128,128]{3,2,1,0:T(8,128)(2,1)S(1)} %collective-permute-done.11, pred[]{:T(512)S(6)} %eq.5), kind=kLoop, calls=%fused_computation | loop fusion | flops 393216 | bytes 1179649 | tf_op jit(solution)/shard_map/jit(_where)/select_n | solution.py:198
  (23 shorter events, 0.1 us)
Async XLA Ops:
  0.0 9.8 %copy-start = (bf16[2,8,128,128]{3,2,1,0:T(8,128)(2,1)S(1)}, bf16[2,8,128,128]{3,2,1,0:T(8,128)(2,1)}, u32[]{:S(2)}) copy-start(bf16[2,8,128,128]{3,2,1,0:T(8,128)(2,1)} %param.7) | copy-start | bytes 1572868
  0.0 19.9 %collective-permute-start.6 = (bf16[2048,128]{1,0:T(8,128)(2,1)}, bf16[2048,128]{1,0:T(8,128)(2,1)S(1)}, u32[]{:S(2)}, u32[]{:S(2)}) collective-permute-start(bf16[2048,128]{1,0:T(8,128)(2,1)} %bitcast.17), channel_id=1, source_target_pairs={{0,12},{1,3},{2,14},{3,1},{4,6},{5,9},{6,4},{7,11},{8,10},{9,5},{1... | collective-permute-start | bytes 1572872 | tf_op jit(solution)/shard_map/ppermute | solution.py:119
  5.1 0.9 %copy-start.1 = (bf16[2,4,128,128]{3,2,1,0:T(8,128)(2,1)S(1)}, bf16[2,4,128,128]{3,2,1,0:T(8,128)(2,1)}, u32[]{:S(2)}) copy-start(bf16[2,4,128,128]{3,2,1,0:T(8,128)(2,1)} %param.5) | copy-start | bytes 786436
  6.0 0.7 %copy-start.4 = (s32[2,4]{1,0:T(2,128)S(1)}, s32[2,4]{1,0:T(2,128)}, u32[]{:S(2)}) copy-start(s32[2,4]{1,0:T(2,128)} %refs_0_.2) | copy-start | bytes 100
  6.7 2.1 %copy-start.2 = (s32[2,8]{1,0:T(2,128)S(1)}, s32[2,8]{1,0:T(2,128)}, u32[]{:S(2)}) copy-start(s32[2,8]{1,0:T(2,128)} %refs_2_.5) | copy-start | bytes 196
  6.7 3.1 %copy-start.3 = (s32[2,6]{1,0:T(2,128)S(1)}, s32[2,6]{1,0:T(2,128)}, u32[]{:S(2)}) copy-start(s32[2,6]{1,0:T(2,128)} %wanted.1) | copy-start | bytes 148
  7.3 8.0 %collective-permute-start = (bf16[1040,128]{1,0:T(8,128)(2,1)S(1)}, bf16[1040,128]{1,0:T(8,128)(2,1)S(1)}, u32[]{:S(2)}, u32[]{:S(2)}) collective-permute-start(bf16[1040,128]{1,0:T(8,128)(2,1)S(1)} %shard_map.55.refs_8_), channel_id=1, source_target_pairs={{0,2},{1,3},{2,0},{3,1},{4,6},{5,7},{6,4},{7,5},{8,10},{9,11},{10,... | collective-permute-start | bytes 798728 | tf_op jit(solution)/shard_map/ppermute | solution.py:111
  8.8 6.4 %collective-permute-start.1 = (bf16[1040,128]{1,0:T(8,128)(2,1)S(1)}, bf16[1040,128]{1,0:T(8,128)(2,1)S(1)}, u32[]{:S(2)}, u32[]{:S(2)}) collective-permute-start(bf16[1040,128]{1,0:T(8,128)(2,1)S(1)} %shard_map.55.refs_8_), channel_id=1, source_target_pairs={{0,1},{1,0},{2,3},{3,2},{4,5},{5,4},{6,7},{7,6},{8,9},{9,8},{10,11... | collective-permute-start | bytes 798728 | tf_op jit(solution)/shard_map/ppermute | solution.py:111
  8.8 11.1 %collective-permute-start.7 = (bf16[1040,128]{1,0:T(8,128)(2,1)S(1)}, bf16[1040,128]{1,0:T(8,128)(2,1)S(1)}, u32[]{:S(2)}, u32[]{:S(2)}) collective-permute-start(bf16[1040,128]{1,0:T(8,128)(2,1)S(1)} %shard_map.55.refs_8_), channel_id=1, source_target_pairs={{0,4},{4,0},{8,12},{12,8},{1,5},{5,1},{9,13},{13,9},{2,6},{6,2},{1... | collective-permute-start | bytes 798728 | tf_op jit(solution)/shard_map/ppermute | solution.py:111
  8.8 22.8 %collective-permute-start.5 = (s32[2,8]{1,0:T(2,128)S(1)}, s32[2,8]{1,0:T(2,128)S(1)}, u32[]{:S(2)}, u32[]{:S(2)}) collective-permute-start(s32[2,8]{1,0:T(2,128)S(1)} %copy-done.2), channel_id=1, source_target_pairs={{0,12},{4,8},{8,4},{12,0},{1,13},{5,9},{9,5},{13,1},{2,14},{6,10},... | collective-permute-start | bytes 200 | tf_op jit(solution)/shard_map/ppermute | solution.py:111
  15.2 16.2 %collective-permute-start.4 = (bf16[2080,128]{1,0:T(8,128)(2,1)S(1)}, bf16[2080,128]{1,0:T(8,128)(2,1)S(1)}, u32[]{:S(2)}, u32[]{:S(2)}) collective-permute-start(bf16[2080,128]{1,0:T(8,128)(2,1)S(1)} %shard_map.56), channel_id=1, source_target_pairs={{0,1},{1,9},{2,3},{3,11},{4,12},{5,4},{6,14},{7,6},{8,0},{9,8},{10... | collective-permute-start | bytes 1597448 | tf_op jit(solution)/shard_map/ppermute | solution.py:119
  15.2 12.5 %collective-permute-start.3 = (bf16[2080,128]{1,0:T(8,128)(2,1)S(1)}, bf16[2080,128]{1,0:T(8,128)(2,1)S(1)}, u32[]{:S(2)}, u32[]{:S(2)}) collective-permute-start(bf16[2080,128]{1,0:T(8,128)(2,1)S(1)} %shard_map.56), channel_id=1, source_target_pairs={{0,1},{1,5},{2,3},{3,7},{4,0},{5,4},{6,2},{7,6},{8,12},{9,8},{10,1... | collective-permute-start | bytes 1597448 | tf_op jit(solution)/shard_map/ppermute | solution.py:119
  19.9 7.0 %collective-permute-start.8 = (bf16[1040,128]{1,0:T(8,128)(2,1)S(1)}, bf16[1040,128]{1,0:T(8,128)(2,1)S(1)}, u32[]{:S(2)}, u32[]{:S(2)}) collective-permute-start(bf16[1040,128]{1,0:T(8,128)(2,1)S(1)} %collective-permute-done.7.refs_8_), channel_id=1, source_target_pairs={{0,2},{1,3},{2,0},{3,1},{4,6},{5,7},{6,4},{7,5},{8,10},{9,11},{10,... | collective-permute-start | bytes 798728 | tf_op jit(solution)/shard_map/ppermute | solution.py:111
  22.1 4.9 %collective-permute-start.9 = (bf16[1040,128]{1,0:T(8,128)(2,1)S(1)}, bf16[1040,128]{1,0:T(8,128)(2,1)S(1)}, u32[]{:S(2)}, u32[]{:S(2)}) collective-permute-start(bf16[1040,128]{1,0:T(8,128)(2,1)S(1)} %collective-permute-done.7.refs_8_), channel_id=1, source_target_pairs={{0,1},{1,0},{2,3},{3,2},{4,5},{5,4},{6,7},{7,6},{8,9},{9,8},{10,11... | collective-permute-start | bytes 798728 | tf_op jit(solution)/shard_map/ppermute | solution.py:111
  26.9 8.5 %collective-permute-start.2 = (bf16[1040,128]{1,0:T(8,128)(2,1)S(1)}, bf16[1040,128]{1,0:T(8,128)(2,1)S(1)}, u32[]{:S(2)}, u32[]{:S(2)}) collective-permute-start(bf16[1040,128]{1,0:T(8,128)(2,1)S(1)} %collective-permute-done.refs_9_), channel_id=1, source_target_pairs={{0,1},{1,0},{2,3},{3,2},{4,5},{5,4},{6,7},{7,6},{8,9},{9,8},{10,11... | collective-permute-start | bytes 798728 | tf_op jit(solution)/shard_map/ppermute | solution.py:111
  27.1 4.4 %collective-permute-start.10 = (bf16[1040,128]{1,0:T(8,128)(2,1)S(1)}, bf16[1040,128]{1,0:T(8,128)(2,1)S(1)}, u32[]{:S(2)}, u32[]{:S(2)}) collective-permute-start(bf16[1040,128]{1,0:T(8,128)(2,1)S(1)} %collective-permute-done.8.refs_9_), channel_id=1, source_target_pairs={{0,1},{1,0},{2,3},{3,2},{4,5},{5,4},{6,7},{7,6},{8,9},{9,8},{10,11... | collective-permute-start | bytes 798728 | tf_op jit(solution)/shard_map/ppermute | solution.py:111
  33.5 4.7 %collective-permute-start.12 = (bf16[1,6,128,128]{3,2,1,0:T(8,128)(2,1)S(1)}, bf16[1,6,128,128]{3,2,1,0:T(8,128)(2,1)S(1)}, u32[]{:S(2)}, u32[]{:S(2)}) collective-permute-start(bf16[1,6,128,128]{3,2,1,0:T(8,128)(2,1)S(1)} %shard_map.59), channel_id=1, source_target_pairs={{0,4},{1,0},{2,6},{3,2},{4,5},{5,1},{6,7},{7,3},{8,9},{9,13},{10,1... | collective-permute-start | bytes 589832 | tf_op jit(solution)/shard_map/ppermute | solution.py:119
  35.3 3.5 %collective-permute-start.11 = (bf16[1,6,128,128]{3,2,1,0:T(8,128)(2,1)S(1)}, bf16[1,6,128,128]{3,2,1,0:T(8,128)(2,1)S(1)}, u32[]{:S(2)}, u32[]{:S(2)}) collective-permute-start(bf16[1,6,128,128]{3,2,1,0:T(8,128)(2,1)S(1)} %shard_map.58), channel_id=1, source_target_pairs={{0,4},{1,0},{2,6},{3,2},{4,5},{5,1},{6,7},{7,3},{8,9},{9,13},{10,1... | collective-permute-start | bytes 589832 | tf_op jit(solution)/shard_map/ppermute | solution.py:119

commit v19 on v17

--- a/solution.py
+++ b/solution.py
@@ -30,7 +30,7 @@
     out[size:, :] = found.astype(out.dtype)
 
 
-def product_kernel(starts, span, parts, place, left_index, wanted, *refs):
+def product_kernel(starts, span, columns, parts, place, left_index, wanted, *refs):
     cols, refs = refs[:parts], refs[parts:]
     tiles, refs = refs[:parts], refs[parts:]
     packs, (out, dense, right, slot) = refs[:-4], refs[-4:]
@@ -68,24 +68,24 @@
                 for l in range(inner_slots):
                     slot[m, read(cols[p], starts[1 + p], m, l, inner_slots) - first] = l
             for i in span:
-                for j in range(slots):
+                for at, j in enumerate(columns):
                     column = read(wanted, starts[0], i, j, slots)
                     for m in range(inner_rows):
                         l = slot[m, column - first]
                         hit = read(cols[p], starts[1 + p], m, l, inner_slots) == column
                         begin = pl.multiple_of((m * inner_slots + l) * block, block)
                         tile = tiles[p][pl.ds(begin, block), :]
-                        right[i, m * block : (m + 1) * block, j * block : (j + 1) * block] = jnp.where(
+                        right[i, m * block : (m + 1) * block, at * block : (at + 1) * block] = jnp.where(
                             hit, tile, jnp.zeros_like(tile)
                         )
             for i in span:
                 left = jnp.concatenate(
                     [dense[i, place[1 + p] * inner_rows + m] for m in range(inner_rows)], axis=1
                 )
-                product = jnp.dot(left, right[i], preferred_element_type=jnp.float32)
+                product = jnp.dot(left, right[i, :, : len(columns) * block], preferred_element_type=jnp.float32)
                 sums[i] = sums[i] + product if i in sums else product
         for at, i in enumerate(span):
-            for j in range(slots):
+            for j in range(len(columns)):
                 out[at, j] = sums[i][:, j * block : (j + 1) * block].astype(out.dtype)
 
 
@@ -171,13 +171,13 @@
         cols[d] = (0, index_of([shards[d]], b_tiles))
     place = jnp.stack([jnp.where(working, first, -1)] + [r ^ d for d in order]).astype(jnp.int32)
 
-    def products(wanted, packs, spans):
+    def products(wanted, packs, pieces):
         index = index_of(packs, a_tiles)
         starts = [wanted[0]] + [cols[d][0] for d in order]
         return [
             pl.pallas_call(
-                functools.partial(product_kernel, starts, span, len(order)),
-                out_shape=jax.ShapeDtypeStruct((len(span), slots, block, block), dtype),
+                functools.partial(product_kernel, starts, span, columns, len(order)),
+                out_shape=jax.ShapeDtypeStruct((len(span), len(columns), block, block), dtype),
                 in_specs=[SMEM] * (3 + len(order)) + [VMEM] * (len(order) + len(packs)),
                 out_specs=VMEM,
                 scratch_shapes=[
@@ -188,12 +188,15 @@
                 compiler_params=PARAMS,
                 cost_estimate=FREE,
             )(place, index, wanted[1], *[cols[d][1] for d in order], *[shards[d] for d in order], *packs)
-            for span in spans
+            for span, columns in pieces
         ]
 
-    given = products((a_cols.size, index_of([other], a_tiles)), other_packs, [[i] for i in every])
+    half = list(range(slots // 2)), list(range(slots // 2, slots))
+    pieces = [([i], columns) for i in every for columns in half]
+    given = products((a_cols.size, index_of([other], a_tiles)), other_packs, pieces)
     given = [give_back(x) for x in given]
-    (kept,) = products((None, c_cols), own_packs, [every])
+    given = [jnp.concatenate(given[2 * i : 2 * i + 2], axis=1) for i in every]
+    (kept,) = products((None, c_cols), own_packs, [(every, list(range(slots)))])
     return jnp.where(working, kept, jnp.concatenate(given, axis=0))
 
 

time: 39.7 us -> 42.5 us (1.071)
  starting transfers between devices: 10.3 us -> 15.1 us
  waiting for transfers between devices: 16.9 us -> 12.7 us
  Pallas kernels: 7.03 us -> 9.15 us
    ppermute x8, waiting for transfers between devices: 13.4 us -> 8.82 us  [swap(): return lax.ppermute(x, axis, [(k, k ^ d) for k in range(n)])]
    ppermute x8, starting transfers between devices: 5.15 us -> 9.06 us  [swap(): return lax.ppermute(x, axis, [(k, k ^ d) for k in range(n)])]
    pallas_call x3 -> x5, Pallas kernels: 5.85 us -> 7.98 us  [products(): pl.pallas_call(functools.partial(product_kernel, starts, span, columns, l...]
    ppermute x5 -> x7, starting transfers between devices: 5.19 us -> 6.07 us  [permute(): return lax.ppermute(x, ('row', 'col'), pairs)]
    ppermute x5 -> x7, waiting for transfers between devices: 3.52 us -> 3.92 us  [permute(): return lax.ppermute(x, ('row', 'col'), pairs)]
  transfers between devices with their start and end apart: 13 -> 15, of which waited for: 5 -> 4; matrix products, arithmetic and copies ran while one was open for 3% -> 3% of each run, Pallas kernels for 18% -> 18%
where the time goes in v19:
time: 42.5 us; the launch traced here: 42.3 us
  starting transfers between devices  15.1 us (36%)
  waiting for transfers between devices  12.7 us (30%)
  Pallas kernels  9.15 us (22%)
  local copies, waits for them, and re-layouts  3.95 us (9%)
  other arithmetic  1.07 us (3%)
    ppermute x8, starting transfers between devices, swap(): return lax.ppermute(x, axis, [(k, k ^ d) for k in range(n)])  9.06 us
    ppermute x8, waiting for transfers between devices, swap(): return lax.ppermute(x, axis, [(k, k ^ d) for k in range(n)])  8.82 us
    pallas_call x5, Pallas kernels, products(): pl.pallas_call(functools.partial(product_kernel, starts, span, columns, l...  7.98 us
    ppermute x7, starting transfers between devices, permute(): return lax.ppermute(x, ('row', 'col'), pairs)  6.07 us
    ppermute x7, waiting for transfers between devices, permute(): return lax.ppermute(x, ('row', 'col'), pairs)  3.92 us
    unnamed x12, local copies, waits for them, and re-layouts  2.98 us
    pallas_call x2, Pallas kernels, pack(): pl.pallas_call(pack_kernel, out_shape=jax.ShapeDtypeStruct((size + -(-cou...  1.17 us
    slice x8, local copies, waits for them, and re-layouts, index_of(): x[tiles.size // block:, 0]  0.89 us
  transfers between devices with their start and end apart: 15, of which 4 were waited for; matrix products, arithmetic and copies ran while one was open for 3% of the time, Pallas kernels for 18%

profile of v19, /device:TPU:0, one launch (start us, length us, event | category | flops | bytes accessed | tf_op | source)
XLA Modules:
  0.0 42.3 jit_solution(18268055385520387938)
XLA Ops:
  0.0 5.0 %collective-permute-start.6 = (bf16[2048,128]{1,0:T(8,128)(2,1)}, bf16[2048,128]{1,0:T(8,128)(2,1)S(1)}, u32[]{:S(2)}, u32[]{:S(2)}) collective-permute-start(bf16[2048,128]{1,0:T(8,128)(2,1)} %bitcast.18), channel_id=1, source_target_pairs={{0,12},{1,3},{2,14},{3,1},{4,6},{5,9},{6,4},{7,11},{8,10},{9,5},{1... | collective-permute-start | bytes 1572872 | tf_op jit(solution)/shard_map/ppermute | solution.py:118
  5.1 0.9 %copy-done.1 = bf16[2,4,128,128]{3,2,1,0:T(8,128)(2,1)S(1)} copy-done((bf16[2,4,128,128]{3,2,1,0:T(8,128)(2,1)S(1)}, bf16[2,4,128,128]{3,2,1,0:T(8,128)(2,1)}, u32[]{:S(2)}) %copy-start.1) | copy-done | bytes 262168
  6.0 0.7 %copy-done.3 = s32[2,6]{1,0:T(2,128)S(1)} copy-done((s32[2,6]{1,0:T(2,128)S(1)}, s32[2,6]{1,0:T(2,128)}, u32[]{:S(2)}) %copy-start.3) | copy-done | bytes 72
  6.7 0.7 %copy-done.5 = s32[2,4]{1,0:T(2,128)S(1)} copy-done((s32[2,4]{1,0:T(2,128)S(1)}, s32[2,4]{1,0:T(2,128)}, u32[]{:S(2)}) %copy-start.5) | copy-done | bytes 56
  7.4 0.6 %shard_map.55.refs_8_ = bf16[1056,128]{1,0:T(8,128)(2,1)S(1)} custom-call(s32[2,4]{1,0:T(2,128)S(1)} %copy-done.5, s32[2,6]{1,0:T(2,128)S(1)} %copy-done.3, bf16[1024,128]{1,0:T(8,128)(2,1)S(1)} %bitcast.25), custom_call_target="tpu_custom_call" | custom-call | flops 1 | bytes 1 | tf_op jit(solution)/shard_map/pallas_call | solution.py:134
  8.0 1.6 %collective-permute-start = (bf16[1056,128]{1,0:T(8,128)(2,1)S(1)}, bf16[1056,128]{1,0:T(8,128)(2,1)S(1)}, u32[]{:S(2)}, u32[]{:S(2)}) collective-permute-start(bf16[1056,128]{1,0:T(8,128)(2,1)S(1)} %shard_map.55.refs_8_), channel_id=1, source_target_pairs={{0,2},{1,3},{2,0},{3,1},{4,6},{5,7},{6,4},{7,5},{8,10},{9,11},{10,... | collective-permute-start | bytes 811016 | tf_op jit(solution)/shard_map/ppermute | solution.py:110
  9.5 0.1 slice_reduce_fusion.6
  9.7 0.6 %shard_map.56 = bf16[2064,128]{1,0:T(8,128)(2,1)S(1)} custom-call(s32[2,8]{1,0:T(2,128)S(1)} %copy-done.2, bf16[2048,128]{1,0:T(8,128)(2,1)S(1)} %bitcast.19), custom_call_target="tpu_custom_call" | custom-call | flops 1 | bytes 1 | tf_op jit(solution)/shard_map/pallas_call | solution.py:134
  10.4 5.0 %collective-permute-done.refs_9_ = bf16[1056,128]{1,0:T(8,128)(2,1)S(1)} collective-permute-done((bf16[1056,128]{1,0:T(8,128)(2,1)S(1)}, bf16[1056,128]{1,0:T(8,128)(2,1)S(1)}, u32[]{:S(2)}, u32[]{:S(2)}) %collective-permute-start) | collective-permute-done | bytes 270368 | tf_op jit(solution)/shard_map/ppermute | solution.py:110
  15.3 3.1 %collective-permute-start.2 = (bf16[1056,128]{1,0:T(8,128)(2,1)S(1)}, bf16[1056,128]{1,0:T(8,128)(2,1)S(1)}, u32[]{:S(2)}, u32[]{:S(2)}) collective-permute-start(bf16[1056,128]{1,0:T(8,128)(2,1)S(1)} %collective-permute-done.refs_9_), channel_id=1, source_target_pairs={{0,1},{1,0},{2,3},{3,2},{4,5},{5,4},{6,7},{7,6},{8,9},{9,8},{10,11... | collective-permute-start | bytes 811016 | tf_op jit(solution)/shard_map/ppermute | solution.py:110
  18.4 0.1 slice_reduce_fusion.4
  18.6 0.1 slice_reduce_fusion.5
  18.7 0.6 %collective-permute-done.7.refs_8_ = bf16[1056,128]{1,0:T(8,128)(2,1)S(1)} collective-permute-done((bf16[1056,128]{1,0:T(8,128)(2,1)S(1)}, bf16[1056,128]{1,0:T(8,128)(2,1)S(1)}, u32[]{:S(2)}, u32[]{:S(2)}) %collective-permute-start.7) | collective-permute-done | bytes 270368 | tf_op jit(solution)/shard_map/ppermute | solution.py:110
  19.3 2.0 %collective-permute-start.8 = (bf16[1056,128]{1,0:T(8,128)(2,1)S(1)}, bf16[1056,128]{1,0:T(8,128)(2,1)S(1)}, u32[]{:S(2)}, u32[]{:S(2)}) collective-permute-start(bf16[1056,128]{1,0:T(8,128)(2,1)S(1)} %collective-permute-done.7.refs_8_), channel_id=1, source_target_pairs={{0,2},{1,3},{2,0},{3,1},{4,6},{5,7},{6,4},{7,5},{8,10},{9,11},{10,... | collective-permute-start | bytes 811016 | tf_op jit(solution)/shard_map/ppermute | solution.py:110
  21.3 0.1 slice_reduce_fusion.7
  21.5 2.4 %collective-permute-start.5 = (s32[2,8]{1,0:T(2,128)S(1)}, s32[2,8]{1,0:T(2,128)S(1)}, u32[]{:S(2)}, u32[]{:S(2)}) collective-permute-start(s32[2,8]{1,0:T(2,128)S(1)} %copy-done.2), channel_id=1, source_target_pairs={{0,12},{4,8},{8,4},{12,0},{1,13},{5,9},{9,5},{13,1},{2,14},{6,10},... | collective-permute-start | bytes 200 | tf_op jit(solution)/shard_map/ppermute | solution.py:110
  23.8 0.1 slice_reduce_fusion.3
  23.9 3.2 %collective-permute-done.8.refs_9_ = bf16[1056,128]{1,0:T(8,128)(2,1)S(1)} collective-permute-done((bf16[1056,128]{1,0:T(8,128)(2,1)S(1)}, bf16[1056,128]{1,0:T(8,128)(2,1)S(1)}, u32[]{:S(2)}, u32[]{:S(2)}) %collective-permute-start.8) | collective-permute-done | bytes 270368 | tf_op jit(solution)/shard_map/ppermute | solution.py:110
  27.2 0.1 slice_reduce_fusion.2
  27.3 0.1 slice_reduce_fusion.1
  27.4 0.1 convert_reduce_fusion.1
  27.5 3.9 %collective-permute-done.4.refs_5_ = bf16[2064,128]{1,0:T(8,128)(2,1)S(1)} collective-permute-done((bf16[2064,128]{1,0:T(8,128)(2,1)S(1)}, bf16[2064,128]{1,0:T(8,128)(2,1)S(1)}, u32[]{:S(2)}, u32[]{:S(2)}) %collective-permute-start.4) | collective-permute-done | bytes 528416 | tf_op jit(solution)/shard_map/ppermute | solution.py:118
  31.4 0.1 convert_reduce_fusion
  31.5 0.1 slice_reduce_fusion
  31.7 1.4 %shard_map.61 = bf16[1,3,128,128]{3,2,1,0:T(8,128)(2,1)S(1)} custom-call(s32[5]{0:T(128)S(1)} %stack.29.place, s32[4,32]{1,0:T(4,128)S(1)} %maximum_convert_fusion.1.left_index, s32[1,32]{1,0:T(1,128)S(1)} %bitcast_convert_fusion.wanted, s32[1,16]{1,0:T(1,128)S(1)} %bitcast.26, s32[1,16]{1,0:T(1,128)S(1)} %bitcast.31, s32[2,8]{1,0:T(2,128)S(1)} %copy-done.2, ...), custom_call_target="tpu_custom_call" | custom-call | flops 1 | bytes 1 | tf_op jit(solution)/shard_map/pallas_call | solution.py:178
  33.1 1.4 %shard_map.60 = bf16[1,3,128,128]{3,2,1,0:T(8,128)(2,1)S(1)} custom-call(s32[5]{0:T(128)S(1)} %stack.29.place, s32[4,32]{1,0:T(4,128)S(1)} %maximum_convert_fusion.1.left_index, s32[1,32]{1,0:T(1,128)S(1)} %bitcast_convert_fusion.wanted, s32[1,16]{1,0:T(1,128)S(1)} %bitcast.27, s32[1,16]{1,0:T(1,128)S(1)} %bitcast.32, s32[2,8]{1,0:T(2,128)S(1)} %copy-done.2, ...), custom_call_target="tpu_custom_call" | custom-call | flops 1 | bytes 1 | tf_op jit(solution)/shard_map/pallas_call | solution.py:178
  34.6 1.4 %shard_map.59 = bf16[1,3,128,128]{3,2,1,0:T(8,128)(2,1)S(1)} custom-call(s32[5]{0:T(128)S(1)} %stack.29.place, s32[4,32]{1,0:T(4,128)S(1)} %maximum_convert_fusion.1.left_index, s32[1,32]{1,0:T(1,128)S(1)} %bitcast_convert_fusion.wanted, s32[1,16]{1,0:T(1,128)S(1)} %bitcast.28, s32[1,16]{1,0:T(1,128)S(1)} %bitcast.33, s32[2,8]{1,0:T(2,128)S(1)} %copy-done.2, ...), custom_call_target="tpu_custom_call" | custom-call | flops 1 | bytes 1 | tf_op jit(solution)/shard_map/pallas_call | solution.py:178
  36.0 1.4 %shard_map.58 = bf16[1,3,128,128]{3,2,1,0:T(8,128)(2,1)S(1)} custom-call(s32[5]{0:T(128)S(1)} %stack.29.place, s32[4,32]{1,0:T(4,128)S(1)} %maximum_convert_fusion.1.left_index, s32[1,32]{1,0:T(1,128)S(1)} %bitcast_convert_fusion.wanted, s32[1,16]{1,0:T(1,128)S(1)} %bitcast.29, s32[1,16]{1,0:T(1,128)S(1)} %bitcast.34, s32[2,8]{1,0:T(2,128)S(1)} %copy-done.2, ...), custom_call_target="tpu_custom_call" | custom-call | flops 1 | bytes 1 | tf_op jit(solution)/shard_map/pallas_call | solution.py:178
  37.4 0.8 %collective-permute-start.11 = (bf16[1,3,128,128]{3,2,1,0:T(8,128)(2,1)S(1)}, bf16[1,3,128,128]{3,2,1,0:T(8,128)(2,1)S(1)}, u32[]{:S(2)}, u32[]{:S(2)}) collective-permute-start(bf16[1,3,128,128]{3,2,1,0:T(8,128)(2,1)S(1)} %shard_map.58), channel_id=1, source_target_pairs={{0,4},{1,0},{2,6},{3,2},{4,5},{5,1},{6,7},{7,3},{8,9},{9,13},{10,1... | collective-permute-start | bytes 294920 | tf_op jit(solution)/shard_map/ppermute | solution.py:118
  38.2 0.7 %copy-done.4 = s32[2,6]{1,0:T(2,128)S(1)} copy-done((s32[2,6]{1,0:T(2,128)S(1)}, s32[2,6]{1,0:T(2,128)}, u32[]{:S(2)}) %copy-start.4) | copy-done | bytes 72
  38.9 2.5 %shard_map.57 = bf16[2,6,128,128]{3,2,1,0:T(8,128)(2,1)S(1)} custom-call(s32[5]{0:T(128)S(1)} %stack.29.place, s32[4,32]{1,0:T(4,128)S(1)} %maximum_convert_fusion.left_index, s32[2,6]{1,0:T(2,128)S(1)} %copy-done.4, s32[1,16]{1,0:T(1,128)S(1)} %bitcast.30, s32[1,16]{1,0:T(1,128)S(1)} %bitcast.35, s32[2,8]{1,0:T(2,128)S(1)} %copy-done.2, ...), custom_call_target="tpu_custom_call" | custom-call | flops 1 | bytes 1 | tf_op jit(solution)/shard_map/pallas_call | solution.py:178
  41.5 0.8 %maximum_select_fusion = bf16[2,6,128,128]{3,2,1,0:T(8,128)(2,1)} fusion(bf16[2,6,128,128]{3,2,1,0:T(8,128)(2,1)S(1)} %shard_map.57, bf16[1,3,128,128]{3,2,1,0:T(8,128)(2,1)S(1)} %collective-permute-done.14, bf16[1,3,128,128]{3,2,1,0:T(8,128)(2,1)S(1)} %collective-permute-done.13, bf16[1,3,128,128]{3,2,1,0:T(8,128)(2,1)S(1)} %collective-permute-done.12, ...), kind=kLoop, calls=%fused_computation | loop fusion | flops 786432 | bytes 1179649 | tf_op jit(solution)/shard_map/jit(_where)/select_n | solution.py:200
  (32 shorter events, 0.4 us)
Async XLA Ops:
  0.0 9.6 %copy-start = (bf16[2,8,128,128]{3,2,1,0:T(8,128)(2,1)S(1)}, bf16[2,8,128,128]{3,2,1,0:T(8,128)(2,1)}, u32[]{:S(2)}) copy-start(bf16[2,8,128,128]{3,2,1,0:T(8,128)(2,1)} %param.7) | copy-start | bytes 1572868
  0.0 19.3 %collective-permute-start.6 = (bf16[2048,128]{1,0:T(8,128)(2,1)}, bf16[2048,128]{1,0:T(8,128)(2,1)S(1)}, u32[]{:S(2)}, u32[]{:S(2)}) collective-permute-start(bf16[2048,128]{1,0:T(8,128)(2,1)} %bitcast.18), channel_id=1, source_target_pairs={{0,12},{1,3},{2,14},{3,1},{4,6},{5,9},{6,4},{7,11},{8,10},{9,5},{1... | collective-permute-start | bytes 1572872 | tf_op jit(solution)/shard_map/ppermute | solution.py:118
  5.1 0.9 %copy-start.1 = (bf16[2,4,128,128]{3,2,1,0:T(8,128)(2,1)S(1)}, bf16[2,4,128,128]{3,2,1,0:T(8,128)(2,1)}, u32[]{:S(2)}) copy-start(bf16[2,4,128,128]{3,2,1,0:T(8,128)(2,1)} %param.5) | copy-start | bytes 786436
  6.0 0.7 %copy-start.3 = (s32[2,6]{1,0:T(2,128)S(1)}, s32[2,6]{1,0:T(2,128)}, u32[]{:S(2)}) copy-start(s32[2,6]{1,0:T(2,128)} %wanted.1) | copy-start | bytes 148
  6.7 0.7 %copy-start.5 = (s32[2,4]{1,0:T(2,128)S(1)}, s32[2,4]{1,0:T(2,128)}, u32[]{:S(2)}) copy-start(s32[2,4]{1,0:T(2,128)} %refs_0_.2) | copy-start | bytes 100
  8.0 1.7 %copy-start.2 = (s32[2,8]{1,0:T(2,128)S(1)}, s32[2,8]{1,0:T(2,128)}, u32[]{:S(2)}) copy-start(s32[2,8]{1,0:T(2,128)} %refs_2_.9) | copy-start | bytes 196
  8.0 7.4 %collective-permute-start = (bf16[1056,128]{1,0:T(8,128)(2,1)S(1)}, bf16[1056,128]{1,0:T(8,128)(2,1)S(1)}, u32[]{:S(2)}, u32[]{:S(2)}) collective-permute-start(bf16[1056,128]{1,0:T(8,128)(2,1)S(1)} %shard_map.55.refs_8_), channel_id=1, source_target_pairs={{0,2},{1,3},{2,0},{3,1},{4,6},{5,7},{6,4},{7,5},{8,10},{9,11},{10,... | collective-permute-start | bytes 811016 | tf_op jit(solution)/shard_map/ppermute | solution.py:110
  9.5 5.8 %collective-permute-start.1 = (bf16[1056,128]{1,0:T(8,128)(2,1)S(1)}, bf16[1056,128]{1,0:T(8,128)(2,1)S(1)}, u32[]{:S(2)}, u32[]{:S(2)}) collective-permute-start(bf16[1056,128]{1,0:T(8,128)(2,1)S(1)} %shard_map.55.refs_8_), channel_id=1, source_target_pairs={{0,1},{1,0},{2,3},{3,2},{4,5},{5,4},{6,7},{7,6},{8,9},{9,8},{10,11... | collective-permute-start | bytes 811016 | tf_op jit(solution)/shard_map/ppermute | solution.py:110
  9.5 9.8 %collective-permute-start.7 = (bf16[1056,128]{1,0:T(8,128)(2,1)S(1)}, bf16[1056,128]{1,0:T(8,128)(2,1)S(1)}, u32[]{:S(2)}, u32[]{:S(2)}) collective-permute-start(bf16[1056,128]{1,0:T(8,128)(2,1)S(1)} %shard_map.55.refs_8_), channel_id=1, source_target_pairs={{0,4},{4,0},{8,12},{12,8},{1,5},{5,1},{9,13},{13,9},{2,6},{6,2},{1... | collective-permute-start | bytes 811016 | tf_op jit(solution)/shard_map/ppermute | solution.py:110
  15.3 16.1 %collective-permute-start.4 = (bf16[2064,128]{1,0:T(8,128)(2,1)S(1)}, bf16[2064,128]{1,0:T(8,128)(2,1)S(1)}, u32[]{:S(2)}, u32[]{:S(2)}) collective-permute-start(bf16[2064,128]{1,0:T(8,128)(2,1)S(1)} %shard_map.56), channel_id=1, source_target_pairs={{0,1},{1,9},{2,3},{3,11},{4,12},{5,4},{6,14},{7,6},{8,0},{9,8},{10... | collective-permute-start | bytes 1585160 | tf_op jit(solution)/shard_map/ppermute | solution.py:118
  15.3 12.1 %collective-permute-start.3 = (bf16[2064,128]{1,0:T(8,128)(2,1)S(1)}, bf16[2064,128]{1,0:T(8,128)(2,1)S(1)}, u32[]{:S(2)}, u32[]{:S(2)}) collective-permute-start(bf16[2064,128]{1,0:T(8,128)(2,1)S(1)} %shard_map.56), channel_id=1, source_target_pairs={{0,1},{1,5},{2,3},{3,7},{4,0},{5,4},{6,2},{7,6},{8,12},{9,8},{10,1... | collective-permute-start | bytes 1585160 | tf_op jit(solution)/shard_map/ppermute | solution.py:118
  15.3 6.1 %collective-permute-start.2 = (bf16[1056,128]{1,0:T(8,128)(2,1)S(1)}, bf16[1056,128]{1,0:T(8,128)(2,1)S(1)}, u32[]{:S(2)}, u32[]{:S(2)}) collective-permute-start(bf16[1056,128]{1,0:T(8,128)(2,1)S(1)} %collective-permute-done.refs_9_), channel_id=1, source_target_pairs={{0,1},{1,0},{2,3},{3,2},{4,5},{5,4},{6,7},{7,6},{8,9},{9,8},{10,11... | collective-permute-start | bytes 811016 | tf_op jit(solution)/shard_map/ppermute | solution.py:110
  19.3 7.8 %collective-permute-start.8 = (bf16[1056,128]{1,0:T(8,128)(2,1)S(1)}, bf16[1056,128]{1,0:T(8,128)(2,1)S(1)}, u32[]{:S(2)}, u32[]{:S(2)}) collective-permute-start(bf16[1056,128]{1,0:T(8,128)(2,1)S(1)} %collective-permute-done.7.refs_8_), channel_id=1, source_target_pairs={{0,2},{1,3},{2,0},{3,1},{4,6},{5,7},{6,4},{7,5},{8,10},{9,11},{10,... | collective-permute-start | bytes 811016 | tf_op jit(solution)/shard_map/ppermute | solution.py:110
  21.3 5.9 %collective-permute-start.9 = (bf16[1056,128]{1,0:T(8,128)(2,1)S(1)}, bf16[1056,128]{1,0:T(8,128)(2,1)S(1)}, u32[]{:S(2)}, u32[]{:S(2)}) collective-permute-start(bf16[1056,128]{1,0:T(8,128)(2,1)S(1)} %collective-permute-done.7.refs_8_), channel_id=1, source_target_pairs={{0,1},{1,0},{2,3},{3,2},{4,5},{5,4},{6,7},{7,6},{8,9},{9,8},{10,11... | collective-permute-start | bytes 811016 | tf_op jit(solution)/shard_map/ppermute | solution.py:110
  21.5 10.2 %collective-permute-start.5 = (s32[2,8]{1,0:T(2,128)S(1)}, s32[2,8]{1,0:T(2,128)S(1)}, u32[]{:S(2)}, u32[]{:S(2)}) collective-permute-start(s32[2,8]{1,0:T(2,128)S(1)} %copy-done.2), channel_id=1, source_target_pairs={{0,12},{4,8},{8,4},{12,0},{1,13},{5,9},{9,5},{13,1},{2,14},{6,10},... | collective-permute-start | bytes 200 | tf_op jit(solution)/shard_map/ppermute | solution.py:110
  27.1 4.4 %collective-permute-start.10 = (bf16[1056,128]{1,0:T(8,128)(2,1)S(1)}, bf16[1056,128]{1,0:T(8,128)(2,1)S(1)}, u32[]{:S(2)}, u32[]{:S(2)}) collective-permute-start(bf16[1056,128]{1,0:T(8,128)(2,1)S(1)} %collective-permute-done.8.refs_9_), channel_id=1, source_target_pairs={{0,1},{1,0},{2,3},{3,2},{4,5},{5,4},{6,7},{7,6},{8,9},{9,8},{10,11... | collective-permute-start | bytes 811016 | tf_op jit(solution)/shard_map/ppermute | solution.py:110
  33.1 8.4 %collective-permute-start.14 = (bf16[1,3,128,128]{3,2,1,0:T(8,128)(2,1)S(1)}, bf16[1,3,128,128]{3,2,1,0:T(8,128)(2,1)S(1)}, u32[]{:S(2)}, u32[]{:S(2)}) collective-permute-start(bf16[1,3,128,128]{3,2,1,0:T(8,128)(2,1)S(1)} %shard_map.61), channel_id=1, source_target_pairs={{0,4},{1,0},{2,6},{3,2},{4,5},{5,1},{6,7},{7,3},{8,9},{9,13},{10,1... | collective-permute-start | bytes 294920 | tf_op jit(solution)/shard_map/ppermute | solution.py:118
  34.5 6.9 %collective-permute-start.13 = (bf16[1,3,128,128]{3,2,1,0:T(8,128)(2,1)S(1)}, bf16[1,3,128,128]{3,2,1,0:T(8,128)(2,1)S(1)}, u32[]{:S(2)}, u32[]{:S(2)}) collective-permute-start(bf16[1,3,128,128]{3,2,1,0:T(8,128)(2,1)S(1)} %shard_map.60), channel_id=1, source_target_pairs={{0,4},{1,0},{2,6},{3,2},{4,5},{5,1},{6,7},{7,3},{8,9},{9,13},{10,1... | collective-permute-start | bytes 294920 | tf_op jit(solution)/shard_map/ppermute | solution.py:118
  36.0 5.5 %collective-permute-start.12 = (bf16[1,3,128,128]{3,2,1,0:T(8,128)(2,1)S(1)}, bf16[1,3,128,128]{3,2,1,0:T(8,128)(2,1)S(1)}, u32[]{:S(2)}, u32[]{:S(2)}) collective-permute-start(bf16[1,3,128,128]{3,2,1,0:T(8,128)(2,1)S(1)} %shard_map.59), channel_id=1, source_target_pairs={{0,4},{1,0},{2,6},{3,2},{4,5},{5,1},{6,7},{7,3},{8,9},{9,13},{10,1... | collective-permute-start | bytes 294920 | tf_op jit(solution)/shard_map/ppermute | solution.py:118
  37.4 4.0 %collective-permute-start.11 = (bf16[1,3,128,128]{3,2,1,0:T(8,128)(2,1)S(1)}, bf16[1,3,128,128]{3,2,1,0:T(8,128)(2,1)S(1)}, u32[]{:S(2)}, u32[]{:S(2)}) collective-permute-start(bf16[1,3,128,128]{3,2,1,0:T(8,128)(2,1)S(1)} %shard_map.58), channel_id=1, source_target_pairs={{0,4},{1,0},{2,6},{3,2},{4,5},{5,1},{6,7},{7,3},{8,9},{9,13},{10,1... | collective-permute-start | bytes 294920 | tf_op jit(solution)/shard_map/ppermute | solution.py:118
  38.2 0.7 %copy-start.4 = (s32[2,6]{1,0:T(2,128)S(1)}, s32[2,6]{1,0:T(2,128)}, u32[]{:S(2)}) copy-start(s32[2,6]{1,0:T(2,128)} %wanted.1) | copy-start | bytes 148

commit v20 on v17

--- a/solution.py
+++ b/solution.py
@@ -30,8 +30,9 @@
     out[size:, :] = found.astype(out.dtype)
 
 
-def product_kernel(starts, span, parts, place, left_index, wanted, *refs):
-    cols, refs = refs[:parts], refs[parts:]
+def product_kernel(starts, span, which, place, left_index, wanted, *refs):
+    parts, arrays = len(which), max(which) + 1
+    cols, refs = [refs[k] for k in which], refs[arrays:]
     tiles, refs = refs[:parts], refs[parts:]
     packs, (out, dense, right, slot) = refs[:-4], refs[-4:]
 
@@ -44,9 +45,10 @@
         inner_slots = tiles[0].shape[0] // block // inner_rows
         rows = right.shape[0]
         left_slots = (packs[0].shape[0] // block) // rows
+        spare = dense.shape[1] - 1
 
         def read(ref, start, i, k, width):
-            return ref[i, k] if start is None else ref[0, start + i * width + k]
+            return ref[i, k] if start is None else ref[start[0], start[1] + i * width + k]
 
         for i in span:
             dense[i] = jnp.zeros_like(dense[i])
@@ -54,10 +56,7 @@
                 for s in range(left_slots):
                     inner = left_index[p, i * left_slots + s]
                     begin = (i * left_slots + s) * block
-
-                    @pl.when(inner >= 0)
-                    def _():
-                        dense[i, inner] = pack[begin : begin + block, :]
+                    dense[i, jnp.where(inner >= 0, inner, spare)] = pack[begin : begin + block, :]
 
         for m in range(inner_rows):
             for c in range(COLS_DEV):
@@ -167,31 +166,34 @@
     own_packs = across(own_packs, far // 4)
     other_packs = across([other], far)
     order, every = list(range(1, end)) + [0, end], list(range(rows))
+    behind = index_of([shards[d] for d in range(1, end)], b_tiles)
     for d in range(1, end):
-        cols[d] = (0, index_of([shards[d]], b_tiles))
+        cols[d] = ((d - 1, 0), behind)
     place = jnp.stack([jnp.where(working, first, -1)] + [r ^ d for d in order]).astype(jnp.int32)
 
     def products(wanted, packs, spans):
         index = index_of(packs, a_tiles)
         starts = [wanted[0]] + [cols[d][0] for d in order]
+        arrays = [b_cols, cols[end][1]] + ([behind] if end > 1 else [])
+        which = [{0: 0, end: 1}.get(d, 2) for d in order]
         return [
             pl.pallas_call(
-                functools.partial(product_kernel, starts, span, len(order)),
+                functools.partial(product_kernel, starts, span, which),
                 out_shape=jax.ShapeDtypeStruct((len(span), slots, block, block), dtype),
-                in_specs=[SMEM] * (3 + len(order)) + [VMEM] * (len(order) + len(packs)),
+                in_specs=[SMEM] * (3 + len(arrays)) + [VMEM] * (len(order) + len(packs)),
                 out_specs=VMEM,
                 scratch_shapes=[
-                    pltpu.VMEM((rows, inner_rows * row_count, block, block), dtype),
+                    pltpu.VMEM((rows, inner_rows * row_count + 1, block, block), dtype),
                     pltpu.VMEM((rows, inner_rows * block, slots * block), dtype),
                     pltpu.SMEM((inner_rows, COLS_DEV), jnp.int32),
                 ],
                 compiler_params=PARAMS,
                 cost_estimate=FREE,
-            )(place, index, wanted[1], *[cols[d][1] for d in order], *[shards[d] for d in order], *packs)
+            )(place, index, wanted[1], *arrays, *[shards[d] for d in order], *packs)
             for span in spans
         ]
 
-    given = products((a_cols.size, index_of([other], a_tiles)), other_packs, [[i] for i in every])
+    given = products(((0, a_cols.size), index_of([other], a_tiles)), other_packs, [[i] for i in every])
     given = [give_back(x) for x in given]
     (kept,) = products((None, c_cols), own_packs, [every])
     return jnp.where(working, kept, jnp.concatenate(given, axis=0))

time: 39.7 us -> 39.7 us (level)
  waiting for transfers between devices: 16.9 us -> 17.4 us
  Pallas kernels: 7.03 us -> 6.55 us
    pallas_call x3, Pallas kernels: 5.85 us -> 5.38 us  [products(): pl.pallas_call(functools.partial(product_kernel, starts, span, which), ou...]
    ppermute x5, waiting for transfers between devices: 3.52 us -> 3.98 us  [permute(): return lax.ppermute(x, ('row', 'col'), pairs)]
    slice x8 -> x10, local copies, waits for them, and re-layouts: 0.89 us -> 1.11 us  [index_of(): x[tiles.size // block:, 0]]
  transfers between devices with their start and end apart: 13 -> 13, of which waited for: 5 -> 5; matrix products, arithmetic and copies ran while one was open for 3% -> 3% of each run, Pallas kernels for 18% -> 17%
where the time goes in v20:
time: 39.7 us; the launch traced here: 39.5 us
  waiting for transfers between devices  17.4 us (44%)
  starting transfers between devices  10.3 us (26%)
  Pallas kernels  6.55 us (16%)
  local copies, waits for them, and re-layouts  4.17 us (11%)
  other arithmetic  0.85 us (2%)
    ppermute x8, waiting for transfers between devices, swap(): return lax.ppermute(x, axis, [(k, k ^ d) for k in range(n)])  13.4 us
    pallas_call x3, Pallas kernels, products(): pl.pallas_call(functools.partial(product_kernel, starts, span, which), ou...  5.38 us
    ppermute x5, starting transfers between devices, permute(): return lax.ppermute(x, ('row', 'col'), pairs)  5.19 us
    ppermute x8, starting transfers between devices, swap(): return lax.ppermute(x, axis, [(k, k ^ d) for k in range(n)])  5.15 us
    ppermute x5, waiting for transfers between devices, permute(): return lax.ppermute(x, ('row', 'col'), pairs)  3.98 us
    unnamed x12, local copies, waits for them, and re-layouts  2.97 us
    pallas_call x2, Pallas kernels, pack(): pl.pallas_call(pack_kernel, out_shape=jax.ShapeDtypeStruct((size + -(-cou...  1.17 us
    slice x10, local copies, waits for them, and re-layouts, index_of(): x[tiles.size // block:, 0]  1.11 us
  transfers between devices with their start and end apart: 13, of which 5 were waited for; matrix products, arithmetic and copies ran while one was open for 3% of the time, Pallas kernels for 17%

profile of v20, /device:TPU:0, one launch (start us, length us, event | category | flops | bytes accessed | tf_op | source)
XLA Modules:
  0.0 39.5 jit_solution(15692291499124185072)
XLA Ops:
  0.0 5.0 %collective-permute-start.6 = (bf16[2048,128]{1,0:T(8,128)(2,1)}, bf16[2048,128]{1,0:T(8,128)(2,1)S(1)}, u32[]{:S(2)}, u32[]{:S(2)}) collective-permute-start(bf16[2048,128]{1,0:T(8,128)(2,1)} %bitcast.18), channel_id=1, source_target_pairs={{0,12},{1,3},{2,14},{3,1},{4,6},{5,9},{6,4},{7,11},{8,10},{9,5},{1... | collective-permute-start | bytes 1572872 | tf_op jit(solution)/shard_map/ppermute | solution.py:117
  5.1 0.9 %copy-done.1 = bf16[2,4,128,128]{3,2,1,0:T(8,128)(2,1)S(1)} copy-done((bf16[2,4,128,128]{3,2,1,0:T(8,128)(2,1)S(1)}, bf16[2,4,128,128]{3,2,1,0:T(8,128)(2,1)}, u32[]{:S(2)}) %copy-start.1) | copy-done | bytes 262168
  6.0 0.7 %copy-done.3 = s32[2,6]{1,0:T(2,128)S(1)} copy-done((s32[2,6]{1,0:T(2,128)S(1)}, s32[2,6]{1,0:T(2,128)}, u32[]{:S(2)}) %copy-start.3) | copy-done | bytes 72
  6.7 0.7 %copy-done.5 = s32[2,4]{1,0:T(2,128)S(1)} copy-done((s32[2,4]{1,0:T(2,128)S(1)}, s32[2,4]{1,0:T(2,128)}, u32[]{:S(2)}) %copy-start.5) | copy-done | bytes 56
  7.4 0.6 %shard_map.55.refs_7_ = bf16[1056,128]{1,0:T(8,128)(2,1)S(1)} custom-call(s32[2,4]{1,0:T(2,128)S(1)} %copy-done.5, s32[2,6]{1,0:T(2,128)S(1)} %copy-done.3, bf16[1024,128]{1,0:T(8,128)(2,1)S(1)} %bitcast.23), custom_call_target="tpu_custom_call" | custom-call | flops 1 | bytes 1 | tf_op jit(solution)/shard_map/pallas_call | solution.py:133
  8.0 1.6 %collective-permute-start = (bf16[1056,128]{1,0:T(8,128)(2,1)S(1)}, bf16[1056,128]{1,0:T(8,128)(2,1)S(1)}, u32[]{:S(2)}, u32[]{:S(2)}) collective-permute-start(bf16[1056,128]{1,0:T(8,128)(2,1)S(1)} %shard_map.55.refs_7_), channel_id=1, source_target_pairs={{0,2},{1,3},{2,0},{3,1},{4,6},{5,7},{6,4},{7,5},{8,10},{9,11},{10,... | collective-permute-start | bytes 811016 | tf_op jit(solution)/shard_map/ppermute | solution.py:109
  9.5 1.0 %collective-permute-start.3 = (s32[2,8]{1,0:T(2,128)S(1)}, s32[2,8]{1,0:T(2,128)S(1)}, u32[]{:S(2)}, u32[]{:S(2)}) collective-permute-start(s32[2,8]{1,0:T(2,128)S(1)} %copy-done.2), channel_id=1, source_target_pairs={{0,12},{4,8},{8,4},{12,0},{1,13},{5,9},{9,5},{13,1},{2,14},{6,10},... | collective-permute-start | bytes 200 | tf_op jit(solution)/shard_map/ppermute | solution.py:109
  10.5 0.1 slice_reduce_fusion.6
  10.6 0.6 %shard_map.56 = bf16[2064,128]{1,0:T(8,128)(2,1)S(1)} custom-call(s32[2,8]{1,0:T(2,128)S(1)} %copy-done.2, bf16[2048,128]{1,0:T(8,128)(2,1)S(1)} %bitcast.19), custom_call_target="tpu_custom_call" | custom-call | flops 1 | bytes 1 | tf_op jit(solution)/shard_map/pallas_call | solution.py:133
  11.2 0.1 stack.32.place
  11.3 4.0 %collective-permute-done.refs_8_ = bf16[1056,128]{1,0:T(8,128)(2,1)S(1)} collective-permute-done((bf16[1056,128]{1,0:T(8,128)(2,1)S(1)}, bf16[1056,128]{1,0:T(8,128)(2,1)S(1)}, u32[]{:S(2)}, u32[]{:S(2)}) %collective-permute-start) | collective-permute-done | bytes 270368 | tf_op jit(solution)/shard_map/ppermute | solution.py:109
  15.3 0.1 slice_reduce_fusion.4
  15.4 0.1 slice_reduce_fusion.5
  15.6 3.8 %collective-permute-done.7.refs_7_ = bf16[1056,128]{1,0:T(8,128)(2,1)S(1)} collective-permute-done((bf16[1056,128]{1,0:T(8,128)(2,1)S(1)}, bf16[1056,128]{1,0:T(8,128)(2,1)S(1)}, u32[]{:S(2)}, u32[]{:S(2)}) %collective-permute-start.7) | collective-permute-done | bytes 270368 | tf_op jit(solution)/shard_map/ppermute | solution.py:109
  19.3 2.0 %collective-permute-start.8 = (bf16[1056,128]{1,0:T(8,128)(2,1)S(1)}, bf16[1056,128]{1,0:T(8,128)(2,1)S(1)}, u32[]{:S(2)}, u32[]{:S(2)}) collective-permute-start(bf16[1056,128]{1,0:T(8,128)(2,1)S(1)} %collective-permute-done.7.refs_7_), channel_id=1, source_target_pairs={{0,2},{1,3},{2,0},{3,1},{4,6},{5,7},{6,4},{7,5},{8,10},{9,11},{10,... | collective-permute-start | bytes 811016 | tf_op jit(solution)/shard_map/ppermute | solution.py:109
  21.4 0.1 slice_reduce_fusion.7
  21.5 5.7 %collective-permute-done.8.refs_8_ = bf16[1056,128]{1,0:T(8,128)(2,1)S(1)} collective-permute-done((bf16[1056,128]{1,0:T(8,128)(2,1)S(1)}, bf16[1056,128]{1,0:T(8,128)(2,1)S(1)}, u32[]{:S(2)}, u32[]{:S(2)}) %collective-permute-start.8) | collective-permute-done | bytes 270368 | tf_op jit(solution)/shard_map/ppermute | solution.py:109
  27.1 0.1 slice_reduce_fusion.2
  27.3 0.6 %collective-permute-start.10 = (bf16[1056,128]{1,0:T(8,128)(2,1)S(1)}, bf16[1056,128]{1,0:T(8,128)(2,1)S(1)}, u32[]{:S(2)}, u32[]{:S(2)}) collective-permute-start(bf16[1056,128]{1,0:T(8,128)(2,1)S(1)} %collective-permute-done.8.refs_8_), channel_id=1, source_target_pairs={{0,1},{1,0},{2,3},{3,2},{4,5},{5,4},{6,7},{7,6},{8,9},{9,8},{10,11... | collective-permute-start | bytes 811016 | tf_op jit(solution)/shard_map/ppermute | solution.py:109
  27.8 0.1 slice_reduce_fusion.1
  28.0 3.4 %collective-permute-done.5.refs_4_ = bf16[2064,128]{1,0:T(8,128)(2,1)S(1)} collective-permute-done((bf16[2064,128]{1,0:T(8,128)(2,1)S(1)}, bf16[2064,128]{1,0:T(8,128)(2,1)S(1)}, u32[]{:S(2)}, u32[]{:S(2)}) %collective-permute-start.5) | collective-permute-done | bytes 528416 | tf_op jit(solution)/shard_map/ppermute | solution.py:117
  31.4 0.1 slice_reduce_fusion.8
  31.5 0.1 slice_reduce_fusion.9
  31.7 0.1 slice_reduce_fusion
  31.8 1.5 %shard_map.59 = bf16[1,6,128,128]{3,2,1,0:T(8,128)(2,1)S(1)} custom-call(s32[5]{0:T(128)S(1)} %stack.32.place, s32[4,32]{1,0:T(4,128)S(1)} %maximum_convert_fusion.1.left_index, s32[1,32]{1,0:T(1,128)S(1)} %bitcast_convert_fusion.wanted, s32[2,8]{1,0:T(2,128)S(1)} %copy-done.2, s32[2,8]{1,0:T(2,128)S(1)} %collective-permute-done.3.refs_1_, ...), custom_call_target="tpu_custom_call" | custom-call | flops 1 | bytes 1 | tf_op jit(solution)/shard_map/pallas_call | solution.py:180
  33.3 0.1 collective-permute-start.12
  33.4 1.5 %shard_map.58 = bf16[1,6,128,128]{3,2,1,0:T(8,128)(2,1)S(1)} custom-call(s32[5]{0:T(128)S(1)} %stack.32.place, s32[4,32]{1,0:T(4,128)S(1)} %maximum_convert_fusion.1.left_index, s32[1,32]{1,0:T(1,128)S(1)} %bitcast_convert_fusion.wanted, s32[2,8]{1,0:T(2,128)S(1)} %copy-done.2, s32[2,8]{1,0:T(2,128)S(1)} %collective-permute-done.3.refs_1_, ...), custom_call_target="tpu_custom_call" | custom-call | flops 1 | bytes 1 | tf_op jit(solution)/shard_map/pallas_call | solution.py:180
  35.0 0.1 slice_reduce_fusion.3
  35.2 0.7 %copy-done.4 = s32[2,6]{1,0:T(2,128)S(1)} copy-done((s32[2,6]{1,0:T(2,128)S(1)}, s32[2,6]{1,0:T(2,128)}, u32[]{:S(2)}) %copy-start.4) | copy-done | bytes 72
  35.8 2.3 %shard_map.57 = bf16[2,6,128,128]{3,2,1,0:T(8,128)(2,1)S(1)} custom-call(s32[5]{0:T(128)S(1)} %stack.32.place, s32[4,32]{1,0:T(4,128)S(1)} %maximum_convert_fusion.left_index, s32[2,6]{1,0:T(2,128)S(1)} %copy-done.4, s32[2,8]{1,0:T(2,128)S(1)} %copy-done.2, s32[2,8]{1,0:T(2,128)S(1)} %collective-permute-done.3.refs_1_, ...), custom_call_target="tpu_custom_call" | custom-call | flops 1 | bytes 1 | tf_op jit(solution)/shard_map/pallas_call | solution.py:180
  38.2 0.5 %collective-permute-done.11 = bf16[1,6,128,128]{3,2,1,0:T(8,128)(2,1)S(1)} collective-permute-done((bf16[1,6,128,128]{3,2,1,0:T(8,128)(2,1)S(1)}, bf16[1,6,128,128]{3,2,1,0:T(8,128)(2,1)S(1)}, u32[]{:S(2)}, u32[]{:S(2)}) %collective-permute-start.11) | collective-permute-done | bytes 196640 | tf_op jit(solution)/shard_map/ppermute | solution.py:117
  38.7 0.8 %maximum_select_fusion = bf16[2,6,128,128]{3,2,1,0:T(8,128)(2,1)} fusion(bf16[2,6,128,128]{3,2,1,0:T(8,128)(2,1)S(1)} %shard_map.57, bf16[1,6,128,128]{3,2,1,0:T(8,128)(2,1)S(1)} %collective-permute-done.12, bf16[1,6,128,128]{3,2,1,0:T(8,128)(2,1)S(1)} %collective-permute-done.11, pred[]{:T(512)S(6)} %eq.5), kind=kLoop, calls=%fused_computation | loop fusion | flops 393216 | bytes 1179649 | tf_op jit(solution)/shard_map/jit(_where)/select_n | solution.py:199
  (27 shorter events, 0.2 us)
Async XLA Ops:
  0.0 10.6 %copy-start = (bf16[2,8,128,128]{3,2,1,0:T(8,128)(2,1)S(1)}, bf16[2,8,128,128]{3,2,1,0:T(8,128)(2,1)}, u32[]{:S(2)}) copy-start(bf16[2,8,128,128]{3,2,1,0:T(8,128)(2,1)} %param.7) | copy-start | bytes 1572868
  0.0 19.3 %collective-permute-start.6 = (bf16[2048,128]{1,0:T(8,128)(2,1)}, bf16[2048,128]{1,0:T(8,128)(2,1)S(1)}, u32[]{:S(2)}, u32[]{:S(2)}) collective-permute-start(bf16[2048,128]{1,0:T(8,128)(2,1)} %bitcast.18), channel_id=1, source_target_pairs={{0,12},{1,3},{2,14},{3,1},{4,6},{5,9},{6,4},{7,11},{8,10},{9,5},{1... | collective-permute-start | bytes 1572872 | tf_op jit(solution)/shard_map/ppermute | solution.py:117
  5.1 0.9 %copy-start.1 = (bf16[2,4,128,128]{3,2,1,0:T(8,128)(2,1)S(1)}, bf16[2,4,128,128]{3,2,1,0:T(8,128)(2,1)}, u32[]{:S(2)}) copy-start(bf16[2,4,128,128]{3,2,1,0:T(8,128)(2,1)} %param.5) | copy-start | bytes 786436
  6.0 0.7 %copy-start.3 = (s32[2,6]{1,0:T(2,128)S(1)}, s32[2,6]{1,0:T(2,128)}, u32[]{:S(2)}) copy-start(s32[2,6]{1,0:T(2,128)} %wanted.1) | copy-start | bytes 148
  6.7 0.7 %copy-start.5 = (s32[2,4]{1,0:T(2,128)S(1)}, s32[2,4]{1,0:T(2,128)}, u32[]{:S(2)}) copy-start(s32[2,4]{1,0:T(2,128)} %refs_0_.5) | copy-start | bytes 100
  7.4 2.2 %copy-start.2 = (s32[2,8]{1,0:T(2,128)S(1)}, s32[2,8]{1,0:T(2,128)}, u32[]{:S(2)}) copy-start(s32[2,8]{1,0:T(2,128)} %refs_0_.9) | copy-start | bytes 196
  8.0 7.4 %collective-permute-start = (bf16[1056,128]{1,0:T(8,128)(2,1)S(1)}, bf16[1056,128]{1,0:T(8,128)(2,1)S(1)}, u32[]{:S(2)}, u32[]{:S(2)}) collective-permute-start(bf16[1056,128]{1,0:T(8,128)(2,1)S(1)} %shard_map.55.refs_7_), channel_id=1, source_target_pairs={{0,2},{1,3},{2,0},{3,1},{4,6},{5,7},{6,4},{7,5},{8,10},{9,11},{10,... | collective-permute-start | bytes 811016 | tf_op jit(solution)/shard_map/ppermute | solution.py:109
  9.5 5.8 %collective-permute-start.1 = (bf16[1056,128]{1,0:T(8,128)(2,1)S(1)}, bf16[1056,128]{1,0:T(8,128)(2,1)S(1)}, u32[]{:S(2)}, u32[]{:S(2)}) collective-permute-start(bf16[1056,128]{1,0:T(8,128)(2,1)S(1)} %shard_map.55.refs_7_), channel_id=1, source_target_pairs={{0,1},{1,0},{2,3},{3,2},{4,5},{5,4},{6,7},{7,6},{8,9},{9,8},{10,11... | collective-permute-start | bytes 811016 | tf_op jit(solution)/shard_map/ppermute | solution.py:109
  9.5 9.8 %collective-permute-start.7 = (bf16[1056,128]{1,0:T(8,128)(2,1)S(1)}, bf16[1056,128]{1,0:T(8,128)(2,1)S(1)}, u32[]{:S(2)}, u32[]{:S(2)}) collective-permute-start(bf16[1056,128]{1,0:T(8,128)(2,1)S(1)} %shard_map.55.refs_7_), channel_id=1, source_target_pairs={{0,4},{4,0},{8,12},{12,8},{1,5},{5,1},{9,13},{13,9},{2,6},{6,2},{1... | collective-permute-start | bytes 811016 | tf_op jit(solution)/shard_map/ppermute | solution.py:109
  9.5 22.3 %collective-permute-start.3 = (s32[2,8]{1,0:T(2,128)S(1)}, s32[2,8]{1,0:T(2,128)S(1)}, u32[]{:S(2)}, u32[]{:S(2)}) collective-permute-start(s32[2,8]{1,0:T(2,128)S(1)} %copy-done.2), channel_id=1, source_target_pairs={{0,12},{4,8},{8,4},{12,0},{1,13},{5,9},{9,5},{13,1},{2,14},{6,10},... | collective-permute-start | bytes 200 | tf_op jit(solution)/shard_map/ppermute | solution.py:109
  15.3 16.1 %collective-permute-start.5 = (bf16[2064,128]{1,0:T(8,128)(2,1)S(1)}, bf16[2064,128]{1,0:T(8,128)(2,1)S(1)}, u32[]{:S(2)}, u32[]{:S(2)}) collective-permute-start(bf16[2064,128]{1,0:T(8,128)(2,1)S(1)} %shard_map.56), channel_id=1, source_target_pairs={{0,1},{1,9},{2,3},{3,11},{4,12},{5,4},{6,14},{7,6},{8,0},{9,8},{10... | collective-permute-start | bytes 1585160 | tf_op jit(solution)/shard_map/ppermute | solution.py:117
  15.3 16.2 %collective-permute-start.4 = (bf16[2064,128]{1,0:T(8,128)(2,1)S(1)}, bf16[2064,128]{1,0:T(8,128)(2,1)S(1)}, u32[]{:S(2)}, u32[]{:S(2)}) collective-permute-start(bf16[2064,128]{1,0:T(8,128)(2,1)S(1)} %shard_map.56), channel_id=1, source_target_pairs={{0,1},{1,5},{2,3},{3,7},{4,0},{5,4},{6,2},{7,6},{8,12},{9,8},{10,1... | collective-permute-start | bytes 1585160 | tf_op jit(solution)/shard_map/ppermute | solution.py:117
  19.3 7.8 %collective-permute-start.8 = (bf16[1056,128]{1,0:T(8,128)(2,1)S(1)}, bf16[1056,128]{1,0:T(8,128)(2,1)S(1)}, u32[]{:S(2)}, u32[]{:S(2)}) collective-permute-start(bf16[1056,128]{1,0:T(8,128)(2,1)S(1)} %collective-permute-done.7.refs_7_), channel_id=1, source_target_pairs={{0,2},{1,3},{2,0},{3,1},{4,6},{5,7},{6,4},{7,5},{8,10},{9,11},{10,... | collective-permute-start | bytes 811016 | tf_op jit(solution)/shard_map/ppermute | solution.py:109
  21.4 5.9 %collective-permute-start.9 = (bf16[1056,128]{1,0:T(8,128)(2,1)S(1)}, bf16[1056,128]{1,0:T(8,128)(2,1)S(1)}, u32[]{:S(2)}, u32[]{:S(2)}) collective-permute-start(bf16[1056,128]{1,0:T(8,128)(2,1)S(1)} %collective-permute-done.7.refs_7_), channel_id=1, source_target_pairs={{0,1},{1,0},{2,3},{3,2},{4,5},{5,4},{6,7},{7,6},{8,9},{9,8},{10,11... | collective-permute-start | bytes 811016 | tf_op jit(solution)/shard_map/ppermute | solution.py:109
  27.1 7.9 %collective-permute-start.2 = (bf16[1056,128]{1,0:T(8,128)(2,1)S(1)}, bf16[1056,128]{1,0:T(8,128)(2,1)S(1)}, u32[]{:S(2)}, u32[]{:S(2)}) collective-permute-start(bf16[1056,128]{1,0:T(8,128)(2,1)S(1)} %collective-permute-done.refs_8_), channel_id=1, source_target_pairs={{0,1},{1,0},{2,3},{3,2},{4,5},{5,4},{6,7},{7,6},{8,9},{9,8},{10,11... | collective-permute-start | bytes 811016 | tf_op jit(solution)/shard_map/ppermute | solution.py:109
  27.3 4.4 %collective-permute-start.10 = (bf16[1056,128]{1,0:T(8,128)(2,1)S(1)}, bf16[1056,128]{1,0:T(8,128)(2,1)S(1)}, u32[]{:S(2)}, u32[]{:S(2)}) collective-permute-start(bf16[1056,128]{1,0:T(8,128)(2,1)S(1)} %collective-permute-done.8.refs_8_), channel_id=1, source_target_pairs={{0,1},{1,0},{2,3},{3,2},{4,5},{5,4},{6,7},{7,6},{8,9},{9,8},{10,11... | collective-permute-start | bytes 811016 | tf_op jit(solution)/shard_map/ppermute | solution.py:109
  33.3 4.8 %collective-permute-start.12 = (bf16[1,6,128,128]{3,2,1,0:T(8,128)(2,1)S(1)}, bf16[1,6,128,128]{3,2,1,0:T(8,128)(2,1)S(1)}, u32[]{:S(2)}, u32[]{:S(2)}) collective-permute-start(bf16[1,6,128,128]{3,2,1,0:T(8,128)(2,1)S(1)} %shard_map.59), channel_id=1, source_target_pairs={{0,4},{1,0},{2,6},{3,2},{4,5},{5,1},{6,7},{7,3},{8,9},{9,13},{10,1... | collective-permute-start | bytes 589832 | tf_op jit(solution)/shard_map/ppermute | solution.py:117
  35.0 3.7 %collective-permute-start.11 = (bf16[1,6,128,128]{3,2,1,0:T(8,128)(2,1)S(1)}, bf16[1,6,128,128]{3,2,1,0:T(8,128)(2,1)S(1)}, u32[]{:S(2)}, u32[]{:S(2)}) collective-permute-start(bf16[1,6,128,128]{3,2,1,0:T(8,128)(2,1)S(1)} %shard_map.58), channel_id=1, source_target_pairs={{0,4},{1,0},{2,6},{3,2},{4,5},{5,1},{6,7},{7,3},{8,9},{9,13},{10,1... | collective-permute-start | bytes 589832 | tf_op jit(solution)/shard_map/ppermute | solution.py:117
  35.2 0.7 %copy-start.4 = (s32[2,6]{1,0:T(2,128)S(1)}, s32[2,6]{1,0:T(2,128)}, u32[]{:S(2)}) copy-start(s32[2,6]{1,0:T(2,128)} %wanted.1) | copy-start | bytes 148

commit v21 on v20

--- a/solution.py
+++ b/solution.py
@@ -30,7 +30,7 @@
     out[size:, :] = found.astype(out.dtype)
 
 
-def product_kernel(starts, span, which, place, left_index, wanted, *refs):
+def product_kernel(starts, span, which, place, left_index, *refs):
     parts, arrays = len(which), max(which) + 1
     cols, refs = [refs[k] for k in which], refs[arrays:]
     tiles, refs = refs[:parts], refs[parts:]
@@ -68,7 +68,7 @@
                     slot[m, read(cols[p], starts[1 + p], m, l, inner_slots) - first] = l
             for i in span:
                 for j in range(slots):
-                    column = read(wanted, starts[0], i, j, slots)
+                    column = read(left_index, starts[0], i, j, slots)
                     for m in range(inner_rows):
                         l = slot[m, column - first]
                         hit = read(cols[p], starts[1 + p], m, l, inner_slots) == column
@@ -171,16 +171,16 @@
         cols[d] = ((d - 1, 0), behind)
     place = jnp.stack([jnp.where(working, first, -1)] + [r ^ d for d in order]).astype(jnp.int32)
 
-    def products(wanted, packs, spans):
+    def products(packs, spans):
         index = index_of(packs, a_tiles)
-        starts = [wanted[0]] + [cols[d][0] for d in order]
+        starts = [(0, a_cols.size)] + [cols[d][0] for d in order]
         arrays = [b_cols, cols[end][1]] + ([behind] if end > 1 else [])
         which = [{0: 0, end: 1}.get(d, 2) for d in order]
         return [
             pl.pallas_call(
                 functools.partial(product_kernel, starts, span, which),
                 out_shape=jax.ShapeDtypeStruct((len(span), slots, block, block), dtype),
-                in_specs=[SMEM] * (3 + len(arrays)) + [VMEM] * (len(order) + len(packs)),
+                in_specs=[SMEM] * (2 + len(arrays)) + [VMEM] * (len(order) + len(packs)),
                 out_specs=VMEM,
                 scratch_shapes=[
                     pltpu.VMEM((rows, inner_rows * row_count + 1, block, block), dtype),
@@ -189,13 +189,13 @@
                 ],
                 compiler_params=PARAMS,
                 cost_estimate=FREE,
-            )(place, index, wanted[1], *arrays, *[shards[d] for d in order], *packs)
+            )(place, index, *arrays, *[shards[d] for d in order], *packs)
             for span in spans
         ]
 
-    given = products(((0, a_cols.size), index_of([other], a_tiles)), other_packs, [[i] for i in every])
+    given = products(other_packs, [[i] for i in every])
     given = [give_back(x) for x in given]
-    (kept,) = products((None, c_cols), own_packs, [every])
+    (kept,) = products(own_packs, [every])
     return jnp.where(working, kept, jnp.concatenate(given, axis=0))
 
 

time: 39.7 us -> 39.7 us (level)
  local copies, waits for them, and re-layouts: 4.17 us -> 3.51 us
  waiting for transfers between devices: 17.4 us -> 18 us
    ppermute x5, waiting for transfers between devices: 3.98 us -> 4.69 us  [permute(): return lax.ppermute(x, ('row', 'col'), pairs)]
    unnamed x12 -> x10, local copies, waits for them, and re-layouts: 2.97 us -> 2.31 us
where the time goes in v21:
time: 39.7 us; the launch traced here: 39.5 us
  waiting for transfers between devices  18 us (45%)
  starting transfers between devices  10.4 us (26%)
  Pallas kernels  6.53 us (16%)
  local copies, waits for them, and re-layouts  3.51 us (9%)
  other arithmetic  0.84 us (2%)
    ppermute x8, waiting for transfers between devices, swap(): return lax.ppermute(x, axis, [(k, k ^ d) for k in range(n)])  13.3 us
    pallas_call x3, Pallas kernels, products(): pl.pallas_call(functools.partial(product_kernel, starts, span, which), ou...  5.36 us
    ppermute x8, starting transfers between devices, swap(): return lax.ppermute(x, axis, [(k, k ^ d) for k in range(n)])  5.22 us
    ppermute x5, starting transfers between devices, permute(): return lax.ppermute(x, ('row', 'col'), pairs)  5.19 us
    ppermute x5, waiting for transfers between devices, permute(): return lax.ppermute(x, ('row', 'col'), pairs)  4.69 us
    unnamed x10, local copies, waits for them, and re-layouts  2.31 us
    pallas_call x2, Pallas kernels, pack(): pl.pallas_call(pack_kernel, out_shape=jax.ShapeDtypeStruct((size + -(-cou...  1.17 us
    slice x10, local copies, waits for them, and re-layouts, index_of(): x[tiles.size // block:, 0]  1.11 us
  transfers between devices with their start and end apart: 13, of which 5 were waited for; matrix products, arithmetic and copies ran while one was open for 3% of the time, Pallas kernels for 17%

profile of v21, /device:TPU:0, one launch (start us, length us, event | category | flops | bytes accessed | tf_op | source)
XLA Modules:
  0.0 39.5 jit_solution(5329319382607103146)
XLA Ops:
  0.0 5.0 %collective-permute-start.6 = (bf16[2048,128]{1,0:T(8,128)(2,1)}, bf16[2048,128]{1,0:T(8,128)(2,1)S(1)}, u32[]{:S(2)}, u32[]{:S(2)}) collective-permute-start(bf16[2048,128]{1,0:T(8,128)(2,1)} %bitcast.17), channel_id=1, source_target_pairs={{0,12},{1,3},{2,14},{3,1},{4,6},{5,9},{6,4},{7,11},{8,10},{9,5},{1... | collective-permute-start | bytes 1572872 | tf_op jit(solution)/shard_map/ppermute | solution.py:117
  5.1 0.9 %copy-done.1 = bf16[2,4,128,128]{3,2,1,0:T(8,128)(2,1)S(1)} copy-done((bf16[2,4,128,128]{3,2,1,0:T(8,128)(2,1)S(1)}, bf16[2,4,128,128]{3,2,1,0:T(8,128)(2,1)}, u32[]{:S(2)}) %copy-start.1) | copy-done | bytes 262168
  6.0 0.7 %copy-done.3 = s32[2,4]{1,0:T(2,128)S(1)} copy-done((s32[2,4]{1,0:T(2,128)S(1)}, s32[2,4]{1,0:T(2,128)}, u32[]{:S(2)}) %copy-start.3) | copy-done | bytes 56
  6.7 0.7 %copy-done.4 = s32[2,6]{1,0:T(2,128)S(1)} copy-done((s32[2,6]{1,0:T(2,128)S(1)}, s32[2,6]{1,0:T(2,128)}, u32[]{:S(2)}) %copy-start.4) | copy-done | bytes 72
  7.4 0.6 %shard_map.55.refs_7_ = bf16[1056,128]{1,0:T(8,128)(2,1)S(1)} custom-call(s32[2,4]{1,0:T(2,128)S(1)} %copy-done.3, s32[2,6]{1,0:T(2,128)S(1)} %copy-done.4, bf16[1024,128]{1,0:T(8,128)(2,1)S(1)} %bitcast.22), custom_call_target="tpu_custom_call" | custom-call | flops 1 | bytes 1 | tf_op jit(solution)/shard_map/pallas_call | solution.py:133
  8.0 1.6 %collective-permute-start = (bf16[1056,128]{1,0:T(8,128)(2,1)S(1)}, bf16[1056,128]{1,0:T(8,128)(2,1)S(1)}, u32[]{:S(2)}, u32[]{:S(2)}) collective-permute-start(bf16[1056,128]{1,0:T(8,128)(2,1)S(1)} %shard_map.55.refs_7_), channel_id=1, source_target_pairs={{0,2},{1,3},{2,0},{3,1},{4,6},{5,7},{6,4},{7,5},{8,10},{9,11},{10,... | collective-permute-start | bytes 811016 | tf_op jit(solution)/shard_map/ppermute | solution.py:109
  9.5 1.0 %collective-permute-start.3 = (s32[2,8]{1,0:T(2,128)S(1)}, s32[2,8]{1,0:T(2,128)S(1)}, u32[]{:S(2)}, u32[]{:S(2)}) collective-permute-start(s32[2,8]{1,0:T(2,128)S(1)} %copy-done.2), channel_id=1, source_target_pairs={{0,12},{4,8},{8,4},{12,0},{1,13},{5,9},{9,5},{13,1},{2,14},{6,10},... | collective-permute-start | bytes 200 | tf_op jit(solution)/shard_map/ppermute | solution.py:109
  10.5 0.6 %shard_map.56 = bf16[2064,128]{1,0:T(8,128)(2,1)S(1)} custom-call(s32[2,8]{1,0:T(2,128)S(1)} %copy-done.2, bf16[2048,128]{1,0:T(8,128)(2,1)S(1)} %bitcast.18), custom_call_target="tpu_custom_call" | custom-call | flops 1 | bytes 1 | tf_op jit(solution)/shard_map/pallas_call | solution.py:133
  11.1 0.1 stack.32.place
  11.2 0.1 slice_reduce_fusion.6
  11.3 4.0 %collective-permute-done.refs_8_ = bf16[1056,128]{1,0:T(8,128)(2,1)S(1)} collective-permute-done((bf16[1056,128]{1,0:T(8,128)(2,1)S(1)}, bf16[1056,128]{1,0:T(8,128)(2,1)S(1)}, u32[]{:S(2)}, u32[]{:S(2)}) %collective-permute-start) | collective-permute-done | bytes 270368 | tf_op jit(solution)/shard_map/ppermute | solution.py:109
  15.3 4.0 %collective-permute-done.7.refs_7_ = bf16[1056,128]{1,0:T(8,128)(2,1)S(1)} collective-permute-done((bf16[1056,128]{1,0:T(8,128)(2,1)S(1)}, bf16[1056,128]{1,0:T(8,128)(2,1)S(1)}, u32[]{:S(2)}, u32[]{:S(2)}) %collective-permute-start.7) | collective-permute-done | bytes 270368 | tf_op jit(solution)/shard_map/ppermute | solution.py:109
  19.3 2.0 %collective-permute-start.8 = (bf16[1056,128]{1,0:T(8,128)(2,1)S(1)}, bf16[1056,128]{1,0:T(8,128)(2,1)S(1)}, u32[]{:S(2)}, u32[]{:S(2)}) collective-permute-start(bf16[1056,128]{1,0:T(8,128)(2,1)S(1)} %collective-permute-done.7.refs_7_), channel_id=1, source_target_pairs={{0,2},{1,3},{2,0},{3,1},{4,6},{5,7},{6,4},{7,5},{8,10},{9,11},{10,... | collective-permute-start | bytes 811016 | tf_op jit(solution)/shard_map/ppermute | solution.py:109
  21.4 0.1 slice_reduce_fusion.4
  21.5 0.1 collective-permute-start.9
  21.6 0.1 slice_reduce_fusion.5
  21.7 0.1 slice_reduce_fusion.7
  21.8 5.3 %collective-permute-done.8.refs_8_ = bf16[1056,128]{1,0:T(8,128)(2,1)S(1)} collective-permute-done((bf16[1056,128]{1,0:T(8,128)(2,1)S(1)}, bf16[1056,128]{1,0:T(8,128)(2,1)S(1)}, u32[]{:S(2)}, u32[]{:S(2)}) %collective-permute-start.8) | collective-permute-done | bytes 270368 | tf_op jit(solution)/shard_map/ppermute | solution.py:109
  27.1 0.1 slice_reduce_fusion.2
  27.2 0.6 %collective-permute-start.10 = (bf16[1056,128]{1,0:T(8,128)(2,1)S(1)}, bf16[1056,128]{1,0:T(8,128)(2,1)S(1)}, u32[]{:S(2)}, u32[]{:S(2)}) collective-permute-start(bf16[1056,128]{1,0:T(8,128)(2,1)S(1)} %collective-permute-done.8.refs_8_), channel_id=1, source_target_pairs={{0,1},{1,0},{2,3},{3,2},{4,5},{5,4},{6,7},{7,6},{8,9},{9,8},{10,11... | collective-permute-start | bytes 811016 | tf_op jit(solution)/shard_map/ppermute | solution.py:109
  27.8 0.1 slice_reduce_fusion.1
  27.9 3.5 %collective-permute-done.5.refs_4_ = bf16[2064,128]{1,0:T(8,128)(2,1)S(1)} collective-permute-done((bf16[2064,128]{1,0:T(8,128)(2,1)S(1)}, bf16[2064,128]{1,0:T(8,128)(2,1)S(1)}, u32[]{:S(2)}, u32[]{:S(2)}) %collective-permute-start.5) | collective-permute-done | bytes 528416 | tf_op jit(solution)/shard_map/ppermute | solution.py:117
  31.4 0.1 slice_reduce_fusion.8
  31.5 0.1 slice_reduce_fusion.9
  31.7 0.1 slice_reduce_fusion
  31.8 1.5 %shard_map.59 = bf16[1,6,128,128]{3,2,1,0:T(8,128)(2,1)S(1)} custom-call(s32[5]{0:T(128)S(1)} %stack.32.place, s32[4,32]{1,0:T(4,128)S(1)} %maximum_convert_fusion.1.left_index, s32[2,8]{1,0:T(2,128)S(1)} %copy-done.2, s32[2,8]{1,0:T(2,128)S(1)} %collective-permute-done.3.refs_1_, s32[2,16]{1,0:T(2,128)S(1)} %maximum_convert_fusion.2.refs_2_, ...), custom_call_target="tpu_custom_call" | custom-call | flops 1 | bytes 1 | tf_op jit(solution)/shard_map/pallas_call | solution.py:180
  33.3 0.1 collective-permute-start.12
  33.4 1.5 %shard_map.58 = bf16[1,6,128,128]{3,2,1,0:T(8,128)(2,1)S(1)} custom-call(s32[5]{0:T(128)S(1)} %stack.32.place, s32[4,32]{1,0:T(4,128)S(1)} %maximum_convert_fusion.1.left_index, s32[2,8]{1,0:T(2,128)S(1)} %copy-done.2, s32[2,8]{1,0:T(2,128)S(1)} %collective-permute-done.3.refs_1_, s32[2,16]{1,0:T(2,128)S(1)} %maximum_convert_fusion.2.refs_2_, ...), custom_call_target="tpu_custom_call" | custom-call | flops 1 | bytes 1 | tf_op jit(solution)/shard_map/pallas_call | solution.py:180
  35.0 0.1 slice_reduce_fusion.3
  35.2 2.3 %shard_map.57 = bf16[2,6,128,128]{3,2,1,0:T(8,128)(2,1)S(1)} custom-call(s32[5]{0:T(128)S(1)} %stack.32.place, s32[4,32]{1,0:T(4,128)S(1)} %maximum_convert_fusion.left_index, s32[2,8]{1,0:T(2,128)S(1)} %copy-done.2, s32[2,8]{1,0:T(2,128)S(1)} %collective-permute-done.3.refs_1_, s32[2,16]{1,0:T(2,128)S(1)} %maximum_convert_fusion.2.refs_2_, ...), custom_call_target="tpu_custom_call" | custom-call | flops 1 | bytes 1 | tf_op jit(solution)/shard_map/pallas_call | solution.py:180
  37.5 1.2 %collective-permute-done.11 = bf16[1,6,128,128]{3,2,1,0:T(8,128)(2,1)S(1)} collective-permute-done((bf16[1,6,128,128]{3,2,1,0:T(8,128)(2,1)S(1)}, bf16[1,6,128,128]{3,2,1,0:T(8,128)(2,1)S(1)}, u32[]{:S(2)}, u32[]{:S(2)}) %collective-permute-start.11) | collective-permute-done | bytes 196640 | tf_op jit(solution)/shard_map/ppermute | solution.py:117
  38.7 0.8 %maximum_select_fusion = bf16[2,6,128,128]{3,2,1,0:T(8,128)(2,1)} fusion(bf16[2,6,128,128]{3,2,1,0:T(8,128)(2,1)S(1)} %shard_map.57, bf16[1,6,128,128]{3,2,1,0:T(8,128)(2,1)S(1)} %collective-permute-done.12, bf16[1,6,128,128]{3,2,1,0:T(8,128)(2,1)S(1)} %collective-permute-done.11, pred[]{:T(512)S(6)} %eq.5), kind=kLoop, calls=%fused_computation | loop fusion | flops 393216 | bytes 1179649 | tf_op jit(solution)/shard_map/jit(_where)/select_n | solution.py:199
  (24 shorter events, 0.2 us)
Async XLA Ops:
  0.0 10.5 %copy-start = (bf16[2,8,128,128]{3,2,1,0:T(8,128)(2,1)S(1)}, bf16[2,8,128,128]{3,2,1,0:T(8,128)(2,1)}, u32[]{:S(2)}) copy-start(bf16[2,8,128,128]{3,2,1,0:T(8,128)(2,1)} %param.7) | copy-start | bytes 1572868
  0.0 19.3 %collective-permute-start.6 = (bf16[2048,128]{1,0:T(8,128)(2,1)}, bf16[2048,128]{1,0:T(8,128)(2,1)S(1)}, u32[]{:S(2)}, u32[]{:S(2)}) collective-permute-start(bf16[2048,128]{1,0:T(8,128)(2,1)} %bitcast.17), channel_id=1, source_target_pairs={{0,12},{1,3},{2,14},{3,1},{4,6},{5,9},{6,4},{7,11},{8,10},{9,5},{1... | collective-permute-start | bytes 1572872 | tf_op jit(solution)/shard_map/ppermute | solution.py:117
  5.1 0.9 %copy-start.1 = (bf16[2,4,128,128]{3,2,1,0:T(8,128)(2,1)S(1)}, bf16[2,4,128,128]{3,2,1,0:T(8,128)(2,1)}, u32[]{:S(2)}) copy-start(bf16[2,4,128,128]{3,2,1,0:T(8,128)(2,1)} %param.5) | copy-start | bytes 786436
  6.0 0.7 %copy-start.3 = (s32[2,4]{1,0:T(2,128)S(1)}, s32[2,4]{1,0:T(2,128)}, u32[]{:S(2)}) copy-start(s32[2,4]{1,0:T(2,128)} %refs_0_.5) | copy-start | bytes 100
  6.7 0.7 %copy-start.4 = (s32[2,6]{1,0:T(2,128)S(1)}, s32[2,6]{1,0:T(2,128)}, u32[]{:S(2)}) copy-start(s32[2,6]{1,0:T(2,128)} %refs_1_.1) | copy-start | bytes 148
  7.4 2.2 %copy-start.2 = (s32[2,8]{1,0:T(2,128)S(1)}, s32[2,8]{1,0:T(2,128)}, u32[]{:S(2)}) copy-start(s32[2,8]{1,0:T(2,128)} %refs_0_.9) | copy-start | bytes 196
  8.0 7.4 %collective-permute-start = (bf16[1056,128]{1,0:T(8,128)(2,1)S(1)}, bf16[1056,128]{1,0:T(8,128)(2,1)S(1)}, u32[]{:S(2)}, u32[]{:S(2)}) collective-permute-start(bf16[1056,128]{1,0:T(8,128)(2,1)S(1)} %shard_map.55.refs_7_), channel_id=1, source_target_pairs={{0,2},{1,3},{2,0},{3,1},{4,6},{5,7},{6,4},{7,5},{8,10},{9,11},{10,... | collective-permute-start | bytes 811016 | tf_op jit(solution)/shard_map/ppermute | solution.py:109
  9.5 5.8 %collective-permute-start.1 = (bf16[1056,128]{1,0:T(8,128)(2,1)S(1)}, bf16[1056,128]{1,0:T(8,128)(2,1)S(1)}, u32[]{:S(2)}, u32[]{:S(2)}) collective-permute-start(bf16[1056,128]{1,0:T(8,128)(2,1)S(1)} %shard_map.55.refs_7_), channel_id=1, source_target_pairs={{0,1},{1,0},{2,3},{3,2},{4,5},{5,4},{6,7},{7,6},{8,9},{9,8},{10,11... | collective-permute-start | bytes 811016 | tf_op jit(solution)/shard_map/ppermute | solution.py:109
  9.5 9.8 %collective-permute-start.7 = (bf16[1056,128]{1,0:T(8,128)(2,1)S(1)}, bf16[1056,128]{1,0:T(8,128)(2,1)S(1)}, u32[]{:S(2)}, u32[]{:S(2)}) collective-permute-start(bf16[1056,128]{1,0:T(8,128)(2,1)S(1)} %shard_map.55.refs_7_), channel_id=1, source_target_pairs={{0,4},{4,0},{8,12},{12,8},{1,5},{5,1},{9,13},{13,9},{2,6},{6,2},{1... | collective-permute-start | bytes 811016 | tf_op jit(solution)/shard_map/ppermute | solution.py:109
  9.5 22.3 %collective-permute-start.3 = (s32[2,8]{1,0:T(2,128)S(1)}, s32[2,8]{1,0:T(2,128)S(1)}, u32[]{:S(2)}, u32[]{:S(2)}) collective-permute-start(s32[2,8]{1,0:T(2,128)S(1)} %copy-done.2), channel_id=1, source_target_pairs={{0,12},{4,8},{8,4},{12,0},{1,13},{5,9},{9,5},{13,1},{2,14},{6,10},... | collective-permute-start | bytes 200 | tf_op jit(solution)/shard_map/ppermute | solution.py:109
  15.3 16.1 %collective-permute-start.5 = (bf16[2064,128]{1,0:T(8,128)(2,1)S(1)}, bf16[2064,128]{1,0:T(8,128)(2,1)S(1)}, u32[]{:S(2)}, u32[]{:S(2)}) collective-permute-start(bf16[2064,128]{1,0:T(8,128)(2,1)S(1)} %shard_map.56), channel_id=1, source_target_pairs={{0,1},{1,9},{2,3},{3,11},{4,12},{5,4},{6,14},{7,6},{8,0},{9,8},{10... | collective-permute-start | bytes 1585160 | tf_op jit(solution)/shard_map/ppermute | solution.py:117
  15.3 16.2 %collective-permute-start.4 = (bf16[2064,128]{1,0:T(8,128)(2,1)S(1)}, bf16[2064,128]{1,0:T(8,128)(2,1)S(1)}, u32[]{:S(2)}, u32[]{:S(2)}) collective-permute-start(bf16[2064,128]{1,0:T(8,128)(2,1)S(1)} %shard_map.56), channel_id=1, source_target_pairs={{0,1},{1,5},{2,3},{3,7},{4,0},{5,4},{6,2},{7,6},{8,12},{9,8},{10,1... | collective-permute-start | bytes 1585160 | tf_op jit(solution)/shard_map/ppermute | solution.py:117
  19.3 7.8 %collective-permute-start.8 = (bf16[1056,128]{1,0:T(8,128)(2,1)S(1)}, bf16[1056,128]{1,0:T(8,128)(2,1)S(1)}, u32[]{:S(2)}, u32[]{:S(2)}) collective-permute-start(bf16[1056,128]{1,0:T(8,128)(2,1)S(1)} %collective-permute-done.7.refs_7_), channel_id=1, source_target_pairs={{0,2},{1,3},{2,0},{3,1},{4,6},{5,7},{6,4},{7,5},{8,10},{9,11},{10,... | collective-permute-start | bytes 811016 | tf_op jit(solution)/shard_map/ppermute | solution.py:109
  21.5 5.8 %collective-permute-start.9 = (bf16[1056,128]{1,0:T(8,128)(2,1)S(1)}, bf16[1056,128]{1,0:T(8,128)(2,1)S(1)}, u32[]{:S(2)}, u32[]{:S(2)}) collective-permute-start(bf16[1056,128]{1,0:T(8,128)(2,1)S(1)} %collective-permute-done.7.refs_7_), channel_id=1, source_target_pairs={{0,1},{1,0},{2,3},{3,2},{4,5},{5,4},{6,7},{7,6},{8,9},{9,8},{10,11... | collective-permute-start | bytes 811016 | tf_op jit(solution)/shard_map/ppermute | solution.py:109
  27.1 7.9 %collective-permute-start.2 = (bf16[1056,128]{1,0:T(8,128)(2,1)S(1)}, bf16[1056,128]{1,0:T(8,128)(2,1)S(1)}, u32[]{:S(2)}, u32[]{:S(2)}) collective-permute-start(bf16[1056,128]{1,0:T(8,128)(2,1)S(1)} %collective-permute-done.refs_8_), channel_id=1, source_target_pairs={{0,1},{1,0},{2,3},{3,2},{4,5},{5,4},{6,7},{7,6},{8,9},{9,8},{10,11... | collective-permute-start | bytes 811016 | tf_op jit(solution)/shard_map/ppermute | solution.py:109
  27.2 4.4 %collective-permute-start.10 = (bf16[1056,128]{1,0:T(8,128)(2,1)S(1)}, bf16[1056,128]{1,0:T(8,128)(2,1)S(1)}, u32[]{:S(2)}, u32[]{:S(2)}) collective-permute-start(bf16[1056,128]{1,0:T(8,128)(2,1)S(1)} %collective-permute-done.8.refs_8_), channel_id=1, source_target_pairs={{0,1},{1,0},{2,3},{3,2},{4,5},{5,4},{6,7},{7,6},{8,9},{9,8},{10,11... | collective-permute-start | bytes 811016 | tf_op jit(solution)/shard_map/ppermute | solution.py:109
  33.3 4.1 %collective-permute-start.12 = (bf16[1,6,128,128]{3,2,1,0:T(8,128)(2,1)S(1)}, bf16[1,6,128,128]{3,2,1,0:T(8,128)(2,1)S(1)}, u32[]{:S(2)}, u32[]{:S(2)}) collective-permute-start(bf16[1,6,128,128]{3,2,1,0:T(8,128)(2,1)S(1)} %shard_map.59), channel_id=1, source_target_pairs={{0,4},{1,0},{2,6},{3,2},{4,5},{5,1},{6,7},{7,3},{8,9},{9,13},{10,1... | collective-permute-start | bytes 589832 | tf_op jit(solution)/shard_map/ppermute | solution.py:117
  34.9 3.8 %collective-permute-start.11 = (bf16[1,6,128,128]{3,2,1,0:T(8,128)(2,1)S(1)}, bf16[1,6,128,128]{3,2,1,0:T(8,128)(2,1)S(1)}, u32[]{:S(2)}, u32[]{:S(2)}) collective-permute-start(bf16[1,6,128,128]{3,2,1,0:T(8,128)(2,1)S(1)} %shard_map.58), channel_id=1, source_target_pairs={{0,4},{1,0},{2,6},{3,2},{4,5},{5,1},{6,7},{7,3},{8,9},{9,13},{10,1... | collective-permute-start | bytes 589832 | tf_op jit(solution)/shard_map/ppermute | solution.py:117

commit v22 on v21

--- a/solution.py
+++ b/solution.py
@@ -88,6 +88,24 @@
                 out[at, j] = sums[i][:, j * block : (j + 1) * block].astype(out.dtype)
 
 
+def choose_kernel(place, kept, *refs):
+    given, out, sems = refs[:-2], refs[-2], refs[-1]
+
+    @pl.when(place[0] >= 0)
+    def _():
+        copy = pltpu.make_async_copy(kept, out, sems.at[0])
+        copy.start()
+        copy.wait()
+
+    @pl.when(place[0] < 0)
+    def _():
+        copies = [pltpu.make_async_copy(x, out.at[i : i + 1], sems.at[i]) for i, x in enumerate(given)]
+        for copy in copies:
+            copy.start()
+        for copy in copies:
+            copy.wait()
+
+
 def parity(k):
     return bin(k).count("1") % 2
 
@@ -196,7 +214,15 @@
     given = products(other_packs, [[i] for i in every])
     given = [give_back(x) for x in given]
     (kept,) = products(own_packs, [every])
-    return jnp.where(working, kept, jnp.concatenate(given, axis=0))
+    return pl.pallas_call(
+        choose_kernel,
+        out_shape=jax.ShapeDtypeStruct((rows, slots, block, block), dtype),
+        in_specs=[SMEM] + [VMEM] * (1 + rows),
+        out_specs=pl.BlockSpec(memory_space=pl.ANY),
+        scratch_shapes=[pltpu.SemaphoreType.DMA((rows,))],
+        compiler_params=PARAMS,
+        cost_estimate=FREE,
+    )(place, kept, *given)
 
 
 def solution(mesh):

time: 39.7 us -> 40.2 us (1.013)
  Pallas kernels: 6.53 us -> 7.83 us
  other arithmetic: 0.84 us -> 0.04 us
    pallas_call x0 -> x1, Pallas kernels: none -> 1.31 us  [body(): pl.pallas_call(choose_kernel, out_shape=jax.ShapeDtypeStruct((rows, slots...]
    select_n x1 -> x0, other arithmetic: 0.8 us -> none  [body(): return jnp.where(working, kept, jnp.concatenate(given, axis=0))]
  transfers between devices with their start and end apart: 13 -> 13, of which waited for: 5 -> 5; matrix products, arithmetic and copies ran while one was open for 3% -> 3% of each run, Pallas kernels for 17% -> 16%
where the time goes in v22:
time: 40.2 us; the launch traced here: 40 us
  waiting for transfers between devices  18 us (45%)
  starting transfers between devices  10.4 us (26%)
  Pallas kernels  7.83 us (19%)
  local copies, waits for them, and re-layouts  3.51 us (9%)
    ppermute x8, waiting for transfers between devices, swap(): return lax.ppermute(x, axis, [(k, k ^ d) for k in range(n)])  13.3 us
    pallas_call x3, Pallas kernels, products(): pl.pallas_call(functools.partial(product_kernel, starts, span, which), ou...  5.36 us
    ppermute x8, starting transfers between devices, swap(): return lax.ppermute(x, axis, [(k, k ^ d) for k in range(n)])  5.22 us
    ppermute x5, starting transfers between devices, permute(): return lax.ppermute(x, ('row', 'col'), pairs)  5.19 us
    ppermute x5, waiting for transfers between devices, permute(): return lax.ppermute(x, ('row', 'col'), pairs)  4.69 us
    unnamed x10, local copies, waits for them, and re-layouts  2.31 us
    pallas_call x1, Pallas kernels, body(): pl.pallas_call(choose_kernel, out_shape=jax.ShapeDtypeStruct((rows, slots...  1.31 us
    pallas_call x2, Pallas kernels, pack(): pl.pallas_call(pack_kernel, out_shape=jax.ShapeDtypeStruct((size + -(-cou...  1.17 us
  transfers between devices with their start and end apart: 13, of which 5 were waited for; matrix products, arithmetic and copies ran while one was open for 3% of the time, Pallas kernels for 16%

profile of v22, /device:TPU:0, one launch (start us, length us, event | category | flops | bytes accessed | tf_op | source)
XLA Modules:
  0.0 40.0 jit_solution(4319209145790180647)
XLA Ops:
  0.0 5.0 %collective-permute-start.6 = (bf16[2048,128]{1,0:T(8,128)(2,1)}, bf16[2048,128]{1,0:T(8,128)(2,1)S(1)}, u32[]{:S(2)}, u32[]{:S(2)}) collective-permute-start(bf16[2048,128]{1,0:T(8,128)(2,1)} %bitcast.17), channel_id=1, source_target_pairs={{0,12},{1,3},{2,14},{3,1},{4,6},{5,9},{6,4},{7,11},{8,10},{9,5},{1... | collective-permute-start | bytes 1572872 | tf_op jit(solution)/shard_map/ppermute | solution.py:135
  5.1 0.9 %copy-done.1 = bf16[2,4,128,128]{3,2,1,0:T(8,128)(2,1)S(1)} copy-done((bf16[2,4,128,128]{3,2,1,0:T(8,128)(2,1)S(1)}, bf16[2,4,128,128]{3,2,1,0:T(8,128)(2,1)}, u32[]{:S(2)}) %copy-start.1) | copy-done | bytes 262168
  6.0 0.7 %copy-done.3 = s32[2,4]{1,0:T(2,128)S(1)} copy-done((s32[2,4]{1,0:T(2,128)S(1)}, s32[2,4]{1,0:T(2,128)}, u32[]{:S(2)}) %copy-start.3) | copy-done | bytes 56
  6.7 0.7 %copy-done.4 = s32[2,6]{1,0:T(2,128)S(1)} copy-done((s32[2,6]{1,0:T(2,128)S(1)}, s32[2,6]{1,0:T(2,128)}, u32[]{:S(2)}) %copy-start.4) | copy-done | bytes 72
  7.4 0.6 %shard_map.55.refs_7_ = bf16[1056,128]{1,0:T(8,128)(2,1)S(1)} custom-call(s32[2,4]{1,0:T(2,128)S(1)} %copy-done.3, s32[2,6]{1,0:T(2,128)S(1)} %copy-done.4, bf16[1024,128]{1,0:T(8,128)(2,1)S(1)} %bitcast.22), custom_call_target="tpu_custom_call" | custom-call | flops 1 | bytes 1 | tf_op jit(solution)/shard_map/pallas_call | solution.py:151
  8.0 1.6 %collective-permute-start = (bf16[1056,128]{1,0:T(8,128)(2,1)S(1)}, bf16[1056,128]{1,0:T(8,128)(2,1)S(1)}, u32[]{:S(2)}, u32[]{:S(2)}) collective-permute-start(bf16[1056,128]{1,0:T(8,128)(2,1)S(1)} %shard_map.55.refs_7_), channel_id=1, source_target_pairs={{0,2},{1,3},{2,0},{3,1},{4,6},{5,7},{6,4},{7,5},{8,10},{9,11},{10,... | collective-permute-start | bytes 811016 | tf_op jit(solution)/shard_map/ppermute | solution.py:127
  9.5 1.0 %collective-permute-start.3 = (s32[2,8]{1,0:T(2,128)S(1)}, s32[2,8]{1,0:T(2,128)S(1)}, u32[]{:S(2)}, u32[]{:S(2)}) collective-permute-start(s32[2,8]{1,0:T(2,128)S(1)} %copy-done.2), channel_id=1, source_target_pairs={{0,12},{4,8},{8,4},{12,0},{1,13},{5,9},{9,5},{13,1},{2,14},{6,10},... | collective-permute-start | bytes 200 | tf_op jit(solution)/shard_map/ppermute | solution.py:127
  10.5 0.6 %shard_map.56 = bf16[2064,128]{1,0:T(8,128)(2,1)S(1)} custom-call(s32[2,8]{1,0:T(2,128)S(1)} %copy-done.2, bf16[2048,128]{1,0:T(8,128)(2,1)S(1)} %bitcast.18), custom_call_target="tpu_custom_call" | custom-call | flops 1 | bytes 1 | tf_op jit(solution)/shard_map/pallas_call | solution.py:151
  11.1 0.1 stack.32.place
  11.2 0.1 slice_reduce_fusion.6
  11.3 4.0 %collective-permute-done.refs_8_ = bf16[1056,128]{1,0:T(8,128)(2,1)S(1)} collective-permute-done((bf16[1056,128]{1,0:T(8,128)(2,1)S(1)}, bf16[1056,128]{1,0:T(8,128)(2,1)S(1)}, u32[]{:S(2)}, u32[]{:S(2)}) %collective-permute-start) | collective-permute-done | bytes 270368 | tf_op jit(solution)/shard_map/ppermute | solution.py:127
  15.3 4.0 %collective-permute-done.7.refs_7_ = bf16[1056,128]{1,0:T(8,128)(2,1)S(1)} collective-permute-done((bf16[1056,128]{1,0:T(8,128)(2,1)S(1)}, bf16[1056,128]{1,0:T(8,128)(2,1)S(1)}, u32[]{:S(2)}, u32[]{:S(2)}) %collective-permute-start.7) | collective-permute-done | bytes 270368 | tf_op jit(solution)/shard_map/ppermute | solution.py:127
  19.3 2.0 %collective-permute-start.8 = (bf16[1056,128]{1,0:T(8,128)(2,1)S(1)}, bf16[1056,128]{1,0:T(8,128)(2,1)S(1)}, u32[]{:S(2)}, u32[]{:S(2)}) collective-permute-start(bf16[1056,128]{1,0:T(8,128)(2,1)S(1)} %collective-permute-done.7.refs_7_), channel_id=1, source_target_pairs={{0,2},{1,3},{2,0},{3,1},{4,6},{5,7},{6,4},{7,5},{8,10},{9,11},{10,... | collective-permute-start | bytes 811016 | tf_op jit(solution)/shard_map/ppermute | solution.py:127
  21.4 0.1 slice_reduce_fusion.4
  21.5 0.1 collective-permute-start.9
  21.6 0.1 slice_reduce_fusion.5
  21.7 0.1 slice_reduce_fusion.7
  21.8 5.3 %collective-permute-done.8.refs_8_ = bf16[1056,128]{1,0:T(8,128)(2,1)S(1)} collective-permute-done((bf16[1056,128]{1,0:T(8,128)(2,1)S(1)}, bf16[1056,128]{1,0:T(8,128)(2,1)S(1)}, u32[]{:S(2)}, u32[]{:S(2)}) %collective-permute-start.8) | collective-permute-done | bytes 270368 | tf_op jit(solution)/shard_map/ppermute | solution.py:127
  27.1 0.1 slice_reduce_fusion.2
  27.2 0.6 %collective-permute-start.10 = (bf16[1056,128]{1,0:T(8,128)(2,1)S(1)}, bf16[1056,128]{1,0:T(8,128)(2,1)S(1)}, u32[]{:S(2)}, u32[]{:S(2)}) collective-permute-start(bf16[1056,128]{1,0:T(8,128)(2,1)S(1)} %collective-permute-done.8.refs_8_), channel_id=1, source_target_pairs={{0,1},{1,0},{2,3},{3,2},{4,5},{5,4},{6,7},{7,6},{8,9},{9,8},{10,11... | collective-permute-start | bytes 811016 | tf_op jit(solution)/shard_map/ppermute | solution.py:127
  27.8 0.1 slice_reduce_fusion.1
  27.9 3.5 %collective-permute-done.5.refs_4_ = bf16[2064,128]{1,0:T(8,128)(2,1)S(1)} collective-permute-done((bf16[2064,128]{1,0:T(8,128)(2,1)S(1)}, bf16[2064,128]{1,0:T(8,128)(2,1)S(1)}, u32[]{:S(2)}, u32[]{:S(2)}) %collective-permute-start.5) | collective-permute-done | bytes 528416 | tf_op jit(solution)/shard_map/ppermute | solution.py:135
  31.4 0.1 slice_reduce_fusion.8
  31.5 0.1 slice_reduce_fusion.9
  31.7 0.1 slice_reduce_fusion
  31.8 1.5 %shard_map.58 = bf16[1,6,128,128]{3,2,1,0:T(8,128)(2,1)S(1)} custom-call(s32[5]{0:T(128)S(1)} %stack.32.place, s32[4,32]{1,0:T(4,128)S(1)} %maximum_convert_fusion.1.left_index, s32[2,8]{1,0:T(2,128)S(1)} %copy-done.2, s32[2,8]{1,0:T(2,128)S(1)} %collective-permute-done.3.refs_1_, s32[2,16]{1,0:T(2,128)S(1)} %maximum_convert_fusion.2.refs_2_, ...), custom_call_target="tpu_custom_call" | custom-call | flops 1 | bytes 1 | tf_op jit(solution)/shard_map/pallas_call | solution.py:198
  33.3 0.1 collective-permute-start.11
  33.4 1.5 %shard_map.59 = bf16[1,6,128,128]{3,2,1,0:T(8,128)(2,1)S(1)} custom-call(s32[5]{0:T(128)S(1)} %stack.32.place, s32[4,32]{1,0:T(4,128)S(1)} %maximum_convert_fusion.1.left_index, s32[2,8]{1,0:T(2,128)S(1)} %copy-done.2, s32[2,8]{1,0:T(2,128)S(1)} %collective-permute-done.3.refs_1_, s32[2,16]{1,0:T(2,128)S(1)} %maximum_convert_fusion.2.refs_2_, ...), custom_call_target="tpu_custom_call" | custom-call | flops 1 | bytes 1 | tf_op jit(solution)/shard_map/pallas_call | solution.py:198
  35.0 0.1 slice_reduce_fusion.3
  35.2 2.3 %shard_map.57.kept = bf16[2,6,128,128]{3,2,1,0:T(8,128)(2,1)S(1)} custom-call(s32[5]{0:T(128)S(1)} %stack.32.place, s32[4,32]{1,0:T(4,128)S(1)} %maximum_convert_fusion.left_index, s32[2,8]{1,0:T(2,128)S(1)} %copy-done.2, s32[2,8]{1,0:T(2,128)S(1)} %collective-permute-done.3.refs_1_, s32[2,16]{1,0:T(2,128)S(1)} %maximum_convert_fusion.2.refs_2_, ...), custom_call_target="tpu_custom_call" | custom-call | flops 1 | bytes 1 | tf_op jit(solution)/shard_map/pallas_call | solution.py:198
  37.5 1.2 %collective-permute-done.12.refs_1_ = bf16[1,6,128,128]{3,2,1,0:T(8,128)(2,1)S(1)} collective-permute-done((bf16[1,6,128,128]{3,2,1,0:T(8,128)(2,1)S(1)}, bf16[1,6,128,128]{3,2,1,0:T(8,128)(2,1)S(1)}, u32[]{:S(2)}, u32[]{:S(2)}) %collective-permute-start.12) | collective-permute-done | bytes 196640 | tf_op jit(solution)/shard_map/ppermute | solution.py:135
  38.7 1.3 %shard_map.60 = bf16[2,6,128,128]{3,2,1,0:T(8,128)(2,1)} custom-call(s32[5]{0:T(128)S(1)} %stack.32.place, bf16[2,6,128,128]{3,2,1,0:T(8,128)(2,1)S(1)} %shard_map.57.kept, bf16[1,6,128,128]{3,2,1,0:T(8,128)(2,1)S(1)} %collective-permute-done.11.refs_0_, bf16[1,6,128,128]{3,2,1,0:T(8,128)(2,1)S(1)} %collective-permute-done.12.refs_1_), custom_call_target="tpu_custom_call" | custom-call | flops 1 | bytes 1 | tf_op jit(solution)/shard_map/pallas_call | solution.py:217
  (24 shorter events, 0.2 us)
Async XLA Ops:
  0.0 10.5 %copy-start = (bf16[2,8,128,128]{3,2,1,0:T(8,128)(2,1)S(1)}, bf16[2,8,128,128]{3,2,1,0:T(8,128)(2,1)}, u32[]{:S(2)}) copy-start(bf16[2,8,128,128]{3,2,1,0:T(8,128)(2,1)} %param.7) | copy-start | bytes 1572868
  0.0 19.3 %collective-permute-start.6 = (bf16[2048,128]{1,0:T(8,128)(2,1)}, bf16[2048,128]{1,0:T(8,128)(2,1)S(1)}, u32[]{:S(2)}, u32[]{:S(2)}) collective-permute-start(bf16[2048,128]{1,0:T(8,128)(2,1)} %bitcast.17), channel_id=1, source_target_pairs={{0,12},{1,3},{2,14},{3,1},{4,6},{5,9},{6,4},{7,11},{8,10},{9,5},{1... | collective-permute-start | bytes 1572872 | tf_op jit(solution)/shard_map/ppermute | solution.py:135
  5.1 0.9 %copy-start.1 = (bf16[2,4,128,128]{3,2,1,0:T(8,128)(2,1)S(1)}, bf16[2,4,128,128]{3,2,1,0:T(8,128)(2,1)}, u32[]{:S(2)}) copy-start(bf16[2,4,128,128]{3,2,1,0:T(8,128)(2,1)} %param.5) | copy-start | bytes 786436
  6.0 0.7 %copy-start.3 = (s32[2,4]{1,0:T(2,128)S(1)}, s32[2,4]{1,0:T(2,128)}, u32[]{:S(2)}) copy-start(s32[2,4]{1,0:T(2,128)} %refs_0_.5) | copy-start | bytes 100
  6.7 0.7 %copy-start.4 = (s32[2,6]{1,0:T(2,128)S(1)}, s32[2,6]{1,0:T(2,128)}, u32[]{:S(2)}) copy-start(s32[2,6]{1,0:T(2,128)} %refs_1_.1) | copy-start | bytes 148
  7.4 2.2 %copy-start.2 = (s32[2,8]{1,0:T(2,128)S(1)}, s32[2,8]{1,0:T(2,128)}, u32[]{:S(2)}) copy-start(s32[2,8]{1,0:T(2,128)} %refs_0_.9) | copy-start | bytes 196
  8.0 7.4 %collective-permute-start = (bf16[1056,128]{1,0:T(8,128)(2,1)S(1)}, bf16[1056,128]{1,0:T(8,128)(2,1)S(1)}, u32[]{:S(2)}, u32[]{:S(2)}) collective-permute-start(bf16[1056,128]{1,0:T(8,128)(2,1)S(1)} %shard_map.55.refs_7_), channel_id=1, source_target_pairs={{0,2},{1,3},{2,0},{3,1},{4,6},{5,7},{6,4},{7,5},{8,10},{9,11},{10,... | collective-permute-start | bytes 811016 | tf_op jit(solution)/shard_map/ppermute | solution.py:127
  9.5 5.8 %collective-permute-start.1 = (bf16[1056,128]{1,0:T(8,128)(2,1)S(1)}, bf16[1056,128]{1,0:T(8,128)(2,1)S(1)}, u32[]{:S(2)}, u32[]{:S(2)}) collective-permute-start(bf16[1056,128]{1,0:T(8,128)(2,1)S(1)} %shard_map.55.refs_7_), channel_id=1, source_target_pairs={{0,1},{1,0},{2,3},{3,2},{4,5},{5,4},{6,7},{7,6},{8,9},{9,8},{10,11... | collective-permute-start | bytes 811016 | tf_op jit(solution)/shard_map/ppermute | solution.py:127
  9.5 9.8 %collective-permute-start.7 = (bf16[1056,128]{1,0:T(8,128)(2,1)S(1)}, bf16[1056,128]{1,0:T(8,128)(2,1)S(1)}, u32[]{:S(2)}, u32[]{:S(2)}) collective-permute-start(bf16[1056,128]{1,0:T(8,128)(2,1)S(1)} %shard_map.55.refs_7_), channel_id=1, source_target_pairs={{0,4},{4,0},{8,12},{12,8},{1,5},{5,1},{9,13},{13,9},{2,6},{6,2},{1... | collective-permute-start | bytes 811016 | tf_op jit(solution)/shard_map/ppermute | solution.py:127
  9.5 22.3 %collective-permute-start.3 = (s32[2,8]{1,0:T(2,128)S(1)}, s32[2,8]{1,0:T(2,128)S(1)}, u32[]{:S(2)}, u32[]{:S(2)}) collective-permute-start(s32[2,8]{1,0:T(2,128)S(1)} %copy-done.2), channel_id=1, source_target_pairs={{0,12},{4,8},{8,4},{12,0},{1,13},{5,9},{9,5},{13,1},{2,14},{6,10},... | collective-permute-start | bytes 200 | tf_op jit(solution)/shard_map/ppermute | solution.py:127
  15.3 16.1 %collective-permute-start.5 = (bf16[2064,128]{1,0:T(8,128)(2,1)S(1)}, bf16[2064,128]{1,0:T(8,128)(2,1)S(1)}, u32[]{:S(2)}, u32[]{:S(2)}) collective-permute-start(bf16[2064,128]{1,0:T(8,128)(2,1)S(1)} %shard_map.56), channel_id=1, source_target_pairs={{0,1},{1,9},{2,3},{3,11},{4,12},{5,4},{6,14},{7,6},{8,0},{9,8},{10... | collective-permute-start | bytes 1585160 | tf_op jit(solution)/shard_map/ppermute | solution.py:135
  15.3 16.2 %collective-permute-start.4 = (bf16[2064,128]{1,0:T(8,128)(2,1)S(1)}, bf16[2064,128]{1,0:T(8,128)(2,1)S(1)}, u32[]{:S(2)}, u32[]{:S(2)}) collective-permute-start(bf16[2064,128]{1,0:T(8,128)(2,1)S(1)} %shard_map.56), channel_id=1, source_target_pairs={{0,1},{1,5},{2,3},{3,7},{4,0},{5,4},{6,2},{7,6},{8,12},{9,8},{10,1... | collective-permute-start | bytes 1585160 | tf_op jit(solution)/shard_map/ppermute | solution.py:135
  19.3 7.8 %collective-permute-start.8 = (bf16[1056,128]{1,0:T(8,128)(2,1)S(1)}, bf16[1056,128]{1,0:T(8,128)(2,1)S(1)}, u32[]{:S(2)}, u32[]{:S(2)}) collective-permute-start(bf16[1056,128]{1,0:T(8,128)(2,1)S(1)} %collective-permute-done.7.refs_7_), channel_id=1, source_target_pairs={{0,2},{1,3},{2,0},{3,1},{4,6},{5,7},{6,4},{7,5},{8,10},{9,11},{10,... | collective-permute-start | bytes 811016 | tf_op jit(solution)/shard_map/ppermute | solution.py:127
  21.5 5.8 %collective-permute-start.9 = (bf16[1056,128]{1,0:T(8,128)(2,1)S(1)}, bf16[1056,128]{1,0:T(8,128)(2,1)S(1)}, u32[]{:S(2)}, u32[]{:S(2)}) collective-permute-start(bf16[1056,128]{1,0:T(8,128)(2,1)S(1)} %collective-permute-done.7.refs_7_), channel_id=1, source_target_pairs={{0,1},{1,0},{2,3},{3,2},{4,5},{5,4},{6,7},{7,6},{8,9},{9,8},{10,11... | collective-permute-start | bytes 811016 | tf_op jit(solution)/shard_map/ppermute | solution.py:127
  27.1 7.9 %collective-permute-start.2 = (bf16[1056,128]{1,0:T(8,128)(2,1)S(1)}, bf16[1056,128]{1,0:T(8,128)(2,1)S(1)}, u32[]{:S(2)}, u32[]{:S(2)}) collective-permute-start(bf16[1056,128]{1,0:T(8,128)(2,1)S(1)} %collective-permute-done.refs_8_), channel_id=1, source_target_pairs={{0,1},{1,0},{2,3},{3,2},{4,5},{5,4},{6,7},{7,6},{8,9},{9,8},{10,11... | collective-permute-start | bytes 811016 | tf_op jit(solution)/shard_map/ppermute | solution.py:127
  27.2 4.4 %collective-permute-start.10 = (bf16[1056,128]{1,0:T(8,128)(2,1)S(1)}, bf16[1056,128]{1,0:T(8,128)(2,1)S(1)}, u32[]{:S(2)}, u32[]{:S(2)}) collective-permute-start(bf16[1056,128]{1,0:T(8,128)(2,1)S(1)} %collective-permute-done.8.refs_8_), channel_id=1, source_target_pairs={{0,1},{1,0},{2,3},{3,2},{4,5},{5,4},{6,7},{7,6},{8,9},{9,8},{10,11... | collective-permute-start | bytes 811016 | tf_op jit(solution)/shard_map/ppermute | solution.py:127
  33.3 4.1 %collective-permute-start.11 = (bf16[1,6,128,128]{3,2,1,0:T(8,128)(2,1)S(1)}, bf16[1,6,128,128]{3,2,1,0:T(8,128)(2,1)S(1)}, u32[]{:S(2)}, u32[]{:S(2)}) collective-permute-start(bf16[1,6,128,128]{3,2,1,0:T(8,128)(2,1)S(1)} %shard_map.58), channel_id=1, source_target_pairs={{0,4},{1,0},{2,6},{3,2},{4,5},{5,1},{6,7},{7,3},{8,9},{9,13},{10,1... | collective-permute-start | bytes 589832 | tf_op jit(solution)/shard_map/ppermute | solution.py:135
  34.9 3.8 %collective-permute-start.12 = (bf16[1,6,128,128]{3,2,1,0:T(8,128)(2,1)S(1)}, bf16[1,6,128,128]{3,2,1,0:T(8,128)(2,1)S(1)}, u32[]{:S(2)}, u32[]{:S(2)}) collective-permute-start(bf16[1,6,128,128]{3,2,1,0:T(8,128)(2,1)S(1)} %shard_map.59), channel_id=1, source_target_pairs={{0,4},{1,0},{2,6},{3,2},{4,5},{5,1},{6,7},{7,3},{8,9},{9,13},{10,1... | collective-permute-start | bytes 589832 | tf_op jit(solution)/shard_map/ppermute | solution.py:135

commit v23 on v21

--- a/solution.py
+++ b/solution.py
@@ -74,14 +74,19 @@
                         hit = read(cols[p], starts[1 + p], m, l, inner_slots) == column
                         begin = pl.multiple_of((m * inner_slots + l) * block, block)
                         tile = tiles[p][pl.ds(begin, block), :]
-                        right[i, m * block : (m + 1) * block, j * block : (j + 1) * block] = jnp.where(
+                        right[i, (p % 4 * inner_rows + m) * block : (p % 4 * inner_rows + m + 1) * block, j * block : (j + 1) * block] = jnp.where(
                             hit, tile, jnp.zeros_like(tile)
                         )
+            if p % 4 != 3 and p + 1 < parts:
+                continue
+            held = range(p - p % 4, p + 1)
             for i in span:
                 left = jnp.concatenate(
-                    [dense[i, place[1 + p] * inner_rows + m] for m in range(inner_rows)], axis=1
+                    [dense[i, place[1 + h] * inner_rows + m] for h in held for m in range(inner_rows)], axis=1
                 )
-                product = jnp.dot(left, right[i], preferred_element_type=jnp.float32)
+                product = jnp.dot(
+                    left, right[i, : len(held) * inner_rows * block], preferred_element_type=jnp.float32
+                )
                 sums[i] = sums[i] + product if i in sums else product
         for at, i in enumerate(span):
             for j in range(slots):
@@ -184,7 +189,7 @@
                 out_specs=VMEM,
                 scratch_shapes=[
                     pltpu.VMEM((rows, inner_rows * row_count + 1, block, block), dtype),
-                    pltpu.VMEM((rows, inner_rows * block, slots * block), dtype),
+                    pltpu.VMEM((rows, min(4, len(order)) * inner_rows * block, slots * block), dtype),
                     pltpu.SMEM((inner_rows, COLS_DEV), jnp.int32),
                 ],
                 compiler_params=PARAMS,

time: 39.7 us -> 39.7 us (level)
  transfers between devices with their start and end apart: 13 -> 13, of which waited for: 5 -> 5; matrix products, arithmetic and copies ran while one was open for 3% -> 3% of each run, Pallas kernels for 17% -> 16%
where the time goes in v23:
time: 39.7 us; the launch traced here: 39.5 us
  waiting for transfers between devices  18.1 us (46%)
  starting transfers between devices  10.4 us (26%)
  Pallas kernels  6.44 us (16%)
  local copies, waits for them, and re-layouts  3.51 us (9%)
  other arithmetic  0.84 us (2%)
    ppermute x8, waiting for transfers between devices, swap(): return lax.ppermute(x, axis, [(k, k ^ d) for k in range(n)])  13.3 us
    pallas_call x3, Pallas kernels, products(): pl.pallas_call(functools.partial(product_kernel, starts, span, which), ou...  5.27 us
    ppermute x8, starting transfers between devices, swap(): return lax.ppermute(x, axis, [(k, k ^ d) for k in range(n)])  5.22 us
    ppermute x5, starting transfers between devices, permute(): return lax.ppermute(x, ('row', 'col'), pairs)  5.19 us
    ppermute x5, waiting for transfers between devices, permute(): return lax.ppermute(x, ('row', 'col'), pairs)  4.76 us
    unnamed x10, local copies, waits for them, and re-layouts  2.31 us
    pallas_call x2, Pallas kernels, pack(): pl.pallas_call(pack_kernel, out_shape=jax.ShapeDtypeStruct((size + -(-cou...  1.17 us
    slice x10, local copies, waits for them, and re-layouts, index_of(): x[tiles.size // block:, 0]  1.11 us
  transfers between devices with their start and end apart: 13, of which 5 were waited for; matrix products, arithmetic and copies ran while one was open for 3% of the time, Pallas kernels for 16%

profile of v23, /device:TPU:0, one launch (start us, length us, event | category | flops | bytes accessed | tf_op | source)
XLA Modules:
  0.0 39.5 jit_solution(4606274156802368722)
XLA Ops:
  0.0 5.0 %collective-permute-start.6 = (bf16[2048,128]{1,0:T(8,128)(2,1)}, bf16[2048,128]{1,0:T(8,128)(2,1)S(1)}, u32[]{:S(2)}, u32[]{:S(2)}) collective-permute-start(bf16[2048,128]{1,0:T(8,128)(2,1)} %bitcast.17), channel_id=1, source_target_pairs={{0,12},{1,3},{2,14},{3,1},{4,6},{5,9},{6,4},{7,11},{8,10},{9,5},{1... | collective-permute-start | bytes 1572872 | tf_op jit(solution)/shard_map/ppermute | solution.py:122
  5.1 0.9 %copy-done.1 = bf16[2,4,128,128]{3,2,1,0:T(8,128)(2,1)S(1)} copy-done((bf16[2,4,128,128]{3,2,1,0:T(8,128)(2,1)S(1)}, bf16[2,4,128,128]{3,2,1,0:T(8,128)(2,1)}, u32[]{:S(2)}) %copy-start.1) | copy-done | bytes 262168
  6.0 0.7 %copy-done.3 = s32[2,4]{1,0:T(2,128)S(1)} copy-done((s32[2,4]{1,0:T(2,128)S(1)}, s32[2,4]{1,0:T(2,128)}, u32[]{:S(2)}) %copy-start.3) | copy-done | bytes 56
  6.7 0.7 %copy-done.4 = s32[2,6]{1,0:T(2,128)S(1)} copy-done((s32[2,6]{1,0:T(2,128)S(1)}, s32[2,6]{1,0:T(2,128)}, u32[]{:S(2)}) %copy-start.4) | copy-done | bytes 72
  7.4 0.6 %shard_map.55.refs_7_ = bf16[1056,128]{1,0:T(8,128)(2,1)S(1)} custom-call(s32[2,4]{1,0:T(2,128)S(1)} %copy-done.3, s32[2,6]{1,0:T(2,128)S(1)} %copy-done.4, bf16[1024,128]{1,0:T(8,128)(2,1)S(1)} %bitcast.22), custom_call_target="tpu_custom_call" | custom-call | flops 1 | bytes 1 | tf_op jit(solution)/shard_map/pallas_call | solution.py:138
  8.0 1.6 %collective-permute-start = (bf16[1056,128]{1,0:T(8,128)(2,1)S(1)}, bf16[1056,128]{1,0:T(8,128)(2,1)S(1)}, u32[]{:S(2)}, u32[]{:S(2)}) collective-permute-start(bf16[1056,128]{1,0:T(8,128)(2,1)S(1)} %shard_map.55.refs_7_), channel_id=1, source_target_pairs={{0,2},{1,3},{2,0},{3,1},{4,6},{5,7},{6,4},{7,5},{8,10},{9,11},{10,... | collective-permute-start | bytes 811016 | tf_op jit(solution)/shard_map/ppermute | solution.py:114
  9.5 1.0 %collective-permute-start.3 = (s32[2,8]{1,0:T(2,128)S(1)}, s32[2,8]{1,0:T(2,128)S(1)}, u32[]{:S(2)}, u32[]{:S(2)}) collective-permute-start(s32[2,8]{1,0:T(2,128)S(1)} %copy-done.2), channel_id=1, source_target_pairs={{0,12},{4,8},{8,4},{12,0},{1,13},{5,9},{9,5},{13,1},{2,14},{6,10},... | collective-permute-start | bytes 200 | tf_op jit(solution)/shard_map/ppermute | solution.py:114
  10.5 0.6 %shard_map.56 = bf16[2064,128]{1,0:T(8,128)(2,1)S(1)} custom-call(s32[2,8]{1,0:T(2,128)S(1)} %copy-done.2, bf16[2048,128]{1,0:T(8,128)(2,1)S(1)} %bitcast.18), custom_call_target="tpu_custom_call" | custom-call | flops 1 | bytes 1 | tf_op jit(solution)/shard_map/pallas_call | solution.py:138
  11.1 0.1 stack.32.place
  11.2 0.1 slice_reduce_fusion.6
  11.3 4.0 %collective-permute-done.refs_8_ = bf16[1056,128]{1,0:T(8,128)(2,1)S(1)} collective-permute-done((bf16[1056,128]{1,0:T(8,128)(2,1)S(1)}, bf16[1056,128]{1,0:T(8,128)(2,1)S(1)}, u32[]{:S(2)}, u32[]{:S(2)}) %collective-permute-start) | collective-permute-done | bytes 270368 | tf_op jit(solution)/shard_map/ppermute | solution.py:114
  15.3 4.0 %collective-permute-done.7.refs_7_ = bf16[1056,128]{1,0:T(8,128)(2,1)S(1)} collective-permute-done((bf16[1056,128]{1,0:T(8,128)(2,1)S(1)}, bf16[1056,128]{1,0:T(8,128)(2,1)S(1)}, u32[]{:S(2)}, u32[]{:S(2)}) %collective-permute-start.7) | collective-permute-done | bytes 270368 | tf_op jit(solution)/shard_map/ppermute | solution.py:114
  19.3 2.0 %collective-permute-start.8 = (bf16[1056,128]{1,0:T(8,128)(2,1)S(1)}, bf16[1056,128]{1,0:T(8,128)(2,1)S(1)}, u32[]{:S(2)}, u32[]{:S(2)}) collective-permute-start(bf16[1056,128]{1,0:T(8,128)(2,1)S(1)} %collective-permute-done.7.refs_7_), channel_id=1, source_target_pairs={{0,2},{1,3},{2,0},{3,1},{4,6},{5,7},{6,4},{7,5},{8,10},{9,11},{10,... | collective-permute-start | bytes 811016 | tf_op jit(solution)/shard_map/ppermute | solution.py:114
  21.4 0.1 slice_reduce_fusion.4
  21.5 0.1 collective-permute-start.9
  21.6 0.1 slice_reduce_fusion.5
  21.7 0.1 slice_reduce_fusion.7
  21.8 5.3 %collective-permute-done.8.refs_8_ = bf16[1056,128]{1,0:T(8,128)(2,1)S(1)} collective-permute-done((bf16[1056,128]{1,0:T(8,128)(2,1)S(1)}, bf16[1056,128]{1,0:T(8,128)(2,1)S(1)}, u32[]{:S(2)}, u32[]{:S(2)}) %collective-permute-start.8) | collective-permute-done | bytes 270368 | tf_op jit(solution)/shard_map/ppermute | solution.py:114
  27.1 0.1 slice_reduce_fusion.2
  27.2 0.6 %collective-permute-start.10 = (bf16[1056,128]{1,0:T(8,128)(2,1)S(1)}, bf16[1056,128]{1,0:T(8,128)(2,1)S(1)}, u32[]{:S(2)}, u32[]{:S(2)}) collective-permute-start(bf16[1056,128]{1,0:T(8,128)(2,1)S(1)} %collective-permute-done.8.refs_8_), channel_id=1, source_target_pairs={{0,1},{1,0},{2,3},{3,2},{4,5},{5,4},{6,7},{7,6},{8,9},{9,8},{10,11... | collective-permute-start | bytes 811016 | tf_op jit(solution)/shard_map/ppermute | solution.py:114
  27.8 0.1 slice_reduce_fusion.1
  27.9 3.5 %collective-permute-done.5.refs_4_ = bf16[2064,128]{1,0:T(8,128)(2,1)S(1)} collective-permute-done((bf16[2064,128]{1,0:T(8,128)(2,1)S(1)}, bf16[2064,128]{1,0:T(8,128)(2,1)S(1)}, u32[]{:S(2)}, u32[]{:S(2)}) %collective-permute-start.5) | collective-permute-done | bytes 528416 | tf_op jit(solution)/shard_map/ppermute | solution.py:122
  31.4 0.1 slice_reduce_fusion.8
  31.5 0.1 slice_reduce_fusion.9
  31.7 0.1 slice_reduce_fusion
  31.8 1.5 %shard_map.59 = bf16[1,6,128,128]{3,2,1,0:T(8,128)(2,1)S(1)} custom-call(s32[5]{0:T(128)S(1)} %stack.32.place, s32[4,32]{1,0:T(4,128)S(1)} %maximum_convert_fusion.1.left_index, s32[2,8]{1,0:T(2,128)S(1)} %copy-done.2, s32[2,8]{1,0:T(2,128)S(1)} %collective-permute-done.3.refs_1_, s32[2,16]{1,0:T(2,128)S(1)} %maximum_convert_fusion.2.refs_2_, ...), custom_call_target="tpu_custom_call" | custom-call | flops 1 | bytes 1 | tf_op jit(solution)/shard_map/pallas_call | solution.py:185
  33.3 0.1 collective-permute-start.12
  33.4 1.5 %shard_map.58 = bf16[1,6,128,128]{3,2,1,0:T(8,128)(2,1)S(1)} custom-call(s32[5]{0:T(128)S(1)} %stack.32.place, s32[4,32]{1,0:T(4,128)S(1)} %maximum_convert_fusion.1.left_index, s32[2,8]{1,0:T(2,128)S(1)} %copy-done.2, s32[2,8]{1,0:T(2,128)S(1)} %collective-permute-done.3.refs_1_, s32[2,16]{1,0:T(2,128)S(1)} %maximum_convert_fusion.2.refs_2_, ...), custom_call_target="tpu_custom_call" | custom-call | flops 1 | bytes 1 | tf_op jit(solution)/shard_map/pallas_call | solution.py:185
  35.0 0.1 slice_reduce_fusion.3
  35.1 2.2 %shard_map.57 = bf16[2,6,128,128]{3,2,1,0:T(8,128)(2,1)S(1)} custom-call(s32[5]{0:T(128)S(1)} %stack.32.place, s32[4,32]{1,0:T(4,128)S(1)} %maximum_convert_fusion.left_index, s32[2,8]{1,0:T(2,128)S(1)} %copy-done.2, s32[2,8]{1,0:T(2,128)S(1)} %collective-permute-done.3.refs_1_, s32[2,16]{1,0:T(2,128)S(1)} %maximum_convert_fusion.2.refs_2_, ...), custom_call_target="tpu_custom_call" | custom-call | flops 1 | bytes 1 | tf_op jit(solution)/shard_map/pallas_call | solution.py:185
  37.4 1.3 %collective-permute-done.11 = bf16[1,6,128,128]{3,2,1,0:T(8,128)(2,1)S(1)} collective-permute-done((bf16[1,6,128,128]{3,2,1,0:T(8,128)(2,1)S(1)}, bf16[1,6,128,128]{3,2,1,0:T(8,128)(2,1)S(1)}, u32[]{:S(2)}, u32[]{:S(2)}) %collective-permute-start.11) | collective-permute-done | bytes 196640 | tf_op jit(solution)/shard_map/ppermute | solution.py:122
  38.7 0.8 %maximum_select_fusion = bf16[2,6,128,128]{3,2,1,0:T(8,128)(2,1)} fusion(bf16[2,6,128,128]{3,2,1,0:T(8,128)(2,1)S(1)} %shard_map.57, bf16[1,6,128,128]{3,2,1,0:T(8,128)(2,1)S(1)} %collective-permute-done.12, bf16[1,6,128,128]{3,2,1,0:T(8,128)(2,1)S(1)} %collective-permute-done.11, pred[]{:T(512)S(6)} %eq.5), kind=kLoop, calls=%fused_computation | loop fusion | flops 393216 | bytes 1179649 | tf_op jit(solution)/shard_map/jit(_where)/select_n | solution.py:204
  (24 shorter events, 0.2 us)
Async XLA Ops:
  0.0 10.5 %copy-start = (bf16[2,8,128,128]{3,2,1,0:T(8,128)(2,1)S(1)}, bf16[2,8,128,128]{3,2,1,0:T(8,128)(2,1)}, u32[]{:S(2)}) copy-start(bf16[2,8,128,128]{3,2,1,0:T(8,128)(2,1)} %param.7) | copy-start | bytes 1572868
  0.0 19.3 %collective-permute-start.6 = (bf16[2048,128]{1,0:T(8,128)(2,1)}, bf16[2048,128]{1,0:T(8,128)(2,1)S(1)}, u32[]{:S(2)}, u32[]{:S(2)}) collective-permute-start(bf16[2048,128]{1,0:T(8,128)(2,1)} %bitcast.17), channel_id=1, source_target_pairs={{0,12},{1,3},{2,14},{3,1},{4,6},{5,9},{6,4},{7,11},{8,10},{9,5},{1... | collective-permute-start | bytes 1572872 | tf_op jit(solution)/shard_map/ppermute | solution.py:122
  5.1 0.9 %copy-start.1 = (bf16[2,4,128,128]{3,2,1,0:T(8,128)(2,1)S(1)}, bf16[2,4,128,128]{3,2,1,0:T(8,128)(2,1)}, u32[]{:S(2)}) copy-start(bf16[2,4,128,128]{3,2,1,0:T(8,128)(2,1)} %param.5) | copy-start | bytes 786436
  6.0 0.7 %copy-start.3 = (s32[2,4]{1,0:T(2,128)S(1)}, s32[2,4]{1,0:T(2,128)}, u32[]{:S(2)}) copy-start(s32[2,4]{1,0:T(2,128)} %refs_0_.5) | copy-start | bytes 100
  6.7 0.7 %copy-start.4 = (s32[2,6]{1,0:T(2,128)S(1)}, s32[2,6]{1,0:T(2,128)}, u32[]{:S(2)}) copy-start(s32[2,6]{1,0:T(2,128)} %refs_1_.1) | copy-start | bytes 148
  7.4 2.2 %copy-start.2 = (s32[2,8]{1,0:T(2,128)S(1)}, s32[2,8]{1,0:T(2,128)}, u32[]{:S(2)}) copy-start(s32[2,8]{1,0:T(2,128)} %refs_0_.9) | copy-start | bytes 196
  8.0 7.4 %collective-permute-start = (bf16[1056,128]{1,0:T(8,128)(2,1)S(1)}, bf16[1056,128]{1,0:T(8,128)(2,1)S(1)}, u32[]{:S(2)}, u32[]{:S(2)}) collective-permute-start(bf16[1056,128]{1,0:T(8,128)(2,1)S(1)} %shard_map.55.refs_7_), channel_id=1, source_target_pairs={{0,2},{1,3},{2,0},{3,1},{4,6},{5,7},{6,4},{7,5},{8,10},{9,11},{10,... | collective-permute-start | bytes 811016 | tf_op jit(solution)/shard_map/ppermute | solution.py:114
  9.5 5.8 %collective-permute-start.1 = (bf16[1056,128]{1,0:T(8,128)(2,1)S(1)}, bf16[1056,128]{1,0:T(8,128)(2,1)S(1)}, u32[]{:S(2)}, u32[]{:S(2)}) collective-permute-start(bf16[1056,128]{1,0:T(8,128)(2,1)S(1)} %shard_map.55.refs_7_), channel_id=1, source_target_pairs={{0,1},{1,0},{2,3},{3,2},{4,5},{5,4},{6,7},{7,6},{8,9},{9,8},{10,11... | collective-permute-start | bytes 811016 | tf_op jit(solution)/shard_map/ppermute | solution.py:114
  9.5 9.8 %collective-permute-start.7 = (bf16[1056,128]{1,0:T(8,128)(2,1)S(1)}, bf16[1056,128]{1,0:T(8,128)(2,1)S(1)}, u32[]{:S(2)}, u32[]{:S(2)}) collective-permute-start(bf16[1056,128]{1,0:T(8,128)(2,1)S(1)} %shard_map.55.refs_7_), channel_id=1, source_target_pairs={{0,4},{4,0},{8,12},{12,8},{1,5},{5,1},{9,13},{13,9},{2,6},{6,2},{1... | collective-permute-start | bytes 811016 | tf_op jit(solution)/shard_map/ppermute | solution.py:114
  9.5 22.3 %collective-permute-start.3 = (s32[2,8]{1,0:T(2,128)S(1)}, s32[2,8]{1,0:T(2,128)S(1)}, u32[]{:S(2)}, u32[]{:S(2)}) collective-permute-start(s32[2,8]{1,0:T(2,128)S(1)} %copy-done.2), channel_id=1, source_target_pairs={{0,12},{4,8},{8,4},{12,0},{1,13},{5,9},{9,5},{13,1},{2,14},{6,10},... | collective-permute-start | bytes 200 | tf_op jit(solution)/shard_map/ppermute | solution.py:114
  15.3 16.1 %collective-permute-start.5 = (bf16[2064,128]{1,0:T(8,128)(2,1)S(1)}, bf16[2064,128]{1,0:T(8,128)(2,1)S(1)}, u32[]{:S(2)}, u32[]{:S(2)}) collective-permute-start(bf16[2064,128]{1,0:T(8,128)(2,1)S(1)} %shard_map.56), channel_id=1, source_target_pairs={{0,1},{1,9},{2,3},{3,11},{4,12},{5,4},{6,14},{7,6},{8,0},{9,8},{10... | collective-permute-start | bytes 1585160 | tf_op jit(solution)/shard_map/ppermute | solution.py:122
  15.3 16.2 %collective-permute-start.4 = (bf16[2064,128]{1,0:T(8,128)(2,1)S(1)}, bf16[2064,128]{1,0:T(8,128)(2,1)S(1)}, u32[]{:S(2)}, u32[]{:S(2)}) collective-permute-start(bf16[2064,128]{1,0:T(8,128)(2,1)S(1)} %shard_map.56), channel_id=1, source_target_pairs={{0,1},{1,5},{2,3},{3,7},{4,0},{5,4},{6,2},{7,6},{8,12},{9,8},{10,1... | collective-permute-start | bytes 1585160 | tf_op jit(solution)/shard_map/ppermute | solution.py:122
  19.3 7.8 %collective-permute-start.8 = (bf16[1056,128]{1,0:T(8,128)(2,1)S(1)}, bf16[1056,128]{1,0:T(8,128)(2,1)S(1)}, u32[]{:S(2)}, u32[]{:S(2)}) collective-permute-start(bf16[1056,128]{1,0:T(8,128)(2,1)S(1)} %collective-permute-done.7.refs_7_), channel_id=1, source_target_pairs={{0,2},{1,3},{2,0},{3,1},{4,6},{5,7},{6,4},{7,5},{8,10},{9,11},{10,... | collective-permute-start | bytes 811016 | tf_op jit(solution)/shard_map/ppermute | solution.py:114
  21.5 5.8 %collective-permute-start.9 = (bf16[1056,128]{1,0:T(8,128)(2,1)S(1)}, bf16[1056,128]{1,0:T(8,128)(2,1)S(1)}, u32[]{:S(2)}, u32[]{:S(2)}) collective-permute-start(bf16[1056,128]{1,0:T(8,128)(2,1)S(1)} %collective-permute-done.7.refs_7_), channel_id=1, source_target_pairs={{0,1},{1,0},{2,3},{3,2},{4,5},{5,4},{6,7},{7,6},{8,9},{9,8},{10,11... | collective-permute-start | bytes 811016 | tf_op jit(solution)/shard_map/ppermute | solution.py:114
  27.1 7.9 %collective-permute-start.2 = (bf16[1056,128]{1,0:T(8,128)(2,1)S(1)}, bf16[1056,128]{1,0:T(8,128)(2,1)S(1)}, u32[]{:S(2)}, u32[]{:S(2)}) collective-permute-start(bf16[1056,128]{1,0:T(8,128)(2,1)S(1)} %collective-permute-done.refs_8_), channel_id=1, source_target_pairs={{0,1},{1,0},{2,3},{3,2},{4,5},{5,4},{6,7},{7,6},{8,9},{9,8},{10,11... | collective-permute-start | bytes 811016 | tf_op jit(solution)/shard_map/ppermute | solution.py:114
  27.2 4.4 %collective-permute-start.10 = (bf16[1056,128]{1,0:T(8,128)(2,1)S(1)}, bf16[1056,128]{1,0:T(8,128)(2,1)S(1)}, u32[]{:S(2)}, u32[]{:S(2)}) collective-permute-start(bf16[1056,128]{1,0:T(8,128)(2,1)S(1)} %collective-permute-done.8.refs_8_), channel_id=1, source_target_pairs={{0,1},{1,0},{2,3},{3,2},{4,5},{5,4},{6,7},{7,6},{8,9},{9,8},{10,11... | collective-permute-start | bytes 811016 | tf_op jit(solution)/shard_map/ppermute | solution.py:114
  33.3 4.1 %collective-permute-start.12 = (bf16[1,6,128,128]{3,2,1,0:T(8,128)(2,1)S(1)}, bf16[1,6,128,128]{3,2,1,0:T(8,128)(2,1)S(1)}, u32[]{:S(2)}, u32[]{:S(2)}) collective-permute-start(bf16[1,6,128,128]{3,2,1,0:T(8,128)(2,1)S(1)} %shard_map.59), channel_id=1, source_target_pairs={{0,4},{1,0},{2,6},{3,2},{4,5},{5,1},{6,7},{7,3},{8,9},{9,13},{10,1... | collective-permute-start | bytes 589832 | tf_op jit(solution)/shard_map/ppermute | solution.py:122
  34.9 3.8 %collective-permute-start.11 = (bf16[1,6,128,128]{3,2,1,0:T(8,128)(2,1)S(1)}, bf16[1,6,128,128]{3,2,1,0:T(8,128)(2,1)S(1)}, u32[]{:S(2)}, u32[]{:S(2)}) collective-permute-start(bf16[1,6,128,128]{3,2,1,0:T(8,128)(2,1)S(1)} %shard_map.58), channel_id=1, source_target_pairs={{0,4},{1,0},{2,6},{3,2},{4,5},{5,1},{6,7},{7,3},{8,9},{9,13},{10,1... | collective-permute-start | bytes 589832 | tf_op jit(solution)/shard_map/ppermute | solution.py:122
